TPU v7x, 32 devices: a whole 2x2x4 slice. The times are simulated.
32 devices in a mesh: seq: 16 (over z, y, x), head: 2 (over core).
Axes of the slice: x: 2, y: 2, z: 4, core: 2. Of those that a mesh axis runs over, the one named last changes fastest.
Arguments:
- queries: bfloat16 [16384, 1024], P('seq', 'head'), may hold values from -8 to 8
- key_rows: bfloat16 [16384, 1024], P('seq', 'head'), may hold values from -8 to 8
- value_rows: bfloat16 [16384, 1024], P('seq', 'head'), may hold values from -6 to 6
- out_weight: bfloat16 [1024, 1024], P('head'), may hold values from -0.1875 to 0.1875
- cotangent: bfloat16 [16384, 1024], P('seq'), may hold values from -6 to 6
Outputs:
- mixed: bfloat16 [16384, 1024], P('seq', 'head')
- query_grad: bfloat16 [16384, 1024], P('seq', 'head')
- key_grad: bfloat16 [16384, 1024], P('seq', 'head')
- value_grad: bfloat16 [16384, 1024], P('seq', 'head')
- weight_grad: float32 [1024, 1024], P('head')
All inputs are finite; a program needn't handle non-finite values.
Results may differ from a plain program's by a relative error of at most 0.02.
Values may be sent and summed in bfloat16 or wider, within the bound.
No kernel may reach another device: no remote copies, remote signals or barrier semaphores. Data moves between devices by JAX's collectives and lax.ppermute only.
A program may use at most 256 MiB of HBM per device.

v0:
```python
import jax
import jax.numpy as jnp
from jax import lax
from jax.sharding import PartitionSpec as P

DH = 64
LANDMARKS = 256
ITERS = 2


softmax_scale_factor = 0.125


def batched_precise_product(spec, left, right):
    return jnp.einsum(spec, left, right, precision=lax.Precision.HIGHEST)


def pseudo_inverse(amat):
    column_top = lax.stop_gradient(jnp.max(jnp.sum(amat, axis=1), axis=-1))
    current = jnp.swapaxes(amat, 1, 2) / column_top[:, None, None]
    ident = jnp.eye(amat.shape[1], dtype=amat.dtype)
    for iteration in range(ITERS):
        apply_z = batched_precise_product("hij,hjk->hik", amat, current)
        inner = 7.0 * ident - apply_z
        inner = 15.0 * ident - batched_precise_product("hij,hjk->hik", apply_z, inner)
        inner = 13.0 * ident - batched_precise_product("hij,hjk->hik", apply_z, inner)
        current = 0.25 * batched_precise_product("hij,hjk->hik", current, inner)
    return current


def local(queries, key_rows, value_rows, out_weight, cotangent):
    float_single = jnp.float32
    bf16 = jnp.bfloat16
    row_count, columns = queries.shape
    local_heads = columns // DH
    land_dev = LANDMARKS // lax.axis_size("seq")
    seg_len = row_count // land_dev
    own_start = lax.axis_index("seq") * land_dev
    grad_attn = jnp.dot(cotangent, out_weight.T, preferred_element_type=float_single).astype(bf16)
    own_q = jnp.mean(
        queries.astype(float_single).reshape(land_dev, seg_len, columns), axis=1
    ).astype(bf16)
    own_k = jnp.mean(
        key_rows.astype(float_single).reshape(land_dev, seg_len, columns), axis=1
    ).astype(bf16)
    landmark_queries, landmark_keys = (
        lax.all_gather(own_q, "seq", axis=0, tiled=True),
        lax.all_gather(own_k, "seq", axis=0, tiled=True),
    )
    landmark_queries = landmark_queries.reshape(LANDMARKS, local_heads, DH)
    landmark_keys = landmark_keys.reshape(LANDMARKS, local_heads, DH)
    query_heads = queries.reshape(row_count, local_heads, DH)
    key_heads = key_rows.reshape(row_count, local_heads, DH)
    value_heads = value_rows.reshape(row_count, local_heads, DH)
    grad_heads = grad_attn.reshape(row_count, local_heads, DH)
    kernel_f = jax.nn.softmax(
        jnp.einsum("thd,lhd->thl", query_heads, landmark_keys, preferred_element_type=float_single)
        * softmax_scale_factor,
        axis=-1,
    )
    kernel_fb = kernel_f.astype(bf16)
    scores_b = (
        jnp.einsum("lhd,thd->hlt", landmark_queries, key_heads, preferred_element_type=float_single)
        * softmax_scale_factor
    )
    top = lax.pmax(jnp.max(scores_b, axis=-1, keepdims=True), "seq")
    weights_p = jnp.exp(scores_b - top)
    weights_pb = weights_p.astype(bf16)
    partial_values = jnp.einsum(
        "hlt,thd->hld", weights_pb, value_heads, preferred_element_type=float_single
    )
    summed, totals = lax.psum((partial_values, jnp.sum(weights_p, axis=-1, keepdims=True)), "seq")
    landmark_value_rows = summed / totals
    kernel_a = jax.nn.softmax(
        jnp.einsum(
            "jtq,itq->tji", landmark_queries, landmark_keys, preferred_element_type=float_single
        )
        * softmax_scale_factor,
        axis=-1,
    )
    approximate_inverse, pull_back = jax.vjp(pseudo_inverse, kernel_a)
    mixing_matrix = batched_precise_product(
        "yzc,ycw->yzw", approximate_inverse, landmark_value_rows
    )
    mixer_b = mixing_matrix.astype(bf16)
    attn_flat = (
        jnp.einsum("thl,hld->thd", kernel_fb, mixer_b, preferred_element_type=float_single)
        .astype(bf16)
        .reshape(row_count, columns)
    )
    partial_out = jnp.dot(attn_flat, out_weight, preferred_element_type=float_single)
    mixed = (
        lax.psum_scatter(partial_out.astype(jnp.bfloat16), "head", scatter_dimension=1, tiled=True)
        .astype(jnp.float32)
        .astype(bf16)
    )
    weight_grad = lax.psum(
        jnp.dot(attn_flat.T, cotangent, preferred_element_type=float_single), "seq"
    )
    local_mixer_grad = jnp.einsum(
        "thl,thd->hld", kernel_fb, grad_heads, preferred_element_type=float_single
    )
    grad_f = jnp.einsum("thd,hld->thl", grad_heads, mixer_b, preferred_element_type=float_single)
    grad_sf = (kernel_f * (grad_f - jnp.sum(kernel_f * grad_f, axis=-1, keepdims=True))).astype(
        bf16
    )
    query_f = (
        jnp.einsum("thl,lhd->thd", grad_sf, landmark_keys, preferred_element_type=float_single)
        * softmax_scale_factor
    )
    land_k_f = (
        jnp.einsum("thl,thd->lhd", grad_sf, query_heads, preferred_element_type=float_single)
        * softmax_scale_factor
    )
    mixing_matrix_gradient = lax.psum(local_mixer_grad, "seq")
    inverse_matrix_gradient = batched_precise_product(
        "pae,pse->pas", mixing_matrix_gradient, landmark_value_rows
    )
    landmark_value_gradient = batched_precise_product(
        "zer,zeq->zrq", approximate_inverse, mixing_matrix_gradient
    )
    grad_a = pull_back(inverse_matrix_gradient)[0]
    query_kernel_gradient = kernel_a * (grad_a - jnp.sum(kernel_a * grad_a, axis=-1, keepdims=True))
    landmark_query_kernel = (
        batched_precise_product(
            "pgz,zpe->gpe", query_kernel_gradient, landmark_keys.astype(float_single)
        )
        * softmax_scale_factor
    )
    landmark_key_kernel = (
        batched_precise_product(
            "kjg,jki->gki", query_kernel_gradient, landmark_queries.astype(float_single)
        )
        * softmax_scale_factor
    )
    grad_norm = landmark_value_gradient / totals
    grad_norm_b = grad_norm.astype(bf16)
    center = jnp.sum(grad_norm * landmark_value_rows, axis=-1, keepdims=True)
    grad_sb = (
        weights_p
        * (
            jnp.einsum(
                "hld,thd->hlt", grad_norm_b, value_heads, preferred_element_type=float_single
            )
            - center
        )
    ).astype(bf16)
    land_q_b = (
        jnp.einsum("hlt,thd->lhd", grad_sb, key_heads, preferred_element_type=float_single)
        * softmax_scale_factor
    )
    key_b = (
        jnp.einsum("hlt,lhd->thd", grad_sb, landmark_queries, preferred_element_type=float_single)
        * softmax_scale_factor
    )
    value_grad = (
        jnp.einsum("hlt,hld->thd", weights_pb, grad_norm_b, preferred_element_type=float_single)
        .astype(bf16)
        .reshape(row_count, columns)
    )
    own_q_grad, own_k_grad = (
        lax.psum_scatter(land_q_b, "seq", scatter_dimension=0, tiled=True),
        lax.psum_scatter(land_k_f, "seq", scatter_dimension=0, tiled=True),
    )
    own_q_grad = own_q_grad + lax.dynamic_slice_in_dim(
        landmark_query_kernel, own_start, land_dev, 0
    )
    own_k_grad = own_k_grad + lax.dynamic_slice_in_dim(landmark_key_kernel, own_start, land_dev, 0)
    spread_q = (own_q_grad / seg_len).reshape(land_dev, 1, columns)
    spread_k = (own_k_grad / seg_len).reshape(land_dev, 1, columns)
    query_grad = (
        (query_f.reshape(land_dev, seg_len, columns) + spread_q)
        .astype(bf16)
        .reshape(row_count, columns)
    )
    key_grad = (
        (key_b.reshape(land_dev, seg_len, columns) + spread_k)
        .astype(bf16)
        .reshape(row_count, columns)
    )
    return (mixed, query_grad, key_grad, value_grad, weight_grad)


def solution(mesh):
    return jax.shard_map(
        local,
        mesh=mesh,
        in_specs=(
            P("seq", "head"),
            P("seq", "head"),
            P("seq", "head"),
            P("head", None),
            P("seq", None),
        ),
        out_specs=(
            P("seq", "head"),
            P("seq", "head"),
            P("seq", "head"),
            P("seq", "head"),
            P("head", None),
        ),
        check_vma=False,
    )
```

profile of v0, /device:TPU:0, one launch (start us, length us, event | category | flops | bytes accessed | tf_op | source)
XLA Modules:
  0.0 584.4 jit_solution(7936197474963061921)
XLA Ops:
  8.8 43.8 %all_gather.6 = bf16[256,512]{1,0:T(8,128)(2,1)S(1)} all-gather(bf16[16,512]{1,0:T(8,128)(2,1)S(1)} %multiply_convert_fusion.2), channel_id=1, replica_groups=mesh['seq'=16,'head'=2] {'seq'}, dimensions={0}, use_global_device_ids=true | all-gather | bytes 278528 | tf_op jit(solution)/shard_map/all_gather | solution.py:47
  54.3 4.5 multiply_reduce_fusion
  58.8 37.1 %pmax.7 = f32[8,256]{1,0:T(8,128)S(1)} all-reduce(f32[8,256]{1,0:T(8,128)S(1)} %get-tuple-element.36), channel_id=1, replica_groups=mesh['seq'=16,'head'=2] {'seq'}, use_global_device_ids=true, to_apply=%region_7.0 | all-reduce | flops 2048 | bytes 16384 | tf_op jit(solution)/shard_map/pmax | solution.py:66
  98.2 6.0 %fusion.104 = f32[8,256,64]{1,2,0:T(8,128)} fusion(bf16[1024,8,64]{0,2,1:T(8,128)(2,1)} %bitcast.126, f32[8,256,1024]{2,1,0:T(8,128)} %get-tuple-element.37, f32[8,256]{1,0:T(8,128)S(1)} %pmax.7), kind=kOutput, calls=%fused_computation.113 | convolution fusion | flops 274726912 | bytes 9969664 | tf_op jit(solution)/shard_map/hlt,thd->hld/dot_general | solution.py:69
  107.2 4.4 fusion.7
  113.8 42.0 %all_gather.7 = bf16[256,512]{1,0:T(8,128)(2,1)} all-gather(bf16[16,512]{1,0:T(8,128)(2,1)S(1)} %multiply_convert_fusion.1), channel_id=1, replica_groups=mesh['seq'=16,'head'=2] {'seq'}, dimensions={0}, use_global_device_ids=true | all-gather | bytes 278528 | tf_op jit(solution)/shard_map/all_gather | solution.py:48
  169.3 8.1 %online-softmax = f32[8,256,256]{2,1,0:T(8,128)} custom-call(f32[8,256,256]{2,1,0:T(8,128)} %copy-done.13, f32[8,256,256]{2,1,0:T(8,128)} %bitcast_divide_fusion), custom_call_target="tpu_custom_call" | custom-call | tf_op online-softmax
  177.4 4.6 fusion.18
  185.7 3.6 fusion.65
  189.3 8.3 %online-softmax.1 = f32[8,256,256]{2,1,0:T(8,128)} custom-call(f32[8,256,256]{2,1,0:T(8,128)} %copy-done.13, f32[8,256,256]{2,1,0:T(8,128)} %fusion.65), custom_call_target="tpu_custom_call" | custom-call | tf_op online-softmax
  197.6 5.7 fusion.14
  203.3 7.3 %fusion.129 = (f32[1024,8]{0,1:T(8,128)S(1)}, f32[1024,8,256]{0,2,1:T(8,128)}) fusion(bf16[256,8,64]{0,2,1:T(8,128)(2,1)} %bitcast.138, bf16[1024,8,64]{0,2,1:T(8,128)(2,1)} %bitcast.134), kind=kOutput, calls=%fused_computation.144 | convolution fusion | flops 274727168 | bytes 9732096 | tf_op jit(solution)/shard_map/sub | solution.py:56
  220.1 37.3 %psum.29 = f32[8,256]{1,0:T(8,128)S(1)} all-reduce(f32[8,256]{1,0:T(8,128)S(1)} %fusion.7), channel_id=1, replica_groups=mesh['seq'=16,'head'=2] {'seq'}, use_global_device_ids=true, to_apply=%region_10.0 | all-reduce | flops 2048 | bytes 16384 | tf_op jit(solution)/shard_map/psum | solution.py:72
  257.3 5.7 fusion.49
  263.1 3.9 fusion.80
  266.9 4.3 fusion.72
  275.9 5.7 fusion.1
  281.6 4.8 fusion.3
  291.1 117.8 %all-reduce.6.cloned.1.call-done = (f32[8,256,64]{1,2,0:T(8,128)}, f32[512,1024]{1,0:T(8,128)}) async-done(((f32[8,256,64]{1,2,0:T(8,128)}, f32[512,1024]{1,0:T(8,128)}), (f32[8,256,64]{1,2,0:T(8,128)}, f32[512,1024]{1,0:T(8,128)})) %all-reduce.6.cloned.1.call-update) | async-done | bytes 2621456 | tf_op jit(solution)/shard_map/psum | solution.py:115
  412.3 4.8 multiply_convert_fusion
  427.2 4.2 convolution_convert_fusion
  432.3 6.2 %convolution_convert_fusion.1 = bf16[8,64,1024]{2,1,0:T(8,128)(2,1)} fusion(f32[8,256,1024]{2,1,0:T(8,128)} %get-tuple-element.37, f32[8,256]{1,0:T(8,128)S(1)} %pmax.7, bf16[8,256,64]{1,2,0:T(8,128)(2,1)S(1)} %copy-done.41), kind=kOutput, calls=%fused_computation.84 | convolution fusion | flops 275251200 | bytes 9707520 | tf_op jit(solution)/shard_map/hlt,hld->thd/dot_general | solution.py:157
  446.1 3.7 fusion.36
  457.9 3.9 fusion.125
  468.0 3.6 fusion.131
  471.6 4.9 fusion.29
  481.8 4.6 fusion.31
  488.7 3.6 negate_add_fusion
  497.1 5.3 multiply_reduce_fusion.1
  504.8 3.5 fusion.101
  508.3 57.2 %reduce-scatter.6.cloned.1.call-done = f32[16,8,64]{2,1,0:T(8,128)} async-done(((f32[256,8,64]{2,1,0:T(8,128)}), f32[16,8,64]{2,1,0:T(8,128)}) %reduce-scatter.6.cloned.1.call-update) | async-done | bytes 32784 | tf_op jit(solution)/shard_map/reduce_scatter | solution.py:162
  570.8 3.6 reduce-scatter.4.cloned.1.call-done
  (158 shorter events, 105.9 us)
Async XLA Ops:
  7.2 203.4 %copy-start = (bf16[1024,1024]{1,0:T(8,128)(2,1)S(1)}, bf16[1024,1024]{1,0:T(8,128)(2,1)}, u32[]{:S(2)}) copy-start(bf16[1024,1024]{1,0:T(8,128)(2,1)} %param.9) | copy-start | bytes 6291460
  7.2 255.9 %all-reduce.4.cloned.1.call-start = ((), (), s32[]{:S(2)}) async-start(), calls=%async_computation.3 | async-start | bytes 1048576 | tf_op jit(solution)/shard_map/psum | solution.py:72
  52.7 6.1 %copy-start.33 = (bf16[256,512]{0,1:T(8,128)(2,1)}, bf16[256,512]{0,1:T(8,128)(2,1)S(1)}, u32[]{:S(2)}) copy-start(bf16[256,512]{0,1:T(8,128)(2,1)S(1)} %copy.135) | copy-start | bytes 786436
  104.2 304.7 %all-reduce.6.cloned.1.call-start = ((), (), s32[]{:S(2)}) async-start(), calls=%async_computation.7 | async-start | bytes 5242880 | tf_op jit(solution)/shard_map/psum | solution.py:115
  177.4 4.6 copy-start.2
  177.4 4.6 copy-start.30
  182.1 3.6 copy-start.6
  210.6 3.7 copy-start.27
  213.3 3.3 copy-start.46
  266.9 4.4 copy-start.43
  274.9 233.4 %reduce-scatter.8.cloned.1.call-start = ((), (), s32[]{:S(2)}) async-start(), calls=%async_computation.6 | async-start | bytes 1114112 | tf_op jit(solution)/shard_map/reduce_scatter | solution.py:163
  281.6 6.7 %copy-start.35 = (bf16[1024,512]{0,1:T(8,128)(2,1)S(1)}, bf16[1024,512]{0,1:T(8,128)(2,1)}, u32[]{:S(2)}) copy-start(bf16[1024,512]{0,1:T(8,128)(2,1)} %copy.141) | copy-start | bytes 3145732
  289.7 119.2 %copy-start.38 = (f32[8,256,64]{1,2,0:T(8,128)S(1)}, f32[8,256,64]{1,2,0:T(8,128)}, u32[]{:S(2)}) copy-start(f32[8,256,64]{1,2,0:T(8,128)} %all-reduce.4.cloned.1.call-done) | copy-start | bytes 1572868
  291.1 274.4 %reduce-scatter.6.cloned.1.call-start = ((), (), s32[]{:S(2)}) async-start(), calls=%async_computation.5 | async-start | bytes 1114112 | tf_op jit(solution)/shard_map/reduce_scatter | solution.py:162
  408.9 3.3 copy-start.26
  412.2 4.8 copy-start.40
  421.8 152.6 %reduce-scatter.4.cloned.1.call-start = ((), (), s32[]{:S(2)}) async-start(), calls=%async_computation.4 | async-start | bytes 3145728 | tf_op jit(solution)/shard_map/reduce_scatter | solution.py:93
  432.3 6.2 %copy-start.12 = (bf16[8,256,1024]{2,1,0:T(8,128)(2,1)S(1)}, bf16[8,256,1024]{2,1,0:T(8,128)(2,1)}, u32[]{:S(2)}) copy-start(bf16[8,256,1024]{2,1,0:T(8,128)(2,1)} %copy-done.11) | copy-start | bytes 12582916
  432.3 6.2 %copy-start.34 = (bf16[256,512]{0,1:T(8,128)(2,1)S(1)}, bf16[256,512]{0,1:T(8,128)(2,1)}, u32[]{:S(2)}) copy-start(bf16[256,512]{0,1:T(8,128)(2,1)} %copy-done.33) | copy-start | bytes 786436
  442.6 3.5 copy-start.5
  446.1 3.7 copy-start.18
  446.1 3.7 copy-start.32
  454.3 3.5 copy-start.24
  461.7 3.8 copy-start.21
  468.0 3.6 copy-start.22
  468.0 3.6 copy-start.3
  471.6 4.9 copy-start.20
  481.8 4.6 copy-start.19
  488.7 3.6 copy-start.8
  494.6 2.5 copy-start.37
  508.3 61.2 %copy-start.28 = (f32[1024,512]{1,0:T(8,128)S(1)}, f32[1024,512]{1,0:T(8,128)}, u32[]{:S(2)}) copy-start(f32[1024,512]{1,0:T(8,128)} %copy.160) | copy-start | bytes 6291460
  574.4 3.3 copy-start.1
  (20 other events, 38.3 us)
Sparse Core Ops, SparseCore 0:
  104.3 106.3 all-reduce.3
  275.1 133.8 all-reduce.5
  411.9 77.3 reduce-scatter.7
  491.4 74.0 reduce-scatter.5
  568.3 6.0 reduce-scatter.3
where the time goes:
time: 590 us; the launch traced here: 584 us
  waiting for transfers between devices  179 us (30%)
  blocking collectives  160 us (27%)
  matrix products  154 us (26%)
  local copies, waits for them, and re-layouts  34.5 us (6%)
  other arithmetic  25.8 us (4%)
  Pallas kernels  16.4 us (3%)
  between operations  14.7 us (2%)
    psum x1, waiting for transfers between devices, local(): mixing_matrix_gradient = lax.psum(local_mixer_grad, 'seq')  118 us
    dot_general x27, matrix products, batched_precise_product(): return jnp.einsum(spec, left, right, precision=lax.Precision.HIGHEST)  94 us
    reduce_scatter x1, waiting for transfers between devices, local(): lax.psum_scatter(land_q_b, 'seq', scatter_dimension=0, tiled=True)  57.2 us
    all_gather x1, blocking collectives, local(): lax.all_gather(own_q, 'seq', axis=0, tiled=True)  43.8 us
    all_gather x1, blocking collectives, local(): lax.all_gather(own_k, 'seq', axis=0, tiled=True)  42 us
    psum x1, blocking collectives, local(): lax.psum((partial_values, jnp.sum(weights_p, axis=-1, keepdims=True)), 's...  37.3 us
    pmax x1, blocking collectives, local(): top = lax.pmax(jnp.max(scores_b, axis=-1, keepdims=True), 'seq')  37.1 us
    unnamed x99, local copies, waits for them, and re-layouts  21.5 us
  transfers between devices with their start and end apart: 5, of which 3 were waited for; matrix products, arithmetic and copies ran while one was open for 30% of the time, Pallas kernels for 3%

commit v1 on v0

v1 whole, which is shorter than its diff:
```python
import functools

import jax
import jax.numpy as jnp
from jax import lax
from jax.experimental import pallas as pl
from jax.experimental.pallas import tpu as pltpu
from jax.sharding import PartitionSpec as P

DH = 64
PAIR = 2 * DH
LANDMARKS = 256
ITERS = 2
SCALE = 0.125
CHUNK = 128
EXTRA = 16
F32 = jnp.float32
BF16 = jnp.bfloat16
PARAMS = pltpu.CompilerParams(vmem_limit_bytes=24 * 1024 * 1024)


def dot(left, right, dims=((1,), (0,))):
    return lax.dot_general(left, right, (dims, ((), ())), preferred_element_type=F32)


NT = ((1,), (1,))
TN = ((0,), (0,))


def halves(value):
    high = value.astype(BF16)
    return high, (value - high.astype(F32)).astype(BF16)


def dot_exact(left, right, dims=((1,), (0,))):
    return dot(left[0], right[0], dims) + (
        dot(left[0], right[1], dims) + dot(left[1], right[0], dims)
    )


def turned(pair):
    return pair[0].T, pair[1].T


def keep_rows(block, which):
    rows = lax.broadcasted_iota(jnp.int32, block.shape, 0) // DH
    return jnp.where(rows == which, block, jnp.zeros_like(block))


def keep_lanes(block, which):
    lanes = lax.broadcasted_iota(jnp.int32, block.shape, 1) // DH
    return jnp.where(lanes == which, block, jnp.zeros_like(block))


def fold(block, op):
    parts = block.reshape(block.shape[0] // 8, 8, block.shape[1])
    return op(parts, axis=0)


def exchange(block, mask, n):
    return lax.ppermute(block, "seq", [(i, i ^ mask) for i in range(n)])


def bit_groups(n):
    bits = n.bit_length() - 1
    groups = []
    while bits > 0:
        take = 2 if bits % 2 == 0 else 1
        bits -= take
        groups.append((bits, 1 << take))
    return groups


def gather_lists(block, n):
    got = [block]
    held = block[None]
    for shift, size in bit_groups(n):
        if len(got) > 1:
            held = jnp.stack(got, axis=1).reshape((-1,) + block.shape)
        got = [held] + [exchange(held, m << shift, n) for m in range(1, size)]
    return got


def gather_ordered(block, n, me):
    got = gather_lists(block, n)
    held = jnp.stack(got, axis=1).reshape((n,) + block.shape)
    return held.at[jnp.arange(n) ^ me].get(mode="promise_in_bounds")


def split_by_partner(blocks, n, me):
    size = bit_groups(n)[-1][1]
    return [
        blocks.at[(jnp.arange(n // size) * size + m) ^ me].get(mode="promise_in_bounds")
        for m in range(size)
    ]


def scatter_step(pieces, shift, size, n):
    got = [pieces[0]] + [exchange(pieces[m], m << shift, n) for m in range(1, size)]
    return sum(part.astype(F32) for part in got)


def scatter_pieces(pieces, n, groups):
    for step, (shift, size) in enumerate(groups):
        held = scatter_step(pieces, shift, size, n)
        if step + 1 < len(groups):
            following = groups[step + 1][1]
            held = held.astype(BF16).reshape((-1, following) + held.shape[1:])
            pieces = [held[:, m] for m in range(following)]
    return held


def means_kernel(seg_len, q_ref, k_ref, out_ref, in_ref, sum_ref, sems):
    rows, columns = q_ref.shape
    steps = sems.shape[1]
    height = rows // steps
    copies = {}
    for c in range(steps):
        part = pl.ds(c * height, height)
        for side, ref in enumerate((q_ref, k_ref)):
            copies[side, c] = pltpu.make_async_copy(ref.at[part], in_ref.at[side, part], sems.at[side, c])
            copies[side, c].start()
    for c in range(steps):
        for side in range(2):
            copies[side, c].wait()
            span = slice(side * columns, (side + 1) * columns)
            for s in range(c * height // seg_len, (c + 1) * height // seg_len):
                total = fold(in_ref[side, s * seg_len : (s + 1) * seg_len, :].astype(F32), jnp.sum)
                sum_ref[s : s + 1, span] = jnp.sum(total, axis=0, keepdims=True)
    out_ref[...] = (sum_ref[...] * (1.0 / seg_len)).astype(BF16)


def forward_kernel(n, heads, count, me_ref, q_ref, k_ref, v_ref, g_ref, *refs):
    size = bit_groups(n)[-1][1]
    in_refs = refs[:count]
    fb_ref, pb_ref, top_ref, land_ref = refs[count : count + 4]
    out_refs = refs[count + 4 : count + 4 + size]
    score_ref, message_ref = refs[count + 4 + size :]
    pair = pl.program_id(0)
    columns = land_ref.shape[1] // 2

    @pl.when(pair == 0)
    def _():
        for m in range(count):
            held, height, _ = in_refs[m].shape
            for t in range(held):
                at = pl.multiple_of(((t * count + m) ^ me_ref[1]) * height, height)
                land_ref[pl.ds(at, height), :] = in_refs[m][t]

    here = pl.multiple_of(pair * PAIR, PAIR)
    lq_pair = land_ref[:, pl.ds(here, PAIR)]
    lk_pair = land_ref[:, pl.ds(columns + here, PAIR)]
    rows = q_ref.shape[0]
    parts = n // heads
    cols = DH // parts
    gt = g_ref[...].T
    vt = v_ref[...].T
    for h in range(2):
        lk = keep_lanes(lk_pair * SCALE, h).astype(BF16)
        lq = keep_lanes(lq_pair * SCALE, h).astype(BF16)
        span = slice(h * LANDMARKS, (h + 1) * LANDMARKS)
        top = None
        for c in range(0, rows, CHUNK):
            part = slice(c, c + CHUNK)
            sb = dot(k_ref[part, :], lq, NT)
            score_ref[part, :] = sb
            high = fold(sb, jnp.max)
            top = high if top is None else jnp.maximum(top, high)
            sf = dot(q_ref[part, :], lk, NT)
            e = jnp.exp(sf - jnp.max(sf, axis=1, keepdims=True))
            fb_ref[part, span] = (e * (1.0 / jnp.sum(e, axis=1, keepdims=True))).astype(BF16)
        top = jnp.max(top, axis=0, keepdims=True).astype(BF16).astype(F32)
        total = None
        for c in range(0, rows, CHUNK):
            part = slice(c, c + CHUNK)
            p = jnp.exp(score_ref[part, :] - top)
            add = fold(p, jnp.sum)
            total = add if total is None else total + add
            pb_ref[part, span] = p.astype(BF16)
        total = jnp.sum(total, axis=0, keepdims=True)
        top_ref[0, h : h + 1, :] = top
        grads = dot(gt[h * DH : (h + 1) * DH], fb_ref[:, span])
        vals = dot(vt[h * DH : (h + 1) * DH], pb_ref[:, span])
        high, low = halves(total)
        extra = three_rows(top, high.astype(F32), low.astype(F32))
        for p in range(parts):
            cut = slice(p * cols, (p + 1) * cols)
            message_ref[(2 * pair + h) * parts + p] = jnp.concatenate(
                [vals[cut], grads[cut], extra], axis=0
            ).astype(BF16)

    @pl.when(pair == pl.num_programs(0) - 1)
    def _():
        for m in range(size):
            for t in range(n // size):
                out_refs[m][t] = message_ref[(t * size + m) ^ me_ref[0]]


def merge(items, cols):
    tops = [item[2 * cols : 2 * cols + 1] for item in items]
    peak = functools.reduce(jnp.maximum, tops)
    vals = grads = total = 0.0
    for item, top in zip(items, tops):
        factor = jnp.exp(top - peak)
        vals = vals + item[:cols] * factor
        grads = grads + item[cols : 2 * cols]
        total = total + (
            item[2 * cols + 1 : 2 * cols + 2] + item[2 * cols + 2 : 2 * cols + 3]
        ) * factor
    return vals, grads, peak, total


def three_rows(first, second, third):
    row = lax.broadcasted_iota(jnp.int32, (EXTRA, LANDMARKS), 0)
    return jnp.where(row == 0, first, jnp.where(row == 1, second, jnp.where(row == 2, third, 0.0)))


def merge_kernel(cols, count, *refs):
    in_refs, out_refs = refs[:count], refs[count:]
    following = len(out_refs)
    for t in range(in_refs[0].shape[0]):
        vals, grads, peak, total = merge([ref[t].astype(F32) for ref in in_refs], cols)
        high, low = halves(total)
        extra = three_rows(peak, high.astype(F32), low.astype(F32))
        out_refs[t % following][t // following] = jnp.concatenate(
            [vals, grads, extra], axis=0
        ).astype(BF16)


def mix_kernel(cols, count, *refs):
    in_refs, z_ref = refs[:count], refs[count]
    reply_ref, values_ref, grads_ref = refs[count + 1 :]
    vals, grads, peak, total = merge([ref[0].astype(F32) for ref in in_refs], cols)
    inverse = halves(z_ref[0])
    values = vals / total
    mixer = dot_exact(halves(values), inverse, NT)
    norm = dot_exact(halves(grads), inverse) / total
    high, low = halves(jnp.sum(norm * values, axis=0, keepdims=True))
    extra = three_rows(peak, high.astype(F32), low.astype(F32))
    reply_ref[0] = jnp.concatenate([mixer, norm, extra], axis=0).astype(BF16)
    values_ref[...] = values
    grads_ref[...] = grads


def soft_rows(scores):
    e = jnp.exp(scores - jnp.max(scores, axis=1, keepdims=True))
    return e / jnp.sum(e, axis=1, keepdims=True)


def eye():
    shape = (LANDMARKS, LANDMARKS)
    same = lax.broadcasted_iota(jnp.int32, shape, 0) == lax.broadcasted_iota(jnp.int32, shape, 1)
    return same.astype(F32)


def column_top(amat):
    return jnp.max(jnp.sum(amat, axis=0, keepdims=True), axis=1, keepdims=True)


def newton_kernel(own_ref, lq_ref, lk_ref, saved_ref, z_ref):
    which = own_ref[1]
    amat = soft_rows(dot(keep_lanes(lq_ref[...] * SCALE, which).astype(BF16), lk_ref[...], NT))
    saved_ref[0] = amat
    current = amat.T / column_top(amat)
    ident = eye()
    amat = halves(amat)
    for i in range(ITERS):
        saved_ref[1 + 4 * i] = current
        z = halves(current)
        x_full = dot_exact(amat, z)
        saved_ref[2 + 4 * i] = x_full
        x = halves(x_full)
        inner = 15.0 * ident - dot_exact(x, halves(7.0 * ident - x_full))
        saved_ref[3 + 4 * i] = inner
        inner = 13.0 * ident - dot_exact(x, halves(inner))
        saved_ref[4 + 4 * i] = inner
        current = 0.25 * dot_exact(z, halves(inner))
    z_ref[0] = current


def newton_grad_kernel(own_ref, saved_ref, values_ref, grads_ref, lq_ref, lk_ref, q_ref, k_ref):
    which = own_ref[1]
    ident = eye()
    amat = saved_ref[0]
    amat_t = turned(halves(amat))
    grad_z = dot_exact(halves(grads_ref[...]), halves(values_ref[...]), TN)
    grad_a = jnp.zeros_like(amat)
    for i in reversed(range(ITERS)):
        z = halves(saved_ref[1 + 4 * i])
        x_full = saved_ref[2 + 4 * i]
        x_t = turned(halves(x_full))
        first = halves(7.0 * ident - x_full)
        second = halves(saved_ref[3 + 4 * i])
        third = halves(saved_ref[4 + 4 * i])
        dz = halves(0.25 * grad_z)
        d_third = halves(dot_exact(turned(z), dz))
        d_second = halves(-dot_exact(x_t, d_third))
        d_x = -dot_exact(d_third, second, NT) - dot_exact(d_second, first, NT)
        d_x = halves(d_x + dot_exact(x_t, d_second))
        grad_a = grad_a + dot_exact(d_x, z, NT)
        grad_z = dot_exact(dz, third, NT) + dot_exact(amat_t, d_x)
    grad_a = grad_a + grad_z.T / column_top(amat)
    grad_s = amat * (grad_a - jnp.sum(amat * grad_a, axis=1, keepdims=True)) * SCALE
    high, low = halves(grad_s)
    lq = keep_lanes(lq_ref[...], which)
    lk = keep_lanes(lk_ref[...], which)
    q_ref[...] = dot(high, lk) + dot(low, lk)
    k_ref[...] = dot(high.T, lq) + dot(low.T, lq)


def attend_kernel(n, heads, me_ref, fb_ref, top_ref, cot_ref, *refs):
    size = bit_groups(n)[-1][1]
    parts = n // heads
    cols = DH // parts
    reply_refs = refs[:size]
    attn_ref, mixer_ref, norm_ref, center_ref = refs[size : size + 4]
    out_refs = refs[size + 4 : 2 * size + 4]
    w_ref, d_ref, e_ref, sum_ref, all_ref = refs[2 * size + 4 :]
    pair = pl.program_id(0)

    @pl.when(pair == 0)
    def _():
        for m in range(size):
            for t in range(n // size):
                reply = reply_refs[m][t].astype(F32)
                at = (t * size + m) ^ me_ref[0]
                w_ref[at] = reply[:cols]
                d_ref[at] = reply[cols : 2 * cols]
                e_ref[at] = reply[2 * cols : 2 * cols + 8]
        for h in range(heads):
            cut = slice(h * parts, (h + 1) * parts)
            span = slice(h * DH, (h + 1) * DH)
            mixer_ref[span, :] = w_ref[cut].reshape(DH, LANDMARKS).astype(BF16)
            extra = e_ref[cut]
            top = top_ref[h // 2, h % 2 : h % 2 + 1, :]
            factor = jnp.exp(top - extra[0, 0:1, :])
            norm_ref[span, :] = (d_ref[cut].reshape(DH, LANDMARKS) * factor).astype(BF16)
            sums = jnp.sum(extra, axis=0)
            center_ref[h : h + 1, :] = (sums[1:2] + sums[2:3]) * factor

    mixer = mixer_ref[pl.ds(pl.multiple_of(pair * PAIR, PAIR), PAIR), :]
    attn = dot(fb_ref[:, :LANDMARKS], keep_rows(mixer, 0), NT) + dot(
        fb_ref[:, LANDMARKS:], keep_rows(mixer, 1), NT
    )
    attn = attn.astype(BF16)
    attn_ref[...] = attn
    all_ref[pl.ds(pl.multiple_of(pair * PAIR, PAIR), PAIR), :] = attn.T

    @pl.when(pair == pl.num_programs(0) - 1)
    def _():
        block, split = sum_ref.shape[1], n // sum_ref.shape[0]
        width = cot_ref.shape[1]
        sum_ref[...] = dot(all_ref[...], cot_ref[...]).reshape(sum_ref.shape)
        for m in range(size):
            for t in range(n // size):
                at = (t * size + m) ^ me_ref[0]
                if split == 1:
                    out_refs[m][t] = sum_ref[at].astype(BF16)
                else:
                    side = pl.multiple_of((at % split) * (width // split), width // split)
                    out_refs[m][t] = sum_ref[at // split, :, pl.ds(side, width // split)].astype(BF16)


def query_kernel(own_ref, q_ref, g_ref, fb_ref, lk_ref, mixer_ref, more_ref, out_ref, land_ref, ds_ref):
    rows = q_ref.shape[0]
    lk = lk_ref[...] * SCALE
    for h in range(2):
        span = slice(h * LANDMARKS, (h + 1) * LANDMARKS)
        mixer = keep_rows(mixer_ref[...], h)
        for c in range(0, rows, CHUNK):
            part = slice(c, c + CHUNK)
            f = fb_ref[part, span].astype(F32)
            df = dot(g_ref[part, :], mixer)
            ds_ref[part, span] = (f * (df - jnp.sum(f * df, axis=1, keepdims=True))).astype(BF16)
    out_ref[...] = (
        dot(ds_ref[:, :LANDMARKS], keep_lanes(lk, 0).astype(BF16))
        + dot(ds_ref[:, LANDMARKS:], keep_lanes(lk, 1).astype(BF16))
    ).astype(BF16)
    qt = q_ref[...].T
    sums = jnp.concatenate(
        [dot(qt[:DH], ds_ref[:, :LANDMARKS]), dot(qt[DH:], ds_ref[:, LANDMARKS:])], axis=0
    )
    here = (own_ref[0] == pl.program_id(0)).astype(F32)
    land_ref[...] = (sums.T * SCALE + more_ref[...] * here).astype(BF16)


def key_half_kernel(
    first, own_ref, k_ref, v_ref, pb_ref, lq_ref, norm_ref, center_ref, more_ref, *refs
):
    out_ref, value_ref, land_ref, ds_ref = refs[-4:]
    key_pair(first, own_ref, k_ref, v_ref, pb_ref, lq_ref, norm_ref, center_ref, more_ref, out_ref, value_ref, land_ref, ds_ref)


def key_rest_kernel(
    first, own_ref, k_ref, v_ref, pb_ref, lq_ref, norm_ref, center_ref, more_ref, *refs
):
    early_ref, other_ref, _, _, out_ref, value_ref = refs[:6]
    out_refs, (land_ref, ds_ref) = refs[6:-2], refs[-2:]
    size = len(out_refs)
    columns = other_ref.shape[1]
    pair = pl.program_id(0)
    at_pair = pl.ds(pl.multiple_of(pair * PAIR, PAIR), PAIR)
    key_pair(
        first, own_ref, k_ref, v_ref, pb_ref, lq_ref, norm_ref, center_ref, more_ref,
        out_ref, value_ref, land_ref.at[:, at_pair], ds_ref,
    )

    @pl.when(pair == pl.num_programs(0) - 1)
    def _():
        early = early_ref.shape[1]
        for m in range(size):
            held, height, _ = out_refs[m].shape
            for t in range(held):
                at = pl.multiple_of(((t * size + m) ^ own_ref[2]) * height, height)
                out_refs[m][t, :, :early] = early_ref[pl.ds(at, height), :]
                out_refs[m][t, :, early:columns] = land_ref[pl.ds(at, height), :]
                out_refs[m][t, :, columns:] = other_ref[pl.ds(at, height), :]


def key_pair(
    first, own_ref, k_ref, v_ref, pb_ref, lq_ref, norm_ref, center_ref, more_ref, out_ref, value_ref, land_ref, ds_ref
):
    rows = k_ref.shape[0]
    lq = lq_ref[...] * SCALE
    pair = first + pl.program_id(0)
    for h in range(2):
        span = slice(h * LANDMARKS, (h + 1) * LANDMARKS)
        norm = keep_rows(norm_ref[...], h)
        center = center_ref[pl.ds(2 * pair + h, 1), :]
        for c in range(0, rows, CHUNK):
            part = slice(c, c + CHUNK)
            dp = dot(v_ref[part, :], norm)
            ds_ref[part, span] = (pb_ref[part, span].astype(F32) * (dp - center)).astype(BF16)
    out_ref[...] = (
        dot(ds_ref[:, :LANDMARKS], keep_lanes(lq, 0).astype(BF16))
        + dot(ds_ref[:, LANDMARKS:], keep_lanes(lq, 1).astype(BF16))
    ).astype(BF16)
    value_ref[...] = (
        dot(pb_ref[:, :LANDMARKS], keep_rows(norm_ref[...], 0), NT)
        + dot(pb_ref[:, LANDMARKS:], keep_rows(norm_ref[...], 1), NT)
    ).astype(BF16)
    kt = k_ref[...].T
    sums = jnp.concatenate(
        [dot(kt[:DH], ds_ref[:, :LANDMARKS]), dot(kt[DH:], ds_ref[:, LANDMARKS:])], axis=0
    )
    here = (own_ref[0] == pair).astype(F32)
    land_ref[...] = (sums.T * SCALE + more_ref[...] * here).astype(BF16)


def unpack_kernel(size, split, me_ref, *refs):
    out_ref = refs[-1]
    block, width = refs[0].shape[1:]
    for m in range(size):
        at = m ^ (me_ref[0] % size)
        row = pl.ds(pl.multiple_of((at // split) * block, block), block)
        column = pl.ds(pl.multiple_of((at % split) * width, width), width)
        if split == 1:
            out_ref[row, :] = refs[m][0].astype(F32)
        else:
            out_ref[row, column] = refs[m][0].astype(F32)


def held_in_hbm(x):
    return pltpu.with_memory_space_constraint(x, pltpu.HBM)


def whole(shape):
    return pl.BlockSpec(shape, lambda *_: (0,) * len(shape))


def shape_of(shape, dtype):
    return jax.ShapeDtypeStruct(shape, dtype)


def call(kernel, grid, scalars, ins, in_specs, outs, out_specs, scratch=(), flops=0, name=None, aliases={}):
    return pl.pallas_call(
        kernel,
        grid_spec=pltpu.PrefetchScalarGridSpec(
            num_scalar_prefetch=len(scalars),
            grid=grid,
            in_specs=in_specs,
            out_specs=out_specs,
            scratch_shapes=list(scratch),
        ),
        out_shape=outs,
        compiler_params=PARAMS,
        input_output_aliases=aliases,
        cost_estimate=pl.CostEstimate(flops=flops, bytes_accessed=4 << 20, transcendentals=0),
        name=name,
    )(*scalars, *ins)


def local(queries, key_rows, value_rows, out_weight, cotangent):
    rows, columns = queries.shape
    width = out_weight.shape[1]
    heads = columns // DH
    pairs = columns // PAIR
    n = lax.axis_size("seq")
    me = lax.axis_index("seq")
    mine = lax.axis_index("head")
    land_dev = LANDMARKS // n
    seg_len = rows // land_dev
    parts = n // heads
    cols = DH // parts
    size = bit_groups(n)[-1][1]
    height = 2 * cols + EXTRA
    own_head = me // parts
    own_arr = jnp.stack([own_head // 2, own_head % 2, me * 0 if land_dev % 16 else me]).astype(jnp.int32)

    steps = 4
    in_hbm = pl.BlockSpec(memory_space=pltpu.HBM)
    own = call(
        functools.partial(means_kernel, seg_len),
        (1,),
        [],
        [held_in_hbm(queries), held_in_hbm(key_rows)],
        [in_hbm, in_hbm],
        shape_of((land_dev, 2 * columns), BF16),
        whole((land_dev, 2 * columns)),
        [
            pltpu.VMEM((2, rows, columns), BF16),
            pltpu.VMEM((land_dev, 2 * columns), F32),
            pltpu.SemaphoreType.DMA((2, steps)),
        ],
        name="means",
    )
    grad_attn = dot(cotangent, out_weight, NT).astype(BF16)
    sorted_here = land_dev % 16 == 0
    if sorted_here:
        lands = gather_lists(own, n)
    else:
        lands = [gather_ordered(own, n, me).reshape(LANDMARKS // 16, 16, 2 * columns)]
    me_arr = jnp.stack([me, me if sorted_here else me * 0]).astype(jnp.int32)

    token_pair = pl.BlockSpec((rows, PAIR), lambda j, *_: (0, j))
    factor_pair = pl.BlockSpec((rows, 2 * LANDMARKS), lambda j, *_: (0, j))
    lq_pair = pl.BlockSpec((LANDMARKS, PAIR), lambda j, *_: (0, j))
    lk_pair = pl.BlockSpec((LANDMARKS, PAIR), lambda j, *_: (0, j + pairs))
    factors = pltpu.HBM((rows, heads * LANDMARKS), BF16)
    piece = shape_of((n // size, height, LANDMARKS), BF16)

    fb, pb, tops, land, *pieces = call(
        functools.partial(forward_kernel, n, heads, len(lands)),
        (pairs,),
        [me_arr],
        [held_in_hbm(x) for x in (queries, key_rows, value_rows, grad_attn)] + lands,
        [token_pair] * 4 + [whole(lands[0].shape)] * len(lands),
        [
            factors,
            factors,
            shape_of((pairs, 8, LANDMARKS), F32),
            shape_of((LANDMARKS, 2 * columns), BF16),
        ]
        + [piece] * size,
        [
            factor_pair,
            factor_pair,
            pl.BlockSpec((1, 8, LANDMARKS), lambda j, *_: (j, 0, 0)),
            whole((LANDMARKS, 2 * columns)),
        ]
        + [whole(piece.shape)] * size,
        [
            pltpu.VMEM((rows, LANDMARKS), F32),
            pltpu.VMEM((n, height, LANDMARKS), BF16),
        ],
        flops=8 << 30,
        name="forward",
    )

    square = (LANDMARKS, LANDMARKS)
    own_lq = pl.BlockSpec((LANDMARKS, PAIR), lambda i, own: (0, own[0]))
    own_lk = pl.BlockSpec((LANDMARKS, PAIR), lambda i, own: (0, own[0] + pairs))
    kept = shape_of((1 + 4 * ITERS,) + square, F32)
    saved, inverse = call(
        newton_kernel,
        (1,),
        [own_arr],
        [land, land],
        [own_lq, own_lk],
        [kept, shape_of((1,) + square, F32)],
        [whole(kept.shape), whole((1,) + square)],
        flops=4 << 30,
        name="newton",
    )

    groups = bit_groups(n)[::-1]
    for step, (shift, count) in enumerate(groups):
        got = [pieces[0]] + [exchange(pieces[m], m << shift, n) for m in range(1, count)]
        specs = [whole(got[0].shape)] * count
        if step == 0:
            got, inverse, saved = lax.optimization_barrier((got, inverse, saved))
        if step + 1 < len(groups):
            following = groups[step + 1][1]
            piece = shape_of((got[0].shape[0] // following, height, LANDMARKS), BF16)
            pieces = call(
                functools.partial(merge_kernel, cols, count),
                (1,),
                [],
                got,
                specs,
                [piece] * following,
                [whole(piece.shape)] * following,
                name="merge",
            )
    small = shape_of((cols, LANDMARKS), F32)
    reply, values, grads = call(
        functools.partial(mix_kernel, cols, count),
        (1,),
        [],
        got + [inverse],
        specs + [whole((1,) + square)],
        [piece, small, small],
        [whole(piece.shape), whole(small.shape), whole(small.shape)],
        name="mix",
    )
    replies = gather_lists(reply[0], n)

    more = shape_of((LANDMARKS, PAIR), F32)
    more_q, more_k = call(
        newton_grad_kernel,
        (1,),
        [own_arr],
        [saved, values, grads, land, land],
        [whole(kept.shape), whole(small.shape), whole(small.shape), own_lq, own_lk],
        [more, more],
        [whole(more.shape)] * 2,
        flops=8 << 30,
        name="newton_grad",
    )

    block = max(columns // n, 16)
    split = n * block // columns
    flat = shape_of((columns, LANDMARKS), BF16)
    weight_piece = shape_of((n // size, block, width // split), BF16)
    attn, mixer, norm, center, *weight_pieces = call(
        functools.partial(attend_kernel, n, heads),
        (pairs,),
        [me_arr],
        [fb, tops, cotangent] + replies,
        [factor_pair, whole(tops.shape), whole(cotangent.shape)] + [whole(replies[0].shape)] * size,
        [shape_of((rows, columns), BF16), flat, flat, shape_of((heads, LANDMARKS), F32)]
        + [weight_piece] * size,
        [token_pair, whole(flat.shape), whole(flat.shape), whole((heads, LANDMARKS))]
        + [whole(weight_piece.shape)] * size,
        [
            pltpu.VMEM((n, cols, LANDMARKS), F32),
            pltpu.VMEM((n, cols, LANDMARKS), F32),
            pltpu.VMEM((n, 8, LANDMARKS), F32),
            pltpu.VMEM((columns // block, block, width), F32),
            pltpu.VMEM((columns, rows), BF16),
        ],
        flops=4 << 30,
        name="attend",
    )
    (shift, count), later = groups[0], groups[1:]
    weight_sum = scatter_step(weight_pieces, shift, count, n).astype(BF16)
    (pb, key_rows, value_rows), weight_sum = lax.optimization_barrier(
        ((pb, key_rows, value_rows), weight_sum)
    )
    following = later[0][1]
    weight_sum = weight_sum.reshape((-1, following) + weight_sum.shape[1:])
    weight_own = scatter_pieces([weight_sum[:, m] for m in range(following)], n, later)[0].astype(BF16)
    half = width // 2
    there = dot(attn, lax.dynamic_slice_in_dim(out_weight, (1 - mine) * half, half, 1))
    arrived = lax.ppermute(there.astype(BF16), "head", [(0, 1), (1, 0)])
    here = dot(attn, lax.dynamic_slice_in_dim(out_weight, mine * half, half, 1))
    mixed = (here + arrived.astype(F32)).astype(BF16)

    flat_pair = pl.BlockSpec((PAIR, LANDMARKS), lambda j, *_: (j, 0))
    land_pair = pl.BlockSpec((LANDMARKS, PAIR), lambda j, *_: (0, j))
    tokens = shape_of((rows, columns), BF16)
    land_shape = shape_of((LANDMARKS, columns), BF16)
    products = [pltpu.VMEM((rows, 2 * LANDMARKS), BF16)]
    query_f, land_k = call(
        query_kernel,
        (pairs,),
        [own_arr],
        [queries, grad_attn, fb, land, mixer, more_k],
        [token_pair, token_pair, factor_pair, lk_pair, flat_pair, whole(more.shape)],
        [tokens, land_shape],
        [token_pair, land_pair],
        products,
        flops=6 << 30,
        name="query_grad",
    )
    if sorted_here:
        land_piece, count = shape_of((n // size, land_dev, 2 * columns), BF16), size
    else:
        land_piece, count = shape_of((LANDMARKS // 16, 16, 2 * columns), BF16), 1
    some = pairs // 2
    key_in = [key_rows, value_rows, pb, land, norm, center, more_q]

    def key_specs(first):
        pair_of = lambda j, *_: (0, j + first)
        tokens_at = pl.BlockSpec((rows, PAIR), pair_of)
        factors_at = pl.BlockSpec((rows, 2 * LANDMARKS), pair_of)
        land_at = pl.BlockSpec((LANDMARKS, PAIR), pair_of)
        flat_at = pl.BlockSpec((PAIR, LANDMARKS), lambda j, *_: (j + first, 0))
        return [tokens_at, tokens_at, factors_at, land_at, flat_at, whole((heads, LANDMARKS)), whole(more.shape)]

    specs = key_specs(0)
    half_shape = shape_of((LANDMARKS, some * PAIR), BF16)
    tokens_hbm = pltpu.HBM((rows, columns), BF16)
    key_b, value_grad, land_early = call(
        functools.partial(key_half_kernel, 0),
        (some,),
        [own_arr],
        key_in,
        specs,
        [tokens_hbm, tokens_hbm, half_shape],
        [specs[0], specs[0], land_pair],
        products,
        flops=3 << 30,
        name="key_grad",
    )
    (pb, land_early), weight_own = lax.optimization_barrier(((pb, land_early), weight_own))
    key_in[2] = pb
    specs = key_specs(some)
    key_b, value_grad, *land_pieces = call(
        functools.partial(key_rest_kernel, some),
        (pairs - some,),
        [own_arr],
        key_in + [land_early, land_k, held_in_hbm(key_b), held_in_hbm(value_grad)],
        specs + [whole(half_shape.shape), whole(land_shape.shape), in_hbm, in_hbm],
        [tokens_hbm, tokens_hbm] + [land_piece] * count,
        [specs[0], specs[0]] + [whole(land_piece.shape)] * count,
        [pltpu.VMEM((LANDMARKS, (pairs - some) * PAIR), BF16)] + products,
        flops=3 << 30,
        name="key_grad_rest",
        aliases={len(key_in) + 3: 0, len(key_in) + 4: 1},
    )
    if not sorted_here:
        land_pieces = split_by_partner(land_pieces[0].reshape(n, land_dev, 2 * columns), n, me)
    land_own = scatter_pieces(land_pieces, n, groups)[0] * (1.0 / seg_len)

    def finish(token_part, land_part):
        return (
            (token_part.reshape(land_dev, seg_len, columns) + land_part[:, None, :])
            .astype(BF16)
            .reshape(rows, columns)
        )

    weights = gather_lists(weight_own, n)
    weights, mixed = lax.optimization_barrier((weights, mixed))
    weight_grad = call(
        functools.partial(unpack_kernel, size, split),
        (n // size,),
        [me_arr],
        weights,
        [pl.BlockSpec((1,) + weights[0].shape[1:], lambda t, me: (t, 0, 0))] * size,
        shape_of((columns, width), F32),
        pl.BlockSpec((size * block // split, width), lambda t, me: (t ^ (me[0] // size), 0)),
        name="unpack",
    )
    query_grad = finish(query_f, land_own[:, :columns])
    key_grad = finish(key_b, land_own[:, columns:])
    return (mixed, query_grad, key_grad, value_grad, weight_grad)


def solution(mesh):
    return jax.shard_map(
        local,
        mesh=mesh,
        in_specs=(
            P("seq", "head"),
            P("seq", "head"),
            P("seq", "head"),
            P("head", None),
            P("seq", None),
        ),
        out_specs=(
            P("seq", "head"),
            P("seq", "head"),
            P("seq", "head"),
            P("seq", "head"),
            P("head", None),
        ),
        check_vma=False,
    )
```

time: 590 us -> 128 us (0.22)
  blocking collectives: 160 us -> 0 us
  waiting for transfers between devices: 179 us -> 24.4 us
  matrix products: 154 us -> 6.86 us
  starting transfers between devices: 0.21 us -> 46.4 us
  local copies, waits for them, and re-layouts: 34.5 us -> 3.15 us
  Pallas kernels: 16.4 us -> 43.3 us
  other arithmetic: 25.8 us -> 2.26 us
  between operations: 14.7 us -> 0.91 us
    dot_general x42 -> x3, matrix products: 147 us -> 6.86 us  [dot(): lax.dot_general(left, right, (dims, ((), ())), preferred_element_type=F32)]
    psum x2 -> x0, waiting for transfers between devices: 118 us -> none  [the longest x1 118 us: local(): mixing_matrix_gradient = lax.psum(local_mixer_grad, 'seq')]
    all_gather x2 -> x0, blocking collectives: 85.7 us -> none  [the longest x1 43.8 us: local(): lax.all_gather(own_q, 'seq', axis=0, tiled=True)]
    reduce_scatter x3 -> x0, waiting for transfers between devices: 60.8 us -> none  [the longest x1 57.2 us: local(): lax.psum_scatter(land_q_b, 'seq', scatter_dimension=0, tiled=True)]
    ppermute x0 -> x37, starting transfers between devices: none -> 46.4 us  [the longest x36 46.4 us: exchange(): return lax.ppermute(block, 'seq', [(i, i ^ mask) for i in range(n)])]
    pallas_call x0 -> x11, Pallas kernels: none -> 43.3 us  [call(): pl.pallas_call(kernel, grid_spec=pltpu.PrefetchScalarGridSpec(num_scalar_...]
    psum x1 -> x0, blocking collectives: 37.3 us -> none  [local(): lax.psum((partial_values, jnp.sum(weights_p, axis=-1, keepdims=True)), 's...]
    pmax x1 -> x0, blocking collectives: 37.1 us -> none  [local(): top = lax.pmax(jnp.max(scores_b, axis=-1, keepdims=True), 'seq')]
  transfers between devices with their start and end apart: 5 -> 37, of which waited for: 3 -> 15; matrix products, arithmetic and copies ran while one was open for 30% -> 7% of each run, Pallas kernels for 3% -> 14%
where the time goes in v1:
time: 128 us; the launch traced here: 127 us
  starting transfers between devices  46.4 us (36%)
  Pallas kernels  43.3 us (34%)
  waiting for transfers between devices  24.4 us (19%)
  matrix products  6.86 us (5%)
  local copies, waits for them, and re-layouts  3.15 us (2%)
  other arithmetic  2.26 us (2%)
    ppermute x36, starting transfers between devices, exchange(): return lax.ppermute(block, 'seq', [(i, i ^ mask) for i in range(n)])  46.4 us
    pallas_call x11, Pallas kernels, call(): pl.pallas_call(kernel, grid_spec=pltpu.PrefetchScalarGridSpec(num_scalar_...  43.3 us
    ppermute x36, waiting for transfers between devices, exchange(): return lax.ppermute(block, 'seq', [(i, i ^ mask) for i in range(n)])  24.4 us
    dot_general x3, matrix products, dot(): lax.dot_general(left, right, (dims, ((), ())), preferred_element_type=F32)  6.86 us
    unnamed x28, local copies, waits for them, and re-layouts  3.12 us
  transfers between devices with their start and end apart: 37, of which 15 were waited for; matrix products, arithmetic and copies ran while one was open for 7% of the time, Pallas kernels for 14%

profile of v1, /device:TPU:0, one launch (start us, length us, event | category | flops | bytes accessed | tf_op | source)
XLA Modules:
  0.0 127.3 jit_solution(514434412769905208)
XLA Ops:
  0.7 1.8 %means.1 = bf16[16,1024]{1,0:T(8,128)(2,1)S(1)} custom-call(bf16[1024,512]{1,0:T(8,128)(2,1)} %q_ref.5, bf16[1024,512]{1,0:T(8,128)(2,1)} %k_ref.5), custom_call_target="tpu_custom_call" | custom-call | bytes 4194304 | tf_op jit(solution)/shard_map/means/pallas_call | solution.py:476
  2.5 5.1 %collective-permute-start.2 = (bf16[1,16,1024]{2,1,0:T(8,128)(2,1)S(1)}, bf16[1,16,1024]{2,1,0:T(8,128)(2,1)S(1)}, u32[]{:S(2)}, u32[]{:S(2)}) collective-permute-start(bf16[1,16,1024]{2,1,0:T(8,128)(2,1)S(1)} %bitcast.64), channel_id=1, source_target_pairs={{0,24},{2,26},{4,28},{6,30},{8,16},{10,18},{12,20},{14,22},{16,8},... | collective-permute-start | bytes 98312 | tf_op jit(solution)/shard_map/ppermute | solution.py:61
  8.2 2.3 %convolution_convert_fusion.g_ref = bf16[1024,512]{1,0:T(8,128)(2,1)} fusion(bf16[1024,1024]{1,0:T(8,128)(2,1)S(1)} %copy-done.3, bf16[512,1024]{1,0:T(8,128)(2,1)S(1)} %copy-done), kind=kOutput, calls=%fused_computation.5 | convolution fusion | flops 1074266112 | bytes 4194304 | tf_op jit(solution)/shard_map/dot_general | solution.py:23
  10.5 1.9 %collective-permute-done.1 = bf16[1,16,1024]{2,1,0:T(8,128)(2,1)S(1)} collective-permute-done((bf16[1,16,1024]{2,1,0:T(8,128)(2,1)S(1)}, bf16[1,16,1024]{2,1,0:T(8,128)(2,1)S(1)}, u32[]{:S(2)}, u32[]{:S(2)}) %collective-permute-start.1) | collective-permute-done | bytes 32800 | tf_op jit(solution)/shard_map/ppermute | solution.py:61
  12.4 2.5 %collective-permute-start.5 = (bf16[4,16,1024]{2,1,0:T(8,128)(2,1)S(1)}, bf16[4,16,1024]{2,1,0:T(8,128)(2,1)S(1)}, u32[]{:S(2)}, u32[]{:S(2)}) collective-permute-start(bf16[4,16,1024]{2,1,0:T(8,128)(2,1)S(1)} %maximum_bitcast_fusion.2.refs_0_), channel_id=1, source_target_pairs={{0,6},{2,4},{4,2},{6,0},{8,14},{10,12},{12,10},{14,8},{16,22},{18,... | collective-permute-start | bytes 393224 | tf_op jit(solution)/shard_map/ppermute | solution.py:61
  16.1 3.6 %collective-permute-done.5.refs_3_ = bf16[4,16,1024]{2,1,0:T(8,128)(2,1)S(1)} collective-permute-done((bf16[4,16,1024]{2,1,0:T(8,128)(2,1)S(1)}, bf16[4,16,1024]{2,1,0:T(8,128)(2,1)S(1)}, u32[]{:S(2)}, u32[]{:S(2)}) %collective-permute-start.5) | collective-permute-done | bytes 131104 | tf_op jit(solution)/shard_map/ppermute | solution.py:61
  20.5 11.1 %forward.1 = (bf16[1024,2048]{1,0:T(8,128)(2,1)}, bf16[1024,2048]{1,0:T(8,128)(2,1)}, f32[4,8,256]{2,1,0:T(8,128)S(1)}, bf16[256,1024]{1,0:T(8,128)(2,1)S(1)}, b...) custom-call(s32[2]{0:T(128)S(1)} %pad_add_fusion.me_ref, ...), custom_call_target="tpu_custom_call" | custom-call | flops 8589934592 | bytes 4194304 | tf_op jit(solution)/shard_map/forward/pallas_call | solution.py:476
  33.5 1.6 %collective-permute-start.8 = (bf16[4,80,256]{2,1,0:T(8,128)(2,1)S(1)}, bf16[4,80,256]{2,1,0:T(8,128)(2,1)S(1)}, u32[]{:S(2)}, u32[]{:S(2)}) collective-permute-start(bf16[4,80,256]{2,1,0:T(8,128)(2,1)S(1)} %get-tuple-element.67), channel_id=1, source_target_pairs={{0,6},{2,4},{4,2},{6,0},{8,14},{10,12},{12,10},{14,8},{16,22},{18,... | collective-permute-start | bytes 491528 | tf_op jit(solution)/shard_map/ppermute | solution.py:61
  35.1 3.7 %newton.1 = (f32[9,256,256]{2,1,0:T(8,128)S(1)}, f32[1,256,256]{2,1,0:T(8,128)S(1)}) custom-call(s32[3]{0:T(128)S(1)} %pad_add_fusion.1.own_ref, bf16[256,1024]{1,0:T(8,128)(2,1)S(1)} %get-tuple-element.68.lq_ref.lk_ref, bf16[256,1024]{1,0:T(8,128)(2,1)S(1)} %get-tuple-element.68.lq_ref.lk_ref), custom_call_target="tpu_custom_call" | custom-call | flops 4294967296 | bytes 4194304 | tf_op jit(solution)/shard_map/newton/pallas_call | solution.py:476
  41.6 2.7 %collective-permute-start.10 = (bf16[1,80,256]{2,1,0:T(8,128)(2,1)S(1)}, bf16[1,80,256]{2,1,0:T(8,128)(2,1)S(1)}, u32[]{:S(2)}, u32[]{:S(2)}) collective-permute-start(bf16[1,80,256]{2,1,0:T(8,128)(2,1)S(1)} %get-tuple-element.77), channel_id=1, source_target_pairs={{0,16},{2,18},{4,20},{6,22},{8,24},{10,26},{12,28},{14,30},{16,0},... | collective-permute-start | bytes 122888 | tf_op jit(solution)/shard_map/ppermute | solution.py:61
  45.0 2.4 %collective-permute-done.10.refs_2_ = bf16[1,80,256]{2,1,0:T(8,128)(2,1)S(1)} collective-permute-done((bf16[1,80,256]{2,1,0:T(8,128)(2,1)S(1)}, bf16[1,80,256]{2,1,0:T(8,128)(2,1)S(1)}, u32[]{:S(2)}, u32[]{:S(2)}) %collective-permute-start.10) | collective-permute-done | bytes 40992 | tf_op jit(solution)/shard_map/ppermute | solution.py:61
  47.5 2.7 %collective-permute-done.11.refs_3_ = bf16[1,80,256]{2,1,0:T(8,128)(2,1)S(1)} collective-permute-done((bf16[1,80,256]{2,1,0:T(8,128)(2,1)S(1)}, bf16[1,80,256]{2,1,0:T(8,128)(2,1)S(1)}, u32[]{:S(2)}, u32[]{:S(2)}) %collective-permute-start.11) | collective-permute-done | bytes 40992 | tf_op jit(solution)/shard_map/ppermute | solution.py:61
  51.2 3.7 %collective-permute-start.12 = (bf16[1,80,256]{2,1,0:T(8,128)(2,1)S(1)}, bf16[1,80,256]{2,1,0:T(8,128)(2,1)S(1)}, u32[]{:S(2)}, u32[]{:S(2)}) collective-permute-start(bf16[1,80,256]{2,1,0:T(8,128)(2,1)S(1)} %get-tuple-element.80), channel_id=1, source_target_pairs={{0,8},{2,10},{4,12},{6,14},{8,0},{10,2},{12,4},{14,6},{16,24},{18,... | collective-permute-start | bytes 122888 | tf_op jit(solution)/shard_map/ppermute | solution.py:61
  55.0 1.5 %collective-permute-done.14 = bf16[1,80,256]{2,1,0:T(8,128)(2,1)S(1)} collective-permute-done((bf16[1,80,256]{2,1,0:T(8,128)(2,1)S(1)}, bf16[1,80,256]{2,1,0:T(8,128)(2,1)S(1)}, u32[]{:S(2)}, u32[]{:S(2)}) %collective-permute-start.14) | collective-permute-done | bytes 40992 | tf_op jit(solution)/shard_map/ppermute | solution.py:61
  57.1 1.7 %collective-permute-start.17 = (bf16[4,80,256]{2,1,0:T(8,128)(2,1)S(1)}, bf16[4,80,256]{2,1,0:T(8,128)(2,1)S(1)}, u32[]{:S(2)}, u32[]{:S(2)}) collective-permute-start(bf16[4,80,256]{2,1,0:T(8,128)(2,1)S(1)} %maximum_bitcast_fusion.1.refs_0_), channel_id=1, source_target_pairs={{0,6},{2,4},{4,2},{6,0},{8,14},{10,12},{12,10},{14,8},{16,22},{18,... | collective-permute-start | bytes 491528 | tf_op jit(solution)/shard_map/ppermute | solution.py:61
  60.6 1.7 %copy-done.12 = f32[9,256,256]{2,1,0:T(8,128)S(1)} copy-done((f32[9,256,256]{2,1,0:T(8,128)S(1)}, f32[9,256,256]{2,1,0:T(8,128)}, u32[]{:S(2)}) %copy-start.12) | copy-done | bytes 2359320
  62.3 4.2 %newton_grad.1 = (f32[256,128]{1,0:T(8,128)S(1)}, f32[256,128]{1,0:T(8,128)S(1)}) custom-call(s32[3]{0:T(128)S(1)} %pad_add_fusion.1.own_ref, f32[9,256,256]{2,1,0:T(8,128)S(1)} %copy-done.12, f32[32,256]{1,0:T(8,128)S(1)} %get-tuple-element.91.values_ref, f32[32,256]{1,0:T(8,128)S(1)} %get-tuple-element.92.grads_ref, ...), custom_call_target="tpu_custom_call" | custom-call | flops 8589934592 | bytes 4194304 | tf_op jit(solution)/shard_map/newton_grad/pallas_call | solution.py:476
  66.6 4.7 %attend.1 = (bf16[1024,512]{1,0:T(8,128)(2,1)S(1)}, bf16[512,256]{1,0:T(8,128)(2,1)S(1)}, bf16[512,256]{1,0:T(8,128)(2,1)S(1)}, f32[8,256]{1,0:T(8,128)S(1)}, bf...) custom-call(s32[2]{0:T(128)S(1)} %pad_add_fusion.me_ref, ...), custom_call_target="tpu_custom_call" | custom-call | flops 4294967296 | bytes 4194304 | tf_op jit(solution)/shard_map/attend/pallas_call | solution.py:476
  74.9 6.2 %query_grad.1 = (bf16[1024,512]{1,0:T(8,128)(2,1)S(1)}, bf16[256,512]{1,0:T(8,128)(2,1)S(1)}) custom-call(s32[3]{0:T(128)S(1)} %pad_add_fusion.1.own_ref, bf16[1024,512]{1,0:T(8,128)(2,1)S(1)} %copy-done.1, bf16[1024,512]{1,0:T(8,128)(2,1)S(1)} %copy-done.10, bf16[1024,2048]{1,0:T(8,128)(2,1)S(1)} %copy-done.9, ...), custom_call_target="tpu_custom_call" | custom-call | flops 6442450944 | bytes 4194304 | tf_op jit(solution)/shard_map/query_grad/pallas_call | solution.py:476
  81.9 1.7 %collective-permute-start.21 = (bf16[1,32,1024]{2,1,0:T(8,128)(2,1)S(1)}, bf16[1,32,1024]{2,1,0:T(8,128)(2,1)S(1)}, u32[]{:S(2)}, u32[]{:S(2)}) collective-permute-start(bf16[1,32,1024]{2,1,0:T(8,128)(2,1)S(1)} %get-tuple-element.117), channel_id=1, source_target_pairs={{0,8},{2,10},{4,12},{6,14},{8,0},{10,2},{12,4},{14,6},{16,24},{18,... | collective-permute-start | bytes 196616 | tf_op jit(solution)/shard_map/ppermute | solution.py:61
  85.5 4.3 %key_grad.1 = (bf16[1024,512]{1,0:T(8,128)(2,1)}, bf16[1024,512]{1,0:T(8,128)(2,1)}, bf16[256,256]{1,0:T(8,128)(2,1)S(1)}) custom-call(s32[3]{0:T(128)S(1)} %pad_add_fusion.1.own_ref, bf16[1024,512]{1,0:T(8,128)(2,1)S(1)} %copy-done.2, bf16[1024,512]{1,0:T(8,128)(2,1)S(1)} %copy-done.5, bf16[1024,2048]{1,0:T(8,128)(2,1)S(1)} %copy-done.8, ...), custom_call_target="tpu_custom_call" | custom-call | flops 3221225472 | bytes 4194304 | tf_op jit(solution)/shard_map/key_grad/pallas_call | solution.py:476
  91.1 4.4 %key_grad_rest.1 = (bf16[1024,512]{1,0:T(8,128)(2,1)}, bf16[1024,512]{1,0:T(8,128)(2,1)}, bf16[4,16,1024]{2,1,0:T(8,128)(2,1)S(1)}, bf16[4,16,1024]{2,1,0:T(8,12...) custom-call(s32[3]{0:T(128)S(1)} %pad_add_fusion.1.own_ref, ...), custom_call_target="tpu_custom_call", output_to_operand_aliasing={{0}: (10, {}), {1}: (11, {})} | custom-call | flops 3221225472 | bytes 4194304 | tf_op jit(solution)/shard_map/key_grad_rest/pallas_call | solution.py:476
  99.0 1.7 %convolution_convert_fusion.1 = bf16[1024,512]{1,0:T(8,128)(2,1)} fusion(bf16[1024,512]{1,0:T(8,128)(2,1)S(1)} %get-tuple-element.97, bf16[512,1024]{1,0:T(8,128)(2,1)S(1)} %copy-done, s32[]{:T(128)S(6)} %select_n.24), kind=kOutput, calls=%fused_computation.6 | convolution fusion | flops 537395200 | bytes 2621444 | tf_op jit(solution)/shard_map/dot_general | solution.py:23
  100.7 1.5 %collective-permute-start.26 = (bf16[1,32,1024]{2,1,0:T(8,128)(2,1)S(1)}, bf16[1,32,1024]{2,1,0:T(8,128)(2,1)S(1)}, u32[]{:S(2)}, u32[]{:S(2)}) collective-permute-start(bf16[1,32,1024]{2,1,0:T(8,128)(2,1)S(1)} %bitcast.71), channel_id=1, source_target_pairs={{0,24},{2,26},{4,28},{6,30},{8,16},{10,18},{12,20},{14,22},{16,8},... | collective-permute-start | bytes 196616 | tf_op jit(solution)/shard_map/ppermute | solution.py:61
  103.4 1.6 %collective-permute-start.24 = (bf16[1,32,1024]{2,1,0:T(8,128)(2,1)S(1)}, bf16[1,32,1024]{2,1,0:T(8,128)(2,1)S(1)}, u32[]{:S(2)}, u32[]{:S(2)}) collective-permute-start(bf16[1,32,1024]{2,1,0:T(8,128)(2,1)S(1)} %bitcast.73), channel_id=1, source_target_pairs={{0,8},{2,10},{4,12},{6,14},{8,0},{10,2},{12,4},{14,6},{16,24},{18,... | collective-permute-start | bytes 196616 | tf_op jit(solution)/shard_map/ppermute | solution.py:61
  105.6 1.8 %collective-permute-done.26 = bf16[1,32,1024]{2,1,0:T(8,128)(2,1)S(1)} collective-permute-done((bf16[1,32,1024]{2,1,0:T(8,128)(2,1)S(1)}, bf16[1,32,1024]{2,1,0:T(8,128)(2,1)S(1)}, u32[]{:S(2)}, u32[]{:S(2)}) %collective-permute-start.26) | collective-permute-done | bytes 65568 | tf_op jit(solution)/shard_map/ppermute | solution.py:61
  107.5 1.5 %collective-permute-start.36 = (bf16[1,16,1024]{2,1,0:T(8,128)(2,1)S(1)}, bf16[1,16,1024]{2,1,0:T(8,128)(2,1)S(1)}, u32[]{:S(2)}, u32[]{:S(2)}) collective-permute-start(bf16[1,16,1024]{2,1,0:T(8,128)(2,1)S(1)} %get-tuple-element.121), channel_id=1, source_target_pairs={{0,24},{2,26},{4,28},{6,30},{8,16},{10,18},{12,20},{14,22},{16,8},... | collective-permute-start | bytes 98312 | tf_op jit(solution)/shard_map/ppermute | solution.py:61
  111.0 1.6 %collective-permute-start.29 = (bf16[4,32,1024]{2,1,0:T(8,128)(2,1)S(1)}, bf16[4,32,1024]{2,1,0:T(8,128)(2,1)S(1)}, u32[]{:S(2)}, u32[]{:S(2)}) collective-permute-start(bf16[4,32,1024]{2,1,0:T(8,128)(2,1)S(1)} %maximum_bitcast_fusion.refs_0_), channel_id=1, source_target_pairs={{0,6},{2,4},{4,2},{6,0},{8,14},{10,12},{12,10},{14,8},{16,22},{18,... | collective-permute-start | bytes 786440 | tf_op jit(solution)/shard_map/ppermute | solution.py:61
  115.3 1.7 %fusion = (bf16[1024,512]{1,0:T(8,128)(2,1)}, bf16[1024,512]{1,0:T(8,128)(2,1)}) fusion(bf16[1024,512]{1,0:T(8,128)(2,1)S(1)} %copy-done.13, f32[16,512]{1,0:T(8,128)S(1)} %get-tuple-element.123, f32[16,512]{1,0:T(8,128)S(1)} %get-tuple-element.124, bf16[1024,512]{1,0:T(8,128)(2,1)S(1)} %get-tuple-element.101), kind=kLoop, calls=%fused_computation.1 | loop fusion | flops 3145728 | bytes 4259840 | tf_op jit(solution)/shard_map/convert_element_type | solution.py:739
  117.0 2.9 %add_convert_fusion = bf16[1024,512]{1,0:T(8,128)(2,1)} fusion(bf16[1024,512]{1,0:T(8,128)(2,1)} %collective-permute-done.30, bf16[1024,512]{1,0:T(8,128)(2,1)S(1)} %copy-done.7, bf16[512,1024]{1,0:T(8,128)(2,1)S(1)} %copy-done, s32[]{:T(128)S(6)} %select_n.23), kind=kOutput, calls=%fused_computation.4 | convolution fusion | flops 538443776 | bytes 3670020 | tf_op jit(solution)/shard_map/dot_general | solution.py:23
  121.3 3.5 %collective-permute-done.28.refs_2_ = bf16[4,32,1024]{2,1,0:T(8,128)(2,1)S(1)} collective-permute-done((bf16[4,32,1024]{2,1,0:T(8,128)(2,1)S(1)}, bf16[4,32,1024]{2,1,0:T(8,128)(2,1)S(1)}, u32[]{:S(2)}, u32[]{:S(2)}) %collective-permute-start.28) | collective-permute-done | bytes 262176 | tf_op jit(solution)/shard_map/ppermute | solution.py:61
  124.8 2.4 %unpack.1 = f32[512,1024]{1,0:T(8,128)} custom-call(s32[2]{0:T(128)S(1)} %pad_add_fusion.me_ref, bf16[4,32,1024]{2,1,0:T(8,128)(2,1)S(1)} %maximum_bitcast_fusion.refs_0_, bf16[4,32,1024]{2,1,0:T(8,128)(2,1)S(1)} %collective-permute-done.27.refs_1_, bf16[4,32,1024]{2,1,0:T(8,128)(2,1)S(1)} %collective-permute-done.28.refs_2_, ...), custom_call_target="tpu_custom_call" | custom-call | bytes 4194304 | tf_op jit(solution)/shard_map/unpack/pallas_call | solution.py:476
  (97 shorter events, 30.5 us)
Async XLA Ops:
  2.5 8.0 %collective-permute-start.2 = (bf16[1,16,1024]{2,1,0:T(8,128)(2,1)S(1)}, bf16[1,16,1024]{2,1,0:T(8,128)(2,1)S(1)}, u32[]{:S(2)}, u32[]{:S(2)}) collective-permute-start(bf16[1,16,1024]{2,1,0:T(8,128)(2,1)S(1)} %bitcast.64), channel_id=1, source_target_pairs={{0,24},{2,26},{4,28},{6,30},{8,16},{10,18},{12,20},{14,22},{16,8},... | collective-permute-start | bytes 98312 | tf_op jit(solution)/shard_map/ppermute | solution.py:61
  12.4 7.3 %collective-permute-start.5 = (bf16[4,16,1024]{2,1,0:T(8,128)(2,1)S(1)}, bf16[4,16,1024]{2,1,0:T(8,128)(2,1)S(1)}, u32[]{:S(2)}, u32[]{:S(2)}) collective-permute-start(bf16[4,16,1024]{2,1,0:T(8,128)(2,1)S(1)} %maximum_bitcast_fusion.2.refs_0_), channel_id=1, source_target_pairs={{0,6},{2,4},{4,2},{6,0},{8,14},{10,12},{12,10},{14,8},{16,22},{18,... | collective-permute-start | bytes 393224 | tf_op jit(solution)/shard_map/ppermute | solution.py:61
  14.9 5.6 %collective-permute-start.4 = (bf16[4,16,1024]{2,1,0:T(8,128)(2,1)S(1)}, bf16[4,16,1024]{2,1,0:T(8,128)(2,1)S(1)}, u32[]{:S(2)}, u32[]{:S(2)}) collective-permute-start(bf16[4,16,1024]{2,1,0:T(8,128)(2,1)S(1)} %maximum_bitcast_fusion.2.refs_0_), channel_id=1, source_target_pairs={{0,4},{2,6},{4,0},{6,2},{8,12},{10,14},{12,8},{14,10},{16,20},{18,... | collective-permute-start | bytes 393224 | tf_op jit(solution)/shard_map/ppermute | solution.py:61
  31.6 8.5 %collective-permute-start.6 = (bf16[4,80,256]{2,1,0:T(8,128)(2,1)S(1)}, bf16[4,80,256]{2,1,0:T(8,128)(2,1)S(1)}, u32[]{:S(2)}, u32[]{:S(2)}) collective-permute-start(bf16[4,80,256]{2,1,0:T(8,128)(2,1)S(1)} %get-tuple-element.65), channel_id=1, source_target_pairs={{0,2},{2,0},{4,6},{6,4},{8,10},{10,8},{12,14},{14,12},{16,18},{18,... | collective-permute-start | bytes 491528 | tf_op jit(solution)/shard_map/ppermute | solution.py:61
  32.7 7.7 %collective-permute-start.7 = (bf16[4,80,256]{2,1,0:T(8,128)(2,1)S(1)}, bf16[4,80,256]{2,1,0:T(8,128)(2,1)S(1)}, u32[]{:S(2)}, u32[]{:S(2)}) collective-permute-start(bf16[4,80,256]{2,1,0:T(8,128)(2,1)S(1)} %get-tuple-element.66), channel_id=1, source_target_pairs={{0,4},{2,6},{4,0},{6,2},{8,12},{10,14},{12,8},{14,10},{16,20},{18,... | collective-permute-start | bytes 491528 | tf_op jit(solution)/shard_map/ppermute | solution.py:61
  33.5 6.9 %collective-permute-start.8 = (bf16[4,80,256]{2,1,0:T(8,128)(2,1)S(1)}, bf16[4,80,256]{2,1,0:T(8,128)(2,1)S(1)}, u32[]{:S(2)}, u32[]{:S(2)}) collective-permute-start(bf16[4,80,256]{2,1,0:T(8,128)(2,1)S(1)} %get-tuple-element.67), channel_id=1, source_target_pairs={{0,6},{2,4},{4,2},{6,0},{8,14},{10,12},{12,10},{14,8},{16,22},{18,... | collective-permute-start | bytes 491528 | tf_op jit(solution)/shard_map/ppermute | solution.py:61
  41.6 5.8 %collective-permute-start.10 = (bf16[1,80,256]{2,1,0:T(8,128)(2,1)S(1)}, bf16[1,80,256]{2,1,0:T(8,128)(2,1)S(1)}, u32[]{:S(2)}, u32[]{:S(2)}) collective-permute-start(bf16[1,80,256]{2,1,0:T(8,128)(2,1)S(1)} %get-tuple-element.77), channel_id=1, source_target_pairs={{0,16},{2,18},{4,20},{6,22},{8,24},{10,26},{12,28},{14,30},{16,0},... | collective-permute-start | bytes 122888 | tf_op jit(solution)/shard_map/ppermute | solution.py:61
  44.4 5.8 %collective-permute-start.11 = (bf16[1,80,256]{2,1,0:T(8,128)(2,1)S(1)}, bf16[1,80,256]{2,1,0:T(8,128)(2,1)S(1)}, u32[]{:S(2)}, u32[]{:S(2)}) collective-permute-start(bf16[1,80,256]{2,1,0:T(8,128)(2,1)S(1)} %get-tuple-element.78), channel_id=1, source_target_pairs={{0,24},{2,26},{4,28},{6,30},{8,16},{10,18},{12,20},{14,22},{16,8},... | collective-permute-start | bytes 122888 | tf_op jit(solution)/shard_map/ppermute | solution.py:61
  50.5 6.0 %collective-permute-start.14 = (bf16[1,80,256]{2,1,0:T(8,128)(2,1)S(1)}, bf16[1,80,256]{2,1,0:T(8,128)(2,1)S(1)}, u32[]{:S(2)}, u32[]{:S(2)}) collective-permute-start(bf16[1,80,256]{2,1,0:T(8,128)(2,1)S(1)} %get-tuple-element.80), channel_id=1, source_target_pairs={{0,24},{2,26},{4,28},{6,30},{8,16},{10,18},{12,20},{14,22},{16,8},... | collective-permute-start | bytes 122888 | tf_op jit(solution)/shard_map/ppermute | solution.py:61
  51.2 5.8 %collective-permute-start.13 = (bf16[1,80,256]{2,1,0:T(8,128)(2,1)S(1)}, bf16[1,80,256]{2,1,0:T(8,128)(2,1)S(1)}, u32[]{:S(2)}, u32[]{:S(2)}) collective-permute-start(bf16[1,80,256]{2,1,0:T(8,128)(2,1)S(1)} %get-tuple-element.80), channel_id=1, source_target_pairs={{0,16},{2,18},{4,20},{6,22},{8,24},{10,26},{12,28},{14,30},{16,0},... | collective-permute-start | bytes 122888 | tf_op jit(solution)/shard_map/ppermute | solution.py:61
  51.2 5.8 %collective-permute-start.12 = (bf16[1,80,256]{2,1,0:T(8,128)(2,1)S(1)}, bf16[1,80,256]{2,1,0:T(8,128)(2,1)S(1)}, u32[]{:S(2)}, u32[]{:S(2)}) collective-permute-start(bf16[1,80,256]{2,1,0:T(8,128)(2,1)S(1)} %get-tuple-element.80), channel_id=1, source_target_pairs={{0,8},{2,10},{4,12},{6,14},{8,0},{10,2},{12,4},{14,6},{16,24},{18,... | collective-permute-start | bytes 122888 | tf_op jit(solution)/shard_map/ppermute | solution.py:61
  57.1 9.5 %collective-permute-start.17 = (bf16[4,80,256]{2,1,0:T(8,128)(2,1)S(1)}, bf16[4,80,256]{2,1,0:T(8,128)(2,1)S(1)}, u32[]{:S(2)}, u32[]{:S(2)}) collective-permute-start(bf16[4,80,256]{2,1,0:T(8,128)(2,1)S(1)} %maximum_bitcast_fusion.1.refs_0_), channel_id=1, source_target_pairs={{0,6},{2,4},{4,2},{6,0},{8,14},{10,12},{12,10},{14,8},{16,22},{18,... | collective-permute-start | bytes 491528 | tf_op jit(solution)/shard_map/ppermute | solution.py:61
  58.8 7.8 %collective-permute-start.16 = (bf16[4,80,256]{2,1,0:T(8,128)(2,1)S(1)}, bf16[4,80,256]{2,1,0:T(8,128)(2,1)S(1)}, u32[]{:S(2)}, u32[]{:S(2)}) collective-permute-start(bf16[4,80,256]{2,1,0:T(8,128)(2,1)S(1)} %maximum_bitcast_fusion.1.refs_0_), channel_id=1, source_target_pairs={{0,4},{2,6},{4,0},{6,2},{8,12},{10,14},{12,8},{14,10},{16,20},{18,... | collective-permute-start | bytes 491528 | tf_op jit(solution)/shard_map/ppermute | solution.py:61
  59.8 6.8 %collective-permute-start.15 = (bf16[4,80,256]{2,1,0:T(8,128)(2,1)S(1)}, bf16[4,80,256]{2,1,0:T(8,128)(2,1)S(1)}, u32[]{:S(2)}, u32[]{:S(2)}) collective-permute-start(bf16[4,80,256]{2,1,0:T(8,128)(2,1)S(1)} %maximum_bitcast_fusion.1.refs_0_), channel_id=1, source_target_pairs={{0,2},{2,0},{4,6},{6,4},{8,10},{10,8},{12,14},{14,12},{16,18},{18,... | collective-permute-start | bytes 491528 | tf_op jit(solution)/shard_map/ppermute | solution.py:61
  71.3 9.8 %collective-permute-start.18 = (bf16[4,32,1024]{2,1,0:T(8,128)(2,1)S(1)}, bf16[4,32,1024]{2,1,0:T(8,128)(2,1)S(1)}, u32[]{:S(2)}, u32[]{:S(2)}) collective-permute-start(bf16[4,32,1024]{2,1,0:T(8,128)(2,1)S(1)} %get-tuple-element.82), channel_id=1, source_target_pairs={{0,2},{2,0},{4,6},{6,4},{8,10},{10,8},{12,14},{14,12},{16,18},{18,... | collective-permute-start | bytes 786440 | tf_op jit(solution)/shard_map/ppermute | solution.py:61
  72.5 9.2 %collective-permute-start.19 = (bf16[4,32,1024]{2,1,0:T(8,128)(2,1)S(1)}, bf16[4,32,1024]{2,1,0:T(8,128)(2,1)S(1)}, u32[]{:S(2)}, u32[]{:S(2)}) collective-permute-start(bf16[4,32,1024]{2,1,0:T(8,128)(2,1)S(1)} %get-tuple-element.83), channel_id=1, source_target_pairs={{0,4},{2,6},{4,0},{6,2},{8,12},{10,14},{12,8},{14,10},{16,20},{18,... | collective-permute-start | bytes 786440 | tf_op jit(solution)/shard_map/ppermute | solution.py:61
  73.6 8.2 %collective-permute-start.20 = (bf16[4,32,1024]{2,1,0:T(8,128)(2,1)S(1)}, bf16[4,32,1024]{2,1,0:T(8,128)(2,1)S(1)}, u32[]{:S(2)}, u32[]{:S(2)}) collective-permute-start(bf16[4,32,1024]{2,1,0:T(8,128)(2,1)S(1)} %get-tuple-element.84), channel_id=1, source_target_pairs={{0,6},{2,4},{4,2},{6,0},{8,14},{10,12},{12,10},{14,8},{16,22},{18,... | collective-permute-start | bytes 786440 | tf_op jit(solution)/shard_map/ppermute | solution.py:61
  81.9 7.9 %collective-permute-start.21 = (bf16[1,32,1024]{2,1,0:T(8,128)(2,1)S(1)}, bf16[1,32,1024]{2,1,0:T(8,128)(2,1)S(1)}, u32[]{:S(2)}, u32[]{:S(2)}) collective-permute-start(bf16[1,32,1024]{2,1,0:T(8,128)(2,1)S(1)} %get-tuple-element.117), channel_id=1, source_target_pairs={{0,8},{2,10},{4,12},{6,14},{8,0},{10,2},{12,4},{14,6},{16,24},{18,... | collective-permute-start | bytes 196616 | tf_op jit(solution)/shard_map/ppermute | solution.py:61
  83.6 6.2 %collective-permute-start.23 = (bf16[1,32,1024]{2,1,0:T(8,128)(2,1)S(1)}, bf16[1,32,1024]{2,1,0:T(8,128)(2,1)S(1)}, u32[]{:S(2)}, u32[]{:S(2)}) collective-permute-start(bf16[1,32,1024]{2,1,0:T(8,128)(2,1)S(1)} %get-tuple-element.118), channel_id=1, source_target_pairs={{0,24},{2,26},{4,28},{6,30},{8,16},{10,18},{12,20},{14,22},{16,8},... | collective-permute-start | bytes 196616 | tf_op jit(solution)/shard_map/ppermute | solution.py:61
  84.8 6.3 %collective-permute-start.22 = (bf16[1,32,1024]{2,1,0:T(8,128)(2,1)S(1)}, bf16[1,32,1024]{2,1,0:T(8,128)(2,1)S(1)}, u32[]{:S(2)}, u32[]{:S(2)}) collective-permute-start(bf16[1,32,1024]{2,1,0:T(8,128)(2,1)S(1)} %get-tuple-element.119), channel_id=1, source_target_pairs={{0,16},{2,18},{4,20},{6,22},{8,24},{10,26},{12,28},{14,30},{16,0},... | collective-permute-start | bytes 196616 | tf_op jit(solution)/shard_map/ppermute | solution.py:61
  95.5 6.7 %collective-permute-start.31 = (bf16[4,16,1024]{2,1,0:T(8,128)(2,1)S(1)}, bf16[4,16,1024]{2,1,0:T(8,128)(2,1)S(1)}, u32[]{:S(2)}, u32[]{:S(2)}) collective-permute-start(bf16[4,16,1024]{2,1,0:T(8,128)(2,1)S(1)} %get-tuple-element.108), channel_id=1, source_target_pairs={{0,2},{2,0},{4,6},{6,4},{8,10},{10,8},{12,14},{14,12},{16,18},{18,... | collective-permute-start | bytes 393224 | tf_op jit(solution)/shard_map/ppermute | solution.py:61
  96.4 7.0 %collective-permute-start.32 = (bf16[4,16,1024]{2,1,0:T(8,128)(2,1)S(1)}, bf16[4,16,1024]{2,1,0:T(8,128)(2,1)S(1)}, u32[]{:S(2)}, u32[]{:S(2)}) collective-permute-start(bf16[4,16,1024]{2,1,0:T(8,128)(2,1)S(1)} %get-tuple-element.109), channel_id=1, source_target_pairs={{0,4},{2,6},{4,0},{6,2},{8,12},{10,14},{12,8},{14,10},{16,20},{18,... | collective-permute-start | bytes 393224 | tf_op jit(solution)/shard_map/ppermute | solution.py:61
  97.6 7.5 %collective-permute-start.33 = (bf16[4,16,1024]{2,1,0:T(8,128)(2,1)S(1)}, bf16[4,16,1024]{2,1,0:T(8,128)(2,1)S(1)}, u32[]{:S(2)}, u32[]{:S(2)}) collective-permute-start(bf16[4,16,1024]{2,1,0:T(8,128)(2,1)S(1)} %get-tuple-element.110), channel_id=1, source_target_pairs={{0,6},{2,4},{4,2},{6,0},{8,14},{10,12},{12,10},{14,8},{16,22},{18,... | collective-permute-start | bytes 393224 | tf_op jit(solution)/shard_map/ppermute | solution.py:61
  100.7 16.3 %collective-permute-start.30 = (bf16[1024,512]{1,0:T(8,128)(2,1)}, bf16[1024,512]{1,0:T(8,128)(2,1)}, u32[]{:S(2)}, u32[]{:S(2)}) collective-permute-start(bf16[1024,512]{1,0:T(8,128)(2,1)} %convolution_convert_fusion.1), channel_id=1, source_target_pairs={{0,1},{1,0},{2,3},{3,2},{4,5},{5,4},{6,7},{7,6},{8,9},{9,8},{10,11... | collective-permute-start | bytes 3145736 | tf_op jit(solution)/shard_map/ppermute | solution.py:665
  100.7 6.8 %collective-permute-start.26 = (bf16[1,32,1024]{2,1,0:T(8,128)(2,1)S(1)}, bf16[1,32,1024]{2,1,0:T(8,128)(2,1)S(1)}, u32[]{:S(2)}, u32[]{:S(2)}) collective-permute-start(bf16[1,32,1024]{2,1,0:T(8,128)(2,1)S(1)} %bitcast.71), channel_id=1, source_target_pairs={{0,24},{2,26},{4,28},{6,30},{8,16},{10,18},{12,20},{14,22},{16,8},... | collective-permute-start | bytes 196616 | tf_op jit(solution)/shard_map/ppermute | solution.py:61
  102.2 8.2 %collective-permute-start.25 = (bf16[1,32,1024]{2,1,0:T(8,128)(2,1)S(1)}, bf16[1,32,1024]{2,1,0:T(8,128)(2,1)S(1)}, u32[]{:S(2)}, u32[]{:S(2)}) collective-permute-start(bf16[1,32,1024]{2,1,0:T(8,128)(2,1)S(1)} %bitcast.72), channel_id=1, source_target_pairs={{0,16},{2,18},{4,20},{6,22},{8,24},{10,26},{12,28},{14,30},{16,0},... | collective-permute-start | bytes 196616 | tf_op jit(solution)/shard_map/ppermute | solution.py:61
  103.4 7.6 %collective-permute-start.24 = (bf16[1,32,1024]{2,1,0:T(8,128)(2,1)S(1)}, bf16[1,32,1024]{2,1,0:T(8,128)(2,1)S(1)}, u32[]{:S(2)}, u32[]{:S(2)}) collective-permute-start(bf16[1,32,1024]{2,1,0:T(8,128)(2,1)S(1)} %bitcast.73), channel_id=1, source_target_pairs={{0,8},{2,10},{4,12},{6,14},{8,0},{10,2},{12,4},{14,6},{16,24},{18,... | collective-permute-start | bytes 196616 | tf_op jit(solution)/shard_map/ppermute | solution.py:61
  105.2 7.4 %collective-permute-start.34 = (bf16[1,16,1024]{2,1,0:T(8,128)(2,1)S(1)}, bf16[1,16,1024]{2,1,0:T(8,128)(2,1)S(1)}, u32[]{:S(2)}, u32[]{:S(2)}) collective-permute-start(bf16[1,16,1024]{2,1,0:T(8,128)(2,1)S(1)} %get-tuple-element.120), channel_id=1, source_target_pairs={{0,8},{2,10},{4,12},{6,14},{8,0},{10,2},{12,4},{14,6},{16,24},{18,... | collective-permute-start | bytes 98312 | tf_op jit(solution)/shard_map/ppermute | solution.py:61
  107.5 6.4 %collective-permute-start.36 = (bf16[1,16,1024]{2,1,0:T(8,128)(2,1)S(1)}, bf16[1,16,1024]{2,1,0:T(8,128)(2,1)S(1)}, u32[]{:S(2)}, u32[]{:S(2)}) collective-permute-start(bf16[1,16,1024]{2,1,0:T(8,128)(2,1)S(1)} %get-tuple-element.121), channel_id=1, source_target_pairs={{0,24},{2,26},{4,28},{6,30},{8,16},{10,18},{12,20},{14,22},{16,8},... | collective-permute-start | bytes 98312 | tf_op jit(solution)/shard_map/ppermute | solution.py:61
  111.0 10.2 %collective-permute-start.29 = (bf16[4,32,1024]{2,1,0:T(8,128)(2,1)S(1)}, bf16[4,32,1024]{2,1,0:T(8,128)(2,1)S(1)}, u32[]{:S(2)}, u32[]{:S(2)}) collective-permute-start(bf16[4,32,1024]{2,1,0:T(8,128)(2,1)S(1)} %maximum_bitcast_fusion.refs_0_), channel_id=1, source_target_pairs={{0,6},{2,4},{4,2},{6,0},{8,14},{10,12},{12,10},{14,8},{16,22},{18,... | collective-permute-start | bytes 786440 | tf_op jit(solution)/shard_map/ppermute | solution.py:61
  112.6 12.2 %collective-permute-start.28 = (bf16[4,32,1024]{2,1,0:T(8,128)(2,1)S(1)}, bf16[4,32,1024]{2,1,0:T(8,128)(2,1)S(1)}, u32[]{:S(2)}, u32[]{:S(2)}) collective-permute-start(bf16[4,32,1024]{2,1,0:T(8,128)(2,1)S(1)} %maximum_bitcast_fusion.refs_0_), channel_id=1, source_target_pairs={{0,4},{2,6},{4,0},{6,2},{8,12},{10,14},{12,8},{14,10},{16,20},{18,... | collective-permute-start | bytes 786440 | tf_op jit(solution)/shard_map/ppermute | solution.py:61
  113.9 11.0 %collective-permute-start.27 = (bf16[4,32,1024]{2,1,0:T(8,128)(2,1)S(1)}, bf16[4,32,1024]{2,1,0:T(8,128)(2,1)S(1)}, u32[]{:S(2)}, u32[]{:S(2)}) collective-permute-start(bf16[4,32,1024]{2,1,0:T(8,128)(2,1)S(1)} %maximum_bitcast_fusion.refs_0_), channel_id=1, source_target_pairs={{0,2},{2,0},{4,6},{6,4},{8,10},{10,8},{12,14},{14,12},{16,18},{18,... | collective-permute-start | bytes 786440 | tf_op jit(solution)/shard_map/ppermute | solution.py:61
  (19 other events, 143.2 us)

commit v2 on v1

--- a/solution.py
+++ b/solution.py
@@ -12,7 +12,7 @@
 LANDMARKS = 256
 ITERS = 2
 SCALE = 0.125
-CHUNK = 128
+CHUNK = 256
 EXTRA = 16
 F32 = jnp.float32
 BF16 = jnp.bfloat16
@@ -71,14 +71,21 @@
     return groups
 
 
-def gather_lists(block, n):
-    got = [block]
+def gather_first(block, n):
+    shift, size = bit_groups(n)[0]
     held = block[None]
-    for shift, size in bit_groups(n):
-        if len(got) > 1:
-            held = jnp.stack(got, axis=1).reshape((-1,) + block.shape)
+    return [held] + [exchange(held, m << shift, n) for m in range(1, size)]
+
+
+def gather_rest(got, n):
+    for shift, size in bit_groups(n)[1:]:
+        held = jnp.stack(got, axis=1).reshape((-1,) + got[0].shape[1:])
         got = [held] + [exchange(held, m << shift, n) for m in range(1, size)]
     return got
+
+
+def gather_lists(block, n):
+    return gather_rest(gather_first(block, n), n)
 
 
 def gather_ordered(block, n, me):
@@ -447,17 +454,25 @@
     land_ref[...] = (sums.T * SCALE + more_ref[...] * here).astype(BF16)
 
 
-def unpack_kernel(size, split, me_ref, *refs):
-    out_ref = refs[-1]
-    block, width = refs[0].shape[1:]
-    for m in range(size):
-        at = m ^ (me_ref[0] % size)
-        row = pl.ds(pl.multiple_of((at // split) * block, block), block)
-        column = pl.ds(pl.multiple_of((at % split) * width, width), width)
-        if split == 1:
-            out_ref[row, :] = refs[m][0].astype(F32)
-        else:
-            out_ref[row, column] = refs[m][0].astype(F32)
+def unpack_kernel(split, me_ref, *refs):
+    in_refs, (out_ref, wide_ref, sems) = refs[:-3], refs[-3:]
+    size = len(in_refs)
+    held, block, width = in_refs[0].shape
+    copies = []
+    for t in range(held):
+        for m in range(size):
+            slot = t * size + m
+            at = slot ^ me_ref[0]
+            row = pl.ds(pl.multiple_of((at // split) * block, block), block)
+            if split == 1:
+                target = out_ref.at[row]
+            else:
+                target = out_ref.at[row, pl.ds(pl.multiple_of((at % split) * width, width), width)]
+            wide_ref[slot] = in_refs[m][t].astype(F32)
+            copies.append(pltpu.make_async_copy(wide_ref.at[slot], target, sems.at[slot]))
+            copies[-1].start()
+    for copy in copies:
+        copy.wait()
 
 
 def held_in_hbm(x):
@@ -570,7 +585,7 @@
     square = (LANDMARKS, LANDMARKS)
     own_lq = pl.BlockSpec((LANDMARKS, PAIR), lambda i, own: (0, own[0]))
     own_lk = pl.BlockSpec((LANDMARKS, PAIR), lambda i, own: (0, own[0] + pairs))
-    kept = shape_of((1 + 4 * ITERS,) + square, F32)
+    kept = pltpu.VMEM((1 + 4 * ITERS,) + square, F32)
     saved, inverse = call(
         newton_kernel,
         (1,),
@@ -620,7 +635,7 @@
         newton_grad_kernel,
         (1,),
         [own_arr],
-        [saved, values, grads, land, land],
+        [pltpu.with_memory_space_constraint(saved, pltpu.VMEM), values, grads, land, land],
         [whole(kept.shape), whole(small.shape), whole(small.shape), own_lq, own_lk],
         [more, more],
         [whole(more.shape)] * 2,
@@ -628,6 +643,7 @@
         name="newton_grad",
     )
 
+    replies, more_q, more_k = lax.optimization_barrier((replies, more_q, more_k))
     block = max(columns // n, 16)
     split = n * block // columns
     flat = shape_of((columns, LANDMARKS), BF16)
@@ -731,6 +747,9 @@
     )
     if not sorted_here:
         land_pieces = split_by_partner(land_pieces[0].reshape(n, land_dev, 2 * columns), n, me)
+    weights = gather_first(weight_own, n)
+    weights, land_pieces = lax.optimization_barrier((weights, land_pieces))
+    weights = gather_rest(weights, n)
     land_own = scatter_pieces(land_pieces, n, groups)[0] * (1.0 / seg_len)
 
     def finish(token_part, land_part):
@@ -740,16 +759,16 @@
             .reshape(rows, columns)
         )
 
-    weights = gather_lists(weight_own, n)
     weights, mixed = lax.optimization_barrier((weights, mixed))
     weight_grad = call(
-        functools.partial(unpack_kernel, size, split),
-        (n // size,),
+        functools.partial(unpack_kernel, split),
+        (1,),
         [me_arr],
         weights,
-        [pl.BlockSpec((1,) + weights[0].shape[1:], lambda t, me: (t, 0, 0))] * size,
-        shape_of((columns, width), F32),
-        pl.BlockSpec((size * block // split, width), lambda t, me: (t ^ (me[0] // size), 0)),
+        [whole(weights[0].shape)] * size,
+        pltpu.HBM((columns, width), F32),
+        in_hbm,
+        [pltpu.VMEM((n,) + weights[0].shape[1:], F32), pltpu.SemaphoreType.DMA((n,))],
         name="unpack",
     )
     query_grad = finish(query_f, land_own[:, :columns])

time: 128 us -> 127 us (level)
  waiting for transfers between devices: 24.4 us -> 23 us
    ppermute x36, waiting for transfers between devices: 24.4 us -> 23 us  [exchange(): return lax.ppermute(block, 'seq', [(i, i ^ mask) for i in range(n)])]
  transfers between devices with their start and end apart: 37 -> 37, of which waited for: 15 -> 15; matrix products, arithmetic and copies ran while one was open for 7% -> 7% of each run, Pallas kernels for 14% -> 18%
where the time goes in v2:
time: 127 us
  starting transfers between devices  47.5 us (37%)
  Pallas kernels  42.8 us (34%)
  waiting for transfers between devices  23 us (18%)
  matrix products  6.86 us (5%)
  local copies, waits for them, and re-layouts  3.15 us (2%)
  other arithmetic  2.26 us (2%)
    ppermute x36, starting transfers between devices, exchange(): return lax.ppermute(block, 'seq', [(i, i ^ mask) for i in range(n)])  47.5 us
    pallas_call x11, Pallas kernels, call(): pl.pallas_call(kernel, grid_spec=pltpu.PrefetchScalarGridSpec(num_scalar_...  42.8 us
    ppermute x36, waiting for transfers between devices, exchange(): return lax.ppermute(block, 'seq', [(i, i ^ mask) for i in range(n)])  23 us
    dot_general x3, matrix products, dot(): lax.dot_general(left, right, (dims, ((), ())), preferred_element_type=F32)  6.86 us
    unnamed x28, local copies, waits for them, and re-layouts  3.12 us
  transfers between devices with their start and end apart: 37, of which 15 were waited for; matrix products, arithmetic and copies ran while one was open for 7% of the time, Pallas kernels for 18%

profile of v2, /device:TPU:0, one launch (start us, length us, event | category | flops | bytes accessed | tf_op | source)
XLA Modules:
  0.0 126.6 jit_solution(3257725011471863876)
XLA Ops:
  0.7 1.8 %means.1 = bf16[16,1024]{1,0:T(8,128)(2,1)S(1)} custom-call(bf16[1024,512]{1,0:T(8,128)(2,1)} %q_ref.5, bf16[1024,512]{1,0:T(8,128)(2,1)} %k_ref.5), custom_call_target="tpu_custom_call" | custom-call | bytes 4194304 | tf_op jit(solution)/shard_map/means/pallas_call | solution.py:491
  2.5 5.1 %collective-permute-start.2 = (bf16[1,16,1024]{2,1,0:T(8,128)(2,1)S(1)}, bf16[1,16,1024]{2,1,0:T(8,128)(2,1)S(1)}, u32[]{:S(2)}, u32[]{:S(2)}) collective-permute-start(bf16[1,16,1024]{2,1,0:T(8,128)(2,1)S(1)} %bitcast.64), channel_id=1, source_target_pairs={{0,24},{2,26},{4,28},{6,30},{8,16},{10,18},{12,20},{14,22},{16,8},... | collective-permute-start | bytes 98312 | tf_op jit(solution)/shard_map/ppermute | solution.py:61
  8.2 2.3 %convolution_convert_fusion.g_ref = bf16[1024,512]{1,0:T(8,128)(2,1)} fusion(bf16[1024,1024]{1,0:T(8,128)(2,1)S(1)} %copy-done.3, bf16[512,1024]{1,0:T(8,128)(2,1)S(1)} %copy-done), kind=kOutput, calls=%fused_computation.5 | convolution fusion | flops 1074266112 | bytes 4194304 | tf_op jit(solution)/shard_map/dot_general | solution.py:23
  10.5 1.9 %collective-permute-done.1 = bf16[1,16,1024]{2,1,0:T(8,128)(2,1)S(1)} collective-permute-done((bf16[1,16,1024]{2,1,0:T(8,128)(2,1)S(1)}, bf16[1,16,1024]{2,1,0:T(8,128)(2,1)S(1)}, u32[]{:S(2)}, u32[]{:S(2)}) %collective-permute-start.1) | collective-permute-done | bytes 32800 | tf_op jit(solution)/shard_map/ppermute | solution.py:61
  12.4 2.5 %collective-permute-start.5 = (bf16[4,16,1024]{2,1,0:T(8,128)(2,1)S(1)}, bf16[4,16,1024]{2,1,0:T(8,128)(2,1)S(1)}, u32[]{:S(2)}, u32[]{:S(2)}) collective-permute-start(bf16[4,16,1024]{2,1,0:T(8,128)(2,1)S(1)} %maximum_bitcast_fusion.2.refs_0_), channel_id=1, source_target_pairs={{0,6},{2,4},{4,2},{6,0},{8,14},{10,12},{12,10},{14,8},{16,22},{18,... | collective-permute-start | bytes 393224 | tf_op jit(solution)/shard_map/ppermute | solution.py:61
  16.1 3.6 %collective-permute-done.5.refs_3_ = bf16[4,16,1024]{2,1,0:T(8,128)(2,1)S(1)} collective-permute-done((bf16[4,16,1024]{2,1,0:T(8,128)(2,1)S(1)}, bf16[4,16,1024]{2,1,0:T(8,128)(2,1)S(1)}, u32[]{:S(2)}, u32[]{:S(2)}) %collective-permute-start.5) | collective-permute-done | bytes 131104 | tf_op jit(solution)/shard_map/ppermute | solution.py:61
  20.5 11.2 %forward.1 = (bf16[1024,2048]{1,0:T(8,128)(2,1)}, bf16[1024,2048]{1,0:T(8,128)(2,1)}, f32[4,8,256]{2,1,0:T(8,128)S(1)}, bf16[256,1024]{1,0:T(8,128)(2,1)S(1)}, b...) custom-call(s32[2]{0:T(128)S(1)} %pad_add_fusion.me_ref, ...), custom_call_target="tpu_custom_call" | custom-call | flops 8589934592 | bytes 4194304 | tf_op jit(solution)/shard_map/forward/pallas_call | solution.py:491
  33.6 1.6 %collective-permute-start.8 = (bf16[4,80,256]{2,1,0:T(8,128)(2,1)S(1)}, bf16[4,80,256]{2,1,0:T(8,128)(2,1)S(1)}, u32[]{:S(2)}, u32[]{:S(2)}) collective-permute-start(bf16[4,80,256]{2,1,0:T(8,128)(2,1)S(1)} %get-tuple-element.81), channel_id=1, source_target_pairs={{0,6},{2,4},{4,2},{6,0},{8,14},{10,12},{12,10},{14,8},{16,22},{18,... | collective-permute-start | bytes 491528 | tf_op jit(solution)/shard_map/ppermute | solution.py:61
  35.2 3.7 %newton.1 = (f32[9,256,256]{2,1,0:T(8,128)S(1)}, f32[1,256,256]{2,1,0:T(8,128)S(1)}) custom-call(s32[3]{0:T(128)S(1)} %pad_add_fusion.1.own_ref, bf16[256,1024]{1,0:T(8,128)(2,1)S(1)} %get-tuple-element.82.lq_ref.lk_ref, bf16[256,1024]{1,0:T(8,128)(2,1)S(1)} %get-tuple-element.82.lq_ref.lk_ref), custom_call_target="tpu_custom_call" | custom-call | flops 4294967296 | bytes 4194304 | tf_op jit(solution)/shard_map/newton/pallas_call | solution.py:491
  41.7 2.8 %collective-permute-start.10 = (bf16[1,80,256]{2,1,0:T(8,128)(2,1)S(1)}, bf16[1,80,256]{2,1,0:T(8,128)(2,1)S(1)}, u32[]{:S(2)}, u32[]{:S(2)}) collective-permute-start(bf16[1,80,256]{2,1,0:T(8,128)(2,1)S(1)} %get-tuple-element.91), channel_id=1, source_target_pairs={{0,16},{2,18},{4,20},{6,22},{8,24},{10,26},{12,28},{14,30},{16,0},... | collective-permute-start | bytes 122888 | tf_op jit(solution)/shard_map/ppermute | solution.py:61
  45.1 2.4 %collective-permute-done.10.refs_2_ = bf16[1,80,256]{2,1,0:T(8,128)(2,1)S(1)} collective-permute-done((bf16[1,80,256]{2,1,0:T(8,128)(2,1)S(1)}, bf16[1,80,256]{2,1,0:T(8,128)(2,1)S(1)}, u32[]{:S(2)}, u32[]{:S(2)}) %collective-permute-start.10) | collective-permute-done | bytes 40992 | tf_op jit(solution)/shard_map/ppermute | solution.py:61
  47.6 2.7 %collective-permute-done.11.refs_3_ = bf16[1,80,256]{2,1,0:T(8,128)(2,1)S(1)} collective-permute-done((bf16[1,80,256]{2,1,0:T(8,128)(2,1)S(1)}, bf16[1,80,256]{2,1,0:T(8,128)(2,1)S(1)}, u32[]{:S(2)}, u32[]{:S(2)}) %collective-permute-start.11) | collective-permute-done | bytes 40992 | tf_op jit(solution)/shard_map/ppermute | solution.py:61
  51.3 3.7 %collective-permute-start.12 = (bf16[1,80,256]{2,1,0:T(8,128)(2,1)S(1)}, bf16[1,80,256]{2,1,0:T(8,128)(2,1)S(1)}, u32[]{:S(2)}, u32[]{:S(2)}) collective-permute-start(bf16[1,80,256]{2,1,0:T(8,128)(2,1)S(1)} %get-tuple-element.94), channel_id=1, source_target_pairs={{0,8},{2,10},{4,12},{6,14},{8,0},{10,2},{12,4},{14,6},{16,24},{18,... | collective-permute-start | bytes 122888 | tf_op jit(solution)/shard_map/ppermute | solution.py:61
  57.2 1.7 %collective-permute-start.17 = (bf16[4,80,256]{2,1,0:T(8,128)(2,1)S(1)}, bf16[4,80,256]{2,1,0:T(8,128)(2,1)S(1)}, u32[]{:S(2)}, u32[]{:S(2)}) collective-permute-start(bf16[4,80,256]{2,1,0:T(8,128)(2,1)S(1)} %maximum_bitcast_fusion.1.refs_0_), channel_id=1, source_target_pairs={{0,6},{2,4},{4,2},{6,0},{8,14},{10,12},{12,10},{14,8},{16,22},{18,... | collective-permute-start | bytes 491528 | tf_op jit(solution)/shard_map/ppermute | solution.py:61
  60.7 1.7 %copy-done.12 = f32[9,256,256]{2,1,0:T(8,128)S(1)} copy-done((f32[9,256,256]{2,1,0:T(8,128)S(1)}, f32[9,256,256]{2,1,0:T(8,128)}, u32[]{:S(2)}) %copy-start.12) | copy-done | bytes 2359320
  62.4 4.2 %newton_grad.1 = (f32[256,128]{1,0:T(8,128)S(1)}, f32[256,128]{1,0:T(8,128)S(1)}) custom-call(s32[3]{0:T(128)S(1)} %pad_add_fusion.1.own_ref, f32[9,256,256]{2,1,0:T(8,128)S(1)} %copy-done.12, f32[32,256]{1,0:T(8,128)S(1)} %get-tuple-element.96.values_ref, f32[32,256]{1,0:T(8,128)S(1)} %get-tuple-element.97.grads_ref, ...), custom_call_target="tpu_custom_call" | custom-call | flops 8589934592 | bytes 4194304 | tf_op jit(solution)/shard_map/newton_grad/pallas_call | solution.py:491
  66.7 4.7 %attend.1 = (bf16[1024,512]{1,0:T(8,128)(2,1)S(1)}, bf16[512,256]{1,0:T(8,128)(2,1)S(1)}, bf16[512,256]{1,0:T(8,128)(2,1)S(1)}, f32[8,256]{1,0:T(8,128)S(1)}, bf...) custom-call(s32[2]{0:T(128)S(1)} %pad_add_fusion.me_ref, ...), custom_call_target="tpu_custom_call" | custom-call | flops 4294967296 | bytes 4194304 | tf_op jit(solution)/shard_map/attend/pallas_call | solution.py:491
  75.0 6.2 %query_grad.1 = (bf16[1024,512]{1,0:T(8,128)(2,1)S(1)}, bf16[256,512]{1,0:T(8,128)(2,1)S(1)}) custom-call(s32[3]{0:T(128)S(1)} %pad_add_fusion.1.own_ref, bf16[1024,512]{1,0:T(8,128)(2,1)S(1)} %copy-done.1, bf16[1024,512]{1,0:T(8,128)(2,1)S(1)} %copy-done.10, bf16[1024,2048]{1,0:T(8,128)(2,1)S(1)} %copy-done.9, ...), custom_call_target="tpu_custom_call" | custom-call | flops 6442450944 | bytes 4194304 | tf_op jit(solution)/shard_map/query_grad/pallas_call | solution.py:491
  82.0 1.7 %collective-permute-start.21 = (bf16[1,32,1024]{2,1,0:T(8,128)(2,1)S(1)}, bf16[1,32,1024]{2,1,0:T(8,128)(2,1)S(1)}, u32[]{:S(2)}, u32[]{:S(2)}) collective-permute-start(bf16[1,32,1024]{2,1,0:T(8,128)(2,1)S(1)} %get-tuple-element.145), channel_id=1, source_target_pairs={{0,8},{2,10},{4,12},{6,14},{8,0},{10,2},{12,4},{14,6},{16,24},{18,... | collective-permute-start | bytes 196616 | tf_op jit(solution)/shard_map/ppermute | solution.py:61
  85.6 4.3 %key_grad.1 = (bf16[1024,512]{1,0:T(8,128)(2,1)}, bf16[1024,512]{1,0:T(8,128)(2,1)}, bf16[256,256]{1,0:T(8,128)(2,1)S(1)}) custom-call(s32[3]{0:T(128)S(1)} %pad_add_fusion.1.own_ref, bf16[1024,512]{1,0:T(8,128)(2,1)S(1)} %copy-done.2, bf16[1024,512]{1,0:T(8,128)(2,1)S(1)} %copy-done.5, bf16[1024,2048]{1,0:T(8,128)(2,1)S(1)} %copy-done.8, ...), custom_call_target="tpu_custom_call" | custom-call | flops 3221225472 | bytes 4194304 | tf_op jit(solution)/shard_map/key_grad/pallas_call | solution.py:491
  90.3 1.8 %collective-permute-done.22 = bf16[1,32,1024]{2,1,0:T(8,128)(2,1)S(1)} collective-permute-done((bf16[1,32,1024]{2,1,0:T(8,128)(2,1)S(1)}, bf16[1,32,1024]{2,1,0:T(8,128)(2,1)S(1)}, u32[]{:S(2)}, u32[]{:S(2)}) %collective-permute-start.22) | collective-permute-done | bytes 65568 | tf_op jit(solution)/shard_map/ppermute | solution.py:61
  92.2 1.8 %collective-permute-start.26 = (bf16[1,32,1024]{2,1,0:T(8,128)(2,1)S(1)}, bf16[1,32,1024]{2,1,0:T(8,128)(2,1)S(1)}, u32[]{:S(2)}, u32[]{:S(2)}) collective-permute-start(bf16[1,32,1024]{2,1,0:T(8,128)(2,1)S(1)} %bitcast.71), channel_id=1, source_target_pairs={{0,24},{2,26},{4,28},{6,30},{8,16},{10,18},{12,20},{14,22},{16,8},... | collective-permute-start | bytes 196616 | tf_op jit(solution)/shard_map/ppermute | solution.py:61
  94.0 2.6 %collective-permute-start.24 = (bf16[1,32,1024]{2,1,0:T(8,128)(2,1)S(1)}, bf16[1,32,1024]{2,1,0:T(8,128)(2,1)S(1)}, u32[]{:S(2)}, u32[]{:S(2)}) collective-permute-start(bf16[1,32,1024]{2,1,0:T(8,128)(2,1)S(1)} %bitcast.73), channel_id=1, source_target_pairs={{0,8},{2,10},{4,12},{6,14},{8,0},{10,2},{12,4},{14,6},{16,24},{18,... | collective-permute-start | bytes 196616 | tf_op jit(solution)/shard_map/ppermute | solution.py:61
  96.7 4.3 %key_grad_rest.1 = (bf16[1024,512]{1,0:T(8,128)(2,1)}, bf16[1024,512]{1,0:T(8,128)(2,1)}, bf16[4,16,1024]{2,1,0:T(8,128)(2,1)S(1)}, bf16[4,16,1024]{2,1,0:T(8,12...) custom-call(s32[3]{0:T(128)S(1)} %pad_add_fusion.1.own_ref, ...), custom_call_target="tpu_custom_call", output_to_operand_aliasing={{0}: (10, {}), {1}: (11, {})} | custom-call | flops 3221225472 | bytes 4194304 | tf_op jit(solution)/shard_map/key_grad_rest/pallas_call | solution.py:491
  104.6 1.7 %convolution_convert_fusion.1 = bf16[1024,512]{1,0:T(8,128)(2,1)} fusion(bf16[1024,512]{1,0:T(8,128)(2,1)S(1)} %get-tuple-element.132, bf16[512,1024]{1,0:T(8,128)(2,1)S(1)} %copy-done, s32[]{:T(128)S(6)} %select_n.24), kind=kOutput, calls=%fused_computation.6 | convolution fusion | flops 537395200 | bytes 2621444 | tf_op jit(solution)/shard_map/dot_general | solution.py:23
  107.2 1.8 %collective-permute-done.33 = bf16[4,16,1024]{2,1,0:T(8,128)(2,1)S(1)} collective-permute-done((bf16[4,16,1024]{2,1,0:T(8,128)(2,1)S(1)}, bf16[4,16,1024]{2,1,0:T(8,128)(2,1)S(1)}, u32[]{:S(2)}, u32[]{:S(2)}) %collective-permute-start.33) | collective-permute-done | bytes 131104 | tf_op jit(solution)/shard_map/ppermute | solution.py:61
  109.1 1.7 %collective-permute-start.36 = (bf16[1,16,1024]{2,1,0:T(8,128)(2,1)S(1)}, bf16[1,16,1024]{2,1,0:T(8,128)(2,1)S(1)}, u32[]{:S(2)}, u32[]{:S(2)}) collective-permute-start(bf16[1,16,1024]{2,1,0:T(8,128)(2,1)S(1)} %get-tuple-element.149), channel_id=1, source_target_pairs={{0,24},{2,26},{4,28},{6,30},{8,16},{10,18},{12,20},{14,22},{16,8},... | collective-permute-start | bytes 98312 | tf_op jit(solution)/shard_map/ppermute | solution.py:61
  110.8 1.8 %collective-permute-start.35 = (bf16[1,16,1024]{2,1,0:T(8,128)(2,1)S(1)}, bf16[1,16,1024]{2,1,0:T(8,128)(2,1)S(1)}, u32[]{:S(2)}, u32[]{:S(2)}) collective-permute-start(bf16[1,16,1024]{2,1,0:T(8,128)(2,1)S(1)} %get-tuple-element.150), channel_id=1, source_target_pairs={{0,16},{2,18},{4,20},{6,22},{8,24},{10,26},{12,28},{14,30},{16,0},... | collective-permute-start | bytes 98312 | tf_op jit(solution)/shard_map/ppermute | solution.py:61
  116.3 1.7 %fusion = (bf16[1024,512]{1,0:T(8,128)(2,1)}, bf16[1024,512]{1,0:T(8,128)(2,1)}) fusion(bf16[1024,512]{1,0:T(8,128)(2,1)S(1)} %copy-done.13, f32[16,512]{1,0:T(8,128)S(1)} %get-tuple-element.151, f32[16,512]{1,0:T(8,128)S(1)} %get-tuple-element.152, bf16[1024,512]{1,0:T(8,128)(2,1)S(1)} %get-tuple-element.134), kind=kLoop, calls=%fused_computation.1 | loop fusion | flops 3145728 | bytes 4259840 | tf_op jit(solution)/shard_map/convert_element_type | solution.py:758
  118.0 2.9 %add_convert_fusion = bf16[1024,512]{1,0:T(8,128)(2,1)} fusion(bf16[1024,512]{1,0:T(8,128)(2,1)} %collective-permute-done.30, bf16[1024,512]{1,0:T(8,128)(2,1)S(1)} %copy-done.7, bf16[512,1024]{1,0:T(8,128)(2,1)S(1)} %copy-done, s32[]{:T(128)S(6)} %select_n.23), kind=kOutput, calls=%fused_computation.4 | convolution fusion | flops 538443776 | bytes 3670020 | tf_op jit(solution)/shard_map/dot_general | solution.py:23
  121.8 2.7 %collective-permute-done.28.refs_2_ = bf16[4,32,1024]{2,1,0:T(8,128)(2,1)S(1)} collective-permute-done((bf16[4,32,1024]{2,1,0:T(8,128)(2,1)S(1)}, bf16[4,32,1024]{2,1,0:T(8,128)(2,1)S(1)}, u32[]{:S(2)}, u32[]{:S(2)}) %collective-permute-start.28) | collective-permute-done | bytes 262176 | tf_op jit(solution)/shard_map/ppermute | solution.py:61
  124.4 2.0 %unpack.1 = f32[512,1024]{1,0:T(8,128)} custom-call(s32[2]{0:T(128)S(1)} %pad_add_fusion.me_ref, bf16[4,32,1024]{2,1,0:T(8,128)(2,1)S(1)} %maximum_bitcast_fusion.refs_0_, bf16[4,32,1024]{2,1,0:T(8,128)(2,1)S(1)} %collective-permute-done.27.refs_1_, bf16[4,32,1024]{2,1,0:T(8,128)(2,1)S(1)} %collective-permute-done.28.refs_2_, ...), custom_call_target="tpu_custom_call" | custom-call | bytes 4194304 | tf_op jit(solution)/shard_map/unpack/pallas_call | solution.py:491
  (97 shorter events, 29.1 us)
Async XLA Ops:
  2.5 8.0 %collective-permute-start.2 = (bf16[1,16,1024]{2,1,0:T(8,128)(2,1)S(1)}, bf16[1,16,1024]{2,1,0:T(8,128)(2,1)S(1)}, u32[]{:S(2)}, u32[]{:S(2)}) collective-permute-start(bf16[1,16,1024]{2,1,0:T(8,128)(2,1)S(1)} %bitcast.64), channel_id=1, source_target_pairs={{0,24},{2,26},{4,28},{6,30},{8,16},{10,18},{12,20},{14,22},{16,8},... | collective-permute-start | bytes 98312 | tf_op jit(solution)/shard_map/ppermute | solution.py:61
  12.4 7.3 %collective-permute-start.5 = (bf16[4,16,1024]{2,1,0:T(8,128)(2,1)S(1)}, bf16[4,16,1024]{2,1,0:T(8,128)(2,1)S(1)}, u32[]{:S(2)}, u32[]{:S(2)}) collective-permute-start(bf16[4,16,1024]{2,1,0:T(8,128)(2,1)S(1)} %maximum_bitcast_fusion.2.refs_0_), channel_id=1, source_target_pairs={{0,6},{2,4},{4,2},{6,0},{8,14},{10,12},{12,10},{14,8},{16,22},{18,... | collective-permute-start | bytes 393224 | tf_op jit(solution)/shard_map/ppermute | solution.py:61
  14.9 5.6 %collective-permute-start.4 = (bf16[4,16,1024]{2,1,0:T(8,128)(2,1)S(1)}, bf16[4,16,1024]{2,1,0:T(8,128)(2,1)S(1)}, u32[]{:S(2)}, u32[]{:S(2)}) collective-permute-start(bf16[4,16,1024]{2,1,0:T(8,128)(2,1)S(1)} %maximum_bitcast_fusion.2.refs_0_), channel_id=1, source_target_pairs={{0,4},{2,6},{4,0},{6,2},{8,12},{10,14},{12,8},{14,10},{16,20},{18,... | collective-permute-start | bytes 393224 | tf_op jit(solution)/shard_map/ppermute | solution.py:61
  31.7 8.6 %collective-permute-start.6 = (bf16[4,80,256]{2,1,0:T(8,128)(2,1)S(1)}, bf16[4,80,256]{2,1,0:T(8,128)(2,1)S(1)}, u32[]{:S(2)}, u32[]{:S(2)}) collective-permute-start(bf16[4,80,256]{2,1,0:T(8,128)(2,1)S(1)} %get-tuple-element.79), channel_id=1, source_target_pairs={{0,2},{2,0},{4,6},{6,4},{8,10},{10,8},{12,14},{14,12},{16,18},{18,... | collective-permute-start | bytes 491528 | tf_op jit(solution)/shard_map/ppermute | solution.py:61
  32.8 7.7 %collective-permute-start.7 = (bf16[4,80,256]{2,1,0:T(8,128)(2,1)S(1)}, bf16[4,80,256]{2,1,0:T(8,128)(2,1)S(1)}, u32[]{:S(2)}, u32[]{:S(2)}) collective-permute-start(bf16[4,80,256]{2,1,0:T(8,128)(2,1)S(1)} %get-tuple-element.80), channel_id=1, source_target_pairs={{0,4},{2,6},{4,0},{6,2},{8,12},{10,14},{12,8},{14,10},{16,20},{18,... | collective-permute-start | bytes 491528 | tf_op jit(solution)/shard_map/ppermute | solution.py:61
  33.6 6.9 %collective-permute-start.8 = (bf16[4,80,256]{2,1,0:T(8,128)(2,1)S(1)}, bf16[4,80,256]{2,1,0:T(8,128)(2,1)S(1)}, u32[]{:S(2)}, u32[]{:S(2)}) collective-permute-start(bf16[4,80,256]{2,1,0:T(8,128)(2,1)S(1)} %get-tuple-element.81), channel_id=1, source_target_pairs={{0,6},{2,4},{4,2},{6,0},{8,14},{10,12},{12,10},{14,8},{16,22},{18,... | collective-permute-start | bytes 491528 | tf_op jit(solution)/shard_map/ppermute | solution.py:61
  41.7 5.8 %collective-permute-start.10 = (bf16[1,80,256]{2,1,0:T(8,128)(2,1)S(1)}, bf16[1,80,256]{2,1,0:T(8,128)(2,1)S(1)}, u32[]{:S(2)}, u32[]{:S(2)}) collective-permute-start(bf16[1,80,256]{2,1,0:T(8,128)(2,1)S(1)} %get-tuple-element.91), channel_id=1, source_target_pairs={{0,16},{2,18},{4,20},{6,22},{8,24},{10,26},{12,28},{14,30},{16,0},... | collective-permute-start | bytes 122888 | tf_op jit(solution)/shard_map/ppermute | solution.py:61
  44.5 5.8 %collective-permute-start.11 = (bf16[1,80,256]{2,1,0:T(8,128)(2,1)S(1)}, bf16[1,80,256]{2,1,0:T(8,128)(2,1)S(1)}, u32[]{:S(2)}, u32[]{:S(2)}) collective-permute-start(bf16[1,80,256]{2,1,0:T(8,128)(2,1)S(1)} %get-tuple-element.92), channel_id=1, source_target_pairs={{0,24},{2,26},{4,28},{6,30},{8,16},{10,18},{12,20},{14,22},{16,8},... | collective-permute-start | bytes 122888 | tf_op jit(solution)/shard_map/ppermute | solution.py:61
  50.6 6.0 %collective-permute-start.14 = (bf16[1,80,256]{2,1,0:T(8,128)(2,1)S(1)}, bf16[1,80,256]{2,1,0:T(8,128)(2,1)S(1)}, u32[]{:S(2)}, u32[]{:S(2)}) collective-permute-start(bf16[1,80,256]{2,1,0:T(8,128)(2,1)S(1)} %get-tuple-element.94), channel_id=1, source_target_pairs={{0,24},{2,26},{4,28},{6,30},{8,16},{10,18},{12,20},{14,22},{16,8},... | collective-permute-start | bytes 122888 | tf_op jit(solution)/shard_map/ppermute | solution.py:61
  51.3 5.8 %collective-permute-start.13 = (bf16[1,80,256]{2,1,0:T(8,128)(2,1)S(1)}, bf16[1,80,256]{2,1,0:T(8,128)(2,1)S(1)}, u32[]{:S(2)}, u32[]{:S(2)}) collective-permute-start(bf16[1,80,256]{2,1,0:T(8,128)(2,1)S(1)} %get-tuple-element.94), channel_id=1, source_target_pairs={{0,16},{2,18},{4,20},{6,22},{8,24},{10,26},{12,28},{14,30},{16,0},... | collective-permute-start | bytes 122888 | tf_op jit(solution)/shard_map/ppermute | solution.py:61
  51.3 5.8 %collective-permute-start.12 = (bf16[1,80,256]{2,1,0:T(8,128)(2,1)S(1)}, bf16[1,80,256]{2,1,0:T(8,128)(2,1)S(1)}, u32[]{:S(2)}, u32[]{:S(2)}) collective-permute-start(bf16[1,80,256]{2,1,0:T(8,128)(2,1)S(1)} %get-tuple-element.94), channel_id=1, source_target_pairs={{0,8},{2,10},{4,12},{6,14},{8,0},{10,2},{12,4},{14,6},{16,24},{18,... | collective-permute-start | bytes 122888 | tf_op jit(solution)/shard_map/ppermute | solution.py:61
  57.2 9.5 %collective-permute-start.17 = (bf16[4,80,256]{2,1,0:T(8,128)(2,1)S(1)}, bf16[4,80,256]{2,1,0:T(8,128)(2,1)S(1)}, u32[]{:S(2)}, u32[]{:S(2)}) collective-permute-start(bf16[4,80,256]{2,1,0:T(8,128)(2,1)S(1)} %maximum_bitcast_fusion.1.refs_0_), channel_id=1, source_target_pairs={{0,6},{2,4},{4,2},{6,0},{8,14},{10,12},{12,10},{14,8},{16,22},{18,... | collective-permute-start | bytes 491528 | tf_op jit(solution)/shard_map/ppermute | solution.py:61
  58.9 7.8 %collective-permute-start.16 = (bf16[4,80,256]{2,1,0:T(8,128)(2,1)S(1)}, bf16[4,80,256]{2,1,0:T(8,128)(2,1)S(1)}, u32[]{:S(2)}, u32[]{:S(2)}) collective-permute-start(bf16[4,80,256]{2,1,0:T(8,128)(2,1)S(1)} %maximum_bitcast_fusion.1.refs_0_), channel_id=1, source_target_pairs={{0,4},{2,6},{4,0},{6,2},{8,12},{10,14},{12,8},{14,10},{16,20},{18,... | collective-permute-start | bytes 491528 | tf_op jit(solution)/shard_map/ppermute | solution.py:61
  59.9 6.8 %collective-permute-start.15 = (bf16[4,80,256]{2,1,0:T(8,128)(2,1)S(1)}, bf16[4,80,256]{2,1,0:T(8,128)(2,1)S(1)}, u32[]{:S(2)}, u32[]{:S(2)}) collective-permute-start(bf16[4,80,256]{2,1,0:T(8,128)(2,1)S(1)} %maximum_bitcast_fusion.1.refs_0_), channel_id=1, source_target_pairs={{0,2},{2,0},{4,6},{6,4},{8,10},{10,8},{12,14},{14,12},{16,18},{18,... | collective-permute-start | bytes 491528 | tf_op jit(solution)/shard_map/ppermute | solution.py:61
  71.4 9.8 %collective-permute-start.18 = (bf16[4,32,1024]{2,1,0:T(8,128)(2,1)S(1)}, bf16[4,32,1024]{2,1,0:T(8,128)(2,1)S(1)}, u32[]{:S(2)}, u32[]{:S(2)}) collective-permute-start(bf16[4,32,1024]{2,1,0:T(8,128)(2,1)S(1)} %get-tuple-element.105), channel_id=1, source_target_pairs={{0,2},{2,0},{4,6},{6,4},{8,10},{10,8},{12,14},{14,12},{16,18},{18,... | collective-permute-start | bytes 786440 | tf_op jit(solution)/shard_map/ppermute | solution.py:61
  72.6 9.2 %collective-permute-start.19 = (bf16[4,32,1024]{2,1,0:T(8,128)(2,1)S(1)}, bf16[4,32,1024]{2,1,0:T(8,128)(2,1)S(1)}, u32[]{:S(2)}, u32[]{:S(2)}) collective-permute-start(bf16[4,32,1024]{2,1,0:T(8,128)(2,1)S(1)} %get-tuple-element.106), channel_id=1, source_target_pairs={{0,4},{2,6},{4,0},{6,2},{8,12},{10,14},{12,8},{14,10},{16,20},{18,... | collective-permute-start | bytes 786440 | tf_op jit(solution)/shard_map/ppermute | solution.py:61
  73.6 8.2 %collective-permute-start.20 = (bf16[4,32,1024]{2,1,0:T(8,128)(2,1)S(1)}, bf16[4,32,1024]{2,1,0:T(8,128)(2,1)S(1)}, u32[]{:S(2)}, u32[]{:S(2)}) collective-permute-start(bf16[4,32,1024]{2,1,0:T(8,128)(2,1)S(1)} %get-tuple-element.107), channel_id=1, source_target_pairs={{0,6},{2,4},{4,2},{6,0},{8,14},{10,12},{12,10},{14,8},{16,22},{18,... | collective-permute-start | bytes 786440 | tf_op jit(solution)/shard_map/ppermute | solution.py:61
  82.0 7.8 %collective-permute-start.21 = (bf16[1,32,1024]{2,1,0:T(8,128)(2,1)S(1)}, bf16[1,32,1024]{2,1,0:T(8,128)(2,1)S(1)}, u32[]{:S(2)}, u32[]{:S(2)}) collective-permute-start(bf16[1,32,1024]{2,1,0:T(8,128)(2,1)S(1)} %get-tuple-element.145), channel_id=1, source_target_pairs={{0,8},{2,10},{4,12},{6,14},{8,0},{10,2},{12,4},{14,6},{16,24},{18,... | collective-permute-start | bytes 196616 | tf_op jit(solution)/shard_map/ppermute | solution.py:61
  83.7 6.7 %collective-permute-start.23 = (bf16[1,32,1024]{2,1,0:T(8,128)(2,1)S(1)}, bf16[1,32,1024]{2,1,0:T(8,128)(2,1)S(1)}, u32[]{:S(2)}, u32[]{:S(2)}) collective-permute-start(bf16[1,32,1024]{2,1,0:T(8,128)(2,1)S(1)} %get-tuple-element.146), channel_id=1, source_target_pairs={{0,24},{2,26},{4,28},{6,30},{8,16},{10,18},{12,20},{14,22},{16,8},... | collective-permute-start | bytes 196616 | tf_op jit(solution)/shard_map/ppermute | solution.py:61
  84.9 7.3 %collective-permute-start.22 = (bf16[1,32,1024]{2,1,0:T(8,128)(2,1)S(1)}, bf16[1,32,1024]{2,1,0:T(8,128)(2,1)S(1)}, u32[]{:S(2)}, u32[]{:S(2)}) collective-permute-start(bf16[1,32,1024]{2,1,0:T(8,128)(2,1)S(1)} %get-tuple-element.147), channel_id=1, source_target_pairs={{0,16},{2,18},{4,20},{6,22},{8,24},{10,26},{12,28},{14,30},{16,0},... | collective-permute-start | bytes 196616 | tf_op jit(solution)/shard_map/ppermute | solution.py:61
  92.2 8.8 %collective-permute-start.26 = (bf16[1,32,1024]{2,1,0:T(8,128)(2,1)S(1)}, bf16[1,32,1024]{2,1,0:T(8,128)(2,1)S(1)}, u32[]{:S(2)}, u32[]{:S(2)}) collective-permute-start(bf16[1,32,1024]{2,1,0:T(8,128)(2,1)S(1)} %bitcast.71), channel_id=1, source_target_pairs={{0,24},{2,26},{4,28},{6,30},{8,16},{10,18},{12,20},{14,22},{16,8},... | collective-permute-start | bytes 196616 | tf_op jit(solution)/shard_map/ppermute | solution.py:61
  94.0 7.0 %collective-permute-start.25 = (bf16[1,32,1024]{2,1,0:T(8,128)(2,1)S(1)}, bf16[1,32,1024]{2,1,0:T(8,128)(2,1)S(1)}, u32[]{:S(2)}, u32[]{:S(2)}) collective-permute-start(bf16[1,32,1024]{2,1,0:T(8,128)(2,1)S(1)} %bitcast.72), channel_id=1, source_target_pairs={{0,16},{2,18},{4,20},{6,22},{8,24},{10,26},{12,28},{14,30},{16,0},... | collective-permute-start | bytes 196616 | tf_op jit(solution)/shard_map/ppermute | solution.py:61
  94.0 7.0 %collective-permute-start.24 = (bf16[1,32,1024]{2,1,0:T(8,128)(2,1)S(1)}, bf16[1,32,1024]{2,1,0:T(8,128)(2,1)S(1)}, u32[]{:S(2)}, u32[]{:S(2)}) collective-permute-start(bf16[1,32,1024]{2,1,0:T(8,128)(2,1)S(1)} %bitcast.73), channel_id=1, source_target_pairs={{0,8},{2,10},{4,12},{6,14},{8,0},{10,2},{12,4},{14,6},{16,24},{18,... | collective-permute-start | bytes 196616 | tf_op jit(solution)/shard_map/ppermute | solution.py:61
  101.0 5.3 %collective-permute-start.31 = (bf16[4,16,1024]{2,1,0:T(8,128)(2,1)S(1)}, bf16[4,16,1024]{2,1,0:T(8,128)(2,1)S(1)}, u32[]{:S(2)}, u32[]{:S(2)}) collective-permute-start(bf16[4,16,1024]{2,1,0:T(8,128)(2,1)S(1)} %get-tuple-element.136), channel_id=1, source_target_pairs={{0,2},{2,0},{4,6},{6,4},{8,10},{10,8},{12,14},{14,12},{16,18},{18,... | collective-permute-start | bytes 393224 | tf_op jit(solution)/shard_map/ppermute | solution.py:61
  103.1 5.9 %collective-permute-start.33 = (bf16[4,16,1024]{2,1,0:T(8,128)(2,1)S(1)}, bf16[4,16,1024]{2,1,0:T(8,128)(2,1)S(1)}, u32[]{:S(2)}, u32[]{:S(2)}) collective-permute-start(bf16[4,16,1024]{2,1,0:T(8,128)(2,1)S(1)} %get-tuple-element.138), channel_id=1, source_target_pairs={{0,6},{2,4},{4,2},{6,0},{8,14},{10,12},{12,10},{14,8},{16,22},{18,... | collective-permute-start | bytes 393224 | tf_op jit(solution)/shard_map/ppermute | solution.py:61
  106.3 11.7 %collective-permute-start.30 = (bf16[1024,512]{1,0:T(8,128)(2,1)}, bf16[1024,512]{1,0:T(8,128)(2,1)}, u32[]{:S(2)}, u32[]{:S(2)}) collective-permute-start(bf16[1024,512]{1,0:T(8,128)(2,1)} %convolution_convert_fusion.1), channel_id=1, source_target_pairs={{0,1},{1,0},{2,3},{3,2},{4,5},{5,4},{6,7},{7,6},{8,9},{9,8},{10,11... | collective-permute-start | bytes 3145736 | tf_op jit(solution)/shard_map/ppermute | solution.py:681
  109.0 5.2 %collective-permute-start.34 = (bf16[1,16,1024]{2,1,0:T(8,128)(2,1)S(1)}, bf16[1,16,1024]{2,1,0:T(8,128)(2,1)S(1)}, u32[]{:S(2)}, u32[]{:S(2)}) collective-permute-start(bf16[1,16,1024]{2,1,0:T(8,128)(2,1)S(1)} %get-tuple-element.148), channel_id=1, source_target_pairs={{0,8},{2,10},{4,12},{6,14},{8,0},{10,2},{12,4},{14,6},{16,24},{18,... | collective-permute-start | bytes 98312 | tf_op jit(solution)/shard_map/ppermute | solution.py:61
  109.1 6.2 %collective-permute-start.36 = (bf16[1,16,1024]{2,1,0:T(8,128)(2,1)S(1)}, bf16[1,16,1024]{2,1,0:T(8,128)(2,1)S(1)}, u32[]{:S(2)}, u32[]{:S(2)}) collective-permute-start(bf16[1,16,1024]{2,1,0:T(8,128)(2,1)S(1)} %get-tuple-element.149), channel_id=1, source_target_pairs={{0,24},{2,26},{4,28},{6,30},{8,16},{10,18},{12,20},{14,22},{16,8},... | collective-permute-start | bytes 98312 | tf_op jit(solution)/shard_map/ppermute | solution.py:61
  110.8 5.4 %collective-permute-start.35 = (bf16[1,16,1024]{2,1,0:T(8,128)(2,1)S(1)}, bf16[1,16,1024]{2,1,0:T(8,128)(2,1)S(1)}, u32[]{:S(2)}, u32[]{:S(2)}) collective-permute-start(bf16[1,16,1024]{2,1,0:T(8,128)(2,1)S(1)} %get-tuple-element.150), channel_id=1, source_target_pairs={{0,16},{2,18},{4,20},{6,22},{8,24},{10,26},{12,28},{14,30},{16,0},... | collective-permute-start | bytes 98312 | tf_op jit(solution)/shard_map/ppermute | solution.py:61
  112.6 9.2 %collective-permute-start.29 = (bf16[4,32,1024]{2,1,0:T(8,128)(2,1)S(1)}, bf16[4,32,1024]{2,1,0:T(8,128)(2,1)S(1)}, u32[]{:S(2)}, u32[]{:S(2)}) collective-permute-start(bf16[4,32,1024]{2,1,0:T(8,128)(2,1)S(1)} %maximum_bitcast_fusion.refs_0_), channel_id=1, source_target_pairs={{0,6},{2,4},{4,2},{6,0},{8,14},{10,12},{12,10},{14,8},{16,22},{18,... | collective-permute-start | bytes 786440 | tf_op jit(solution)/shard_map/ppermute | solution.py:61
  114.2 10.3 %collective-permute-start.28 = (bf16[4,32,1024]{2,1,0:T(8,128)(2,1)S(1)}, bf16[4,32,1024]{2,1,0:T(8,128)(2,1)S(1)}, u32[]{:S(2)}, u32[]{:S(2)}) collective-permute-start(bf16[4,32,1024]{2,1,0:T(8,128)(2,1)S(1)} %maximum_bitcast_fusion.refs_0_), channel_id=1, source_target_pairs={{0,4},{2,6},{4,0},{6,2},{8,12},{10,14},{12,8},{14,10},{16,20},{18,... | collective-permute-start | bytes 786440 | tf_op jit(solution)/shard_map/ppermute | solution.py:61
  115.3 9.1 %collective-permute-start.27 = (bf16[4,32,1024]{2,1,0:T(8,128)(2,1)S(1)}, bf16[4,32,1024]{2,1,0:T(8,128)(2,1)S(1)}, u32[]{:S(2)}, u32[]{:S(2)}) collective-permute-start(bf16[4,32,1024]{2,1,0:T(8,128)(2,1)S(1)} %maximum_bitcast_fusion.refs_0_), channel_id=1, source_target_pairs={{0,2},{2,0},{4,6},{6,4},{8,10},{10,8},{12,14},{14,12},{16,18},{18,... | collective-permute-start | bytes 786440 | tf_op jit(solution)/shard_map/ppermute | solution.py:61
  (19 other events, 144.2 us)

commit v3 on v2

--- a/solution.py
+++ b/solution.py
@@ -391,45 +391,14 @@
     land_ref[...] = (sums.T * SCALE + more_ref[...] * here).astype(BF16)
 
 
-def key_half_kernel(
-    first, own_ref, k_ref, v_ref, pb_ref, lq_ref, norm_ref, center_ref, more_ref, *refs
-):
-    out_ref, value_ref, land_ref, ds_ref = refs[-4:]
-    key_pair(first, own_ref, k_ref, v_ref, pb_ref, lq_ref, norm_ref, center_ref, more_ref, out_ref, value_ref, land_ref, ds_ref)
-
-
-def key_rest_kernel(
-    first, own_ref, k_ref, v_ref, pb_ref, lq_ref, norm_ref, center_ref, more_ref, *refs
-):
-    early_ref, other_ref, _, _, out_ref, value_ref = refs[:6]
-    out_refs, (land_ref, ds_ref) = refs[6:-2], refs[-2:]
+def key_kernel(own_ref, k_ref, v_ref, pb_ref, lq_ref, norm_ref, center_ref, more_ref, other_ref, *refs):
+    out_ref, value_ref = refs[:2]
+    out_refs, (land_ref, ds_ref) = refs[2:-2], refs[-2:]
     size = len(out_refs)
     columns = other_ref.shape[1]
     pair = pl.program_id(0)
-    at_pair = pl.ds(pl.multiple_of(pair * PAIR, PAIR), PAIR)
-    key_pair(
-        first, own_ref, k_ref, v_ref, pb_ref, lq_ref, norm_ref, center_ref, more_ref,
-        out_ref, value_ref, land_ref.at[:, at_pair], ds_ref,
-    )
-
-    @pl.when(pair == pl.num_programs(0) - 1)
-    def _():
-        early = early_ref.shape[1]
-        for m in range(size):
-            held, height, _ = out_refs[m].shape
-            for t in range(held):
-                at = pl.multiple_of(((t * size + m) ^ own_ref[2]) * height, height)
-                out_refs[m][t, :, :early] = early_ref[pl.ds(at, height), :]
-                out_refs[m][t, :, early:columns] = land_ref[pl.ds(at, height), :]
-                out_refs[m][t, :, columns:] = other_ref[pl.ds(at, height), :]
-
-
-def key_pair(
-    first, own_ref, k_ref, v_ref, pb_ref, lq_ref, norm_ref, center_ref, more_ref, out_ref, value_ref, land_ref, ds_ref
-):
     rows = k_ref.shape[0]
     lq = lq_ref[...] * SCALE
-    pair = first + pl.program_id(0)
     for h in range(2):
         span = slice(h * LANDMARKS, (h + 1) * LANDMARKS)
         norm = keep_rows(norm_ref[...], h)
@@ -451,7 +420,26 @@
         [dot(kt[:DH], ds_ref[:, :LANDMARKS]), dot(kt[DH:], ds_ref[:, LANDMARKS:])], axis=0
     )
     here = (own_ref[0] == pair).astype(F32)
-    land_ref[...] = (sums.T * SCALE + more_ref[...] * here).astype(BF16)
+    land_ref[:, pl.ds(pl.multiple_of(pair * PAIR, PAIR), PAIR)] = (
+        sums.T * SCALE + more_ref[...] * here
+    ).astype(BF16)
+
+    @pl.when(pair == pl.num_programs(0) - 1)
+    def _():
+        for m in range(size):
+            held, height, _ = out_refs[m].shape
+            for t in range(held):
+                at = pl.multiple_of(((t * size + m) ^ own_ref[2]) * height, height)
+                out_refs[m][t, :, :columns] = land_ref[pl.ds(at, height), :]
+                out_refs[m][t, :, columns:] = other_ref[pl.ds(at, height), :]
+
+
+def part_kernel(_, attn_ref, weight_ref, out_ref):
+    out_ref[...] = dot(attn_ref[...], weight_ref[...]).astype(BF16)
+
+
+def mixed_kernel(_, attn_ref, weight_ref, other_ref, out_ref):
+    out_ref[...] = (dot(attn_ref[...], weight_ref[...]) + other_ref[...].astype(F32)).astype(BF16)
 
 
 def unpack_kernel(split, me_ref, *refs):
@@ -670,18 +658,28 @@
     )
     (shift, count), later = groups[0], groups[1:]
     weight_sum = scatter_step(weight_pieces, shift, count, n).astype(BF16)
-    (pb, key_rows, value_rows), weight_sum = lax.optimization_barrier(
-        ((pb, key_rows, value_rows), weight_sum)
-    )
+    half = width // 2
+    mine_arr = mine.reshape(1).astype(jnp.int32)
+    row_block = pl.BlockSpec((rows // 4, columns), lambda j, _: (j, 0))
+    half_block = pl.BlockSpec((rows // 4, half), lambda j, _: (j, 0))
+    there = call(
+        part_kernel,
+        (4,),
+        [mine_arr],
+        [attn, out_weight],
+        [row_block, pl.BlockSpec((columns, half), lambda j, mine: (0, 1 - mine[0]))],
+        shape_of((rows, half), BF16),
+        half_block,
+        flops=1 << 30,
+        name="part",
+    )
+    (pb, key_rows, value_rows), weight_sum, there = lax.optimization_barrier(
+        ((pb, key_rows, value_rows), weight_sum, there)
+    )
+    arrived = lax.ppermute(there, "head", [(0, 1), (1, 0)])
     following = later[0][1]
     weight_sum = weight_sum.reshape((-1, following) + weight_sum.shape[1:])
     weight_own = scatter_pieces([weight_sum[:, m] for m in range(following)], n, later)[0].astype(BF16)
-    half = width // 2
-    there = dot(attn, lax.dynamic_slice_in_dim(out_weight, (1 - mine) * half, half, 1))
-    arrived = lax.ppermute(there.astype(BF16), "head", [(0, 1), (1, 0)])
-    here = dot(attn, lax.dynamic_slice_in_dim(out_weight, mine * half, half, 1))
-    mixed = (here + arrived.astype(F32)).astype(BF16)
-
     flat_pair = pl.BlockSpec((PAIR, LANDMARKS), lambda j, *_: (j, 0))
     land_pair = pl.BlockSpec((LANDMARKS, PAIR), lambda j, *_: (0, j))
     tokens = shape_of((rows, columns), BF16)
@@ -703,54 +701,39 @@
         land_piece, count = shape_of((n // size, land_dev, 2 * columns), BF16), size
     else:
         land_piece, count = shape_of((LANDMARKS // 16, 16, 2 * columns), BF16), 1
-    some = pairs // 2
-    key_in = [key_rows, value_rows, pb, land, norm, center, more_q]
-
-    def key_specs(first):
-        pair_of = lambda j, *_: (0, j + first)
-        tokens_at = pl.BlockSpec((rows, PAIR), pair_of)
-        factors_at = pl.BlockSpec((rows, 2 * LANDMARKS), pair_of)
-        land_at = pl.BlockSpec((LANDMARKS, PAIR), pair_of)
-        flat_at = pl.BlockSpec((PAIR, LANDMARKS), lambda j, *_: (j + first, 0))
-        return [tokens_at, tokens_at, factors_at, land_at, flat_at, whole((heads, LANDMARKS)), whole(more.shape)]
-
-    specs = key_specs(0)
-    half_shape = shape_of((LANDMARKS, some * PAIR), BF16)
-    tokens_hbm = pltpu.HBM((rows, columns), BF16)
-    key_b, value_grad, land_early = call(
-        functools.partial(key_half_kernel, 0),
-        (some,),
+    key_b, value_grad, *land_pieces = call(
+        key_kernel,
+        (pairs,),
         [own_arr],
-        key_in,
-        specs,
-        [tokens_hbm, tokens_hbm, half_shape],
-        [specs[0], specs[0], land_pair],
-        products,
-        flops=3 << 30,
+        [key_rows, value_rows, pb, land, norm, center, more_q, land_k],
+        [token_pair, token_pair, factor_pair, lq_pair, flat_pair, whole((heads, LANDMARKS))]
+        + [whole(more.shape), whole(land_shape.shape)],
+        [tokens, tokens] + [land_piece] * count,
+        [token_pair, token_pair] + [whole(land_piece.shape)] * count,
+        [pltpu.VMEM(land_shape.shape, BF16)] + products,
+        flops=6 << 30,
         name="key_grad",
-    )
-    (pb, land_early), weight_own = lax.optimization_barrier(((pb, land_early), weight_own))
-    key_in[2] = pb
-    specs = key_specs(some)
-    key_b, value_grad, *land_pieces = call(
-        functools.partial(key_rest_kernel, some),
-        (pairs - some,),
-        [own_arr],
-        key_in + [land_early, land_k, held_in_hbm(key_b), held_in_hbm(value_grad)],
-        specs + [whole(half_shape.shape), whole(land_shape.shape), in_hbm, in_hbm],
-        [tokens_hbm, tokens_hbm] + [land_piece] * count,
-        [specs[0], specs[0]] + [whole(land_piece.shape)] * count,
-        [pltpu.VMEM((LANDMARKS, (pairs - some) * PAIR), BF16)] + products,
-        flops=3 << 30,
-        name="key_grad_rest",
-        aliases={len(key_in) + 3: 0, len(key_in) + 4: 1},
     )
     if not sorted_here:
         land_pieces = split_by_partner(land_pieces[0].reshape(n, land_dev, 2 * columns), n, me)
+    mixed = call(
+        mixed_kernel,
+        (4,),
+        [mine_arr],
+        [attn, out_weight, arrived],
+        [row_block, pl.BlockSpec((columns, half), lambda j, mine: (0, mine[0])), half_block],
+        shape_of((rows, half), BF16),
+        half_block,
+        flops=1 << 30,
+        name="mixed",
+    )
     weights = gather_first(weight_own, n)
-    weights, land_pieces = lax.optimization_barrier((weights, land_pieces))
+    (shift, count), later = groups[0], groups[1:]
+    land_sum = scatter_step(land_pieces, shift, count, n).astype(BF16)
+    weights, land_sum, mixed = lax.optimization_barrier((weights, land_sum, mixed))
     weights = gather_rest(weights, n)
-    land_own = scatter_pieces(land_pieces, n, groups)[0] * (1.0 / seg_len)
+    land_sum = land_sum.reshape((-1, following) + land_sum.shape[1:])
+    land_own = scatter_pieces([land_sum[:, m] for m in range(following)], n, later)[0] * (1.0 / seg_len)
 
     def finish(token_part, land_part):
         return (
@@ -759,7 +742,6 @@
             .reshape(rows, columns)
         )
 
-    weights, mixed = lax.optimization_barrier((weights, mixed))
     weight_grad = call(
         functools.partial(unpack_kernel, split),
         (1,),

time: 127 us -> 128 us (level)
  matrix products: 6.86 us -> 3.84 us
  Pallas kernels: 42.8 us -> 45.5 us
  starting transfers between devices: 47.5 us -> 50.1 us
  waiting for transfers between devices: 23 us -> 21.7 us
    dot_general x3 -> x1, matrix products: 6.86 us -> 3.84 us  [dot(): lax.dot_general(left, right, (dims, ((), ())), preferred_element_type=F32)]
    pallas_call x11 -> x12, Pallas kernels: 42.8 us -> 45.5 us  [call(): pl.pallas_call(kernel, grid_spec=pltpu.PrefetchScalarGridSpec(num_scalar_...]
    ppermute x36, starting transfers between devices: 47.5 us -> 50.1 us  [exchange(): return lax.ppermute(block, 'seq', [(i, i ^ mask) for i in range(n)])]
    ppermute x36, waiting for transfers between devices: 23 us -> 21.7 us  [exchange(): return lax.ppermute(block, 'seq', [(i, i ^ mask) for i in range(n)])]
    unnamed x28 -> x20, local copies, waits for them, and re-layouts: 3.12 us -> 3.08 us
  transfers between devices with their start and end apart: 37 -> 37, of which waited for: 15 -> 14; matrix products, arithmetic and copies ran while one was open for 7% -> 5% of each run, Pallas kernels for 18% -> 20%
where the time goes in v3:
time: 128 us
  starting transfers between devices  50.1 us (39%)
  Pallas kernels  45.5 us (36%)
  waiting for transfers between devices  21.7 us (17%)
  matrix products  3.84 us (3%)
  local copies, waits for them, and re-layouts  3.11 us (2%)
  other arithmetic  2.32 us (2%)
    ppermute x36, starting transfers between devices, exchange(): return lax.ppermute(block, 'seq', [(i, i ^ mask) for i in range(n)])  50.1 us
    pallas_call x12, Pallas kernels, call(): pl.pallas_call(kernel, grid_spec=pltpu.PrefetchScalarGridSpec(num_scalar_...  45.5 us
    ppermute x36, waiting for transfers between devices, exchange(): return lax.ppermute(block, 'seq', [(i, i ^ mask) for i in range(n)])  21.7 us
    dot_general x1, matrix products, dot(): lax.dot_general(left, right, (dims, ((), ())), preferred_element_type=F32)  3.84 us
    unnamed x20, local copies, waits for them, and re-layouts  3.08 us
  transfers between devices with their start and end apart: 37, of which 14 were waited for; matrix products, arithmetic and copies ran while one was open for 5% of the time, Pallas kernels for 20%

profile of v3, /device:TPU:0, one launch (start us, length us, event | category | flops | bytes accessed | tf_op | source)
XLA Modules:
  0.0 127.7 jit_solution(4874608133086779100)
XLA Ops:
  0.6 1.7 %means.1 = bf16[16,1024]{1,0:T(8,128)(2,1)S(1)} custom-call(bf16[1024,512]{1,0:T(8,128)(2,1)} %q_ref.5, bf16[1024,512]{1,0:T(8,128)(2,1)} %k_ref.4), custom_call_target="tpu_custom_call" | custom-call | bytes 4194304 | tf_op jit(solution)/shard_map/means/pallas_call | solution.py:479
  2.4 5.1 %collective-permute-start.2 = (bf16[1,16,1024]{2,1,0:T(8,128)(2,1)S(1)}, bf16[1,16,1024]{2,1,0:T(8,128)(2,1)S(1)}, u32[]{:S(2)}, u32[]{:S(2)}) collective-permute-start(bf16[1,16,1024]{2,1,0:T(8,128)(2,1)S(1)} %bitcast.59), channel_id=1, source_target_pairs={{0,24},{2,26},{4,28},{6,30},{8,16},{10,18},{12,20},{14,22},{16,8},... | collective-permute-start | bytes 98312 | tf_op jit(solution)/shard_map/ppermute | solution.py:61
  8.1 3.8 %convolution_convert_fusion.g_ref = bf16[1024,512]{1,0:T(8,128)(2,1)} fusion(bf16[1024,1024]{1,0:T(8,128)(2,1)} %cot_ref.1, bf16[512,1024]{1,0:T(8,128)(2,1)S(1)} %copy-done), kind=kOutput, calls=%fused_computation.4 | convolution fusion | flops 1074266112 | bytes 4194304 | tf_op jit(solution)/shard_map/dot_general | solution.py:23
  12.3 2.5 %collective-permute-start.5 = (bf16[4,16,1024]{2,1,0:T(8,128)(2,1)S(1)}, bf16[4,16,1024]{2,1,0:T(8,128)(2,1)S(1)}, u32[]{:S(2)}, u32[]{:S(2)}) collective-permute-start(bf16[4,16,1024]{2,1,0:T(8,128)(2,1)S(1)} %maximum_bitcast_fusion.2.refs_0_), channel_id=1, source_target_pairs={{0,6},{2,4},{4,2},{6,0},{8,14},{10,12},{12,10},{14,8},{16,22},{18,... | collective-permute-start | bytes 393224 | tf_op jit(solution)/shard_map/ppermute | solution.py:61
  16.0 3.3 %collective-permute-done.5.refs_3_ = bf16[4,16,1024]{2,1,0:T(8,128)(2,1)S(1)} collective-permute-done((bf16[4,16,1024]{2,1,0:T(8,128)(2,1)S(1)}, bf16[4,16,1024]{2,1,0:T(8,128)(2,1)S(1)}, u32[]{:S(2)}, u32[]{:S(2)}) %collective-permute-start.5) | collective-permute-done | bytes 131104 | tf_op jit(solution)/shard_map/ppermute | solution.py:61
  20.6 11.2 %forward.1 = (bf16[1024,2048]{1,0:T(8,128)(2,1)}, bf16[1024,2048]{1,0:T(8,128)(2,1)}, f32[4,8,256]{2,1,0:T(8,128)S(1)}, bf16[256,1024]{1,0:T(8,128)(2,1)S(1)}, b...) custom-call(s32[2]{0:T(128)S(1)} %pad_add_fusion.me_ref, ...), custom_call_target="tpu_custom_call" | custom-call | flops 8589934592 | bytes 4194304 | tf_op jit(solution)/shard_map/forward/pallas_call | solution.py:479
  31.8 1.5 %collective-permute-start.6 = (bf16[4,80,256]{2,1,0:T(8,128)(2,1)S(1)}, bf16[4,80,256]{2,1,0:T(8,128)(2,1)S(1)}, u32[]{:S(2)}, u32[]{:S(2)}) collective-permute-start(bf16[4,80,256]{2,1,0:T(8,128)(2,1)S(1)} %get-tuple-element.67), channel_id=1, source_target_pairs={{0,2},{2,0},{4,6},{6,4},{8,10},{10,8},{12,14},{14,12},{16,18},{18,... | collective-permute-start | bytes 491528 | tf_op jit(solution)/shard_map/ppermute | solution.py:61
  35.3 3.7 %newton.1 = (f32[9,256,256]{2,1,0:T(8,128)S(1)}, f32[1,256,256]{2,1,0:T(8,128)S(1)}) custom-call(s32[3]{0:T(128)S(1)} %pad_add_fusion.1.own_ref, bf16[256,1024]{1,0:T(8,128)(2,1)S(1)} %get-tuple-element.70.lq_ref.lk_ref, bf16[256,1024]{1,0:T(8,128)(2,1)S(1)} %get-tuple-element.70.lq_ref.lk_ref), custom_call_target="tpu_custom_call" | custom-call | flops 4294967296 | bytes 4194304 | tf_op jit(solution)/shard_map/newton/pallas_call | solution.py:479
  41.9 1.7 %collective-permute-start.9 = (bf16[1,80,256]{2,1,0:T(8,128)(2,1)S(1)}, bf16[1,80,256]{2,1,0:T(8,128)(2,1)S(1)}, u32[]{:S(2)}, u32[]{:S(2)}) collective-permute-start(bf16[1,80,256]{2,1,0:T(8,128)(2,1)S(1)} %get-tuple-element.78), channel_id=1, source_target_pairs={{0,8},{2,10},{4,12},{6,14},{8,0},{10,2},{12,4},{14,6},{16,24},{18,... | collective-permute-start | bytes 122888 | tf_op jit(solution)/shard_map/ppermute | solution.py:61
  43.7 2.4 %collective-permute-start.10 = (bf16[1,80,256]{2,1,0:T(8,128)(2,1)S(1)}, bf16[1,80,256]{2,1,0:T(8,128)(2,1)S(1)}, u32[]{:S(2)}, u32[]{:S(2)}) collective-permute-start(bf16[1,80,256]{2,1,0:T(8,128)(2,1)S(1)} %get-tuple-element.79), channel_id=1, source_target_pairs={{0,16},{2,18},{4,20},{6,22},{8,24},{10,26},{12,28},{14,30},{16,0},... | collective-permute-start | bytes 122888 | tf_op jit(solution)/shard_map/ppermute | solution.py:61
  46.4 2.8 %collective-permute-done.10.refs_2_ = bf16[1,80,256]{2,1,0:T(8,128)(2,1)S(1)} collective-permute-done((bf16[1,80,256]{2,1,0:T(8,128)(2,1)S(1)}, bf16[1,80,256]{2,1,0:T(8,128)(2,1)S(1)}, u32[]{:S(2)}, u32[]{:S(2)}) %collective-permute-start.10) | collective-permute-done | bytes 40992 | tf_op jit(solution)/shard_map/ppermute | solution.py:61
  49.2 2.7 %collective-permute-done.11.refs_3_ = bf16[1,80,256]{2,1,0:T(8,128)(2,1)S(1)} collective-permute-done((bf16[1,80,256]{2,1,0:T(8,128)(2,1)S(1)}, bf16[1,80,256]{2,1,0:T(8,128)(2,1)S(1)}, u32[]{:S(2)}, u32[]{:S(2)}) %collective-permute-start.11) | collective-permute-done | bytes 40992 | tf_op jit(solution)/shard_map/ppermute | solution.py:61
  52.8 3.9 %collective-permute-start.12 = (bf16[1,80,256]{2,1,0:T(8,128)(2,1)S(1)}, bf16[1,80,256]{2,1,0:T(8,128)(2,1)S(1)}, u32[]{:S(2)}, u32[]{:S(2)}) collective-permute-start(bf16[1,80,256]{2,1,0:T(8,128)(2,1)S(1)} %get-tuple-element.82), channel_id=1, source_target_pairs={{0,8},{2,10},{4,12},{6,14},{8,0},{10,2},{12,4},{14,6},{16,24},{18,... | collective-permute-start | bytes 122888 | tf_op jit(solution)/shard_map/ppermute | solution.py:61
  58.7 1.5 %collective-permute-start.17 = (bf16[4,80,256]{2,1,0:T(8,128)(2,1)S(1)}, bf16[4,80,256]{2,1,0:T(8,128)(2,1)S(1)}, u32[]{:S(2)}, u32[]{:S(2)}) collective-permute-start(bf16[4,80,256]{2,1,0:T(8,128)(2,1)S(1)} %maximum_bitcast_fusion.1.refs_0_), channel_id=1, source_target_pairs={{0,6},{2,4},{4,2},{6,0},{8,14},{10,12},{12,10},{14,8},{16,22},{18,... | collective-permute-start | bytes 491528 | tf_op jit(solution)/shard_map/ppermute | solution.py:61
  62.2 1.7 %copy-done.9 = f32[9,256,256]{2,1,0:T(8,128)S(1)} copy-done((f32[9,256,256]{2,1,0:T(8,128)S(1)}, f32[9,256,256]{2,1,0:T(8,128)}, u32[]{:S(2)}) %copy-start.9) | copy-done | bytes 2359320
  63.9 4.2 %newton_grad.1 = (f32[256,128]{1,0:T(8,128)S(1)}, f32[256,128]{1,0:T(8,128)S(1)}) custom-call(s32[3]{0:T(128)S(1)} %pad_add_fusion.1.own_ref, f32[9,256,256]{2,1,0:T(8,128)S(1)} %copy-done.9, f32[32,256]{1,0:T(8,128)S(1)} %get-tuple-element.84.values_ref, f32[32,256]{1,0:T(8,128)S(1)} %get-tuple-element.85.grads_ref, ...), custom_call_target="tpu_custom_call" | custom-call | flops 8589934592 | bytes 4194304 | tf_op jit(solution)/shard_map/newton_grad/pallas_call | solution.py:479
  68.2 4.7 %attend.1 = (bf16[1024,512]{1,0:T(8,128)(2,1)S(1)}, bf16[512,256]{1,0:T(8,128)(2,1)S(1)}, bf16[512,256]{1,0:T(8,128)(2,1)S(1)}, f32[8,256]{1,0:T(8,128)S(1)}, bf...) custom-call(s32[2]{0:T(128)S(1)} %pad_add_fusion.me_ref, ...), custom_call_target="tpu_custom_call" | custom-call | flops 4294967296 | bytes 4194304 | tf_op jit(solution)/shard_map/attend/pallas_call | solution.py:479
  75.0 1.5 %collective-permute-start.20 = (bf16[4,32,1024]{2,1,0:T(8,128)(2,1)S(1)}, bf16[4,32,1024]{2,1,0:T(8,128)(2,1)S(1)}, u32[]{:S(2)}, u32[]{:S(2)}) collective-permute-start(bf16[4,32,1024]{2,1,0:T(8,128)(2,1)S(1)} %get-tuple-element.95), channel_id=1, source_target_pairs={{0,6},{2,4},{4,2},{6,0},{8,14},{10,12},{12,10},{14,8},{16,22},{18,... | collective-permute-start | bytes 786440 | tf_op jit(solution)/shard_map/ppermute | solution.py:61
  76.4 6.2 %query_grad.1 = (bf16[1024,512]{1,0:T(8,128)(2,1)S(1)}, bf16[256,512]{1,0:T(8,128)(2,1)S(1)}) custom-call(s32[3]{0:T(128)S(1)} %pad_add_fusion.1.own_ref, bf16[1024,512]{1,0:T(8,128)(2,1)S(1)} %copy-done.1, bf16[1024,512]{1,0:T(8,128)(2,1)S(1)} %copy-done.6, bf16[1024,2048]{1,0:T(8,128)(2,1)S(1)} %copy-done.5, ...), custom_call_target="tpu_custom_call" | custom-call | flops 6442450944 | bytes 4194304 | tf_op jit(solution)/shard_map/query_grad/pallas_call | solution.py:479
  84.2 2.1 %collective-permute-start.21 = (bf16[1,32,1024]{2,1,0:T(8,128)(2,1)S(1)}, bf16[1,32,1024]{2,1,0:T(8,128)(2,1)S(1)}, u32[]{:S(2)}, u32[]{:S(2)}) collective-permute-start(bf16[1,32,1024]{2,1,0:T(8,128)(2,1)S(1)} %get-tuple-element.121), channel_id=1, source_target_pairs={{0,8},{2,10},{4,12},{6,14},{8,0},{10,2},{12,4},{14,6},{16,24},{18,... | collective-permute-start | bytes 196616 | tf_op jit(solution)/shard_map/ppermute | solution.py:61
  87.9 7.6 %key_grad.1 = (bf16[1024,512]{1,0:T(8,128)(2,1)S(1)}, bf16[1024,512]{1,0:T(8,128)(2,1)}, bf16[4,16,1024]{2,1,0:T(8,128)(2,1)S(1)}, bf16[4,16,1024]{2,1,0:T(8,128...) custom-call(s32[3]{0:T(128)S(1)} %pad_add_fusion.1.own_ref, ...), custom_call_target="tpu_custom_call" | custom-call | flops 6442450944 | bytes 4194304 | tf_op jit(solution)/shard_map/key_grad/pallas_call | solution.py:479
  97.5 1.5 %collective-permute-start.29 = (bf16[4,16,1024]{2,1,0:T(8,128)(2,1)S(1)}, bf16[4,16,1024]{2,1,0:T(8,128)(2,1)S(1)}, u32[]{:S(2)}, u32[]{:S(2)}) collective-permute-start(bf16[4,16,1024]{2,1,0:T(8,128)(2,1)S(1)} %get-tuple-element.110), channel_id=1, source_target_pairs={{0,6},{2,4},{4,2},{6,0},{8,14},{10,12},{12,10},{14,8},{16,22},{18,... | collective-permute-start | bytes 393224 | tf_op jit(solution)/shard_map/ppermute | solution.py:61
  99.0 2.4 %collective-permute-start.26 = (bf16[1,32,1024]{2,1,0:T(8,128)(2,1)S(1)}, bf16[1,32,1024]{2,1,0:T(8,128)(2,1)S(1)}, u32[]{:S(2)}, u32[]{:S(2)}) collective-permute-start(bf16[1,32,1024]{2,1,0:T(8,128)(2,1)S(1)} %fusion.4), channel_id=1, source_target_pairs={{0,24},{2,26},{4,28},{6,30},{8,16},{10,18},{12,20},{14,22},{16,8},... | collective-permute-start | bytes 196616 | tf_op jit(solution)/shard_map/ppermute | solution.py:61
  101.7 1.9 %collective-permute-start.25 = (bf16[1,32,1024]{2,1,0:T(8,128)(2,1)S(1)}, bf16[1,32,1024]{2,1,0:T(8,128)(2,1)S(1)}, u32[]{:S(2)}, u32[]{:S(2)}) collective-permute-start(bf16[1,32,1024]{2,1,0:T(8,128)(2,1)S(1)} %fusion.4), channel_id=1, source_target_pairs={{0,16},{2,18},{4,20},{6,22},{8,24},{10,26},{12,28},{14,30},{16,0},... | collective-permute-start | bytes 196616 | tf_op jit(solution)/shard_map/ppermute | solution.py:61
  104.7 2.8 %collective-permute-start.24 = (bf16[1,32,1024]{2,1,0:T(8,128)(2,1)S(1)}, bf16[1,32,1024]{2,1,0:T(8,128)(2,1)S(1)}, u32[]{:S(2)}, u32[]{:S(2)}) collective-permute-start(bf16[1,32,1024]{2,1,0:T(8,128)(2,1)S(1)} %fusion.4), channel_id=1, source_target_pairs={{0,8},{2,10},{4,12},{6,14},{8,0},{10,2},{12,4},{14,6},{16,24},{18,... | collective-permute-start | bytes 196616 | tf_op jit(solution)/shard_map/ppermute | solution.py:61
  107.7 2.4 %mixed.1 = bf16[1024,512]{1,0:T(8,128)(2,1)} custom-call(s32[1]{0:T(128)} %bitcast.14._, bf16[1024,512]{1,0:T(8,128)(2,1)S(1)} %get-tuple-element.96.attn_ref, bf16[512,1024]{1,0:T(8,128)(2,1)S(1)} %copy-done, bf16[1024,512]{1,0:T(8,128)(2,1)S(1)} %collective-permute-done.30.other_ref), custom_call_target="tpu_custom_call" | custom-call | flops 1073741824 | bytes 4194304 | tf_op jit(solution)/shard_map/mixed/pallas_call | solution.py:479
  110.1 1.8 %collective-permute-start.31 = (bf16[1,16,1024]{2,1,0:T(8,128)(2,1)S(1)}, bf16[1,16,1024]{2,1,0:T(8,128)(2,1)S(1)}, u32[]{:S(2)}, u32[]{:S(2)}) collective-permute-start(bf16[1,16,1024]{2,1,0:T(8,128)(2,1)S(1)} %get-tuple-element.124), channel_id=1, source_target_pairs={{0,8},{2,10},{4,12},{6,14},{8,0},{10,2},{12,4},{14,6},{16,24},{18,... | collective-permute-start | bytes 98312 | tf_op jit(solution)/shard_map/ppermute | solution.py:61
  113.7 1.6 %collective-permute-start.36 = (bf16[4,32,1024]{2,1,0:T(8,128)(2,1)S(1)}, bf16[4,32,1024]{2,1,0:T(8,128)(2,1)S(1)}, u32[]{:S(2)}, u32[]{:S(2)}) collective-permute-start(bf16[4,32,1024]{2,1,0:T(8,128)(2,1)S(1)} %maximum_bitcast_fusion.refs_0_), channel_id=1, source_target_pairs={{0,6},{2,4},{4,2},{6,0},{8,14},{10,12},{12,10},{14,8},{16,22},{18,... | collective-permute-start | bytes 786440 | tf_op jit(solution)/shard_map/ppermute | solution.py:61
  117.7 1.8 %fusion = (bf16[1024,512]{1,0:T(8,128)(2,1)}, bf16[1024,512]{1,0:T(8,128)(2,1)}) fusion(bf16[1024,512]{1,0:T(8,128)(2,1)S(1)} %get-tuple-element.115, f32[16,512]{1,0:T(8,128)S(1)} %get-tuple-element.127, f32[16,512]{1,0:T(8,128)S(1)} %get-tuple-element.128, bf16[1024,512]{1,0:T(8,128)(2,1)S(1)} %get-tuple-element.113), kind=kLoop, calls=%fused_computation.1 | loop fusion | flops 3145728 | bytes 4259840 | tf_op jit(solution)/shard_map/convert_element_type | solution.py:741
  119.5 3.4 %collective-permute-done.36.refs_3_ = bf16[4,32,1024]{2,1,0:T(8,128)(2,1)S(1)} collective-permute-done((bf16[4,32,1024]{2,1,0:T(8,128)(2,1)S(1)}, bf16[4,32,1024]{2,1,0:T(8,128)(2,1)S(1)}, u32[]{:S(2)}, u32[]{:S(2)}) %collective-permute-start.36) | collective-permute-done | bytes 262176 | tf_op jit(solution)/shard_map/ppermute | solution.py:61
  122.8 2.7 %collective-permute-done.35.refs_2_ = bf16[4,32,1024]{2,1,0:T(8,128)(2,1)S(1)} collective-permute-done((bf16[4,32,1024]{2,1,0:T(8,128)(2,1)S(1)}, bf16[4,32,1024]{2,1,0:T(8,128)(2,1)S(1)}, u32[]{:S(2)}, u32[]{:S(2)}) %collective-permute-start.35) | collective-permute-done | bytes 262176 | tf_op jit(solution)/shard_map/ppermute | solution.py:61
  125.5 2.0 %unpack.1 = f32[512,1024]{1,0:T(8,128)} custom-call(s32[2]{0:T(128)S(1)} %pad_add_fusion.me_ref, bf16[4,32,1024]{2,1,0:T(8,128)(2,1)S(1)} %maximum_bitcast_fusion.refs_0_, bf16[4,32,1024]{2,1,0:T(8,128)(2,1)S(1)} %collective-permute-done.34.refs_1_, bf16[4,32,1024]{2,1,0:T(8,128)(2,1)S(1)} %collective-permute-done.35.refs_2_, ...), custom_call_target="tpu_custom_call" | custom-call | bytes 4194304 | tf_op jit(solution)/shard_map/unpack/pallas_call | solution.py:479
  (88 shorter events, 26.7 us)
Async XLA Ops:
  2.4 9.6 %collective-permute-start.2 = (bf16[1,16,1024]{2,1,0:T(8,128)(2,1)S(1)}, bf16[1,16,1024]{2,1,0:T(8,128)(2,1)S(1)}, u32[]{:S(2)}, u32[]{:S(2)}) collective-permute-start(bf16[1,16,1024]{2,1,0:T(8,128)(2,1)S(1)} %bitcast.59), channel_id=1, source_target_pairs={{0,24},{2,26},{4,28},{6,30},{8,16},{10,18},{12,20},{14,22},{16,8},... | collective-permute-start | bytes 98312 | tf_op jit(solution)/shard_map/ppermute | solution.py:61
  12.3 7.0 %collective-permute-start.5 = (bf16[4,16,1024]{2,1,0:T(8,128)(2,1)S(1)}, bf16[4,16,1024]{2,1,0:T(8,128)(2,1)S(1)}, u32[]{:S(2)}, u32[]{:S(2)}) collective-permute-start(bf16[4,16,1024]{2,1,0:T(8,128)(2,1)S(1)} %maximum_bitcast_fusion.2.refs_0_), channel_id=1, source_target_pairs={{0,6},{2,4},{4,2},{6,0},{8,14},{10,12},{12,10},{14,8},{16,22},{18,... | collective-permute-start | bytes 393224 | tf_op jit(solution)/shard_map/ppermute | solution.py:61
  14.8 5.6 %collective-permute-start.4 = (bf16[4,16,1024]{2,1,0:T(8,128)(2,1)S(1)}, bf16[4,16,1024]{2,1,0:T(8,128)(2,1)S(1)}, u32[]{:S(2)}, u32[]{:S(2)}) collective-permute-start(bf16[4,16,1024]{2,1,0:T(8,128)(2,1)S(1)} %maximum_bitcast_fusion.2.refs_0_), channel_id=1, source_target_pairs={{0,4},{2,6},{4,0},{6,2},{8,12},{10,14},{12,8},{14,10},{16,20},{18,... | collective-permute-start | bytes 393224 | tf_op jit(solution)/shard_map/ppermute | solution.py:61
  31.8 8.5 %collective-permute-start.6 = (bf16[4,80,256]{2,1,0:T(8,128)(2,1)S(1)}, bf16[4,80,256]{2,1,0:T(8,128)(2,1)S(1)}, u32[]{:S(2)}, u32[]{:S(2)}) collective-permute-start(bf16[4,80,256]{2,1,0:T(8,128)(2,1)S(1)} %get-tuple-element.67), channel_id=1, source_target_pairs={{0,2},{2,0},{4,6},{6,4},{8,10},{10,8},{12,14},{14,12},{16,18},{18,... | collective-permute-start | bytes 491528 | tf_op jit(solution)/shard_map/ppermute | solution.py:61
  33.3 8.5 %collective-permute-start.7 = (bf16[4,80,256]{2,1,0:T(8,128)(2,1)S(1)}, bf16[4,80,256]{2,1,0:T(8,128)(2,1)S(1)}, u32[]{:S(2)}, u32[]{:S(2)}) collective-permute-start(bf16[4,80,256]{2,1,0:T(8,128)(2,1)S(1)} %get-tuple-element.68), channel_id=1, source_target_pairs={{0,4},{2,6},{4,0},{6,2},{8,12},{10,14},{12,8},{14,10},{16,20},{18,... | collective-permute-start | bytes 491528 | tf_op jit(solution)/shard_map/ppermute | solution.py:61
  34.0 7.8 %collective-permute-start.8 = (bf16[4,80,256]{2,1,0:T(8,128)(2,1)S(1)}, bf16[4,80,256]{2,1,0:T(8,128)(2,1)S(1)}, u32[]{:S(2)}, u32[]{:S(2)}) collective-permute-start(bf16[4,80,256]{2,1,0:T(8,128)(2,1)S(1)} %get-tuple-element.69), channel_id=1, source_target_pairs={{0,6},{2,4},{4,2},{6,0},{8,14},{10,12},{12,10},{14,8},{16,22},{18,... | collective-permute-start | bytes 491528 | tf_op jit(solution)/shard_map/ppermute | solution.py:61
  43.7 5.5 %collective-permute-start.10 = (bf16[1,80,256]{2,1,0:T(8,128)(2,1)S(1)}, bf16[1,80,256]{2,1,0:T(8,128)(2,1)S(1)}, u32[]{:S(2)}, u32[]{:S(2)}) collective-permute-start(bf16[1,80,256]{2,1,0:T(8,128)(2,1)S(1)} %get-tuple-element.79), channel_id=1, source_target_pairs={{0,16},{2,18},{4,20},{6,22},{8,24},{10,26},{12,28},{14,30},{16,0},... | collective-permute-start | bytes 122888 | tf_op jit(solution)/shard_map/ppermute | solution.py:61
  46.1 5.8 %collective-permute-start.11 = (bf16[1,80,256]{2,1,0:T(8,128)(2,1)S(1)}, bf16[1,80,256]{2,1,0:T(8,128)(2,1)S(1)}, u32[]{:S(2)}, u32[]{:S(2)}) collective-permute-start(bf16[1,80,256]{2,1,0:T(8,128)(2,1)S(1)} %get-tuple-element.80), channel_id=1, source_target_pairs={{0,24},{2,26},{4,28},{6,30},{8,16},{10,18},{12,20},{14,22},{16,8},... | collective-permute-start | bytes 122888 | tf_op jit(solution)/shard_map/ppermute | solution.py:61
  52.2 5.9 %collective-permute-start.14 = (bf16[1,80,256]{2,1,0:T(8,128)(2,1)S(1)}, bf16[1,80,256]{2,1,0:T(8,128)(2,1)S(1)}, u32[]{:S(2)}, u32[]{:S(2)}) collective-permute-start(bf16[1,80,256]{2,1,0:T(8,128)(2,1)S(1)} %get-tuple-element.82), channel_id=1, source_target_pairs={{0,24},{2,26},{4,28},{6,30},{8,16},{10,18},{12,20},{14,22},{16,8},... | collective-permute-start | bytes 122888 | tf_op jit(solution)/shard_map/ppermute | solution.py:61
  52.8 5.3 %collective-permute-start.13 = (bf16[1,80,256]{2,1,0:T(8,128)(2,1)S(1)}, bf16[1,80,256]{2,1,0:T(8,128)(2,1)S(1)}, u32[]{:S(2)}, u32[]{:S(2)}) collective-permute-start(bf16[1,80,256]{2,1,0:T(8,128)(2,1)S(1)} %get-tuple-element.82), channel_id=1, source_target_pairs={{0,16},{2,18},{4,20},{6,22},{8,24},{10,26},{12,28},{14,30},{16,0},... | collective-permute-start | bytes 122888 | tf_op jit(solution)/shard_map/ppermute | solution.py:61
  52.8 5.9 %collective-permute-start.12 = (bf16[1,80,256]{2,1,0:T(8,128)(2,1)S(1)}, bf16[1,80,256]{2,1,0:T(8,128)(2,1)S(1)}, u32[]{:S(2)}, u32[]{:S(2)}) collective-permute-start(bf16[1,80,256]{2,1,0:T(8,128)(2,1)S(1)} %get-tuple-element.82), channel_id=1, source_target_pairs={{0,8},{2,10},{4,12},{6,14},{8,0},{10,2},{12,4},{14,6},{16,24},{18,... | collective-permute-start | bytes 122888 | tf_op jit(solution)/shard_map/ppermute | solution.py:61
  58.7 9.5 %collective-permute-start.17 = (bf16[4,80,256]{2,1,0:T(8,128)(2,1)S(1)}, bf16[4,80,256]{2,1,0:T(8,128)(2,1)S(1)}, u32[]{:S(2)}, u32[]{:S(2)}) collective-permute-start(bf16[4,80,256]{2,1,0:T(8,128)(2,1)S(1)} %maximum_bitcast_fusion.1.refs_0_), channel_id=1, source_target_pairs={{0,6},{2,4},{4,2},{6,0},{8,14},{10,12},{12,10},{14,8},{16,22},{18,... | collective-permute-start | bytes 491528 | tf_op jit(solution)/shard_map/ppermute | solution.py:61
  60.2 8.0 %collective-permute-start.16 = (bf16[4,80,256]{2,1,0:T(8,128)(2,1)S(1)}, bf16[4,80,256]{2,1,0:T(8,128)(2,1)S(1)}, u32[]{:S(2)}, u32[]{:S(2)}) collective-permute-start(bf16[4,80,256]{2,1,0:T(8,128)(2,1)S(1)} %maximum_bitcast_fusion.1.refs_0_), channel_id=1, source_target_pairs={{0,4},{2,6},{4,0},{6,2},{8,12},{10,14},{12,8},{14,10},{16,20},{18,... | collective-permute-start | bytes 491528 | tf_op jit(solution)/shard_map/ppermute | solution.py:61
  61.0 7.1 %collective-permute-start.15 = (bf16[4,80,256]{2,1,0:T(8,128)(2,1)S(1)}, bf16[4,80,256]{2,1,0:T(8,128)(2,1)S(1)}, u32[]{:S(2)}, u32[]{:S(2)}) collective-permute-start(bf16[4,80,256]{2,1,0:T(8,128)(2,1)S(1)} %maximum_bitcast_fusion.1.refs_0_), channel_id=1, source_target_pairs={{0,2},{2,0},{4,6},{6,4},{8,10},{10,8},{12,14},{14,12},{16,18},{18,... | collective-permute-start | bytes 491528 | tf_op jit(solution)/shard_map/ppermute | solution.py:61
  72.9 11.1 %collective-permute-start.18 = (bf16[4,32,1024]{2,1,0:T(8,128)(2,1)S(1)}, bf16[4,32,1024]{2,1,0:T(8,128)(2,1)S(1)}, u32[]{:S(2)}, u32[]{:S(2)}) collective-permute-start(bf16[4,32,1024]{2,1,0:T(8,128)(2,1)S(1)} %get-tuple-element.93), channel_id=1, source_target_pairs={{0,2},{2,0},{4,6},{6,4},{8,10},{10,8},{12,14},{14,12},{16,18},{18,... | collective-permute-start | bytes 786440 | tf_op jit(solution)/shard_map/ppermute | solution.py:61
  73.8 10.2 %collective-permute-start.19 = (bf16[4,32,1024]{2,1,0:T(8,128)(2,1)S(1)}, bf16[4,32,1024]{2,1,0:T(8,128)(2,1)S(1)}, u32[]{:S(2)}, u32[]{:S(2)}) collective-permute-start(bf16[4,32,1024]{2,1,0:T(8,128)(2,1)S(1)} %get-tuple-element.94), channel_id=1, source_target_pairs={{0,4},{2,6},{4,0},{6,2},{8,12},{10,14},{12,8},{14,10},{16,20},{18,... | collective-permute-start | bytes 786440 | tf_op jit(solution)/shard_map/ppermute | solution.py:61
  75.0 9.1 %collective-permute-start.20 = (bf16[4,32,1024]{2,1,0:T(8,128)(2,1)S(1)}, bf16[4,32,1024]{2,1,0:T(8,128)(2,1)S(1)}, u32[]{:S(2)}, u32[]{:S(2)}) collective-permute-start(bf16[4,32,1024]{2,1,0:T(8,128)(2,1)S(1)} %get-tuple-element.95), channel_id=1, source_target_pairs={{0,6},{2,4},{4,2},{6,0},{8,14},{10,12},{12,10},{14,8},{16,22},{18,... | collective-permute-start | bytes 786440 | tf_op jit(solution)/shard_map/ppermute | solution.py:61
  84.2 12.1 %collective-permute-start.21 = (bf16[1,32,1024]{2,1,0:T(8,128)(2,1)S(1)}, bf16[1,32,1024]{2,1,0:T(8,128)(2,1)S(1)}, u32[]{:S(2)}, u32[]{:S(2)}) collective-permute-start(bf16[1,32,1024]{2,1,0:T(8,128)(2,1)S(1)} %get-tuple-element.121), channel_id=1, source_target_pairs={{0,8},{2,10},{4,12},{6,14},{8,0},{10,2},{12,4},{14,6},{16,24},{18,... | collective-permute-start | bytes 196616 | tf_op jit(solution)/shard_map/ppermute | solution.py:61
  86.3 11.2 %collective-permute-start.23 = (bf16[1,32,1024]{2,1,0:T(8,128)(2,1)S(1)}, bf16[1,32,1024]{2,1,0:T(8,128)(2,1)S(1)}, u32[]{:S(2)}, u32[]{:S(2)}) collective-permute-start(bf16[1,32,1024]{2,1,0:T(8,128)(2,1)S(1)} %get-tuple-element.122), channel_id=1, source_target_pairs={{0,24},{2,26},{4,28},{6,30},{8,16},{10,18},{12,20},{14,22},{16,8},... | collective-permute-start | bytes 196616 | tf_op jit(solution)/shard_map/ppermute | solution.py:61
  86.8 12.1 %collective-permute-start.22 = (bf16[1,32,1024]{2,1,0:T(8,128)(2,1)S(1)}, bf16[1,32,1024]{2,1,0:T(8,128)(2,1)S(1)}, u32[]{:S(2)}, u32[]{:S(2)}) collective-permute-start(bf16[1,32,1024]{2,1,0:T(8,128)(2,1)S(1)} %get-tuple-element.123), channel_id=1, source_target_pairs={{0,16},{2,18},{4,20},{6,22},{8,24},{10,26},{12,28},{14,30},{16,0},... | collective-permute-start | bytes 196616 | tf_op jit(solution)/shard_map/ppermute | solution.py:61
  87.9 19.8 %collective-permute-start.30 = (bf16[1024,512]{1,0:T(8,128)(2,1)S(1)}, bf16[1024,512]{1,0:T(8,128)(2,1)S(1)}, u32[]{:S(2)}, u32[]{:S(2)}) collective-permute-start(bf16[1024,512]{1,0:T(8,128)(2,1)S(1)} %part.1), channel_id=1, source_target_pairs={{0,1},{1,0},{2,3},{3,2},{4,5},{5,4},{6,7},{7,6},{8,9},{9,8},{10,11... | collective-permute-start | bytes 3145736 | tf_op jit(solution)/shard_map/ppermute | solution.py:679
  95.4 6.3 %collective-permute-start.27 = (bf16[4,16,1024]{2,1,0:T(8,128)(2,1)S(1)}, bf16[4,16,1024]{2,1,0:T(8,128)(2,1)S(1)}, u32[]{:S(2)}, u32[]{:S(2)}) collective-permute-start(bf16[4,16,1024]{2,1,0:T(8,128)(2,1)S(1)} %get-tuple-element.108), channel_id=1, source_target_pairs={{0,2},{2,0},{4,6},{6,4},{8,10},{10,8},{12,14},{14,12},{16,18},{18,... | collective-permute-start | bytes 393224 | tf_op jit(solution)/shard_map/ppermute | solution.py:61
  96.3 8.4 %collective-permute-start.28 = (bf16[4,16,1024]{2,1,0:T(8,128)(2,1)S(1)}, bf16[4,16,1024]{2,1,0:T(8,128)(2,1)S(1)}, u32[]{:S(2)}, u32[]{:S(2)}) collective-permute-start(bf16[4,16,1024]{2,1,0:T(8,128)(2,1)S(1)} %get-tuple-element.109), channel_id=1, source_target_pairs={{0,4},{2,6},{4,0},{6,2},{8,12},{10,14},{12,8},{14,10},{16,20},{18,... | collective-permute-start | bytes 393224 | tf_op jit(solution)/shard_map/ppermute | solution.py:61
  97.5 10.1 %collective-permute-start.29 = (bf16[4,16,1024]{2,1,0:T(8,128)(2,1)S(1)}, bf16[4,16,1024]{2,1,0:T(8,128)(2,1)S(1)}, u32[]{:S(2)}, u32[]{:S(2)}) collective-permute-start(bf16[4,16,1024]{2,1,0:T(8,128)(2,1)S(1)} %get-tuple-element.110), channel_id=1, source_target_pairs={{0,6},{2,4},{4,2},{6,0},{8,14},{10,12},{12,10},{14,8},{16,22},{18,... | collective-permute-start | bytes 393224 | tf_op jit(solution)/shard_map/ppermute | solution.py:61
  99.0 11.1 %collective-permute-start.26 = (bf16[1,32,1024]{2,1,0:T(8,128)(2,1)S(1)}, bf16[1,32,1024]{2,1,0:T(8,128)(2,1)S(1)}, u32[]{:S(2)}, u32[]{:S(2)}) collective-permute-start(bf16[1,32,1024]{2,1,0:T(8,128)(2,1)S(1)} %fusion.4), channel_id=1, source_target_pairs={{0,24},{2,26},{4,28},{6,30},{8,16},{10,18},{12,20},{14,22},{16,8},... | collective-permute-start | bytes 196616 | tf_op jit(solution)/shard_map/ppermute | solution.py:61
  101.7 8.3 %collective-permute-start.25 = (bf16[1,32,1024]{2,1,0:T(8,128)(2,1)S(1)}, bf16[1,32,1024]{2,1,0:T(8,128)(2,1)S(1)}, u32[]{:S(2)}, u32[]{:S(2)}) collective-permute-start(bf16[1,32,1024]{2,1,0:T(8,128)(2,1)S(1)} %fusion.4), channel_id=1, source_target_pairs={{0,16},{2,18},{4,20},{6,22},{8,24},{10,26},{12,28},{14,30},{16,0},... | collective-permute-start | bytes 196616 | tf_op jit(solution)/shard_map/ppermute | solution.py:61
  104.7 5.3 %collective-permute-start.24 = (bf16[1,32,1024]{2,1,0:T(8,128)(2,1)S(1)}, bf16[1,32,1024]{2,1,0:T(8,128)(2,1)S(1)}, u32[]{:S(2)}, u32[]{:S(2)}) collective-permute-start(bf16[1,32,1024]{2,1,0:T(8,128)(2,1)S(1)} %fusion.4), channel_id=1, source_target_pairs={{0,8},{2,10},{4,12},{6,14},{8,0},{10,2},{12,4},{14,6},{16,24},{18,... | collective-permute-start | bytes 196616 | tf_op jit(solution)/shard_map/ppermute | solution.py:61
  110.1 6.3 %collective-permute-start.31 = (bf16[1,16,1024]{2,1,0:T(8,128)(2,1)S(1)}, bf16[1,16,1024]{2,1,0:T(8,128)(2,1)S(1)}, u32[]{:S(2)}, u32[]{:S(2)}) collective-permute-start(bf16[1,16,1024]{2,1,0:T(8,128)(2,1)S(1)} %get-tuple-element.124), channel_id=1, source_target_pairs={{0,8},{2,10},{4,12},{6,14},{8,0},{10,2},{12,4},{14,6},{16,24},{18,... | collective-permute-start | bytes 98312 | tf_op jit(solution)/shard_map/ppermute | solution.py:61
  111.9 5.7 %collective-permute-start.33 = (bf16[1,16,1024]{2,1,0:T(8,128)(2,1)S(1)}, bf16[1,16,1024]{2,1,0:T(8,128)(2,1)S(1)}, u32[]{:S(2)}, u32[]{:S(2)}) collective-permute-start(bf16[1,16,1024]{2,1,0:T(8,128)(2,1)S(1)} %get-tuple-element.125), channel_id=1, source_target_pairs={{0,24},{2,26},{4,28},{6,30},{8,16},{10,18},{12,20},{14,22},{16,8},... | collective-permute-start | bytes 98312 | tf_op jit(solution)/shard_map/ppermute | solution.py:61
  113.7 9.1 %collective-permute-start.36 = (bf16[4,32,1024]{2,1,0:T(8,128)(2,1)S(1)}, bf16[4,32,1024]{2,1,0:T(8,128)(2,1)S(1)}, u32[]{:S(2)}, u32[]{:S(2)}) collective-permute-start(bf16[4,32,1024]{2,1,0:T(8,128)(2,1)S(1)} %maximum_bitcast_fusion.refs_0_), channel_id=1, source_target_pairs={{0,6},{2,4},{4,2},{6,0},{8,14},{10,12},{12,10},{14,8},{16,22},{18,... | collective-permute-start | bytes 786440 | tf_op jit(solution)/shard_map/ppermute | solution.py:61
  115.3 10.2 %collective-permute-start.35 = (bf16[4,32,1024]{2,1,0:T(8,128)(2,1)S(1)}, bf16[4,32,1024]{2,1,0:T(8,128)(2,1)S(1)}, u32[]{:S(2)}, u32[]{:S(2)}) collective-permute-start(bf16[4,32,1024]{2,1,0:T(8,128)(2,1)S(1)} %maximum_bitcast_fusion.refs_0_), channel_id=1, source_target_pairs={{0,4},{2,6},{4,0},{6,2},{8,12},{10,14},{12,8},{14,10},{16,20},{18,... | collective-permute-start | bytes 786440 | tf_op jit(solution)/shard_map/ppermute | solution.py:61
  116.4 9.1 %collective-permute-start.34 = (bf16[4,32,1024]{2,1,0:T(8,128)(2,1)S(1)}, bf16[4,32,1024]{2,1,0:T(8,128)(2,1)S(1)}, u32[]{:S(2)}, u32[]{:S(2)}) collective-permute-start(bf16[4,32,1024]{2,1,0:T(8,128)(2,1)S(1)} %maximum_bitcast_fusion.refs_0_), channel_id=1, source_target_pairs={{0,2},{2,0},{4,6},{6,4},{8,10},{10,8},{12,14},{14,12},{16,18},{18,... | collective-permute-start | bytes 786440 | tf_op jit(solution)/shard_map/ppermute | solution.py:61
  (15 other events, 82.0 us)

commit v4 on v2

--- a/solution.py
+++ b/solution.py
@@ -13,7 +13,7 @@
 ITERS = 2
 SCALE = 0.125
 CHUNK = 256
-EXTRA = 16
+EXTRA = 8
 F32 = jnp.float32
 BF16 = jnp.bfloat16
 PARAMS = pltpu.CompilerParams(vmem_limit_bytes=24 * 1024 * 1024)
@@ -454,6 +454,14 @@
     land_ref[...] = (sums.T * SCALE + more_ref[...] * here).astype(BF16)
 
 
+def part_kernel(_, attn_ref, weight_ref, out_ref):
+    out_ref[...] = dot(attn_ref[...], weight_ref[...]).astype(BF16)
+
+
+def mixed_kernel(_, attn_ref, weight_ref, other_ref, out_ref):
+    out_ref[...] = (dot(attn_ref[...], weight_ref[...]) + other_ref[...].astype(F32)).astype(BF16)
+
+
 def unpack_kernel(split, me_ref, *refs):
     in_refs, (out_ref, wide_ref, sems) = refs[:-3], refs[-3:]
     size = len(in_refs)
@@ -520,8 +528,11 @@
     size = bit_groups(n)[-1][1]
     height = 2 * cols + EXTRA
     own_head = me // parts
+
+    sorted_here = land_dev % 16 == 0
+    me_arr = jnp.stack([me, me if sorted_here else me * 0]).astype(jnp.int32)
+    mine_arr = mine.reshape(1).astype(jnp.int32)
     own_arr = jnp.stack([own_head // 2, own_head % 2, me * 0 if land_dev % 16 else me]).astype(jnp.int32)
-
     steps = 4
     in_hbm = pl.BlockSpec(memory_space=pltpu.HBM)
     own = call(
@@ -539,26 +550,25 @@
         ],
         name="means",
     )
+    own, me_arr, mine_arr, own_arr = lax.optimization_barrier((own, me_arr, mine_arr, own_arr))
     grad_attn = dot(cotangent, out_weight, NT).astype(BF16)
-    sorted_here = land_dev % 16 == 0
     if sorted_here:
         lands = gather_lists(own, n)
     else:
         lands = [gather_ordered(own, n, me).reshape(LANDMARKS // 16, 16, 2 * columns)]
-    me_arr = jnp.stack([me, me if sorted_here else me * 0]).astype(jnp.int32)
 
     token_pair = pl.BlockSpec((rows, PAIR), lambda j, *_: (0, j))
     factor_pair = pl.BlockSpec((rows, 2 * LANDMARKS), lambda j, *_: (0, j))
     lq_pair = pl.BlockSpec((LANDMARKS, PAIR), lambda j, *_: (0, j))
     lk_pair = pl.BlockSpec((LANDMARKS, PAIR), lambda j, *_: (0, j + pairs))
-    factors = pltpu.HBM((rows, heads * LANDMARKS), BF16)
+    factors = shape_of((rows, heads * LANDMARKS), BF16)
     piece = shape_of((n // size, height, LANDMARKS), BF16)
 
     fb, pb, tops, land, *pieces = call(
         functools.partial(forward_kernel, n, heads, len(lands)),
         (pairs,),
         [me_arr],
-        [held_in_hbm(x) for x in (queries, key_rows, value_rows, grad_attn)] + lands,
+        [queries, key_rows, value_rows, grad_attn] + lands,
         [token_pair] * 4 + [whole(lands[0].shape)] * len(lands),
         [
             factors,
@@ -585,7 +595,7 @@
     square = (LANDMARKS, LANDMARKS)
     own_lq = pl.BlockSpec((LANDMARKS, PAIR), lambda i, own: (0, own[0]))
     own_lk = pl.BlockSpec((LANDMARKS, PAIR), lambda i, own: (0, own[0] + pairs))
-    kept = pltpu.VMEM((1 + 4 * ITERS,) + square, F32)
+    kept = shape_of((1 + 4 * ITERS,) + square, F32)
     saved, inverse = call(
         newton_kernel,
         (1,),
@@ -603,7 +613,7 @@
         got = [pieces[0]] + [exchange(pieces[m], m << shift, n) for m in range(1, count)]
         specs = [whole(got[0].shape)] * count
         if step == 0:
-            got, inverse, saved = lax.optimization_barrier((got, inverse, saved))
+            got, inverse = lax.optimization_barrier((got, inverse))
         if step + 1 < len(groups):
             following = groups[step + 1][1]
             piece = shape_of((got[0].shape[0] // following, height, LANDMARKS), BF16)
@@ -635,7 +645,7 @@
         newton_grad_kernel,
         (1,),
         [own_arr],
-        [pltpu.with_memory_space_constraint(saved, pltpu.VMEM), values, grads, land, land],
+        [saved, values, grads, land, land],
         [whole(kept.shape), whole(small.shape), whole(small.shape), own_lq, own_lk],
         [more, more],
         [whole(more.shape)] * 2,
@@ -677,10 +687,31 @@
     weight_sum = weight_sum.reshape((-1, following) + weight_sum.shape[1:])
     weight_own = scatter_pieces([weight_sum[:, m] for m in range(following)], n, later)[0].astype(BF16)
     half = width // 2
-    there = dot(attn, lax.dynamic_slice_in_dim(out_weight, (1 - mine) * half, half, 1))
-    arrived = lax.ppermute(there.astype(BF16), "head", [(0, 1), (1, 0)])
-    here = dot(attn, lax.dynamic_slice_in_dim(out_weight, mine * half, half, 1))
-    mixed = (here + arrived.astype(F32)).astype(BF16)
+    row_block = pl.BlockSpec((rows // 4, columns), lambda j, _: (j, 0))
+    half_block = pl.BlockSpec((rows // 4, half), lambda j, _: (j, 0))
+    there = call(
+        part_kernel,
+        (4,),
+        [mine_arr],
+        [attn, out_weight],
+        [row_block, pl.BlockSpec((columns, half), lambda j, mine: (0, 1 - mine[0]))],
+        shape_of((rows, half), BF16),
+        half_block,
+        flops=1 << 30,
+        name="part",
+    )
+    arrived = lax.ppermute(there, "head", [(0, 1), (1, 0)])
+    mixed = call(
+        mixed_kernel,
+        (4,),
+        [mine_arr],
+        [attn, out_weight, arrived],
+        [row_block, pl.BlockSpec((columns, half), lambda j, mine: (0, mine[0])), half_block],
+        shape_of((rows, half), BF16),
+        half_block,
+        flops=1 << 30,
+        name="mixed",
+    )
 
     flat_pair = pl.BlockSpec((PAIR, LANDMARKS), lambda j, *_: (j, 0))
     land_pair = pl.BlockSpec((LANDMARKS, PAIR), lambda j, *_: (0, j))

time: 127 us -> 123 us (0.969)
  matrix products: 6.86 us -> 2.87 us
  local copies, waits for them, and re-layouts: 3.15 us -> 0.06 us
  Pallas kernels: 42.8 us -> 45.3 us
    dot_general x3 -> x1, matrix products: 6.86 us -> 2.87 us  [dot(): lax.dot_general(left, right, (dims, ((), ())), preferred_element_type=F32)]
    unnamed x28 -> x12, local copies, waits for them, and re-layouts: 3.12 us -> 0.03 us
    pallas_call x11 -> x13, Pallas kernels: 42.8 us -> 45.3 us  [call(): pl.pallas_call(kernel, grid_spec=pltpu.PrefetchScalarGridSpec(num_scalar_...]
  transfers between devices with their start and end apart: 37 -> 37, of which waited for: 15 -> 18; matrix products, arithmetic and copies ran while one was open for 7% -> 4% of each run, Pallas kernels for 18% -> 21%
where the time goes in v4:
time: 123 us
  starting transfers between devices  47.6 us (39%)
  Pallas kernels  45.3 us (37%)
  waiting for transfers between devices  23.5 us (19%)
  matrix products  2.87 us (2%)
  other arithmetic  2.32 us (2%)
    ppermute x36, starting transfers between devices, exchange(): return lax.ppermute(block, 'seq', [(i, i ^ mask) for i in range(n)])  47.5 us
    pallas_call x13, Pallas kernels, call(): pl.pallas_call(kernel, grid_spec=pltpu.PrefetchScalarGridSpec(num_scalar_...  45.3 us
    ppermute x36, waiting for transfers between devices, exchange(): return lax.ppermute(block, 'seq', [(i, i ^ mask) for i in range(n)])  23.5 us
    dot_general x1, matrix products, dot(): lax.dot_general(left, right, (dims, ((), ())), preferred_element_type=F32)  2.87 us
  transfers between devices with their start and end apart: 37, of which 18 were waited for; matrix products, arithmetic and copies ran while one was open for 4% of the time, Pallas kernels for 21%

profile of v4, /device:TPU:0, one launch (start us, length us, event | category | flops | bytes accessed | tf_op | source)
XLA Modules:
  0.0 122.7 jit_solution(48693964580202965)
XLA Ops:
  0.8 1.7 %means.1 = bf16[16,1024]{1,0:T(8,128)(2,1)S(1)} custom-call(bf16[1024,512]{1,0:T(8,128)(2,1)} %q_ref.5, bf16[1024,512]{1,0:T(8,128)(2,1)} %k_ref.5), custom_call_target="tpu_custom_call" | custom-call | bytes 4194304 | tf_op jit(solution)/shard_map/means/pallas_call | solution.py:499
  2.6 5.1 %collective-permute-start.2 = (bf16[1,16,1024]{2,1,0:T(8,128)(2,1)S(1)}, bf16[1,16,1024]{2,1,0:T(8,128)(2,1)S(1)}, u32[]{:S(2)}, u32[]{:S(2)}) collective-permute-start(bf16[1,16,1024]{2,1,0:T(8,128)(2,1)S(1)} %bitcast.63), channel_id=1, source_target_pairs={{0,24},{2,26},{4,28},{6,30},{8,16},{10,18},{12,20},{14,22},{16,8},... | collective-permute-start | bytes 98312 | tf_op jit(solution)/shard_map/ppermute | solution.py:61
  9.6 2.9 %collective-permute-done.1 = bf16[1,16,1024]{2,1,0:T(8,128)(2,1)S(1)} collective-permute-done((bf16[1,16,1024]{2,1,0:T(8,128)(2,1)S(1)}, bf16[1,16,1024]{2,1,0:T(8,128)(2,1)S(1)}, u32[]{:S(2)}, u32[]{:S(2)}) %collective-permute-start.1) | collective-permute-done | bytes 32800 | tf_op jit(solution)/shard_map/ppermute | solution.py:61
  12.6 2.5 %collective-permute-start.5 = (bf16[4,16,1024]{2,1,0:T(8,128)(2,1)S(1)}, bf16[4,16,1024]{2,1,0:T(8,128)(2,1)S(1)}, u32[]{:S(2)}, u32[]{:S(2)}) collective-permute-start(bf16[4,16,1024]{2,1,0:T(8,128)(2,1)S(1)} %maximum_bitcast_fusion.2.refs_0_), channel_id=1, source_target_pairs={{0,6},{2,4},{4,2},{6,0},{8,14},{10,12},{12,10},{14,8},{16,22},{18,... | collective-permute-start | bytes 393224 | tf_op jit(solution)/shard_map/ppermute | solution.py:61
  16.1 2.9 %convolution_convert_fusion.g_ref = bf16[1024,512]{1,0:T(8,128)(2,1)S(1)} fusion(bf16[1024,1024]{1,0:T(8,128)(2,1)} %cot_ref.1, bf16[512,1024]{1,0:T(8,128)(2,1)S(1)} %copy-done), kind=kOutput, calls=%fused_computation.4 | convolution fusion | flops 1074266112 | bytes 4194304 | tf_op jit(solution)/shard_map/dot_general | solution.py:23
  20.7 10.0 %forward.1 = (bf16[1024,2048]{1,0:T(8,128)(2,1)S(1)}, bf16[1024,2048]{1,0:T(8,128)(2,1)S(1)}, f32[4,8,256]{2,1,0:T(8,128)S(1)}, bf16[256,1024]{1,0:T(8,128)(2,1)...) custom-call(s32[2]{0:T(128)S(1)} %pad_add_fusion.me_ref, ...), custom_call_target="tpu_custom_call" | custom-call | flops 8589934592 | bytes 4194304 | tf_op jit(solution)/shard_map/forward/pallas_call | solution.py:499
  32.7 1.6 %collective-permute-start.8 = (bf16[4,72,256]{2,1,0:T(8,128)(2,1)S(1)}, bf16[4,72,256]{2,1,0:T(8,128)(2,1)S(1)}, u32[]{:S(2)}, u32[]{:S(2)}) collective-permute-start(bf16[4,72,256]{2,1,0:T(8,128)(2,1)S(1)} %get-tuple-element.86), channel_id=1, source_target_pairs={{0,6},{2,4},{4,2},{6,0},{8,14},{10,12},{12,10},{14,8},{16,22},{18,... | collective-permute-start | bytes 442376 | tf_op jit(solution)/shard_map/ppermute | solution.py:61
  34.3 3.7 %newton.1 = (f32[9,256,256]{2,1,0:T(8,128)S(1)}, f32[1,256,256]{2,1,0:T(8,128)S(1)}) custom-call(s32[3]{0:T(128)S(1)} %pad_add_fusion.1.own_ref, bf16[256,1024]{1,0:T(8,128)(2,1)S(1)} %get-tuple-element.88.lq_ref.lk_ref, bf16[256,1024]{1,0:T(8,128)(2,1)S(1)} %get-tuple-element.88.lq_ref.lk_ref), custom_call_target="tpu_custom_call" | custom-call | flops 4294967296 | bytes 4194304 | tf_op jit(solution)/shard_map/newton/pallas_call | solution.py:499
  39.5 2.6 %collective-permute-start.10 = (bf16[1,72,256]{2,1,0:T(8,128)(2,1)S(1)}, bf16[1,72,256]{2,1,0:T(8,128)(2,1)S(1)}, u32[]{:S(2)}, u32[]{:S(2)}) collective-permute-start(bf16[1,72,256]{2,1,0:T(8,128)(2,1)S(1)} %get-tuple-element.96), channel_id=1, source_target_pairs={{0,16},{2,18},{4,20},{6,22},{8,24},{10,26},{12,28},{14,30},{16,0},... | collective-permute-start | bytes 110600 | tf_op jit(solution)/shard_map/ppermute | solution.py:61
  42.1 1.5 %collective-permute-start.11 = (bf16[1,72,256]{2,1,0:T(8,128)(2,1)S(1)}, bf16[1,72,256]{2,1,0:T(8,128)(2,1)S(1)}, u32[]{:S(2)}, u32[]{:S(2)}) collective-permute-start(bf16[1,72,256]{2,1,0:T(8,128)(2,1)S(1)} %get-tuple-element.97), channel_id=1, source_target_pairs={{0,24},{2,26},{4,28},{6,30},{8,16},{10,18},{12,20},{14,22},{16,8},... | collective-permute-start | bytes 110600 | tf_op jit(solution)/shard_map/ppermute | solution.py:61
  44.4 3.5 %collective-permute-done.11.refs_3_ = bf16[1,72,256]{2,1,0:T(8,128)(2,1)S(1)} collective-permute-done((bf16[1,72,256]{2,1,0:T(8,128)(2,1)S(1)}, bf16[1,72,256]{2,1,0:T(8,128)(2,1)S(1)}, u32[]{:S(2)}, u32[]{:S(2)}) %collective-permute-start.11) | collective-permute-done | bytes 36896 | tf_op jit(solution)/shard_map/ppermute | solution.py:61
  48.2 1.5 %collective-permute-start.14 = (bf16[1,72,256]{2,1,0:T(8,128)(2,1)S(1)}, bf16[1,72,256]{2,1,0:T(8,128)(2,1)S(1)}, u32[]{:S(2)}, u32[]{:S(2)}) collective-permute-start(bf16[1,72,256]{2,1,0:T(8,128)(2,1)S(1)} %get-tuple-element.99), channel_id=1, source_target_pairs={{0,24},{2,26},{4,28},{6,30},{8,16},{10,18},{12,20},{14,22},{16,8},... | collective-permute-start | bytes 110600 | tf_op jit(solution)/shard_map/ppermute | solution.py:61
  49.7 2.9 %collective-permute-start.12 = (bf16[1,72,256]{2,1,0:T(8,128)(2,1)S(1)}, bf16[1,72,256]{2,1,0:T(8,128)(2,1)S(1)}, u32[]{:S(2)}, u32[]{:S(2)}) collective-permute-start(bf16[1,72,256]{2,1,0:T(8,128)(2,1)S(1)} %get-tuple-element.99), channel_id=1, source_target_pairs={{0,8},{2,10},{4,12},{6,14},{8,0},{10,2},{12,4},{14,6},{16,24},{18,... | collective-permute-start | bytes 110600 | tf_op jit(solution)/shard_map/ppermute | solution.py:61
  55.0 1.5 %collective-permute-start.17 = (bf16[4,72,256]{2,1,0:T(8,128)(2,1)S(1)}, bf16[4,72,256]{2,1,0:T(8,128)(2,1)S(1)}, u32[]{:S(2)}, u32[]{:S(2)}) collective-permute-start(bf16[4,72,256]{2,1,0:T(8,128)(2,1)S(1)} %maximum_bitcast_fusion.1.refs_0_), channel_id=1, source_target_pairs={{0,6},{2,4},{4,2},{6,0},{8,14},{10,12},{12,10},{14,8},{16,22},{18,... | collective-permute-start | bytes 442376 | tf_op jit(solution)/shard_map/ppermute | solution.py:61
  58.5 4.3 %newton_grad.1 = (f32[256,128]{1,0:T(8,128)S(1)}, f32[256,128]{1,0:T(8,128)S(1)}) custom-call(s32[3]{0:T(128)S(1)} %pad_add_fusion.1.own_ref, f32[9,256,256]{2,1,0:T(8,128)S(1)} %get-tuple-element.100.saved_ref, f32[32,256]{1,0:T(8,128)S(1)} %get-tuple-element.101.values_ref, f32[32,256]{1,0:T(8,128)S(1)} %get-tuple-element.102.grads_ref, ...), custom_call_target="tpu_custom_call" | custom-call | flops 8589934592 | bytes 4194304 | tf_op jit(solution)/shard_map/newton_grad/pallas_call | solution.py:499
  62.9 4.7 %attend.1 = (bf16[1024,512]{1,0:T(8,128)(2,1)S(1)}, bf16[512,256]{1,0:T(8,128)(2,1)S(1)}, bf16[512,256]{1,0:T(8,128)(2,1)S(1)}, f32[8,256]{1,0:T(8,128)S(1)}, bf...) custom-call(s32[2]{0:T(128)S(1)} %pad_add_fusion.me_ref, ...), custom_call_target="tpu_custom_call" | custom-call | flops 4294967296 | bytes 4194304 | tf_op jit(solution)/shard_map/attend/pallas_call | solution.py:499
  71.1 6.2 %query_grad.1 = (bf16[1024,512]{1,0:T(8,128)(2,1)S(1)}, bf16[256,512]{1,0:T(8,128)(2,1)S(1)}) custom-call(s32[3]{0:T(128)S(1)} %pad_add_fusion.1.own_ref, bf16[1024,512]{1,0:T(8,128)(2,1)S(1)} %copy-done.1, bf16[1024,512]{1,0:T(8,128)(2,1)S(1)} %convolution_convert_fusion.g_ref, bf16[1024,2048]{1,0:T(8,128)(2,1)S(1)} %get-tuple-element.81.fb_ref, ...), custom_call_target="tpu_custom_call" | custom-call | flops 6442450944 | bytes 4194304 | tf_op jit(solution)/shard_map/query_grad/pallas_call | solution.py:499
  78.2 1.7 %collective-permute-start.21 = (bf16[1,32,1024]{2,1,0:T(8,128)(2,1)S(1)}, bf16[1,32,1024]{2,1,0:T(8,128)(2,1)S(1)}, u32[]{:S(2)}, u32[]{:S(2)}) collective-permute-start(bf16[1,32,1024]{2,1,0:T(8,128)(2,1)S(1)} %get-tuple-element.151), channel_id=1, source_target_pairs={{0,8},{2,10},{4,12},{6,14},{8,0},{10,2},{12,4},{14,6},{16,24},{18,... | collective-permute-start | bytes 196616 | tf_op jit(solution)/shard_map/ppermute | solution.py:61
  79.8 1.9 %collective-permute-start.23 = (bf16[1,32,1024]{2,1,0:T(8,128)(2,1)S(1)}, bf16[1,32,1024]{2,1,0:T(8,128)(2,1)S(1)}, u32[]{:S(2)}, u32[]{:S(2)}) collective-permute-start(bf16[1,32,1024]{2,1,0:T(8,128)(2,1)S(1)} %get-tuple-element.152), channel_id=1, source_target_pairs={{0,24},{2,26},{4,28},{6,30},{8,16},{10,18},{12,20},{14,22},{16,8},... | collective-permute-start | bytes 196616 | tf_op jit(solution)/shard_map/ppermute | solution.py:61
  81.7 4.3 %key_grad.1 = (bf16[1024,512]{1,0:T(8,128)(2,1)}, bf16[1024,512]{1,0:T(8,128)(2,1)}, bf16[256,256]{1,0:T(8,128)(2,1)S(1)}) custom-call(s32[3]{0:T(128)S(1)} %pad_add_fusion.1.own_ref, bf16[1024,512]{1,0:T(8,128)(2,1)S(1)} %copy-done.2, bf16[1024,512]{1,0:T(8,128)(2,1)S(1)} %copy-done.4, bf16[1024,2048]{1,0:T(8,128)(2,1)S(1)} %get-tuple-element.122.pb_ref, ...), custom_call_target="tpu_custom_call" | custom-call | flops 3221225472 | bytes 4194304 | tf_op jit(solution)/shard_map/key_grad/pallas_call | solution.py:499
  86.6 2.2 %collective-permute-done.22 = bf16[1,32,1024]{2,1,0:T(8,128)(2,1)S(1)} collective-permute-done((bf16[1,32,1024]{2,1,0:T(8,128)(2,1)S(1)}, bf16[1,32,1024]{2,1,0:T(8,128)(2,1)S(1)}, u32[]{:S(2)}, u32[]{:S(2)}) %collective-permute-start.22) | collective-permute-done | bytes 65568 | tf_op jit(solution)/shard_map/ppermute | solution.py:61
  90.2 3.1 %collective-permute-start.24 = (bf16[1,32,1024]{2,1,0:T(8,128)(2,1)S(1)}, bf16[1,32,1024]{2,1,0:T(8,128)(2,1)S(1)}, u32[]{:S(2)}, u32[]{:S(2)}) collective-permute-start(bf16[1,32,1024]{2,1,0:T(8,128)(2,1)S(1)} %bitcast.72), channel_id=1, source_target_pairs={{0,8},{2,10},{4,12},{6,14},{8,0},{10,2},{12,4},{14,6},{16,24},{18,... | collective-permute-start | bytes 196616 | tf_op jit(solution)/shard_map/ppermute | solution.py:61
  93.3 4.3 %key_grad_rest.1 = (bf16[1024,512]{1,0:T(8,128)(2,1)}, bf16[1024,512]{1,0:T(8,128)(2,1)}, bf16[4,16,1024]{2,1,0:T(8,128)(2,1)S(1)}, bf16[4,16,1024]{2,1,0:T(8,12...) custom-call(s32[3]{0:T(128)S(1)} %pad_add_fusion.1.own_ref, ...), custom_call_target="tpu_custom_call", output_to_operand_aliasing={{0}: (10, {}), {1}: (11, {})} | custom-call | flops 3221225472 | bytes 4194304 | tf_op jit(solution)/shard_map/key_grad_rest/pallas_call | solution.py:499
  99.3 1.9 %collective-permute-start.33 = (bf16[4,16,1024]{2,1,0:T(8,128)(2,1)S(1)}, bf16[4,16,1024]{2,1,0:T(8,128)(2,1)S(1)}, u32[]{:S(2)}, u32[]{:S(2)}) collective-permute-start(bf16[4,16,1024]{2,1,0:T(8,128)(2,1)S(1)} %get-tuple-element.144), channel_id=1, source_target_pairs={{0,6},{2,4},{4,2},{6,0},{8,14},{10,12},{12,10},{14,8},{16,22},{18,... | collective-permute-start | bytes 393224 | tf_op jit(solution)/shard_map/ppermute | solution.py:61
  103.5 1.6 %collective-permute-done.33 = bf16[4,16,1024]{2,1,0:T(8,128)(2,1)S(1)} collective-permute-done((bf16[4,16,1024]{2,1,0:T(8,128)(2,1)S(1)}, bf16[4,16,1024]{2,1,0:T(8,128)(2,1)S(1)}, u32[]{:S(2)}, u32[]{:S(2)}) %collective-permute-start.33) | collective-permute-done | bytes 131104 | tf_op jit(solution)/shard_map/ppermute | solution.py:61
  105.3 1.9 %collective-permute-start.36 = (bf16[1,16,1024]{2,1,0:T(8,128)(2,1)S(1)}, bf16[1,16,1024]{2,1,0:T(8,128)(2,1)S(1)}, u32[]{:S(2)}, u32[]{:S(2)}) collective-permute-start(bf16[1,16,1024]{2,1,0:T(8,128)(2,1)S(1)} %get-tuple-element.155), channel_id=1, source_target_pairs={{0,24},{2,26},{4,28},{6,30},{8,16},{10,18},{12,20},{14,22},{16,8},... | collective-permute-start | bytes 98312 | tf_op jit(solution)/shard_map/ppermute | solution.py:61
  107.2 1.6 %collective-permute-start.35 = (bf16[1,16,1024]{2,1,0:T(8,128)(2,1)S(1)}, bf16[1,16,1024]{2,1,0:T(8,128)(2,1)S(1)}, u32[]{:S(2)}, u32[]{:S(2)}) collective-permute-start(bf16[1,16,1024]{2,1,0:T(8,128)(2,1)S(1)} %get-tuple-element.156), channel_id=1, source_target_pairs={{0,16},{2,18},{4,20},{6,22},{8,24},{10,26},{12,28},{14,30},{16,0},... | collective-permute-start | bytes 98312 | tf_op jit(solution)/shard_map/ppermute | solution.py:61
  108.8 2.0 %collective-permute-start.29 = (bf16[4,32,1024]{2,1,0:T(8,128)(2,1)S(1)}, bf16[4,32,1024]{2,1,0:T(8,128)(2,1)S(1)}, u32[]{:S(2)}, u32[]{:S(2)}) collective-permute-start(bf16[4,32,1024]{2,1,0:T(8,128)(2,1)S(1)} %maximum_bitcast_fusion.refs_0_), channel_id=1, source_target_pairs={{0,6},{2,4},{4,2},{6,0},{8,14},{10,12},{12,10},{14,8},{16,22},{18,... | collective-permute-start | bytes 786440 | tf_op jit(solution)/shard_map/ppermute | solution.py:61
  112.4 1.8 %fusion = (bf16[1024,512]{1,0:T(8,128)(2,1)}, bf16[1024,512]{1,0:T(8,128)(2,1)}) fusion(bf16[1024,512]{1,0:T(8,128)(2,1)S(1)} %copy-done.5, f32[16,512]{1,0:T(8,128)S(1)} %get-tuple-element.157, f32[16,512]{1,0:T(8,128)S(1)} %get-tuple-element.158, bf16[1024,512]{1,0:T(8,128)(2,1)S(1)} %get-tuple-element.140), kind=kLoop, calls=%fused_computation.1 | loop fusion | flops 3145728 | bytes 4259840 | tf_op jit(solution)/shard_map/convert_element_type | solution.py:789
  114.2 2.4 %mixed.1 = bf16[1024,512]{1,0:T(8,128)(2,1)} custom-call(s32[1]{0:T(128)} %bitcast.1._, bf16[1024,512]{1,0:T(8,128)(2,1)S(1)} %get-tuple-element.138.attn_ref, bf16[512,1024]{1,0:T(8,128)(2,1)S(1)} %copy-done, bf16[1024,512]{1,0:T(8,128)(2,1)S(1)} %collective-permute-done.30.other_ref), custom_call_target="tpu_custom_call" | custom-call | flops 1073741824 | bytes 4194304 | tf_op jit(solution)/shard_map/mixed/pallas_call | solution.py:499
  118.1 2.5 %collective-permute-done.28.refs_2_ = bf16[4,32,1024]{2,1,0:T(8,128)(2,1)S(1)} collective-permute-done((bf16[4,32,1024]{2,1,0:T(8,128)(2,1)S(1)}, bf16[4,32,1024]{2,1,0:T(8,128)(2,1)S(1)}, u32[]{:S(2)}, u32[]{:S(2)}) %collective-permute-start.28) | collective-permute-done | bytes 262176 | tf_op jit(solution)/shard_map/ppermute | solution.py:61
  120.5 2.0 %unpack.1 = f32[512,1024]{1,0:T(8,128)} custom-call(s32[2]{0:T(128)S(1)} %pad_add_fusion.me_ref, bf16[4,32,1024]{2,1,0:T(8,128)(2,1)S(1)} %maximum_bitcast_fusion.refs_0_, bf16[4,32,1024]{2,1,0:T(8,128)(2,1)S(1)} %collective-permute-done.27.refs_1_, bf16[4,32,1024]{2,1,0:T(8,128)(2,1)S(1)} %collective-permute-done.28.refs_2_, ...), custom_call_target="tpu_custom_call" | custom-call | bytes 4194304 | tf_op jit(solution)/shard_map/unpack/pallas_call | solution.py:499
  (81 shorter events, 27.4 us)
Async XLA Ops:
  2.6 7.0 %collective-permute-start.2 = (bf16[1,16,1024]{2,1,0:T(8,128)(2,1)S(1)}, bf16[1,16,1024]{2,1,0:T(8,128)(2,1)S(1)}, u32[]{:S(2)}, u32[]{:S(2)}) collective-permute-start(bf16[1,16,1024]{2,1,0:T(8,128)(2,1)S(1)} %bitcast.63), channel_id=1, source_target_pairs={{0,24},{2,26},{4,28},{6,30},{8,16},{10,18},{12,20},{14,22},{16,8},... | collective-permute-start | bytes 98312 | tf_op jit(solution)/shard_map/ppermute | solution.py:61
  12.6 7.3 %collective-permute-start.5 = (bf16[4,16,1024]{2,1,0:T(8,128)(2,1)S(1)}, bf16[4,16,1024]{2,1,0:T(8,128)(2,1)S(1)}, u32[]{:S(2)}, u32[]{:S(2)}) collective-permute-start(bf16[4,16,1024]{2,1,0:T(8,128)(2,1)S(1)} %maximum_bitcast_fusion.2.refs_0_), channel_id=1, source_target_pairs={{0,6},{2,4},{4,2},{6,0},{8,14},{10,12},{12,10},{14,8},{16,22},{18,... | collective-permute-start | bytes 393224 | tf_op jit(solution)/shard_map/ppermute | solution.py:61
  15.1 5.6 %collective-permute-start.4 = (bf16[4,16,1024]{2,1,0:T(8,128)(2,1)S(1)}, bf16[4,16,1024]{2,1,0:T(8,128)(2,1)S(1)}, u32[]{:S(2)}, u32[]{:S(2)}) collective-permute-start(bf16[4,16,1024]{2,1,0:T(8,128)(2,1)S(1)} %maximum_bitcast_fusion.2.refs_0_), channel_id=1, source_target_pairs={{0,4},{2,6},{4,0},{6,2},{8,12},{10,14},{12,8},{14,10},{16,20},{18,... | collective-permute-start | bytes 393224 | tf_op jit(solution)/shard_map/ppermute | solution.py:61
  15.6 5.1 %collective-permute-start.3 = (bf16[4,16,1024]{2,1,0:T(8,128)(2,1)S(1)}, bf16[4,16,1024]{2,1,0:T(8,128)(2,1)S(1)}, u32[]{:S(2)}, u32[]{:S(2)}) collective-permute-start(bf16[4,16,1024]{2,1,0:T(8,128)(2,1)S(1)} %maximum_bitcast_fusion.2.refs_0_), channel_id=1, source_target_pairs={{0,2},{2,0},{4,6},{6,4},{8,10},{10,8},{12,14},{14,12},{16,18},{18,... | collective-permute-start | bytes 393224 | tf_op jit(solution)/shard_map/ppermute | solution.py:61
  30.8 7.2 %collective-permute-start.6 = (bf16[4,72,256]{2,1,0:T(8,128)(2,1)S(1)}, bf16[4,72,256]{2,1,0:T(8,128)(2,1)S(1)}, u32[]{:S(2)}, u32[]{:S(2)}) collective-permute-start(bf16[4,72,256]{2,1,0:T(8,128)(2,1)S(1)} %get-tuple-element.84), channel_id=1, source_target_pairs={{0,2},{2,0},{4,6},{6,4},{8,10},{10,8},{12,14},{14,12},{16,18},{18,... | collective-permute-start | bytes 442376 | tf_op jit(solution)/shard_map/ppermute | solution.py:61
  31.9 7.0 %collective-permute-start.7 = (bf16[4,72,256]{2,1,0:T(8,128)(2,1)S(1)}, bf16[4,72,256]{2,1,0:T(8,128)(2,1)S(1)}, u32[]{:S(2)}, u32[]{:S(2)}) collective-permute-start(bf16[4,72,256]{2,1,0:T(8,128)(2,1)S(1)} %get-tuple-element.85), channel_id=1, source_target_pairs={{0,4},{2,6},{4,0},{6,2},{8,12},{10,14},{12,8},{14,10},{16,20},{18,... | collective-permute-start | bytes 442376 | tf_op jit(solution)/shard_map/ppermute | solution.py:61
  32.7 6.2 %collective-permute-start.8 = (bf16[4,72,256]{2,1,0:T(8,128)(2,1)S(1)}, bf16[4,72,256]{2,1,0:T(8,128)(2,1)S(1)}, u32[]{:S(2)}, u32[]{:S(2)}) collective-permute-start(bf16[4,72,256]{2,1,0:T(8,128)(2,1)S(1)} %get-tuple-element.86), channel_id=1, source_target_pairs={{0,6},{2,4},{4,2},{6,0},{8,14},{10,12},{12,10},{14,8},{16,22},{18,... | collective-permute-start | bytes 442376 | tf_op jit(solution)/shard_map/ppermute | solution.py:61
  42.1 5.8 %collective-permute-start.11 = (bf16[1,72,256]{2,1,0:T(8,128)(2,1)S(1)}, bf16[1,72,256]{2,1,0:T(8,128)(2,1)S(1)}, u32[]{:S(2)}, u32[]{:S(2)}) collective-permute-start(bf16[1,72,256]{2,1,0:T(8,128)(2,1)S(1)} %get-tuple-element.97), channel_id=1, source_target_pairs={{0,24},{2,26},{4,28},{6,30},{8,16},{10,18},{12,20},{14,22},{16,8},... | collective-permute-start | bytes 110600 | tf_op jit(solution)/shard_map/ppermute | solution.py:61
  48.2 5.8 %collective-permute-start.14 = (bf16[1,72,256]{2,1,0:T(8,128)(2,1)S(1)}, bf16[1,72,256]{2,1,0:T(8,128)(2,1)S(1)}, u32[]{:S(2)}, u32[]{:S(2)}) collective-permute-start(bf16[1,72,256]{2,1,0:T(8,128)(2,1)S(1)} %get-tuple-element.99), channel_id=1, source_target_pairs={{0,24},{2,26},{4,28},{6,30},{8,16},{10,18},{12,20},{14,22},{16,8},... | collective-permute-start | bytes 110600 | tf_op jit(solution)/shard_map/ppermute | solution.py:61
  49.7 5.2 %collective-permute-start.13 = (bf16[1,72,256]{2,1,0:T(8,128)(2,1)S(1)}, bf16[1,72,256]{2,1,0:T(8,128)(2,1)S(1)}, u32[]{:S(2)}, u32[]{:S(2)}) collective-permute-start(bf16[1,72,256]{2,1,0:T(8,128)(2,1)S(1)} %get-tuple-element.99), channel_id=1, source_target_pairs={{0,16},{2,18},{4,20},{6,22},{8,24},{10,26},{12,28},{14,30},{16,0},... | collective-permute-start | bytes 110600 | tf_op jit(solution)/shard_map/ppermute | solution.py:61
  49.7 5.2 %collective-permute-start.12 = (bf16[1,72,256]{2,1,0:T(8,128)(2,1)S(1)}, bf16[1,72,256]{2,1,0:T(8,128)(2,1)S(1)}, u32[]{:S(2)}, u32[]{:S(2)}) collective-permute-start(bf16[1,72,256]{2,1,0:T(8,128)(2,1)S(1)} %get-tuple-element.99), channel_id=1, source_target_pairs={{0,8},{2,10},{4,12},{6,14},{8,0},{10,2},{12,4},{14,6},{16,24},{18,... | collective-permute-start | bytes 110600 | tf_op jit(solution)/shard_map/ppermute | solution.py:61
  55.0 7.8 %collective-permute-start.17 = (bf16[4,72,256]{2,1,0:T(8,128)(2,1)S(1)}, bf16[4,72,256]{2,1,0:T(8,128)(2,1)S(1)}, u32[]{:S(2)}, u32[]{:S(2)}) collective-permute-start(bf16[4,72,256]{2,1,0:T(8,128)(2,1)S(1)} %maximum_bitcast_fusion.1.refs_0_), channel_id=1, source_target_pairs={{0,6},{2,4},{4,2},{6,0},{8,14},{10,12},{12,10},{14,8},{16,22},{18,... | collective-permute-start | bytes 442376 | tf_op jit(solution)/shard_map/ppermute | solution.py:61
  56.5 6.3 %collective-permute-start.16 = (bf16[4,72,256]{2,1,0:T(8,128)(2,1)S(1)}, bf16[4,72,256]{2,1,0:T(8,128)(2,1)S(1)}, u32[]{:S(2)}, u32[]{:S(2)}) collective-permute-start(bf16[4,72,256]{2,1,0:T(8,128)(2,1)S(1)} %maximum_bitcast_fusion.1.refs_0_), channel_id=1, source_target_pairs={{0,4},{2,6},{4,0},{6,2},{8,12},{10,14},{12,8},{14,10},{16,20},{18,... | collective-permute-start | bytes 442376 | tf_op jit(solution)/shard_map/ppermute | solution.py:61
  57.7 5.1 %collective-permute-start.15 = (bf16[4,72,256]{2,1,0:T(8,128)(2,1)S(1)}, bf16[4,72,256]{2,1,0:T(8,128)(2,1)S(1)}, u32[]{:S(2)}, u32[]{:S(2)}) collective-permute-start(bf16[4,72,256]{2,1,0:T(8,128)(2,1)S(1)} %maximum_bitcast_fusion.1.refs_0_), channel_id=1, source_target_pairs={{0,2},{2,0},{4,6},{6,4},{8,10},{10,8},{12,14},{14,12},{16,18},{18,... | collective-permute-start | bytes 442376 | tf_op jit(solution)/shard_map/ppermute | solution.py:61
  67.5 9.8 %collective-permute-start.18 = (bf16[4,32,1024]{2,1,0:T(8,128)(2,1)S(1)}, bf16[4,32,1024]{2,1,0:T(8,128)(2,1)S(1)}, u32[]{:S(2)}, u32[]{:S(2)}) collective-permute-start(bf16[4,32,1024]{2,1,0:T(8,128)(2,1)S(1)} %get-tuple-element.110), channel_id=1, source_target_pairs={{0,2},{2,0},{4,6},{6,4},{8,10},{10,8},{12,14},{14,12},{16,18},{18,... | collective-permute-start | bytes 786440 | tf_op jit(solution)/shard_map/ppermute | solution.py:61
  68.8 9.2 %collective-permute-start.19 = (bf16[4,32,1024]{2,1,0:T(8,128)(2,1)S(1)}, bf16[4,32,1024]{2,1,0:T(8,128)(2,1)S(1)}, u32[]{:S(2)}, u32[]{:S(2)}) collective-permute-start(bf16[4,32,1024]{2,1,0:T(8,128)(2,1)S(1)} %get-tuple-element.111), channel_id=1, source_target_pairs={{0,4},{2,6},{4,0},{6,2},{8,12},{10,14},{12,8},{14,10},{16,20},{18,... | collective-permute-start | bytes 786440 | tf_op jit(solution)/shard_map/ppermute | solution.py:61
  69.7 8.3 %collective-permute-start.20 = (bf16[4,32,1024]{2,1,0:T(8,128)(2,1)S(1)}, bf16[4,32,1024]{2,1,0:T(8,128)(2,1)S(1)}, u32[]{:S(2)}, u32[]{:S(2)}) collective-permute-start(bf16[4,32,1024]{2,1,0:T(8,128)(2,1)S(1)} %get-tuple-element.112), channel_id=1, source_target_pairs={{0,6},{2,4},{4,2},{6,0},{8,14},{10,12},{12,10},{14,8},{16,22},{18,... | collective-permute-start | bytes 786440 | tf_op jit(solution)/shard_map/ppermute | solution.py:61
  78.2 7.8 %collective-permute-start.21 = (bf16[1,32,1024]{2,1,0:T(8,128)(2,1)S(1)}, bf16[1,32,1024]{2,1,0:T(8,128)(2,1)S(1)}, u32[]{:S(2)}, u32[]{:S(2)}) collective-permute-start(bf16[1,32,1024]{2,1,0:T(8,128)(2,1)S(1)} %get-tuple-element.151), channel_id=1, source_target_pairs={{0,8},{2,10},{4,12},{6,14},{8,0},{10,2},{12,4},{14,6},{16,24},{18,... | collective-permute-start | bytes 196616 | tf_op jit(solution)/shard_map/ppermute | solution.py:61
  79.8 6.8 %collective-permute-start.23 = (bf16[1,32,1024]{2,1,0:T(8,128)(2,1)S(1)}, bf16[1,32,1024]{2,1,0:T(8,128)(2,1)S(1)}, u32[]{:S(2)}, u32[]{:S(2)}) collective-permute-start(bf16[1,32,1024]{2,1,0:T(8,128)(2,1)S(1)} %get-tuple-element.152), channel_id=1, source_target_pairs={{0,24},{2,26},{4,28},{6,30},{8,16},{10,18},{12,20},{14,22},{16,8},... | collective-permute-start | bytes 196616 | tf_op jit(solution)/shard_map/ppermute | solution.py:61
  81.7 7.1 %collective-permute-start.22 = (bf16[1,32,1024]{2,1,0:T(8,128)(2,1)S(1)}, bf16[1,32,1024]{2,1,0:T(8,128)(2,1)S(1)}, u32[]{:S(2)}, u32[]{:S(2)}) collective-permute-start(bf16[1,32,1024]{2,1,0:T(8,128)(2,1)S(1)} %get-tuple-element.153), channel_id=1, source_target_pairs={{0,16},{2,18},{4,20},{6,22},{8,24},{10,26},{12,28},{14,30},{16,0},... | collective-permute-start | bytes 196616 | tf_op jit(solution)/shard_map/ppermute | solution.py:61
  88.9 8.8 %collective-permute-start.26 = (bf16[1,32,1024]{2,1,0:T(8,128)(2,1)S(1)}, bf16[1,32,1024]{2,1,0:T(8,128)(2,1)S(1)}, u32[]{:S(2)}, u32[]{:S(2)}) collective-permute-start(bf16[1,32,1024]{2,1,0:T(8,128)(2,1)S(1)} %bitcast.70), channel_id=1, source_target_pairs={{0,24},{2,26},{4,28},{6,30},{8,16},{10,18},{12,20},{14,22},{16,8},... | collective-permute-start | bytes 196616 | tf_op jit(solution)/shard_map/ppermute | solution.py:61
  90.2 7.4 %collective-permute-start.25 = (bf16[1,32,1024]{2,1,0:T(8,128)(2,1)S(1)}, bf16[1,32,1024]{2,1,0:T(8,128)(2,1)S(1)}, u32[]{:S(2)}, u32[]{:S(2)}) collective-permute-start(bf16[1,32,1024]{2,1,0:T(8,128)(2,1)S(1)} %bitcast.71), channel_id=1, source_target_pairs={{0,16},{2,18},{4,20},{6,22},{8,24},{10,26},{12,28},{14,30},{16,0},... | collective-permute-start | bytes 196616 | tf_op jit(solution)/shard_map/ppermute | solution.py:61
  90.2 7.4 %collective-permute-start.24 = (bf16[1,32,1024]{2,1,0:T(8,128)(2,1)S(1)}, bf16[1,32,1024]{2,1,0:T(8,128)(2,1)S(1)}, u32[]{:S(2)}, u32[]{:S(2)}) collective-permute-start(bf16[1,32,1024]{2,1,0:T(8,128)(2,1)S(1)} %bitcast.72), channel_id=1, source_target_pairs={{0,8},{2,10},{4,12},{6,14},{8,0},{10,2},{12,4},{14,6},{16,24},{18,... | collective-permute-start | bytes 196616 | tf_op jit(solution)/shard_map/ppermute | solution.py:61
  97.6 5.0 %collective-permute-start.31 = (bf16[4,16,1024]{2,1,0:T(8,128)(2,1)S(1)}, bf16[4,16,1024]{2,1,0:T(8,128)(2,1)S(1)}, u32[]{:S(2)}, u32[]{:S(2)}) collective-permute-start(bf16[4,16,1024]{2,1,0:T(8,128)(2,1)S(1)} %get-tuple-element.142), channel_id=1, source_target_pairs={{0,2},{2,0},{4,6},{6,4},{8,10},{10,8},{12,14},{14,12},{16,18},{18,... | collective-permute-start | bytes 393224 | tf_op jit(solution)/shard_map/ppermute | solution.py:61
  99.3 5.9 %collective-permute-start.33 = (bf16[4,16,1024]{2,1,0:T(8,128)(2,1)S(1)}, bf16[4,16,1024]{2,1,0:T(8,128)(2,1)S(1)}, u32[]{:S(2)}, u32[]{:S(2)}) collective-permute-start(bf16[4,16,1024]{2,1,0:T(8,128)(2,1)S(1)} %get-tuple-element.144), channel_id=1, source_target_pairs={{0,6},{2,4},{4,2},{6,0},{8,14},{10,12},{12,10},{14,8},{16,22},{18,... | collective-permute-start | bytes 393224 | tf_op jit(solution)/shard_map/ppermute | solution.py:61
  102.5 11.7 %collective-permute-start.30 = (bf16[1024,512]{1,0:T(8,128)(2,1)S(1)}, bf16[1024,512]{1,0:T(8,128)(2,1)S(1)}, u32[]{:S(2)}, u32[]{:S(2)}) collective-permute-start(bf16[1024,512]{1,0:T(8,128)(2,1)S(1)} %part.1), channel_id=1, source_target_pairs={{0,1},{1,0},{2,3},{3,2},{4,5},{5,4},{6,7},{7,6},{8,9},{9,8},{10,11... | collective-permute-start | bytes 3145736 | tf_op jit(solution)/shard_map/ppermute | solution.py:703
  105.2 5.6 %collective-permute-start.34 = (bf16[1,16,1024]{2,1,0:T(8,128)(2,1)S(1)}, bf16[1,16,1024]{2,1,0:T(8,128)(2,1)S(1)}, u32[]{:S(2)}, u32[]{:S(2)}) collective-permute-start(bf16[1,16,1024]{2,1,0:T(8,128)(2,1)S(1)} %get-tuple-element.154), channel_id=1, source_target_pairs={{0,8},{2,10},{4,12},{6,14},{8,0},{10,2},{12,4},{14,6},{16,24},{18,... | collective-permute-start | bytes 98312 | tf_op jit(solution)/shard_map/ppermute | solution.py:61
  105.3 6.2 %collective-permute-start.36 = (bf16[1,16,1024]{2,1,0:T(8,128)(2,1)S(1)}, bf16[1,16,1024]{2,1,0:T(8,128)(2,1)S(1)}, u32[]{:S(2)}, u32[]{:S(2)}) collective-permute-start(bf16[1,16,1024]{2,1,0:T(8,128)(2,1)S(1)} %get-tuple-element.155), channel_id=1, source_target_pairs={{0,24},{2,26},{4,28},{6,30},{8,16},{10,18},{12,20},{14,22},{16,8},... | collective-permute-start | bytes 98312 | tf_op jit(solution)/shard_map/ppermute | solution.py:61
  107.2 5.2 %collective-permute-start.35 = (bf16[1,16,1024]{2,1,0:T(8,128)(2,1)S(1)}, bf16[1,16,1024]{2,1,0:T(8,128)(2,1)S(1)}, u32[]{:S(2)}, u32[]{:S(2)}) collective-permute-start(bf16[1,16,1024]{2,1,0:T(8,128)(2,1)S(1)} %get-tuple-element.156), channel_id=1, source_target_pairs={{0,16},{2,18},{4,20},{6,22},{8,24},{10,26},{12,28},{14,30},{16,0},... | collective-permute-start | bytes 98312 | tf_op jit(solution)/shard_map/ppermute | solution.py:61
  108.8 9.2 %collective-permute-start.29 = (bf16[4,32,1024]{2,1,0:T(8,128)(2,1)S(1)}, bf16[4,32,1024]{2,1,0:T(8,128)(2,1)S(1)}, u32[]{:S(2)}, u32[]{:S(2)}) collective-permute-start(bf16[4,32,1024]{2,1,0:T(8,128)(2,1)S(1)} %maximum_bitcast_fusion.refs_0_), channel_id=1, source_target_pairs={{0,6},{2,4},{4,2},{6,0},{8,14},{10,12},{12,10},{14,8},{16,22},{18,... | collective-permute-start | bytes 786440 | tf_op jit(solution)/shard_map/ppermute | solution.py:61
  110.8 9.7 %collective-permute-start.28 = (bf16[4,32,1024]{2,1,0:T(8,128)(2,1)S(1)}, bf16[4,32,1024]{2,1,0:T(8,128)(2,1)S(1)}, u32[]{:S(2)}, u32[]{:S(2)}) collective-permute-start(bf16[4,32,1024]{2,1,0:T(8,128)(2,1)S(1)} %maximum_bitcast_fusion.refs_0_), channel_id=1, source_target_pairs={{0,4},{2,6},{4,0},{6,2},{8,12},{10,14},{12,8},{14,10},{16,20},{18,... | collective-permute-start | bytes 786440 | tf_op jit(solution)/shard_map/ppermute | solution.py:61
  111.4 9.1 %collective-permute-start.27 = (bf16[4,32,1024]{2,1,0:T(8,128)(2,1)S(1)}, bf16[4,32,1024]{2,1,0:T(8,128)(2,1)S(1)}, u32[]{:S(2)}, u32[]{:S(2)}) collective-permute-start(bf16[4,32,1024]{2,1,0:T(8,128)(2,1)S(1)} %maximum_bitcast_fusion.refs_0_), channel_id=1, source_target_pairs={{0,2},{2,0},{4,6},{6,4},{8,10},{10,8},{12,14},{14,12},{16,18},{18,... | collective-permute-start | bytes 786440 | tf_op jit(solution)/shard_map/ppermute | solution.py:61
  (11 other events, 79.4 us)

commit v5 on v3

--- a/solution.py
+++ b/solution.py
@@ -13,7 +13,7 @@
 ITERS = 2
 SCALE = 0.125
 CHUNK = 256
-EXTRA = 16
+EXTRA = 8
 F32 = jnp.float32
 BF16 = jnp.bfloat16
 PARAMS = pltpu.CompilerParams(vmem_limit_bytes=24 * 1024 * 1024)
@@ -368,61 +368,59 @@
                     out_refs[m][t] = sum_ref[at // split, :, pl.ds(side, width // split)].astype(BF16)
 
 
-def query_kernel(own_ref, q_ref, g_ref, fb_ref, lk_ref, mixer_ref, more_ref, out_ref, land_ref, ds_ref):
-    rows = q_ref.shape[0]
-    lk = lk_ref[...] * SCALE
+def soft_grad(fb_ref, g_ref, mixer_ref, ds_ref):
     for h in range(2):
         span = slice(h * LANDMARKS, (h + 1) * LANDMARKS)
         mixer = keep_rows(mixer_ref[...], h)
-        for c in range(0, rows, CHUNK):
+        for c in range(0, fb_ref.shape[0], CHUNK):
             part = slice(c, c + CHUNK)
             f = fb_ref[part, span].astype(F32)
             df = dot(g_ref[part, :], mixer)
             ds_ref[part, span] = (f * (df - jnp.sum(f * df, axis=1, keepdims=True))).astype(BF16)
-    out_ref[...] = (
-        dot(ds_ref[:, :LANDMARKS], keep_lanes(lk, 0).astype(BF16))
-        + dot(ds_ref[:, LANDMARKS:], keep_lanes(lk, 1).astype(BF16))
-    ).astype(BF16)
-    qt = q_ref[...].T
+
+
+def weight_soft_grad(pb_ref, v_ref, norm_ref, center_ref, ds_ref):
+    for h in range(2):
+        span = slice(h * LANDMARKS, (h + 1) * LANDMARKS)
+        norm = keep_rows(norm_ref[...], h)
+        center = center_ref[pl.ds(2 * pl.program_id(0) + h, 1), :]
+        for c in range(0, pb_ref.shape[0], CHUNK):
+            part = slice(c, c + CHUNK)
+            dp = dot(v_ref[part, :], norm)
+            ds_ref[part, span] = (pb_ref[part, span].astype(F32) * (dp - center)).astype(BF16)
+
+
+def land_sums(ds_ref, x_ref, own_ref, more_ref):
+    xt = x_ref[...].T
     sums = jnp.concatenate(
-        [dot(qt[:DH], ds_ref[:, :LANDMARKS]), dot(qt[DH:], ds_ref[:, LANDMARKS:])], axis=0
+        [dot(xt[:DH], ds_ref[:, :LANDMARKS]), dot(xt[DH:], ds_ref[:, LANDMARKS:])], axis=0
     )
     here = (own_ref[0] == pl.program_id(0)).astype(F32)
-    land_ref[...] = (sums.T * SCALE + more_ref[...] * here).astype(BF16)
-
-
-def key_kernel(own_ref, k_ref, v_ref, pb_ref, lq_ref, norm_ref, center_ref, more_ref, other_ref, *refs):
-    out_ref, value_ref = refs[:2]
-    out_refs, (land_ref, ds_ref) = refs[2:-2], refs[-2:]
+    return (sums.T * SCALE + more_ref[...] * here).astype(BF16)
+
+
+def token_part(ds_ref, land_ref, out_ref):
+    land = land_ref[...] * SCALE
+    total = dot(ds_ref[:, :LANDMARKS], keep_lanes(land, 0).astype(BF16)) + dot(
+        ds_ref[:, LANDMARKS:], keep_lanes(land, 1).astype(BF16)
+    )
+    out_ref[...] = total.astype(BF16)
+
+
+def query_land_kernel(own_ref, q_ref, g_ref, fb_ref, mixer_ref, more_ref, land_ref, ds_ref):
+    soft_grad(fb_ref, g_ref, mixer_ref, ds_ref)
+    land_ref[...] = land_sums(ds_ref, q_ref, own_ref, more_ref)
+
+
+def key_land_kernel(own_ref, k_ref, v_ref, pb_ref, norm_ref, center_ref, more_ref, other_ref, *refs):
+    ds_ref, out_refs, land_ref = refs[0], refs[1:-1], refs[-1]
     size = len(out_refs)
     columns = other_ref.shape[1]
     pair = pl.program_id(0)
-    rows = k_ref.shape[0]
-    lq = lq_ref[...] * SCALE
-    for h in range(2):
-        span = slice(h * LANDMARKS, (h + 1) * LANDMARKS)
-        norm = keep_rows(norm_ref[...], h)
-        center = center_ref[pl.ds(2 * pair + h, 1), :]
-        for c in range(0, rows, CHUNK):
-            part = slice(c, c + CHUNK)
-            dp = dot(v_ref[part, :], norm)
-            ds_ref[part, span] = (pb_ref[part, span].astype(F32) * (dp - center)).astype(BF16)
-    out_ref[...] = (
-        dot(ds_ref[:, :LANDMARKS], keep_lanes(lq, 0).astype(BF16))
-        + dot(ds_ref[:, LANDMARKS:], keep_lanes(lq, 1).astype(BF16))
-    ).astype(BF16)
-    value_ref[...] = (
-        dot(pb_ref[:, :LANDMARKS], keep_rows(norm_ref[...], 0), NT)
-        + dot(pb_ref[:, LANDMARKS:], keep_rows(norm_ref[...], 1), NT)
-    ).astype(BF16)
-    kt = k_ref[...].T
-    sums = jnp.concatenate(
-        [dot(kt[:DH], ds_ref[:, :LANDMARKS]), dot(kt[DH:], ds_ref[:, LANDMARKS:])], axis=0
-    )
-    here = (own_ref[0] == pair).astype(F32)
-    land_ref[:, pl.ds(pl.multiple_of(pair * PAIR, PAIR), PAIR)] = (
-        sums.T * SCALE + more_ref[...] * here
-    ).astype(BF16)
+    weight_soft_grad(pb_ref, v_ref, norm_ref, center_ref, ds_ref)
+    land_ref[:, pl.ds(pl.multiple_of(pair * PAIR, PAIR), PAIR)] = land_sums(
+        ds_ref, k_ref, own_ref, more_ref
+    )
 
     @pl.when(pair == pl.num_programs(0) - 1)
     def _():
@@ -432,6 +430,18 @@
                 at = pl.multiple_of(((t * size + m) ^ own_ref[2]) * height, height)
                 out_refs[m][t, :, :columns] = land_ref[pl.ds(at, height), :]
                 out_refs[m][t, :, columns:] = other_ref[pl.ds(at, height), :]
+
+
+def query_kernel(ds_ref, lk_ref, out_ref):
+    token_part(ds_ref, lk_ref, out_ref)
+
+
+def key_kernel(ds_ref, pb_ref, lq_ref, norm_ref, out_ref, value_ref):
+    token_part(ds_ref, lq_ref, out_ref)
+    value_ref[...] = (
+        dot(pb_ref[:, :LANDMARKS], keep_rows(norm_ref[...], 0), NT)
+        + dot(pb_ref[:, LANDMARKS:], keep_rows(norm_ref[...], 1), NT)
+    ).astype(BF16)
 
 
 def part_kernel(_, attn_ref, weight_ref, out_ref):
@@ -508,8 +518,11 @@
     size = bit_groups(n)[-1][1]
     height = 2 * cols + EXTRA
     own_head = me // parts
+
+    sorted_here = land_dev % 16 == 0
+    me_arr = jnp.stack([me, me if sorted_here else me * 0]).astype(jnp.int32)
+    mine_arr = mine.reshape(1).astype(jnp.int32)
     own_arr = jnp.stack([own_head // 2, own_head % 2, me * 0 if land_dev % 16 else me]).astype(jnp.int32)
-
     steps = 4
     in_hbm = pl.BlockSpec(memory_space=pltpu.HBM)
     own = call(
@@ -527,26 +540,25 @@
         ],
         name="means",
     )
+    own, me_arr, mine_arr, own_arr = lax.optimization_barrier((own, me_arr, mine_arr, own_arr))
     grad_attn = dot(cotangent, out_weight, NT).astype(BF16)
-    sorted_here = land_dev % 16 == 0
     if sorted_here:
         lands = gather_lists(own, n)
     else:
         lands = [gather_ordered(own, n, me).reshape(LANDMARKS // 16, 16, 2 * columns)]
-    me_arr = jnp.stack([me, me if sorted_here else me * 0]).astype(jnp.int32)
 
     token_pair = pl.BlockSpec((rows, PAIR), lambda j, *_: (0, j))
     factor_pair = pl.BlockSpec((rows, 2 * LANDMARKS), lambda j, *_: (0, j))
     lq_pair = pl.BlockSpec((LANDMARKS, PAIR), lambda j, *_: (0, j))
     lk_pair = pl.BlockSpec((LANDMARKS, PAIR), lambda j, *_: (0, j + pairs))
-    factors = pltpu.HBM((rows, heads * LANDMARKS), BF16)
+    factors = shape_of((rows, heads * LANDMARKS), BF16)
     piece = shape_of((n // size, height, LANDMARKS), BF16)
 
     fb, pb, tops, land, *pieces = call(
         functools.partial(forward_kernel, n, heads, len(lands)),
         (pairs,),
         [me_arr],
-        [held_in_hbm(x) for x in (queries, key_rows, value_rows, grad_attn)] + lands,
+        [queries, key_rows, value_rows, grad_attn] + lands,
         [token_pair] * 4 + [whole(lands[0].shape)] * len(lands),
         [
             factors,
@@ -573,7 +585,7 @@
     square = (LANDMARKS, LANDMARKS)
     own_lq = pl.BlockSpec((LANDMARKS, PAIR), lambda i, own: (0, own[0]))
     own_lk = pl.BlockSpec((LANDMARKS, PAIR), lambda i, own: (0, own[0] + pairs))
-    kept = pltpu.VMEM((1 + 4 * ITERS,) + square, F32)
+    kept = shape_of((1 + 4 * ITERS,) + square, F32)
     saved, inverse = call(
         newton_kernel,
         (1,),
@@ -591,7 +603,7 @@
         got = [pieces[0]] + [exchange(pieces[m], m << shift, n) for m in range(1, count)]
         specs = [whole(got[0].shape)] * count
         if step == 0:
-            got, inverse, saved = lax.optimization_barrier((got, inverse, saved))
+            got, inverse = lax.optimization_barrier((got, inverse))
         if step + 1 < len(groups):
             following = groups[step + 1][1]
             piece = shape_of((got[0].shape[0] // following, height, LANDMARKS), BF16)
@@ -623,7 +635,7 @@
         newton_grad_kernel,
         (1,),
         [own_arr],
-        [pltpu.with_memory_space_constraint(saved, pltpu.VMEM), values, grads, land, land],
+        [saved, values, grads, land, land],
         [whole(kept.shape), whole(small.shape), whole(small.shape), own_lq, own_lk],
         [more, more],
         [whole(more.shape)] * 2,
@@ -658,8 +670,64 @@
     )
     (shift, count), later = groups[0], groups[1:]
     weight_sum = scatter_step(weight_pieces, shift, count, n).astype(BF16)
+    (pb, key_rows, value_rows), weight_sum = lax.optimization_barrier(
+        ((pb, key_rows, value_rows), weight_sum)
+    )
+    following = later[0][1]
+    weight_sum = weight_sum.reshape((-1, following) + weight_sum.shape[1:])
+    weight_own = scatter_pieces([weight_sum[:, m] for m in range(following)], n, later)[0].astype(BF16)
+    flat_pair = pl.BlockSpec((PAIR, LANDMARKS), lambda j, *_: (j, 0))
+    land_pair = pl.BlockSpec((LANDMARKS, PAIR), lambda j, *_: (0, j))
+    centers = whole((heads, LANDMARKS))
+    tokens = shape_of((rows, columns), BF16)
+    land_shape = shape_of((LANDMARKS, columns), BF16)
+    land_k, grad_sf = call(
+        query_land_kernel,
+        (pairs,),
+        [own_arr],
+        [queries, grad_attn, fb, mixer, more_k],
+        [token_pair, token_pair, factor_pair, flat_pair, whole(more.shape)],
+        [land_shape, factors],
+        [land_pair, factor_pair],
+        flops=4 << 30,
+        name="query_land",
+    )
+    (shift, count), later = groups[0], groups[1:]
+    following = later[0][1]
+    weight_sum = scatter_step(weight_pieces, shift, count, n).astype(BF16)
+    (pb, key_rows, value_rows), weight_sum, land_k = lax.optimization_barrier(
+        ((pb, key_rows, value_rows), weight_sum, land_k)
+    )
+    if sorted_here:
+        land_piece, pieces_count = shape_of((n // size, land_dev, 2 * columns), BF16), size
+    else:
+        land_piece, pieces_count = shape_of((LANDMARKS // 16, 16, 2 * columns), BF16), 1
+    grad_sb, *land_pieces = call(
+        key_land_kernel,
+        (pairs,),
+        [own_arr],
+        [key_rows, value_rows, pb, norm, center, more_q, land_k],
+        [token_pair, token_pair, factor_pair, flat_pair, centers, whole(more.shape)]
+        + [whole(land_shape.shape)],
+        [factors] + [land_piece] * pieces_count,
+        [factor_pair] + [whole(land_piece.shape)] * pieces_count,
+        [pltpu.VMEM(land_shape.shape, BF16)],
+        flops=4 << 30,
+        name="key_land",
+    )
+    land_pieces, grad_sf, attn = lax.optimization_barrier((land_pieces, grad_sf, attn))
+    query_f = call(
+        query_kernel,
+        (pairs,),
+        [],
+        [grad_sf, land],
+        [factor_pair, lk_pair],
+        tokens,
+        token_pair,
+        flops=2 << 30,
+        name="query_grad",
+    )
     half = width // 2
-    mine_arr = mine.reshape(1).astype(jnp.int32)
     row_block = pl.BlockSpec((rows // 4, columns), lambda j, _: (j, 0))
     half_block = pl.BlockSpec((rows // 4, half), lambda j, _: (j, 0))
     there = call(
@@ -673,49 +741,30 @@
         flops=1 << 30,
         name="part",
     )
-    (pb, key_rows, value_rows), weight_sum, there = lax.optimization_barrier(
-        ((pb, key_rows, value_rows), weight_sum, there)
-    )
-    arrived = lax.ppermute(there, "head", [(0, 1), (1, 0)])
-    following = later[0][1]
+
+    if not sorted_here:
+        land_pieces = split_by_partner(land_pieces[0].reshape(n, land_dev, 2 * columns), n, me)
     weight_sum = weight_sum.reshape((-1, following) + weight_sum.shape[1:])
     weight_own = scatter_pieces([weight_sum[:, m] for m in range(following)], n, later)[0].astype(BF16)
-    flat_pair = pl.BlockSpec((PAIR, LANDMARKS), lambda j, *_: (j, 0))
-    land_pair = pl.BlockSpec((LANDMARKS, PAIR), lambda j, *_: (0, j))
-    tokens = shape_of((rows, columns), BF16)
-    land_shape = shape_of((LANDMARKS, columns), BF16)
-    products = [pltpu.VMEM((rows, 2 * LANDMARKS), BF16)]
-    query_f, land_k = call(
-        query_kernel,
-        (pairs,),
-        [own_arr],
-        [queries, grad_attn, fb, land, mixer, more_k],
-        [token_pair, token_pair, factor_pair, lk_pair, flat_pair, whole(more.shape)],
-        [tokens, land_shape],
-        [token_pair, land_pair],
-        products,
-        flops=6 << 30,
-        name="query_grad",
-    )
-    if sorted_here:
-        land_piece, count = shape_of((n // size, land_dev, 2 * columns), BF16), size
-    else:
-        land_piece, count = shape_of((LANDMARKS // 16, 16, 2 * columns), BF16), 1
-    key_b, value_grad, *land_pieces = call(
+    land_pieces, weight_own = lax.optimization_barrier((land_pieces, weight_own))
+    land_sum = scatter_step(land_pieces, shift, count, n).astype(BF16)
+    land_sum, weight_own, query_f, there = lax.optimization_barrier(
+        (land_sum, weight_own, query_f, there)
+    )
+    land_sum, weight_own, grad_sb = lax.optimization_barrier((land_sum, weight_own, grad_sb))
+    key_b, value_grad = call(
         key_kernel,
         (pairs,),
-        [own_arr],
-        [key_rows, value_rows, pb, land, norm, center, more_q, land_k],
-        [token_pair, token_pair, factor_pair, lq_pair, flat_pair, whole((heads, LANDMARKS))]
-        + [whole(more.shape), whole(land_shape.shape)],
-        [tokens, tokens] + [land_piece] * count,
-        [token_pair, token_pair] + [whole(land_piece.shape)] * count,
-        [pltpu.VMEM(land_shape.shape, BF16)] + products,
-        flops=6 << 30,
+        [],
+        [grad_sb, pb, land, norm],
+        [factor_pair, factor_pair, lq_pair, flat_pair],
+        [tokens, tokens],
+        [token_pair, token_pair],
+        flops=4 << 30,
         name="key_grad",
     )
-    if not sorted_here:
-        land_pieces = split_by_partner(land_pieces[0].reshape(n, land_dev, 2 * columns), n, me)
+
+    arrived = lax.ppermute(there, "head", [(0, 1), (1, 0)])
     mixed = call(
         mixed_kernel,
         (4,),
@@ -727,21 +776,22 @@
         flops=1 << 30,
         name="mixed",
     )
-    weights = gather_first(weight_own, n)
-    (shift, count), later = groups[0], groups[1:]
-    land_sum = scatter_step(land_pieces, shift, count, n).astype(BF16)
-    weights, land_sum, mixed = lax.optimization_barrier((weights, land_sum, mixed))
+    if len(later) == 1 and weight_own.shape[1] == land_sum.shape[2]:
+        (shift, count), tall = later[0], weight_own.shape[0]
+        got = [
+            exchange(jnp.concatenate([weight_own, land_sum[m]], axis=0), m << shift, n)
+            for m in range(1, count)
+        ]
+        weights = [weight_own[None]] + [part[None, :tall] for part in got]
+        land_own = sum(part.astype(F32) for part in [land_sum[0]] + [part[tall:] for part in got])
+    else:
+        weights = gather_first(weight_own, n)
+        land_sum = land_sum.reshape((-1, following) + land_sum.shape[1:])
+        land_own = scatter_pieces([land_sum[:, m] for m in range(following)], n, later)[0]
+    land_own = land_own * (1.0 / seg_len)
+    weights, key_b = lax.optimization_barrier((weights, key_b))
     weights = gather_rest(weights, n)
-    land_sum = land_sum.reshape((-1, following) + land_sum.shape[1:])
-    land_own = scatter_pieces([land_sum[:, m] for m in range(following)], n, later)[0] * (1.0 / seg_len)
-
-    def finish(token_part, land_part):
-        return (
-            (token_part.reshape(land_dev, seg_len, columns) + land_part[:, None, :])
-            .astype(BF16)
-            .reshape(rows, columns)
-        )
-
+    weights, mixed = lax.optimization_barrier((weights, mixed))
     weight_grad = call(
         functools.partial(unpack_kernel, split),
         (1,),
@@ -753,6 +803,14 @@
         [pltpu.VMEM((n,) + weights[0].shape[1:], F32), pltpu.SemaphoreType.DMA((n,))],
         name="unpack",
     )
+
+    def finish(token_part, land_part):
+        return (
+            (token_part.reshape(land_dev, seg_len, columns) + land_part[:, None, :])
+            .astype(BF16)
+            .reshape(rows, columns)
+        )
+
     query_grad = finish(query_f, land_own[:, :columns])
     key_grad = finish(key_b, land_own[:, columns:])
     return (mixed, query_grad, key_grad, value_grad, weight_grad)

time: 128 us -> 122 us (0.953)
  starting transfers between devices: 50.1 us -> 44.9 us
  local copies, waits for them, and re-layouts: 3.11 us -> 0.07 us
  Pallas kernels: 45.5 us -> 47.3 us
    ppermute x36 -> x33, starting transfers between devices: 50.1 us -> 44.9 us  [exchange(): return lax.ppermute(block, 'seq', [(i, i ^ mask) for i in range(n)])]
    unnamed x20 -> x10, local copies, waits for them, and re-layouts: 3.08 us -> 0.03 us
    pallas_call x12 -> x14, Pallas kernels: 45.5 us -> 47.3 us  [call(): pl.pallas_call(kernel, grid_spec=pltpu.PrefetchScalarGridSpec(num_scalar_...]
    ppermute x36 -> x33, waiting for transfers between devices: 21.7 us -> 22.4 us  [exchange(): return lax.ppermute(block, 'seq', [(i, i ^ mask) for i in range(n)])]
  transfers between devices with their start and end apart: 37 -> 34, of which waited for: 14 -> 15; matrix products, arithmetic and copies ran while one was open for 5% -> 4% of each run, Pallas kernels for 20% -> 23%
where the time goes in v5:
time: 122 us
  Pallas kernels  47.3 us (39%)
  starting transfers between devices  44.9 us (37%)
  waiting for transfers between devices  22.4 us (18%)
  other arithmetic  2.91 us (2%)
  matrix products  2.87 us (2%)
    pallas_call x14, Pallas kernels, call(): pl.pallas_call(kernel, grid_spec=pltpu.PrefetchScalarGridSpec(num_scalar_...  47.3 us
    ppermute x33, starting transfers between devices, exchange(): return lax.ppermute(block, 'seq', [(i, i ^ mask) for i in range(n)])  44.9 us
    ppermute x33, waiting for transfers between devices, exchange(): return lax.ppermute(block, 'seq', [(i, i ^ mask) for i in range(n)])  22.4 us
    dot_general x1, matrix products, dot(): lax.dot_general(left, right, (dims, ((), ())), preferred_element_type=F32)  2.87 us
  transfers between devices with their start and end apart: 34, of which 15 were waited for; matrix products, arithmetic and copies ran while one was open for 4% of the time, Pallas kernels for 23%

profile of v5, /device:TPU:0, one launch (start us, length us, event | category | flops | bytes accessed | tf_op | source)
XLA Modules:
  0.0 121.7 jit_solution(11025957599383920010)
XLA Ops:
  0.8 1.7 %means.1 = bf16[16,1024]{1,0:T(8,128)(2,1)S(1)} custom-call(bf16[1024,512]{1,0:T(8,128)(2,1)} %q_ref.5, bf16[1024,512]{1,0:T(8,128)(2,1)} %k_ref.4), custom_call_target="tpu_custom_call" | custom-call | bytes 4194304 | tf_op jit(solution)/shard_map/means/pallas_call | solution.py:489
  2.5 5.1 %collective-permute-start.2 = (bf16[1,16,1024]{2,1,0:T(8,128)(2,1)S(1)}, bf16[1,16,1024]{2,1,0:T(8,128)(2,1)S(1)}, u32[]{:S(2)}, u32[]{:S(2)}) collective-permute-start(bf16[1,16,1024]{2,1,0:T(8,128)(2,1)S(1)} %bitcast.63), channel_id=1, source_target_pairs={{0,24},{2,26},{4,28},{6,30},{8,16},{10,18},{12,20},{14,22},{16,8},... | collective-permute-start | bytes 98312 | tf_op jit(solution)/shard_map/ppermute | solution.py:61
  9.5 2.9 %collective-permute-done.1 = bf16[1,16,1024]{2,1,0:T(8,128)(2,1)S(1)} collective-permute-done((bf16[1,16,1024]{2,1,0:T(8,128)(2,1)S(1)}, bf16[1,16,1024]{2,1,0:T(8,128)(2,1)S(1)}, u32[]{:S(2)}, u32[]{:S(2)}) %collective-permute-start.1) | collective-permute-done | bytes 32800 | tf_op jit(solution)/shard_map/ppermute | solution.py:61
  12.5 1.6 %collective-permute-start.3 = (bf16[4,16,1024]{2,1,0:T(8,128)(2,1)S(1)}, bf16[4,16,1024]{2,1,0:T(8,128)(2,1)S(1)}, u32[]{:S(2)}, u32[]{:S(2)}) collective-permute-start(bf16[4,16,1024]{2,1,0:T(8,128)(2,1)S(1)} %maximum_bitcast_fusion.2.refs_0_), channel_id=1, source_target_pairs={{0,2},{2,0},{4,6},{6,4},{8,10},{10,8},{12,14},{14,12},{16,18},{18,... | collective-permute-start | bytes 393224 | tf_op jit(solution)/shard_map/ppermute | solution.py:61
  14.0 1.5 %collective-permute-start.4 = (bf16[4,16,1024]{2,1,0:T(8,128)(2,1)S(1)}, bf16[4,16,1024]{2,1,0:T(8,128)(2,1)S(1)}, u32[]{:S(2)}, u32[]{:S(2)}) collective-permute-start(bf16[4,16,1024]{2,1,0:T(8,128)(2,1)S(1)} %maximum_bitcast_fusion.2.refs_0_), channel_id=1, source_target_pairs={{0,4},{2,6},{4,0},{6,2},{8,12},{10,14},{12,8},{14,10},{16,20},{18,... | collective-permute-start | bytes 393224 | tf_op jit(solution)/shard_map/ppermute | solution.py:61
  16.0 2.9 %convolution_convert_fusion.g_ref = bf16[1024,512]{1,0:T(8,128)(2,1)S(1)} fusion(bf16[1024,1024]{1,0:T(8,128)(2,1)} %cot_ref.1, bf16[512,1024]{1,0:T(8,128)(2,1)S(1)} %copy-done), kind=kOutput, calls=%fused_computation.4 | convolution fusion | flops 1074266112 | bytes 4194304 | tf_op jit(solution)/shard_map/dot_general | solution.py:23
  20.0 1.5 %collective-permute-done.5.refs_3_ = bf16[4,16,1024]{2,1,0:T(8,128)(2,1)S(1)} collective-permute-done((bf16[4,16,1024]{2,1,0:T(8,128)(2,1)S(1)}, bf16[4,16,1024]{2,1,0:T(8,128)(2,1)S(1)}, u32[]{:S(2)}, u32[]{:S(2)}) %collective-permute-start.5) | collective-permute-done | bytes 131104 | tf_op jit(solution)/shard_map/ppermute | solution.py:61
  21.4 10.0 %forward.1 = (bf16[1024,2048]{1,0:T(8,128)(2,1)S(1)}, bf16[1024,2048]{1,0:T(8,128)(2,1)S(1)}, f32[4,8,256]{2,1,0:T(8,128)S(1)}, bf16[256,1024]{1,0:T(8,128)(2,1)...) custom-call(s32[2]{0:T(128)S(1)} %pad_add_fusion.me_ref, ...), custom_call_target="tpu_custom_call" | custom-call | flops 8589934592 | bytes 4194304 | tf_op jit(solution)/shard_map/forward/pallas_call | solution.py:489
  32.6 2.4 %collective-permute-start.8 = (bf16[4,72,256]{2,1,0:T(8,128)(2,1)S(1)}, bf16[4,72,256]{2,1,0:T(8,128)(2,1)S(1)}, u32[]{:S(2)}, u32[]{:S(2)}) collective-permute-start(bf16[4,72,256]{2,1,0:T(8,128)(2,1)S(1)} %get-tuple-element.101), channel_id=1, source_target_pairs={{0,6},{2,4},{4,2},{6,0},{8,14},{10,12},{12,10},{14,8},{16,22},{18,... | collective-permute-start | bytes 442376 | tf_op jit(solution)/shard_map/ppermute | solution.py:61
  35.0 3.6 %newton.1 = (f32[9,256,256]{2,1,0:T(8,128)S(1)}, f32[1,256,256]{2,1,0:T(8,128)S(1)}) custom-call(s32[3]{0:T(128)S(1)} %pad_add_fusion.1.own_ref, bf16[256,1024]{1,0:T(8,128)(2,1)S(1)} %get-tuple-element.102.lq_ref.lk_ref, bf16[256,1024]{1,0:T(8,128)(2,1)S(1)} %get-tuple-element.102.lq_ref.lk_ref), custom_call_target="tpu_custom_call" | custom-call | flops 4294967296 | bytes 4194304 | tf_op jit(solution)/shard_map/newton/pallas_call | solution.py:489
  39.1 2.2 %collective-permute-start.10 = (bf16[1,72,256]{2,1,0:T(8,128)(2,1)S(1)}, bf16[1,72,256]{2,1,0:T(8,128)(2,1)S(1)}, u32[]{:S(2)}, u32[]{:S(2)}) collective-permute-start(bf16[1,72,256]{2,1,0:T(8,128)(2,1)S(1)} %get-tuple-element.110), channel_id=1, source_target_pairs={{0,16},{2,18},{4,20},{6,22},{8,24},{10,26},{12,28},{14,30},{16,0},... | collective-permute-start | bytes 110600 | tf_op jit(solution)/shard_map/ppermute | solution.py:61
  41.3 2.1 %collective-permute-start.11 = (bf16[1,72,256]{2,1,0:T(8,128)(2,1)S(1)}, bf16[1,72,256]{2,1,0:T(8,128)(2,1)S(1)}, u32[]{:S(2)}, u32[]{:S(2)}) collective-permute-start(bf16[1,72,256]{2,1,0:T(8,128)(2,1)S(1)} %get-tuple-element.111), channel_id=1, source_target_pairs={{0,24},{2,26},{4,28},{6,30},{8,16},{10,18},{12,20},{14,22},{16,8},... | collective-permute-start | bytes 110600 | tf_op jit(solution)/shard_map/ppermute | solution.py:61
  44.0 3.1 %collective-permute-done.11.refs_3_ = bf16[1,72,256]{2,1,0:T(8,128)(2,1)S(1)} collective-permute-done((bf16[1,72,256]{2,1,0:T(8,128)(2,1)S(1)}, bf16[1,72,256]{2,1,0:T(8,128)(2,1)S(1)}, u32[]{:S(2)}, u32[]{:S(2)}) %collective-permute-start.11) | collective-permute-done | bytes 36896 | tf_op jit(solution)/shard_map/ppermute | solution.py:61
  47.4 2.2 %collective-permute-start.14 = (bf16[1,72,256]{2,1,0:T(8,128)(2,1)S(1)}, bf16[1,72,256]{2,1,0:T(8,128)(2,1)S(1)}, u32[]{:S(2)}, u32[]{:S(2)}) collective-permute-start(bf16[1,72,256]{2,1,0:T(8,128)(2,1)S(1)} %get-tuple-element.113), channel_id=1, source_target_pairs={{0,24},{2,26},{4,28},{6,30},{8,16},{10,18},{12,20},{14,22},{16,8},... | collective-permute-start | bytes 110600 | tf_op jit(solution)/shard_map/ppermute | solution.py:61
  49.6 2.3 %collective-permute-start.12 = (bf16[1,72,256]{2,1,0:T(8,128)(2,1)S(1)}, bf16[1,72,256]{2,1,0:T(8,128)(2,1)S(1)}, u32[]{:S(2)}, u32[]{:S(2)}) collective-permute-start(bf16[1,72,256]{2,1,0:T(8,128)(2,1)S(1)} %get-tuple-element.113), channel_id=1, source_target_pairs={{0,8},{2,10},{4,12},{6,14},{8,0},{10,2},{12,4},{14,6},{16,24},{18,... | collective-permute-start | bytes 110600 | tf_op jit(solution)/shard_map/ppermute | solution.py:61
  51.8 1.4 %collective-permute-done.14 = bf16[1,72,256]{2,1,0:T(8,128)(2,1)S(1)} collective-permute-done((bf16[1,72,256]{2,1,0:T(8,128)(2,1)S(1)}, bf16[1,72,256]{2,1,0:T(8,128)(2,1)S(1)}, u32[]{:S(2)}, u32[]{:S(2)}) %collective-permute-start.14) | collective-permute-done | bytes 36896 | tf_op jit(solution)/shard_map/ppermute | solution.py:61
  54.5 2.1 %collective-permute-start.15 = (bf16[4,72,256]{2,1,0:T(8,128)(2,1)S(1)}, bf16[4,72,256]{2,1,0:T(8,128)(2,1)S(1)}, u32[]{:S(2)}, u32[]{:S(2)}) collective-permute-start(bf16[4,72,256]{2,1,0:T(8,128)(2,1)S(1)} %maximum_bitcast_fusion.1.refs_0_), channel_id=1, source_target_pairs={{0,2},{2,0},{4,6},{6,4},{8,10},{10,8},{12,14},{14,12},{16,18},{18,... | collective-permute-start | bytes 442376 | tf_op jit(solution)/shard_map/ppermute | solution.py:61
  58.1 4.3 %newton_grad.1 = (f32[256,128]{1,0:T(8,128)S(1)}, f32[256,128]{1,0:T(8,128)S(1)}) custom-call(s32[3]{0:T(128)S(1)} %pad_add_fusion.1.own_ref, f32[9,256,256]{2,1,0:T(8,128)S(1)} %get-tuple-element.114.saved_ref, f32[32,256]{1,0:T(8,128)S(1)} %get-tuple-element.115.values_ref, f32[32,256]{1,0:T(8,128)S(1)} %get-tuple-element.116.grads_ref, ...), custom_call_target="tpu_custom_call" | custom-call | flops 8589934592 | bytes 4194304 | tf_op jit(solution)/shard_map/newton_grad/pallas_call | solution.py:489
  63.5 4.7 %attend.1 = (bf16[1024,512]{1,0:T(8,128)(2,1)S(1)}, bf16[512,256]{1,0:T(8,128)(2,1)S(1)}, bf16[512,256]{1,0:T(8,128)(2,1)S(1)}, f32[8,256]{1,0:T(8,128)S(1)}, bf...) custom-call(s32[2]{0:T(128)S(1)} %pad_add_fusion.me_ref, ...), custom_call_target="tpu_custom_call" | custom-call | flops 4294967296 | bytes 4194304 | tf_op jit(solution)/shard_map/attend/pallas_call | solution.py:489
  71.8 5.4 %query_land.1 = (bf16[256,512]{1,0:T(8,128)(2,1)S(1)}, bf16[1024,2048]{1,0:T(8,128)(2,1)S(1)}) custom-call(s32[3]{0:T(128)S(1)} %pad_add_fusion.1.own_ref, bf16[1024,512]{1,0:T(8,128)(2,1)S(1)} %copy-done.1, bf16[1024,512]{1,0:T(8,128)(2,1)S(1)} %convolution_convert_fusion.g_ref, bf16[1024,2048]{1,0:T(8,128)(2,1)S(1)} %get-tuple-element.96.fb_ref, ...), custom_call_target="tpu_custom_call" | custom-call | flops 4294967296 | bytes 4194304 | tf_op jit(solution)/shard_map/query_land/pallas_call | solution.py:489
  78.6 2.0 %collective-permute-start.23 = (bf16[1,32,1024]{2,1,0:T(8,128)(2,1)S(1)}, bf16[1,32,1024]{2,1,0:T(8,128)(2,1)S(1)}, u32[]{:S(2)}, u32[]{:S(2)}) collective-permute-start(bf16[1,32,1024]{2,1,0:T(8,128)(2,1)S(1)} %get-tuple-element.180), channel_id=1, source_target_pairs={{0,24},{2,26},{4,28},{6,30},{8,16},{10,18},{12,20},{14,22},{16,8},... | collective-permute-start | bytes 196616 | tf_op jit(solution)/shard_map/ppermute | solution.py:61
  81.7 1.3 %collective-permute-start.21 = (bf16[1,32,1024]{2,1,0:T(8,128)(2,1)S(1)}, bf16[1,32,1024]{2,1,0:T(8,128)(2,1)S(1)}, u32[]{:S(2)}, u32[]{:S(2)}) collective-permute-start(bf16[1,32,1024]{2,1,0:T(8,128)(2,1)S(1)} %get-tuple-element.179), channel_id=1, source_target_pairs={{0,8},{2,10},{4,12},{6,14},{8,0},{10,2},{12,4},{14,6},{16,24},{18,... | collective-permute-start | bytes 196616 | tf_op jit(solution)/shard_map/ppermute | solution.py:61
  83.0 4.6 %key_land.1 = (bf16[1024,2048]{1,0:T(8,128)(2,1)S(1)}, bf16[4,16,1024]{2,1,0:T(8,128)(2,1)S(1)}, bf16[4,16,1024]{2,1,0:T(8,128)(2,1)S(1)}, bf16[4,16,1024]{2,1,0:T(8,128)(2,1)S(1)}, bf16[4,16,1024]{2,1,0:T(8,128)(2,1)S(1)}) custom-call(s32[3]{0:T(128)S(1)} %pad_add_fusion.1.own_ref, bf16[1024,512]{1,0:T(8,128)(2,1)S(1)} %copy-done.2, ...), custom_call_target="tpu_custom_call" | custom-call | flops 4294967296 | bytes 4194304 | tf_op jit(solution)/shard_map/key_land/pallas_call | solution.py:489
  91.3 2.3 %query_grad.1 = bf16[1024,512]{1,0:T(8,128)(2,1)S(1)} custom-call(bf16[1024,2048]{1,0:T(8,128)(2,1)S(1)} %get-tuple-element.156.ds_ref, bf16[256,1024]{1,0:T(8,128)(2,1)S(1)} %get-tuple-element.102.lq_ref.lk_ref), custom_call_target="tpu_custom_call" | custom-call | flops 2147483648 | bytes 4194304 | tf_op jit(solution)/shard_map/query_grad/pallas_call | solution.py:489
  93.6 1.3 %part.1 = bf16[1024,512]{1,0:T(8,128)(2,1)S(1)} custom-call(s32[1]{0:T(128)} %bitcast.1._, bf16[1024,512]{1,0:T(8,128)(2,1)S(1)} %get-tuple-element.158.attn_ref, bf16[512,1024]{1,0:T(8,128)(2,1)S(1)} %copy-done), custom_call_target="tpu_custom_call" | custom-call | flops 1073741824 | bytes 4194304 | tf_op jit(solution)/shard_map/part/pallas_call | solution.py:489
  96.0 1.8 %collective-permute-start.28 = (bf16[48,1024]{1,0:T(8,128)(2,1)S(1)}, bf16[48,1024]{1,0:T(8,128)(2,1)S(1)}, u32[]{:S(2)}, u32[]{:S(2)}) collective-permute-start(bf16[48,1024]{1,0:T(8,128)(2,1)S(1)} %get-tuple-element.188), channel_id=1, source_target_pairs={{0,16},{2,18},{4,20},{6,22},{8,24},{10,26},{12,28},{14,30},{16,0},... | collective-permute-start | bytes 294920 | tf_op jit(solution)/shard_map/ppermute | solution.py:61
  97.8 1.9 %collective-permute-start.29 = (bf16[48,1024]{1,0:T(8,128)(2,1)S(1)}, bf16[48,1024]{1,0:T(8,128)(2,1)S(1)}, u32[]{:S(2)}, u32[]{:S(2)}) collective-permute-start(bf16[48,1024]{1,0:T(8,128)(2,1)S(1)} %get-tuple-element.187), channel_id=1, source_target_pairs={{0,24},{2,26},{4,28},{6,30},{8,16},{10,18},{12,20},{14,22},{16,8},... | collective-permute-start | bytes 294920 | tf_op jit(solution)/shard_map/ppermute | solution.py:61
  99.6 4.5 %key_grad.1 = (bf16[1024,512]{1,0:T(8,128)(2,1)S(1)}, bf16[1024,512]{1,0:T(8,128)(2,1)}) custom-call(bf16[1024,2048]{1,0:T(8,128)(2,1)S(1)} %get-tuple-element.164.ds_ref, bf16[1024,2048]{1,0:T(8,128)(2,1)S(1)} %get-tuple-element.135.pb_ref, bf16[256,1024]{1,0:T(8,128)(2,1)S(1)} %get-tuple-element.102.lq_ref.lk_ref, ...), custom_call_target="tpu_custom_call" | custom-call | flops 4294967296 | bytes 4194304 | tf_op jit(solution)/shard_map/key_grad/pallas_call | solution.py:489
  106.5 1.4 %collective-permute-start.32 = (bf16[4,32,1024]{2,1,0:T(8,128)(2,1)S(1)}, bf16[4,32,1024]{2,1,0:T(8,128)(2,1)S(1)}, u32[]{:S(2)}, u32[]{:S(2)}) collective-permute-start(bf16[4,32,1024]{2,1,0:T(8,128)(2,1)S(1)} %maximum_bitcast_fusion.refs_0_), channel_id=1, source_target_pairs={{0,6},{2,4},{4,2},{6,0},{8,14},{10,12},{12,10},{14,8},{16,22},{18,... | collective-permute-start | bytes 786440 | tf_op jit(solution)/shard_map/ppermute | solution.py:61
  110.3 2.4 %mixed.1 = bf16[1024,512]{1,0:T(8,128)(2,1)} custom-call(s32[1]{0:T(128)} %bitcast.1._, bf16[1024,512]{1,0:T(8,128)(2,1)S(1)} %get-tuple-element.158.attn_ref, bf16[512,1024]{1,0:T(8,128)(2,1)S(1)} %copy-done, bf16[1024,512]{1,0:T(8,128)(2,1)S(1)} %collective-permute-done.33.other_ref), custom_call_target="tpu_custom_call" | custom-call | flops 1073741824 | bytes 4194304 | tf_op jit(solution)/shard_map/mixed/pallas_call | solution.py:489
  113.5 6.0 %collective-permute-done.31.refs_2_ = bf16[4,32,1024]{2,1,0:T(8,128)(2,1)S(1)} collective-permute-done((bf16[4,32,1024]{2,1,0:T(8,128)(2,1)S(1)}, bf16[4,32,1024]{2,1,0:T(8,128)(2,1)S(1)}, u32[]{:S(2)}, u32[]{:S(2)}) %collective-permute-start.31) | collective-permute-done | bytes 262176 | tf_op jit(solution)/shard_map/ppermute | solution.py:61
  119.5 2.0 %unpack.1 = f32[512,1024]{1,0:T(8,128)} custom-call(s32[2]{0:T(128)S(1)} %pad_add_fusion.me_ref, bf16[4,32,1024]{2,1,0:T(8,128)(2,1)S(1)} %maximum_bitcast_fusion.refs_0_, bf16[4,32,1024]{2,1,0:T(8,128)(2,1)S(1)} %collective-permute-done.30.refs_1_, bf16[4,32,1024]{2,1,0:T(8,128)(2,1)S(1)} %collective-permute-done.31.refs_2_, ...), custom_call_target="tpu_custom_call" | custom-call | bytes 4194304 | tf_op jit(solution)/shard_map/unpack/pallas_call | solution.py:489
  (79 shorter events, 26.2 us)
Async XLA Ops:
  2.5 7.0 %collective-permute-start.2 = (bf16[1,16,1024]{2,1,0:T(8,128)(2,1)S(1)}, bf16[1,16,1024]{2,1,0:T(8,128)(2,1)S(1)}, u32[]{:S(2)}, u32[]{:S(2)}) collective-permute-start(bf16[1,16,1024]{2,1,0:T(8,128)(2,1)S(1)} %bitcast.63), channel_id=1, source_target_pairs={{0,24},{2,26},{4,28},{6,30},{8,16},{10,18},{12,20},{14,22},{16,8},... | collective-permute-start | bytes 98312 | tf_op jit(solution)/shard_map/ppermute | solution.py:61
  7.6 4.8 %collective-permute-start.1 = (bf16[1,16,1024]{2,1,0:T(8,128)(2,1)S(1)}, bf16[1,16,1024]{2,1,0:T(8,128)(2,1)S(1)}, u32[]{:S(2)}, u32[]{:S(2)}) collective-permute-start(bf16[1,16,1024]{2,1,0:T(8,128)(2,1)S(1)} %bitcast.64), channel_id=1, source_target_pairs={{0,16},{2,18},{4,20},{6,22},{8,24},{10,26},{12,28},{14,30},{16,0},... | collective-permute-start | bytes 98312 | tf_op jit(solution)/shard_map/ppermute | solution.py:61
  12.5 6.4 %collective-permute-start.3 = (bf16[4,16,1024]{2,1,0:T(8,128)(2,1)S(1)}, bf16[4,16,1024]{2,1,0:T(8,128)(2,1)S(1)}, u32[]{:S(2)}, u32[]{:S(2)}) collective-permute-start(bf16[4,16,1024]{2,1,0:T(8,128)(2,1)S(1)} %maximum_bitcast_fusion.2.refs_0_), channel_id=1, source_target_pairs={{0,2},{2,0},{4,6},{6,4},{8,10},{10,8},{12,14},{14,12},{16,18},{18,... | collective-permute-start | bytes 393224 | tf_op jit(solution)/shard_map/ppermute | solution.py:61
  14.0 5.9 %collective-permute-start.4 = (bf16[4,16,1024]{2,1,0:T(8,128)(2,1)S(1)}, bf16[4,16,1024]{2,1,0:T(8,128)(2,1)S(1)}, u32[]{:S(2)}, u32[]{:S(2)}) collective-permute-start(bf16[4,16,1024]{2,1,0:T(8,128)(2,1)S(1)} %maximum_bitcast_fusion.2.refs_0_), channel_id=1, source_target_pairs={{0,4},{2,6},{4,0},{6,2},{8,12},{10,14},{12,8},{14,10},{16,20},{18,... | collective-permute-start | bytes 393224 | tf_op jit(solution)/shard_map/ppermute | solution.py:61
  15.6 5.9 %collective-permute-start.5 = (bf16[4,16,1024]{2,1,0:T(8,128)(2,1)S(1)}, bf16[4,16,1024]{2,1,0:T(8,128)(2,1)S(1)}, u32[]{:S(2)}, u32[]{:S(2)}) collective-permute-start(bf16[4,16,1024]{2,1,0:T(8,128)(2,1)S(1)} %maximum_bitcast_fusion.2.refs_0_), channel_id=1, source_target_pairs={{0,6},{2,4},{4,2},{6,0},{8,14},{10,12},{12,10},{14,8},{16,22},{18,... | collective-permute-start | bytes 393224 | tf_op jit(solution)/shard_map/ppermute | solution.py:61
  31.5 7.2 %collective-permute-start.6 = (bf16[4,72,256]{2,1,0:T(8,128)(2,1)S(1)}, bf16[4,72,256]{2,1,0:T(8,128)(2,1)S(1)}, u32[]{:S(2)}, u32[]{:S(2)}) collective-permute-start(bf16[4,72,256]{2,1,0:T(8,128)(2,1)S(1)} %get-tuple-element.99), channel_id=1, source_target_pairs={{0,2},{2,0},{4,6},{6,4},{8,10},{10,8},{12,14},{14,12},{16,18},{18,... | collective-permute-start | bytes 442376 | tf_op jit(solution)/shard_map/ppermute | solution.py:61
  32.1 6.7 %collective-permute-start.7 = (bf16[4,72,256]{2,1,0:T(8,128)(2,1)S(1)}, bf16[4,72,256]{2,1,0:T(8,128)(2,1)S(1)}, u32[]{:S(2)}, u32[]{:S(2)}) collective-permute-start(bf16[4,72,256]{2,1,0:T(8,128)(2,1)S(1)} %get-tuple-element.100), channel_id=1, source_target_pairs={{0,4},{2,6},{4,0},{6,2},{8,12},{10,14},{12,8},{14,10},{16,20},{18,... | collective-permute-start | bytes 442376 | tf_op jit(solution)/shard_map/ppermute | solution.py:61
  32.6 6.2 %collective-permute-start.8 = (bf16[4,72,256]{2,1,0:T(8,128)(2,1)S(1)}, bf16[4,72,256]{2,1,0:T(8,128)(2,1)S(1)}, u32[]{:S(2)}, u32[]{:S(2)}) collective-permute-start(bf16[4,72,256]{2,1,0:T(8,128)(2,1)S(1)} %get-tuple-element.101), channel_id=1, source_target_pairs={{0,6},{2,4},{4,2},{6,0},{8,14},{10,12},{12,10},{14,8},{16,22},{18,... | collective-permute-start | bytes 442376 | tf_op jit(solution)/shard_map/ppermute | solution.py:61
  39.1 4.9 %collective-permute-start.10 = (bf16[1,72,256]{2,1,0:T(8,128)(2,1)S(1)}, bf16[1,72,256]{2,1,0:T(8,128)(2,1)S(1)}, u32[]{:S(2)}, u32[]{:S(2)}) collective-permute-start(bf16[1,72,256]{2,1,0:T(8,128)(2,1)S(1)} %get-tuple-element.110), channel_id=1, source_target_pairs={{0,16},{2,18},{4,20},{6,22},{8,24},{10,26},{12,28},{14,30},{16,0},... | collective-permute-start | bytes 110600 | tf_op jit(solution)/shard_map/ppermute | solution.py:61
  41.3 5.8 %collective-permute-start.11 = (bf16[1,72,256]{2,1,0:T(8,128)(2,1)S(1)}, bf16[1,72,256]{2,1,0:T(8,128)(2,1)S(1)}, u32[]{:S(2)}, u32[]{:S(2)}) collective-permute-start(bf16[1,72,256]{2,1,0:T(8,128)(2,1)S(1)} %get-tuple-element.111), channel_id=1, source_target_pairs={{0,24},{2,26},{4,28},{6,30},{8,16},{10,18},{12,20},{14,22},{16,8},... | collective-permute-start | bytes 110600 | tf_op jit(solution)/shard_map/ppermute | solution.py:61
  47.4 5.8 %collective-permute-start.14 = (bf16[1,72,256]{2,1,0:T(8,128)(2,1)S(1)}, bf16[1,72,256]{2,1,0:T(8,128)(2,1)S(1)}, u32[]{:S(2)}, u32[]{:S(2)}) collective-permute-start(bf16[1,72,256]{2,1,0:T(8,128)(2,1)S(1)} %get-tuple-element.113), channel_id=1, source_target_pairs={{0,24},{2,26},{4,28},{6,30},{8,16},{10,18},{12,20},{14,22},{16,8},... | collective-permute-start | bytes 110600 | tf_op jit(solution)/shard_map/ppermute | solution.py:61
  49.6 4.9 %collective-permute-start.13 = (bf16[1,72,256]{2,1,0:T(8,128)(2,1)S(1)}, bf16[1,72,256]{2,1,0:T(8,128)(2,1)S(1)}, u32[]{:S(2)}, u32[]{:S(2)}) collective-permute-start(bf16[1,72,256]{2,1,0:T(8,128)(2,1)S(1)} %get-tuple-element.113), channel_id=1, source_target_pairs={{0,16},{2,18},{4,20},{6,22},{8,24},{10,26},{12,28},{14,30},{16,0},... | collective-permute-start | bytes 110600 | tf_op jit(solution)/shard_map/ppermute | solution.py:61
  49.6 4.9 %collective-permute-start.12 = (bf16[1,72,256]{2,1,0:T(8,128)(2,1)S(1)}, bf16[1,72,256]{2,1,0:T(8,128)(2,1)S(1)}, u32[]{:S(2)}, u32[]{:S(2)}) collective-permute-start(bf16[1,72,256]{2,1,0:T(8,128)(2,1)S(1)} %get-tuple-element.113), channel_id=1, source_target_pairs={{0,8},{2,10},{4,12},{6,14},{8,0},{10,2},{12,4},{14,6},{16,24},{18,... | collective-permute-start | bytes 110600 | tf_op jit(solution)/shard_map/ppermute | solution.py:61
  54.5 7.9 %collective-permute-start.15 = (bf16[4,72,256]{2,1,0:T(8,128)(2,1)S(1)}, bf16[4,72,256]{2,1,0:T(8,128)(2,1)S(1)}, u32[]{:S(2)}, u32[]{:S(2)}) collective-permute-start(bf16[4,72,256]{2,1,0:T(8,128)(2,1)S(1)} %maximum_bitcast_fusion.1.refs_0_), channel_id=1, source_target_pairs={{0,2},{2,0},{4,6},{6,4},{8,10},{10,8},{12,14},{14,12},{16,18},{18,... | collective-permute-start | bytes 442376 | tf_op jit(solution)/shard_map/ppermute | solution.py:61
  56.5 5.8 %collective-permute-start.16 = (bf16[4,72,256]{2,1,0:T(8,128)(2,1)S(1)}, bf16[4,72,256]{2,1,0:T(8,128)(2,1)S(1)}, u32[]{:S(2)}, u32[]{:S(2)}) collective-permute-start(bf16[4,72,256]{2,1,0:T(8,128)(2,1)S(1)} %maximum_bitcast_fusion.1.refs_0_), channel_id=1, source_target_pairs={{0,4},{2,6},{4,0},{6,2},{8,12},{10,14},{12,8},{14,10},{16,20},{18,... | collective-permute-start | bytes 442376 | tf_op jit(solution)/shard_map/ppermute | solution.py:61
  57.5 6.0 %collective-permute-start.17 = (bf16[4,72,256]{2,1,0:T(8,128)(2,1)S(1)}, bf16[4,72,256]{2,1,0:T(8,128)(2,1)S(1)}, u32[]{:S(2)}, u32[]{:S(2)}) collective-permute-start(bf16[4,72,256]{2,1,0:T(8,128)(2,1)S(1)} %maximum_bitcast_fusion.1.refs_0_), channel_id=1, source_target_pairs={{0,6},{2,4},{4,2},{6,0},{8,14},{10,12},{12,10},{14,8},{16,22},{18,... | collective-permute-start | bytes 442376 | tf_op jit(solution)/shard_map/ppermute | solution.py:61
  68.2 9.0 %collective-permute-start.20 = (bf16[4,32,1024]{2,1,0:T(8,128)(2,1)S(1)}, bf16[4,32,1024]{2,1,0:T(8,128)(2,1)S(1)}, u32[]{:S(2)}, u32[]{:S(2)}) collective-permute-start(bf16[4,32,1024]{2,1,0:T(8,128)(2,1)S(1)} %get-tuple-element.126), channel_id=1, source_target_pairs={{0,6},{2,4},{4,2},{6,0},{8,14},{10,12},{12,10},{14,8},{16,22},{18,... | collective-permute-start | bytes 786440 | tf_op jit(solution)/shard_map/ppermute | solution.py:61
  69.5 8.9 %collective-permute-start.19 = (bf16[4,32,1024]{2,1,0:T(8,128)(2,1)S(1)}, bf16[4,32,1024]{2,1,0:T(8,128)(2,1)S(1)}, u32[]{:S(2)}, u32[]{:S(2)}) collective-permute-start(bf16[4,32,1024]{2,1,0:T(8,128)(2,1)S(1)} %get-tuple-element.125), channel_id=1, source_target_pairs={{0,4},{2,6},{4,0},{6,2},{8,12},{10,14},{12,8},{14,10},{16,20},{18,... | collective-permute-start | bytes 786440 | tf_op jit(solution)/shard_map/ppermute | solution.py:61
  70.5 7.8 %collective-permute-start.18 = (bf16[4,32,1024]{2,1,0:T(8,128)(2,1)S(1)}, bf16[4,32,1024]{2,1,0:T(8,128)(2,1)S(1)}, u32[]{:S(2)}, u32[]{:S(2)}) collective-permute-start(bf16[4,32,1024]{2,1,0:T(8,128)(2,1)S(1)} %get-tuple-element.124), channel_id=1, source_target_pairs={{0,2},{2,0},{4,6},{6,4},{8,10},{10,8},{12,14},{14,12},{16,18},{18,... | collective-permute-start | bytes 786440 | tf_op jit(solution)/shard_map/ppermute | solution.py:61
  78.6 9.1 %collective-permute-start.23 = (bf16[1,32,1024]{2,1,0:T(8,128)(2,1)S(1)}, bf16[1,32,1024]{2,1,0:T(8,128)(2,1)S(1)}, u32[]{:S(2)}, u32[]{:S(2)}) collective-permute-start(bf16[1,32,1024]{2,1,0:T(8,128)(2,1)S(1)} %get-tuple-element.180), channel_id=1, source_target_pairs={{0,24},{2,26},{4,28},{6,30},{8,16},{10,18},{12,20},{14,22},{16,8},... | collective-permute-start | bytes 196616 | tf_op jit(solution)/shard_map/ppermute | solution.py:61
  80.6 7.1 %collective-permute-start.22 = (bf16[1,32,1024]{2,1,0:T(8,128)(2,1)S(1)}, bf16[1,32,1024]{2,1,0:T(8,128)(2,1)S(1)}, u32[]{:S(2)}, u32[]{:S(2)}) collective-permute-start(bf16[1,32,1024]{2,1,0:T(8,128)(2,1)S(1)} %get-tuple-element.181), channel_id=1, source_target_pairs={{0,16},{2,18},{4,20},{6,22},{8,24},{10,26},{12,28},{14,30},{16,0},... | collective-permute-start | bytes 196616 | tf_op jit(solution)/shard_map/ppermute | solution.py:61
  81.7 5.9 %collective-permute-start.21 = (bf16[1,32,1024]{2,1,0:T(8,128)(2,1)S(1)}, bf16[1,32,1024]{2,1,0:T(8,128)(2,1)S(1)}, u32[]{:S(2)}, u32[]{:S(2)}) collective-permute-start(bf16[1,32,1024]{2,1,0:T(8,128)(2,1)S(1)} %get-tuple-element.179), channel_id=1, source_target_pairs={{0,8},{2,10},{4,12},{6,14},{8,0},{10,2},{12,4},{14,6},{16,24},{18,... | collective-permute-start | bytes 196616 | tf_op jit(solution)/shard_map/ppermute | solution.py:61
  87.7 7.2 %collective-permute-start.26 = (bf16[4,16,1024]{2,1,0:T(8,128)(2,1)S(1)}, bf16[4,16,1024]{2,1,0:T(8,128)(2,1)S(1)}, u32[]{:S(2)}, u32[]{:S(2)}) collective-permute-start(bf16[4,16,1024]{2,1,0:T(8,128)(2,1)S(1)} %get-tuple-element.154), channel_id=1, source_target_pairs={{0,6},{2,4},{4,2},{6,0},{8,14},{10,12},{12,10},{14,8},{16,22},{18,... | collective-permute-start | bytes 393224 | tf_op jit(solution)/shard_map/ppermute | solution.py:61
  89.0 6.1 %collective-permute-start.25 = (bf16[4,16,1024]{2,1,0:T(8,128)(2,1)S(1)}, bf16[4,16,1024]{2,1,0:T(8,128)(2,1)S(1)}, u32[]{:S(2)}, u32[]{:S(2)}) collective-permute-start(bf16[4,16,1024]{2,1,0:T(8,128)(2,1)S(1)} %get-tuple-element.153), channel_id=1, source_target_pairs={{0,4},{2,6},{4,0},{6,2},{8,12},{10,14},{12,8},{14,10},{16,20},{18,... | collective-permute-start | bytes 393224 | tf_op jit(solution)/shard_map/ppermute | solution.py:61
  90.0 5.0 %collective-permute-start.24 = (bf16[4,16,1024]{2,1,0:T(8,128)(2,1)S(1)}, bf16[4,16,1024]{2,1,0:T(8,128)(2,1)S(1)}, u32[]{:S(2)}, u32[]{:S(2)}) collective-permute-start(bf16[4,16,1024]{2,1,0:T(8,128)(2,1)S(1)} %get-tuple-element.152), channel_id=1, source_target_pairs={{0,2},{2,0},{4,6},{6,4},{8,10},{10,8},{12,14},{14,12},{16,18},{18,... | collective-permute-start | bytes 393224 | tf_op jit(solution)/shard_map/ppermute | solution.py:61
  95.2 8.9 %collective-permute-start.27 = (bf16[48,1024]{1,0:T(8,128)(2,1)S(1)}, bf16[48,1024]{1,0:T(8,128)(2,1)S(1)}, u32[]{:S(2)}, u32[]{:S(2)}) collective-permute-start(bf16[48,1024]{1,0:T(8,128)(2,1)S(1)} %get-tuple-element.189), channel_id=1, source_target_pairs={{0,8},{2,10},{4,12},{6,14},{8,0},{10,2},{12,4},{14,6},{16,24},{18,... | collective-permute-start | bytes 294920 | tf_op jit(solution)/shard_map/ppermute | solution.py:61
  96.0 8.2 %collective-permute-start.28 = (bf16[48,1024]{1,0:T(8,128)(2,1)S(1)}, bf16[48,1024]{1,0:T(8,128)(2,1)S(1)}, u32[]{:S(2)}, u32[]{:S(2)}) collective-permute-start(bf16[48,1024]{1,0:T(8,128)(2,1)S(1)} %get-tuple-element.188), channel_id=1, source_target_pairs={{0,16},{2,18},{4,20},{6,22},{8,24},{10,26},{12,28},{14,30},{16,0},... | collective-permute-start | bytes 294920 | tf_op jit(solution)/shard_map/ppermute | solution.py:61
  97.8 6.5 %collective-permute-start.29 = (bf16[48,1024]{1,0:T(8,128)(2,1)S(1)}, bf16[48,1024]{1,0:T(8,128)(2,1)S(1)}, u32[]{:S(2)}, u32[]{:S(2)}) collective-permute-start(bf16[48,1024]{1,0:T(8,128)(2,1)S(1)} %get-tuple-element.187), channel_id=1, source_target_pairs={{0,24},{2,26},{4,28},{6,30},{8,16},{10,18},{12,20},{14,22},{16,8},... | collective-permute-start | bytes 294920 | tf_op jit(solution)/shard_map/ppermute | solution.py:61
  104.1 6.2 %collective-permute-start.33 = (bf16[1024,512]{1,0:T(8,128)(2,1)S(1)}, bf16[1024,512]{1,0:T(8,128)(2,1)S(1)}, u32[]{:S(2)}, u32[]{:S(2)}) collective-permute-start(bf16[1024,512]{1,0:T(8,128)(2,1)S(1)} %part.1), channel_id=1, source_target_pairs={{0,1},{1,0},{2,3},{3,2},{4,5},{5,4},{6,7},{7,6},{8,9},{9,8},{10,11... | collective-permute-start | bytes 3145736 | tf_op jit(solution)/shard_map/ppermute | solution.py:767
  104.3 9.2 %collective-permute-start.30 = (bf16[4,32,1024]{2,1,0:T(8,128)(2,1)S(1)}, bf16[4,32,1024]{2,1,0:T(8,128)(2,1)S(1)}, u32[]{:S(2)}, u32[]{:S(2)}) collective-permute-start(bf16[4,32,1024]{2,1,0:T(8,128)(2,1)S(1)} %maximum_bitcast_fusion.refs_0_), channel_id=1, source_target_pairs={{0,2},{2,0},{4,6},{6,4},{8,10},{10,8},{12,14},{14,12},{16,18},{18,... | collective-permute-start | bytes 786440 | tf_op jit(solution)/shard_map/ppermute | solution.py:61
  105.6 13.9 %collective-permute-start.31 = (bf16[4,32,1024]{2,1,0:T(8,128)(2,1)S(1)}, bf16[4,32,1024]{2,1,0:T(8,128)(2,1)S(1)}, u32[]{:S(2)}, u32[]{:S(2)}) collective-permute-start(bf16[4,32,1024]{2,1,0:T(8,128)(2,1)S(1)} %maximum_bitcast_fusion.refs_0_), channel_id=1, source_target_pairs={{0,4},{2,6},{4,0},{6,2},{8,12},{10,14},{12,8},{14,10},{16,20},{18,... | collective-permute-start | bytes 786440 | tf_op jit(solution)/shard_map/ppermute | solution.py:61
  106.5 13.0 %collective-permute-start.32 = (bf16[4,32,1024]{2,1,0:T(8,128)(2,1)S(1)}, bf16[4,32,1024]{2,1,0:T(8,128)(2,1)S(1)}, u32[]{:S(2)}, u32[]{:S(2)}) collective-permute-start(bf16[4,32,1024]{2,1,0:T(8,128)(2,1)S(1)} %maximum_bitcast_fusion.refs_0_), channel_id=1, source_target_pairs={{0,6},{2,4},{4,2},{6,0},{8,14},{10,12},{12,10},{14,8},{16,22},{18,... | collective-permute-start | bytes 786440 | tf_op jit(solution)/shard_map/ppermute | solution.py:61
  (7 other events, 57.1 us)

commit v6 on v5

--- a/solution.py
+++ b/solution.py
@@ -752,6 +752,8 @@
         (land_sum, weight_own, query_f, there)
     )
     land_sum, weight_own, grad_sb = lax.optimization_barrier((land_sum, weight_own, grad_sb))
+    arrived = lax.ppermute(there, "head", [(0, 1), (1, 0)])
+    arrived, grad_sb = lax.optimization_barrier((arrived, grad_sb))
     key_b, value_grad = call(
         key_kernel,
         (pairs,),
@@ -764,7 +766,6 @@
         name="key_grad",
     )
 
-    arrived = lax.ppermute(there, "head", [(0, 1), (1, 0)])
     mixed = call(
         mixed_kernel,
         (4,),

time: 122 us -> 127 us (1.041)
  waiting for transfers between devices: 22.4 us -> 27.2 us
    ppermute x33, waiting for transfers between devices: 22.4 us -> 27.2 us  [exchange(): return lax.ppermute(block, 'seq', [(i, i ^ mask) for i in range(n)])]
  transfers between devices with their start and end apart: 34 -> 34, of which waited for: 15 -> 16; matrix products, arithmetic and copies ran while one was open for 4% -> 4% of each run, Pallas kernels for 23% -> 19%
where the time goes in v6:
time: 127 us
  Pallas kernels  47.3 us (37%)
  starting transfers between devices  44.9 us (35%)
  waiting for transfers between devices  27.2 us (21%)
  other arithmetic  2.94 us (2%)
  matrix products  2.87 us (2%)
    pallas_call x14, Pallas kernels, call(): pl.pallas_call(kernel, grid_spec=pltpu.PrefetchScalarGridSpec(num_scalar_...  47.3 us
    ppermute x33, starting transfers between devices, exchange(): return lax.ppermute(block, 'seq', [(i, i ^ mask) for i in range(n)])  44.9 us
    ppermute x33, waiting for transfers between devices, exchange(): return lax.ppermute(block, 'seq', [(i, i ^ mask) for i in range(n)])  27.2 us
    dot_general x1, matrix products, dot(): lax.dot_general(left, right, (dims, ((), ())), preferred_element_type=F32)  2.87 us
  transfers between devices with their start and end apart: 34, of which 16 were waited for; matrix products, arithmetic and copies ran while one was open for 4% of the time, Pallas kernels for 19%

profile of v6, /device:TPU:0, one launch (start us, length us, event | category | flops | bytes accessed | tf_op | source)
XLA Modules:
  0.0 126.5 jit_solution(13945571856451372425)
XLA Ops:
  0.8 1.7 %means.1 = bf16[16,1024]{1,0:T(8,128)(2,1)S(1)} custom-call(bf16[1024,512]{1,0:T(8,128)(2,1)} %q_ref.5, bf16[1024,512]{1,0:T(8,128)(2,1)} %k_ref.4), custom_call_target="tpu_custom_call" | custom-call | bytes 4194304 | tf_op jit(solution)/shard_map/means/pallas_call | solution.py:489
  2.5 5.1 %collective-permute-start.2 = (bf16[1,16,1024]{2,1,0:T(8,128)(2,1)S(1)}, bf16[1,16,1024]{2,1,0:T(8,128)(2,1)S(1)}, u32[]{:S(2)}, u32[]{:S(2)}) collective-permute-start(bf16[1,16,1024]{2,1,0:T(8,128)(2,1)S(1)} %bitcast.63), channel_id=1, source_target_pairs={{0,24},{2,26},{4,28},{6,30},{8,16},{10,18},{12,20},{14,22},{16,8},... | collective-permute-start | bytes 98312 | tf_op jit(solution)/shard_map/ppermute | solution.py:61
  9.5 2.9 %collective-permute-done.1 = bf16[1,16,1024]{2,1,0:T(8,128)(2,1)S(1)} collective-permute-done((bf16[1,16,1024]{2,1,0:T(8,128)(2,1)S(1)}, bf16[1,16,1024]{2,1,0:T(8,128)(2,1)S(1)}, u32[]{:S(2)}, u32[]{:S(2)}) %collective-permute-start.1) | collective-permute-done | bytes 32800 | tf_op jit(solution)/shard_map/ppermute | solution.py:61
  12.5 1.6 %collective-permute-start.3 = (bf16[4,16,1024]{2,1,0:T(8,128)(2,1)S(1)}, bf16[4,16,1024]{2,1,0:T(8,128)(2,1)S(1)}, u32[]{:S(2)}, u32[]{:S(2)}) collective-permute-start(bf16[4,16,1024]{2,1,0:T(8,128)(2,1)S(1)} %maximum_bitcast_fusion.2.refs_0_), channel_id=1, source_target_pairs={{0,2},{2,0},{4,6},{6,4},{8,10},{10,8},{12,14},{14,12},{16,18},{18,... | collective-permute-start | bytes 393224 | tf_op jit(solution)/shard_map/ppermute | solution.py:61
  14.0 1.5 %collective-permute-start.4 = (bf16[4,16,1024]{2,1,0:T(8,128)(2,1)S(1)}, bf16[4,16,1024]{2,1,0:T(8,128)(2,1)S(1)}, u32[]{:S(2)}, u32[]{:S(2)}) collective-permute-start(bf16[4,16,1024]{2,1,0:T(8,128)(2,1)S(1)} %maximum_bitcast_fusion.2.refs_0_), channel_id=1, source_target_pairs={{0,4},{2,6},{4,0},{6,2},{8,12},{10,14},{12,8},{14,10},{16,20},{18,... | collective-permute-start | bytes 393224 | tf_op jit(solution)/shard_map/ppermute | solution.py:61
  16.0 2.9 %convolution_convert_fusion.g_ref = bf16[1024,512]{1,0:T(8,128)(2,1)S(1)} fusion(bf16[1024,1024]{1,0:T(8,128)(2,1)} %cot_ref.1, bf16[512,1024]{1,0:T(8,128)(2,1)S(1)} %copy-done), kind=kOutput, calls=%fused_computation.4 | convolution fusion | flops 1074266112 | bytes 4194304 | tf_op jit(solution)/shard_map/dot_general | solution.py:23
  20.0 1.5 %collective-permute-done.5.refs_3_ = bf16[4,16,1024]{2,1,0:T(8,128)(2,1)S(1)} collective-permute-done((bf16[4,16,1024]{2,1,0:T(8,128)(2,1)S(1)}, bf16[4,16,1024]{2,1,0:T(8,128)(2,1)S(1)}, u32[]{:S(2)}, u32[]{:S(2)}) %collective-permute-start.5) | collective-permute-done | bytes 131104 | tf_op jit(solution)/shard_map/ppermute | solution.py:61
  21.4 10.0 %forward.1 = (bf16[1024,2048]{1,0:T(8,128)(2,1)S(1)}, bf16[1024,2048]{1,0:T(8,128)(2,1)S(1)}, f32[4,8,256]{2,1,0:T(8,128)S(1)}, bf16[256,1024]{1,0:T(8,128)(2,1)...) custom-call(s32[2]{0:T(128)S(1)} %pad_add_fusion.me_ref, ...), custom_call_target="tpu_custom_call" | custom-call | flops 8589934592 | bytes 4194304 | tf_op jit(solution)/shard_map/forward/pallas_call | solution.py:489
  32.6 2.4 %collective-permute-start.8 = (bf16[4,72,256]{2,1,0:T(8,128)(2,1)S(1)}, bf16[4,72,256]{2,1,0:T(8,128)(2,1)S(1)}, u32[]{:S(2)}, u32[]{:S(2)}) collective-permute-start(bf16[4,72,256]{2,1,0:T(8,128)(2,1)S(1)} %get-tuple-element.103), channel_id=1, source_target_pairs={{0,6},{2,4},{4,2},{6,0},{8,14},{10,12},{12,10},{14,8},{16,22},{18,... | collective-permute-start | bytes 442376 | tf_op jit(solution)/shard_map/ppermute | solution.py:61
  35.0 3.6 %newton.1 = (f32[9,256,256]{2,1,0:T(8,128)S(1)}, f32[1,256,256]{2,1,0:T(8,128)S(1)}) custom-call(s32[3]{0:T(128)S(1)} %pad_add_fusion.1.own_ref, bf16[256,1024]{1,0:T(8,128)(2,1)S(1)} %get-tuple-element.104.lq_ref.lk_ref, bf16[256,1024]{1,0:T(8,128)(2,1)S(1)} %get-tuple-element.104.lq_ref.lk_ref), custom_call_target="tpu_custom_call" | custom-call | flops 4294967296 | bytes 4194304 | tf_op jit(solution)/shard_map/newton/pallas_call | solution.py:489
  39.1 2.2 %collective-permute-start.10 = (bf16[1,72,256]{2,1,0:T(8,128)(2,1)S(1)}, bf16[1,72,256]{2,1,0:T(8,128)(2,1)S(1)}, u32[]{:S(2)}, u32[]{:S(2)}) collective-permute-start(bf16[1,72,256]{2,1,0:T(8,128)(2,1)S(1)} %get-tuple-element.112), channel_id=1, source_target_pairs={{0,16},{2,18},{4,20},{6,22},{8,24},{10,26},{12,28},{14,30},{16,0},... | collective-permute-start | bytes 110600 | tf_op jit(solution)/shard_map/ppermute | solution.py:61
  41.3 2.1 %collective-permute-start.11 = (bf16[1,72,256]{2,1,0:T(8,128)(2,1)S(1)}, bf16[1,72,256]{2,1,0:T(8,128)(2,1)S(1)}, u32[]{:S(2)}, u32[]{:S(2)}) collective-permute-start(bf16[1,72,256]{2,1,0:T(8,128)(2,1)S(1)} %get-tuple-element.113), channel_id=1, source_target_pairs={{0,24},{2,26},{4,28},{6,30},{8,16},{10,18},{12,20},{14,22},{16,8},... | collective-permute-start | bytes 110600 | tf_op jit(solution)/shard_map/ppermute | solution.py:61
  44.0 3.1 %collective-permute-done.11.refs_3_ = bf16[1,72,256]{2,1,0:T(8,128)(2,1)S(1)} collective-permute-done((bf16[1,72,256]{2,1,0:T(8,128)(2,1)S(1)}, bf16[1,72,256]{2,1,0:T(8,128)(2,1)S(1)}, u32[]{:S(2)}, u32[]{:S(2)}) %collective-permute-start.11) | collective-permute-done | bytes 36896 | tf_op jit(solution)/shard_map/ppermute | solution.py:61
  47.4 2.2 %collective-permute-start.14 = (bf16[1,72,256]{2,1,0:T(8,128)(2,1)S(1)}, bf16[1,72,256]{2,1,0:T(8,128)(2,1)S(1)}, u32[]{:S(2)}, u32[]{:S(2)}) collective-permute-start(bf16[1,72,256]{2,1,0:T(8,128)(2,1)S(1)} %get-tuple-element.115), channel_id=1, source_target_pairs={{0,24},{2,26},{4,28},{6,30},{8,16},{10,18},{12,20},{14,22},{16,8},... | collective-permute-start | bytes 110600 | tf_op jit(solution)/shard_map/ppermute | solution.py:61
  49.6 2.3 %collective-permute-start.12 = (bf16[1,72,256]{2,1,0:T(8,128)(2,1)S(1)}, bf16[1,72,256]{2,1,0:T(8,128)(2,1)S(1)}, u32[]{:S(2)}, u32[]{:S(2)}) collective-permute-start(bf16[1,72,256]{2,1,0:T(8,128)(2,1)S(1)} %get-tuple-element.115), channel_id=1, source_target_pairs={{0,8},{2,10},{4,12},{6,14},{8,0},{10,2},{12,4},{14,6},{16,24},{18,... | collective-permute-start | bytes 110600 | tf_op jit(solution)/shard_map/ppermute | solution.py:61
  51.8 1.4 %collective-permute-done.14 = bf16[1,72,256]{2,1,0:T(8,128)(2,1)S(1)} collective-permute-done((bf16[1,72,256]{2,1,0:T(8,128)(2,1)S(1)}, bf16[1,72,256]{2,1,0:T(8,128)(2,1)S(1)}, u32[]{:S(2)}, u32[]{:S(2)}) %collective-permute-start.14) | collective-permute-done | bytes 36896 | tf_op jit(solution)/shard_map/ppermute | solution.py:61
  54.5 2.1 %collective-permute-start.15 = (bf16[4,72,256]{2,1,0:T(8,128)(2,1)S(1)}, bf16[4,72,256]{2,1,0:T(8,128)(2,1)S(1)}, u32[]{:S(2)}, u32[]{:S(2)}) collective-permute-start(bf16[4,72,256]{2,1,0:T(8,128)(2,1)S(1)} %maximum_bitcast_fusion.1.refs_0_), channel_id=1, source_target_pairs={{0,2},{2,0},{4,6},{6,4},{8,10},{10,8},{12,14},{14,12},{16,18},{18,... | collective-permute-start | bytes 442376 | tf_op jit(solution)/shard_map/ppermute | solution.py:61
  58.1 4.3 %newton_grad.1 = (f32[256,128]{1,0:T(8,128)S(1)}, f32[256,128]{1,0:T(8,128)S(1)}) custom-call(s32[3]{0:T(128)S(1)} %pad_add_fusion.1.own_ref, f32[9,256,256]{2,1,0:T(8,128)S(1)} %get-tuple-element.116.saved_ref, f32[32,256]{1,0:T(8,128)S(1)} %get-tuple-element.117.values_ref, f32[32,256]{1,0:T(8,128)S(1)} %get-tuple-element.118.grads_ref, ...), custom_call_target="tpu_custom_call" | custom-call | flops 8589934592 | bytes 4194304 | tf_op jit(solution)/shard_map/newton_grad/pallas_call | solution.py:489
  63.5 4.7 %attend.1 = (bf16[1024,512]{1,0:T(8,128)(2,1)S(1)}, bf16[512,256]{1,0:T(8,128)(2,1)S(1)}, bf16[512,256]{1,0:T(8,128)(2,1)S(1)}, f32[8,256]{1,0:T(8,128)S(1)}, bf...) custom-call(s32[2]{0:T(128)S(1)} %pad_add_fusion.me_ref, ...), custom_call_target="tpu_custom_call" | custom-call | flops 4294967296 | bytes 4194304 | tf_op jit(solution)/shard_map/attend/pallas_call | solution.py:489
  71.8 5.4 %query_land.1 = (bf16[256,512]{1,0:T(8,128)(2,1)S(1)}, bf16[1024,2048]{1,0:T(8,128)(2,1)S(1)}) custom-call(s32[3]{0:T(128)S(1)} %pad_add_fusion.1.own_ref, bf16[1024,512]{1,0:T(8,128)(2,1)S(1)} %copy-done.1, bf16[1024,512]{1,0:T(8,128)(2,1)S(1)} %convolution_convert_fusion.g_ref, bf16[1024,2048]{1,0:T(8,128)(2,1)S(1)} %get-tuple-element.98.fb_ref, ...), custom_call_target="tpu_custom_call" | custom-call | flops 4294967296 | bytes 4194304 | tf_op jit(solution)/shard_map/query_land/pallas_call | solution.py:489
  78.6 2.0 %collective-permute-start.23 = (bf16[1,32,1024]{2,1,0:T(8,128)(2,1)S(1)}, bf16[1,32,1024]{2,1,0:T(8,128)(2,1)S(1)}, u32[]{:S(2)}, u32[]{:S(2)}) collective-permute-start(bf16[1,32,1024]{2,1,0:T(8,128)(2,1)S(1)} %get-tuple-element.184), channel_id=1, source_target_pairs={{0,24},{2,26},{4,28},{6,30},{8,16},{10,18},{12,20},{14,22},{16,8},... | collective-permute-start | bytes 196616 | tf_op jit(solution)/shard_map/ppermute | solution.py:61
  83.0 4.6 %key_land.1 = (bf16[1024,2048]{1,0:T(8,128)(2,1)S(1)}, bf16[4,16,1024]{2,1,0:T(8,128)(2,1)S(1)}, bf16[4,16,1024]{2,1,0:T(8,128)(2,1)S(1)}, bf16[4,16,1024]{2,1,0:T(8,128)(2,1)S(1)}, bf16[4,16,1024]{2,1,0:T(8,128)(2,1)S(1)}) custom-call(s32[3]{0:T(128)S(1)} %pad_add_fusion.1.own_ref, bf16[1024,512]{1,0:T(8,128)(2,1)S(1)} %copy-done.2, ...), custom_call_target="tpu_custom_call" | custom-call | flops 4294967296 | bytes 4194304 | tf_op jit(solution)/shard_map/key_land/pallas_call | solution.py:489
  91.3 2.3 %query_grad.1 = bf16[1024,512]{1,0:T(8,128)(2,1)S(1)} custom-call(bf16[1024,2048]{1,0:T(8,128)(2,1)S(1)} %get-tuple-element.158.ds_ref, bf16[256,1024]{1,0:T(8,128)(2,1)S(1)} %get-tuple-element.104.lq_ref.lk_ref), custom_call_target="tpu_custom_call" | custom-call | flops 2147483648 | bytes 4194304 | tf_op jit(solution)/shard_map/query_grad/pallas_call | solution.py:489
  96.0 1.8 %collective-permute-start.28 = (bf16[48,1024]{1,0:T(8,128)(2,1)S(1)}, bf16[48,1024]{1,0:T(8,128)(2,1)S(1)}, u32[]{:S(2)}, u32[]{:S(2)}) collective-permute-start(bf16[48,1024]{1,0:T(8,128)(2,1)S(1)} %get-tuple-element.192), channel_id=1, source_target_pairs={{0,16},{2,18},{4,20},{6,22},{8,24},{10,26},{12,28},{14,30},{16,0},... | collective-permute-start | bytes 294920 | tf_op jit(solution)/shard_map/ppermute | solution.py:61
  97.8 1.9 %collective-permute-start.29 = (bf16[48,1024]{1,0:T(8,128)(2,1)S(1)}, bf16[48,1024]{1,0:T(8,128)(2,1)S(1)}, u32[]{:S(2)}, u32[]{:S(2)}) collective-permute-start(bf16[48,1024]{1,0:T(8,128)(2,1)S(1)} %get-tuple-element.191), channel_id=1, source_target_pairs={{0,24},{2,26},{4,28},{6,30},{8,16},{10,18},{12,20},{14,22},{16,8},... | collective-permute-start | bytes 294920 | tf_op jit(solution)/shard_map/ppermute | solution.py:61
  99.7 2.2 %collective-permute-done.27 = bf16[48,1024]{1,0:T(8,128)(2,1)S(1)} collective-permute-done((bf16[48,1024]{1,0:T(8,128)(2,1)S(1)}, bf16[48,1024]{1,0:T(8,128)(2,1)S(1)}, u32[]{:S(2)}, u32[]{:S(2)}) %collective-permute-start.27) | collective-permute-done | bytes 98336 | tf_op jit(solution)/shard_map/ppermute | solution.py:61
  101.9 4.9 %collective-permute-done.28 = bf16[48,1024]{1,0:T(8,128)(2,1)S(1)} collective-permute-done((bf16[48,1024]{1,0:T(8,128)(2,1)S(1)}, bf16[48,1024]{1,0:T(8,128)(2,1)S(1)}, u32[]{:S(2)}, u32[]{:S(2)}) %collective-permute-start.28) | collective-permute-done | bytes 98336 | tf_op jit(solution)/shard_map/ppermute | solution.py:61
  106.8 4.5 %key_grad.1 = (bf16[1024,512]{1,0:T(8,128)(2,1)S(1)}, bf16[1024,512]{1,0:T(8,128)(2,1)}) custom-call(bf16[1024,2048]{1,0:T(8,128)(2,1)S(1)} %get-tuple-element.168.ds_ref, bf16[1024,2048]{1,0:T(8,128)(2,1)S(1)} %get-tuple-element.137.pb_ref, bf16[256,1024]{1,0:T(8,128)(2,1)S(1)} %get-tuple-element.104.lq_ref.lk_ref, ...), custom_call_target="tpu_custom_call" | custom-call | flops 4294967296 | bytes 4194304 | tf_op jit(solution)/shard_map/key_grad/pallas_call | solution.py:489
  113.3 1.6 %collective-permute-start.33 = (bf16[4,32,1024]{2,1,0:T(8,128)(2,1)S(1)}, bf16[4,32,1024]{2,1,0:T(8,128)(2,1)S(1)}, u32[]{:S(2)}, u32[]{:S(2)}) collective-permute-start(bf16[4,32,1024]{2,1,0:T(8,128)(2,1)S(1)} %maximum_bitcast_fusion.refs_0_), channel_id=1, source_target_pairs={{0,6},{2,4},{4,2},{6,0},{8,14},{10,12},{12,10},{14,8},{16,22},{18,... | collective-permute-start | bytes 786440 | tf_op jit(solution)/shard_map/ppermute | solution.py:61
  117.3 2.4 %mixed.1 = bf16[1024,512]{1,0:T(8,128)(2,1)} custom-call(s32[1]{0:T(128)} %bitcast.1._, bf16[1024,512]{1,0:T(8,128)(2,1)S(1)} %get-tuple-element.160.attn_ref, bf16[512,1024]{1,0:T(8,128)(2,1)S(1)} %copy-done, bf16[1024,512]{1,0:T(8,128)(2,1)S(1)} %collective-permute-done.30.other_ref), custom_call_target="tpu_custom_call" | custom-call | flops 1073741824 | bytes 4194304 | tf_op jit(solution)/shard_map/mixed/pallas_call | solution.py:489
  120.7 3.7 %collective-permute-done.32.refs_2_ = bf16[4,32,1024]{2,1,0:T(8,128)(2,1)S(1)} collective-permute-done((bf16[4,32,1024]{2,1,0:T(8,128)(2,1)S(1)}, bf16[4,32,1024]{2,1,0:T(8,128)(2,1)S(1)}, u32[]{:S(2)}, u32[]{:S(2)}) %collective-permute-start.32) | collective-permute-done | bytes 262176 | tf_op jit(solution)/shard_map/ppermute | solution.py:61
  124.4 2.0 %unpack.1 = f32[512,1024]{1,0:T(8,128)} custom-call(s32[2]{0:T(128)S(1)} %pad_add_fusion.me_ref, bf16[4,32,1024]{2,1,0:T(8,128)(2,1)S(1)} %maximum_bitcast_fusion.refs_0_, bf16[4,32,1024]{2,1,0:T(8,128)(2,1)S(1)} %collective-permute-done.31.refs_1_, bf16[4,32,1024]{2,1,0:T(8,128)(2,1)S(1)} %collective-permute-done.32.refs_2_, ...), custom_call_target="tpu_custom_call" | custom-call | bytes 4194304 | tf_op jit(solution)/shard_map/unpack/pallas_call | solution.py:489
  (79 shorter events, 28.7 us)
Async XLA Ops:
  2.5 7.0 %collective-permute-start.2 = (bf16[1,16,1024]{2,1,0:T(8,128)(2,1)S(1)}, bf16[1,16,1024]{2,1,0:T(8,128)(2,1)S(1)}, u32[]{:S(2)}, u32[]{:S(2)}) collective-permute-start(bf16[1,16,1024]{2,1,0:T(8,128)(2,1)S(1)} %bitcast.63), channel_id=1, source_target_pairs={{0,24},{2,26},{4,28},{6,30},{8,16},{10,18},{12,20},{14,22},{16,8},... | collective-permute-start | bytes 98312 | tf_op jit(solution)/shard_map/ppermute | solution.py:61
  7.6 4.8 %collective-permute-start.1 = (bf16[1,16,1024]{2,1,0:T(8,128)(2,1)S(1)}, bf16[1,16,1024]{2,1,0:T(8,128)(2,1)S(1)}, u32[]{:S(2)}, u32[]{:S(2)}) collective-permute-start(bf16[1,16,1024]{2,1,0:T(8,128)(2,1)S(1)} %bitcast.64), channel_id=1, source_target_pairs={{0,16},{2,18},{4,20},{6,22},{8,24},{10,26},{12,28},{14,30},{16,0},... | collective-permute-start | bytes 98312 | tf_op jit(solution)/shard_map/ppermute | solution.py:61
  12.5 6.4 %collective-permute-start.3 = (bf16[4,16,1024]{2,1,0:T(8,128)(2,1)S(1)}, bf16[4,16,1024]{2,1,0:T(8,128)(2,1)S(1)}, u32[]{:S(2)}, u32[]{:S(2)}) collective-permute-start(bf16[4,16,1024]{2,1,0:T(8,128)(2,1)S(1)} %maximum_bitcast_fusion.2.refs_0_), channel_id=1, source_target_pairs={{0,2},{2,0},{4,6},{6,4},{8,10},{10,8},{12,14},{14,12},{16,18},{18,... | collective-permute-start | bytes 393224 | tf_op jit(solution)/shard_map/ppermute | solution.py:61
  14.0 5.9 %collective-permute-start.4 = (bf16[4,16,1024]{2,1,0:T(8,128)(2,1)S(1)}, bf16[4,16,1024]{2,1,0:T(8,128)(2,1)S(1)}, u32[]{:S(2)}, u32[]{:S(2)}) collective-permute-start(bf16[4,16,1024]{2,1,0:T(8,128)(2,1)S(1)} %maximum_bitcast_fusion.2.refs_0_), channel_id=1, source_target_pairs={{0,4},{2,6},{4,0},{6,2},{8,12},{10,14},{12,8},{14,10},{16,20},{18,... | collective-permute-start | bytes 393224 | tf_op jit(solution)/shard_map/ppermute | solution.py:61
  15.6 5.9 %collective-permute-start.5 = (bf16[4,16,1024]{2,1,0:T(8,128)(2,1)S(1)}, bf16[4,16,1024]{2,1,0:T(8,128)(2,1)S(1)}, u32[]{:S(2)}, u32[]{:S(2)}) collective-permute-start(bf16[4,16,1024]{2,1,0:T(8,128)(2,1)S(1)} %maximum_bitcast_fusion.2.refs_0_), channel_id=1, source_target_pairs={{0,6},{2,4},{4,2},{6,0},{8,14},{10,12},{12,10},{14,8},{16,22},{18,... | collective-permute-start | bytes 393224 | tf_op jit(solution)/shard_map/ppermute | solution.py:61
  31.5 7.2 %collective-permute-start.6 = (bf16[4,72,256]{2,1,0:T(8,128)(2,1)S(1)}, bf16[4,72,256]{2,1,0:T(8,128)(2,1)S(1)}, u32[]{:S(2)}, u32[]{:S(2)}) collective-permute-start(bf16[4,72,256]{2,1,0:T(8,128)(2,1)S(1)} %get-tuple-element.101), channel_id=1, source_target_pairs={{0,2},{2,0},{4,6},{6,4},{8,10},{10,8},{12,14},{14,12},{16,18},{18,... | collective-permute-start | bytes 442376 | tf_op jit(solution)/shard_map/ppermute | solution.py:61
  32.1 6.7 %collective-permute-start.7 = (bf16[4,72,256]{2,1,0:T(8,128)(2,1)S(1)}, bf16[4,72,256]{2,1,0:T(8,128)(2,1)S(1)}, u32[]{:S(2)}, u32[]{:S(2)}) collective-permute-start(bf16[4,72,256]{2,1,0:T(8,128)(2,1)S(1)} %get-tuple-element.102), channel_id=1, source_target_pairs={{0,4},{2,6},{4,0},{6,2},{8,12},{10,14},{12,8},{14,10},{16,20},{18,... | collective-permute-start | bytes 442376 | tf_op jit(solution)/shard_map/ppermute | solution.py:61
  32.6 6.2 %collective-permute-start.8 = (bf16[4,72,256]{2,1,0:T(8,128)(2,1)S(1)}, bf16[4,72,256]{2,1,0:T(8,128)(2,1)S(1)}, u32[]{:S(2)}, u32[]{:S(2)}) collective-permute-start(bf16[4,72,256]{2,1,0:T(8,128)(2,1)S(1)} %get-tuple-element.103), channel_id=1, source_target_pairs={{0,6},{2,4},{4,2},{6,0},{8,14},{10,12},{12,10},{14,8},{16,22},{18,... | collective-permute-start | bytes 442376 | tf_op jit(solution)/shard_map/ppermute | solution.py:61
  39.1 4.9 %collective-permute-start.10 = (bf16[1,72,256]{2,1,0:T(8,128)(2,1)S(1)}, bf16[1,72,256]{2,1,0:T(8,128)(2,1)S(1)}, u32[]{:S(2)}, u32[]{:S(2)}) collective-permute-start(bf16[1,72,256]{2,1,0:T(8,128)(2,1)S(1)} %get-tuple-element.112), channel_id=1, source_target_pairs={{0,16},{2,18},{4,20},{6,22},{8,24},{10,26},{12,28},{14,30},{16,0},... | collective-permute-start | bytes 110600 | tf_op jit(solution)/shard_map/ppermute | solution.py:61
  41.3 5.8 %collective-permute-start.11 = (bf16[1,72,256]{2,1,0:T(8,128)(2,1)S(1)}, bf16[1,72,256]{2,1,0:T(8,128)(2,1)S(1)}, u32[]{:S(2)}, u32[]{:S(2)}) collective-permute-start(bf16[1,72,256]{2,1,0:T(8,128)(2,1)S(1)} %get-tuple-element.113), channel_id=1, source_target_pairs={{0,24},{2,26},{4,28},{6,30},{8,16},{10,18},{12,20},{14,22},{16,8},... | collective-permute-start | bytes 110600 | tf_op jit(solution)/shard_map/ppermute | solution.py:61
  47.4 5.8 %collective-permute-start.14 = (bf16[1,72,256]{2,1,0:T(8,128)(2,1)S(1)}, bf16[1,72,256]{2,1,0:T(8,128)(2,1)S(1)}, u32[]{:S(2)}, u32[]{:S(2)}) collective-permute-start(bf16[1,72,256]{2,1,0:T(8,128)(2,1)S(1)} %get-tuple-element.115), channel_id=1, source_target_pairs={{0,24},{2,26},{4,28},{6,30},{8,16},{10,18},{12,20},{14,22},{16,8},... | collective-permute-start | bytes 110600 | tf_op jit(solution)/shard_map/ppermute | solution.py:61
  49.6 4.9 %collective-permute-start.13 = (bf16[1,72,256]{2,1,0:T(8,128)(2,1)S(1)}, bf16[1,72,256]{2,1,0:T(8,128)(2,1)S(1)}, u32[]{:S(2)}, u32[]{:S(2)}) collective-permute-start(bf16[1,72,256]{2,1,0:T(8,128)(2,1)S(1)} %get-tuple-element.115), channel_id=1, source_target_pairs={{0,16},{2,18},{4,20},{6,22},{8,24},{10,26},{12,28},{14,30},{16,0},... | collective-permute-start | bytes 110600 | tf_op jit(solution)/shard_map/ppermute | solution.py:61
  49.6 4.9 %collective-permute-start.12 = (bf16[1,72,256]{2,1,0:T(8,128)(2,1)S(1)}, bf16[1,72,256]{2,1,0:T(8,128)(2,1)S(1)}, u32[]{:S(2)}, u32[]{:S(2)}) collective-permute-start(bf16[1,72,256]{2,1,0:T(8,128)(2,1)S(1)} %get-tuple-element.115), channel_id=1, source_target_pairs={{0,8},{2,10},{4,12},{6,14},{8,0},{10,2},{12,4},{14,6},{16,24},{18,... | collective-permute-start | bytes 110600 | tf_op jit(solution)/shard_map/ppermute | solution.py:61
  54.5 7.9 %collective-permute-start.15 = (bf16[4,72,256]{2,1,0:T(8,128)(2,1)S(1)}, bf16[4,72,256]{2,1,0:T(8,128)(2,1)S(1)}, u32[]{:S(2)}, u32[]{:S(2)}) collective-permute-start(bf16[4,72,256]{2,1,0:T(8,128)(2,1)S(1)} %maximum_bitcast_fusion.1.refs_0_), channel_id=1, source_target_pairs={{0,2},{2,0},{4,6},{6,4},{8,10},{10,8},{12,14},{14,12},{16,18},{18,... | collective-permute-start | bytes 442376 | tf_op jit(solution)/shard_map/ppermute | solution.py:61
  56.5 5.8 %collective-permute-start.16 = (bf16[4,72,256]{2,1,0:T(8,128)(2,1)S(1)}, bf16[4,72,256]{2,1,0:T(8,128)(2,1)S(1)}, u32[]{:S(2)}, u32[]{:S(2)}) collective-permute-start(bf16[4,72,256]{2,1,0:T(8,128)(2,1)S(1)} %maximum_bitcast_fusion.1.refs_0_), channel_id=1, source_target_pairs={{0,4},{2,6},{4,0},{6,2},{8,12},{10,14},{12,8},{14,10},{16,20},{18,... | collective-permute-start | bytes 442376 | tf_op jit(solution)/shard_map/ppermute | solution.py:61
  57.5 6.0 %collective-permute-start.17 = (bf16[4,72,256]{2,1,0:T(8,128)(2,1)S(1)}, bf16[4,72,256]{2,1,0:T(8,128)(2,1)S(1)}, u32[]{:S(2)}, u32[]{:S(2)}) collective-permute-start(bf16[4,72,256]{2,1,0:T(8,128)(2,1)S(1)} %maximum_bitcast_fusion.1.refs_0_), channel_id=1, source_target_pairs={{0,6},{2,4},{4,2},{6,0},{8,14},{10,12},{12,10},{14,8},{16,22},{18,... | collective-permute-start | bytes 442376 | tf_op jit(solution)/shard_map/ppermute | solution.py:61
  68.2 9.0 %collective-permute-start.20 = (bf16[4,32,1024]{2,1,0:T(8,128)(2,1)S(1)}, bf16[4,32,1024]{2,1,0:T(8,128)(2,1)S(1)}, u32[]{:S(2)}, u32[]{:S(2)}) collective-permute-start(bf16[4,32,1024]{2,1,0:T(8,128)(2,1)S(1)} %get-tuple-element.128), channel_id=1, source_target_pairs={{0,6},{2,4},{4,2},{6,0},{8,14},{10,12},{12,10},{14,8},{16,22},{18,... | collective-permute-start | bytes 786440 | tf_op jit(solution)/shard_map/ppermute | solution.py:61
  69.5 8.9 %collective-permute-start.19 = (bf16[4,32,1024]{2,1,0:T(8,128)(2,1)S(1)}, bf16[4,32,1024]{2,1,0:T(8,128)(2,1)S(1)}, u32[]{:S(2)}, u32[]{:S(2)}) collective-permute-start(bf16[4,32,1024]{2,1,0:T(8,128)(2,1)S(1)} %get-tuple-element.127), channel_id=1, source_target_pairs={{0,4},{2,6},{4,0},{6,2},{8,12},{10,14},{12,8},{14,10},{16,20},{18,... | collective-permute-start | bytes 786440 | tf_op jit(solution)/shard_map/ppermute | solution.py:61
  70.5 7.8 %collective-permute-start.18 = (bf16[4,32,1024]{2,1,0:T(8,128)(2,1)S(1)}, bf16[4,32,1024]{2,1,0:T(8,128)(2,1)S(1)}, u32[]{:S(2)}, u32[]{:S(2)}) collective-permute-start(bf16[4,32,1024]{2,1,0:T(8,128)(2,1)S(1)} %get-tuple-element.126), channel_id=1, source_target_pairs={{0,2},{2,0},{4,6},{6,4},{8,10},{10,8},{12,14},{14,12},{16,18},{18,... | collective-permute-start | bytes 786440 | tf_op jit(solution)/shard_map/ppermute | solution.py:61
  78.6 9.1 %collective-permute-start.23 = (bf16[1,32,1024]{2,1,0:T(8,128)(2,1)S(1)}, bf16[1,32,1024]{2,1,0:T(8,128)(2,1)S(1)}, u32[]{:S(2)}, u32[]{:S(2)}) collective-permute-start(bf16[1,32,1024]{2,1,0:T(8,128)(2,1)S(1)} %get-tuple-element.184), channel_id=1, source_target_pairs={{0,24},{2,26},{4,28},{6,30},{8,16},{10,18},{12,20},{14,22},{16,8},... | collective-permute-start | bytes 196616 | tf_op jit(solution)/shard_map/ppermute | solution.py:61
  80.6 7.1 %collective-permute-start.22 = (bf16[1,32,1024]{2,1,0:T(8,128)(2,1)S(1)}, bf16[1,32,1024]{2,1,0:T(8,128)(2,1)S(1)}, u32[]{:S(2)}, u32[]{:S(2)}) collective-permute-start(bf16[1,32,1024]{2,1,0:T(8,128)(2,1)S(1)} %get-tuple-element.185), channel_id=1, source_target_pairs={{0,16},{2,18},{4,20},{6,22},{8,24},{10,26},{12,28},{14,30},{16,0},... | collective-permute-start | bytes 196616 | tf_op jit(solution)/shard_map/ppermute | solution.py:61
  81.7 5.9 %collective-permute-start.21 = (bf16[1,32,1024]{2,1,0:T(8,128)(2,1)S(1)}, bf16[1,32,1024]{2,1,0:T(8,128)(2,1)S(1)}, u32[]{:S(2)}, u32[]{:S(2)}) collective-permute-start(bf16[1,32,1024]{2,1,0:T(8,128)(2,1)S(1)} %get-tuple-element.183), channel_id=1, source_target_pairs={{0,8},{2,10},{4,12},{6,14},{8,0},{10,2},{12,4},{14,6},{16,24},{18,... | collective-permute-start | bytes 196616 | tf_op jit(solution)/shard_map/ppermute | solution.py:61
  87.7 7.2 %collective-permute-start.26 = (bf16[4,16,1024]{2,1,0:T(8,128)(2,1)S(1)}, bf16[4,16,1024]{2,1,0:T(8,128)(2,1)S(1)}, u32[]{:S(2)}, u32[]{:S(2)}) collective-permute-start(bf16[4,16,1024]{2,1,0:T(8,128)(2,1)S(1)} %get-tuple-element.156), channel_id=1, source_target_pairs={{0,6},{2,4},{4,2},{6,0},{8,14},{10,12},{12,10},{14,8},{16,22},{18,... | collective-permute-start | bytes 393224 | tf_op jit(solution)/shard_map/ppermute | solution.py:61
  89.0 6.1 %collective-permute-start.25 = (bf16[4,16,1024]{2,1,0:T(8,128)(2,1)S(1)}, bf16[4,16,1024]{2,1,0:T(8,128)(2,1)S(1)}, u32[]{:S(2)}, u32[]{:S(2)}) collective-permute-start(bf16[4,16,1024]{2,1,0:T(8,128)(2,1)S(1)} %get-tuple-element.155), channel_id=1, source_target_pairs={{0,4},{2,6},{4,0},{6,2},{8,12},{10,14},{12,8},{14,10},{16,20},{18,... | collective-permute-start | bytes 393224 | tf_op jit(solution)/shard_map/ppermute | solution.py:61
  90.0 5.0 %collective-permute-start.24 = (bf16[4,16,1024]{2,1,0:T(8,128)(2,1)S(1)}, bf16[4,16,1024]{2,1,0:T(8,128)(2,1)S(1)}, u32[]{:S(2)}, u32[]{:S(2)}) collective-permute-start(bf16[4,16,1024]{2,1,0:T(8,128)(2,1)S(1)} %get-tuple-element.154), channel_id=1, source_target_pairs={{0,2},{2,0},{4,6},{6,4},{8,10},{10,8},{12,14},{14,12},{16,18},{18,... | collective-permute-start | bytes 393224 | tf_op jit(solution)/shard_map/ppermute | solution.py:61
  95.1 11.7 %collective-permute-start.30 = (bf16[1024,512]{1,0:T(8,128)(2,1)S(1)}, bf16[1024,512]{1,0:T(8,128)(2,1)S(1)}, u32[]{:S(2)}, u32[]{:S(2)}) collective-permute-start(bf16[1024,512]{1,0:T(8,128)(2,1)S(1)} %part.1), channel_id=1, source_target_pairs={{0,1},{1,0},{2,3},{3,2},{4,5},{5,4},{6,7},{7,6},{8,9},{9,8},{10,11... | collective-permute-start | bytes 3145736 | tf_op jit(solution)/shard_map/ppermute | solution.py:755
  95.2 6.7 %collective-permute-start.27 = (bf16[48,1024]{1,0:T(8,128)(2,1)S(1)}, bf16[48,1024]{1,0:T(8,128)(2,1)S(1)}, u32[]{:S(2)}, u32[]{:S(2)}) collective-permute-start(bf16[48,1024]{1,0:T(8,128)(2,1)S(1)} %get-tuple-element.193), channel_id=1, source_target_pairs={{0,8},{2,10},{4,12},{6,14},{8,0},{10,2},{12,4},{14,6},{16,24},{18,... | collective-permute-start | bytes 294920 | tf_op jit(solution)/shard_map/ppermute | solution.py:61
  96.0 10.7 %collective-permute-start.28 = (bf16[48,1024]{1,0:T(8,128)(2,1)S(1)}, bf16[48,1024]{1,0:T(8,128)(2,1)S(1)}, u32[]{:S(2)}, u32[]{:S(2)}) collective-permute-start(bf16[48,1024]{1,0:T(8,128)(2,1)S(1)} %get-tuple-element.192), channel_id=1, source_target_pairs={{0,16},{2,18},{4,20},{6,22},{8,24},{10,26},{12,28},{14,30},{16,0},... | collective-permute-start | bytes 294920 | tf_op jit(solution)/shard_map/ppermute | solution.py:61
  97.8 8.9 %collective-permute-start.29 = (bf16[48,1024]{1,0:T(8,128)(2,1)S(1)}, bf16[48,1024]{1,0:T(8,128)(2,1)S(1)}, u32[]{:S(2)}, u32[]{:S(2)}) collective-permute-start(bf16[48,1024]{1,0:T(8,128)(2,1)S(1)} %get-tuple-element.191), channel_id=1, source_target_pairs={{0,24},{2,26},{4,28},{6,30},{8,16},{10,18},{12,20},{14,22},{16,8},... | collective-permute-start | bytes 294920 | tf_op jit(solution)/shard_map/ppermute | solution.py:61
  111.4 9.3 %collective-permute-start.31 = (bf16[4,32,1024]{2,1,0:T(8,128)(2,1)S(1)}, bf16[4,32,1024]{2,1,0:T(8,128)(2,1)S(1)}, u32[]{:S(2)}, u32[]{:S(2)}) collective-permute-start(bf16[4,32,1024]{2,1,0:T(8,128)(2,1)S(1)} %maximum_bitcast_fusion.refs_0_), channel_id=1, source_target_pairs={{0,2},{2,0},{4,6},{6,4},{8,10},{10,8},{12,14},{14,12},{16,18},{18,... | collective-permute-start | bytes 786440 | tf_op jit(solution)/shard_map/ppermute | solution.py:61
  112.6 11.8 %collective-permute-start.32 = (bf16[4,32,1024]{2,1,0:T(8,128)(2,1)S(1)}, bf16[4,32,1024]{2,1,0:T(8,128)(2,1)S(1)}, u32[]{:S(2)}, u32[]{:S(2)}) collective-permute-start(bf16[4,32,1024]{2,1,0:T(8,128)(2,1)S(1)} %maximum_bitcast_fusion.refs_0_), channel_id=1, source_target_pairs={{0,4},{2,6},{4,0},{6,2},{8,12},{10,14},{12,8},{14,10},{16,20},{18,... | collective-permute-start | bytes 786440 | tf_op jit(solution)/shard_map/ppermute | solution.py:61
  113.3 11.0 %collective-permute-start.33 = (bf16[4,32,1024]{2,1,0:T(8,128)(2,1)S(1)}, bf16[4,32,1024]{2,1,0:T(8,128)(2,1)S(1)}, u32[]{:S(2)}, u32[]{:S(2)}) collective-permute-start(bf16[4,32,1024]{2,1,0:T(8,128)(2,1)S(1)} %maximum_bitcast_fusion.refs_0_), channel_id=1, source_target_pairs={{0,6},{2,4},{4,2},{6,0},{8,14},{10,12},{12,10},{14,8},{16,22},{18,... | collective-permute-start | bytes 786440 | tf_op jit(solution)/shard_map/ppermute | solution.py:61
  (7 other events, 57.1 us)

commit v7 on v5

--- a/solution.py
+++ b/solution.py
@@ -765,17 +765,6 @@
     )
 
     arrived = lax.ppermute(there, "head", [(0, 1), (1, 0)])
-    mixed = call(
-        mixed_kernel,
-        (4,),
-        [mine_arr],
-        [attn, out_weight, arrived],
-        [row_block, pl.BlockSpec((columns, half), lambda j, mine: (0, mine[0])), half_block],
-        shape_of((rows, half), BF16),
-        half_block,
-        flops=1 << 30,
-        name="mixed",
-    )
     if len(later) == 1 and weight_own.shape[1] == land_sum.shape[2]:
         (shift, count), tall = later[0], weight_own.shape[0]
         got = [
@@ -789,7 +778,18 @@
         land_sum = land_sum.reshape((-1, following) + land_sum.shape[1:])
         land_own = scatter_pieces([land_sum[:, m] for m in range(following)], n, later)[0]
     land_own = land_own * (1.0 / seg_len)
-    weights, key_b = lax.optimization_barrier((weights, key_b))
+    weights, key_b, arrived = lax.optimization_barrier((weights, key_b, arrived))
+    mixed = call(
+        mixed_kernel,
+        (4,),
+        [mine_arr],
+        [attn, out_weight, arrived],
+        [row_block, pl.BlockSpec((columns, half), lambda j, mine: (0, mine[0])), half_block],
+        shape_of((rows, half), BF16),
+        half_block,
+        flops=1 << 30,
+        name="mixed",
+    )
     weights = gather_rest(weights, n)
     weights, mixed = lax.optimization_barrier((weights, mixed))
     weight_grad = call(

time: 122 us -> 122 us (level)
  no operation moved by 1% of the time
where the time goes in v7:
time: 122 us
  Pallas kernels  47.3 us (39%)
  starting transfers between devices  44.9 us (37%)
  waiting for transfers between devices  22.4 us (18%)
  other arithmetic  2.94 us (2%)
  matrix products  2.87 us (2%)
    pallas_call x14, Pallas kernels, call(): pl.pallas_call(kernel, grid_spec=pltpu.PrefetchScalarGridSpec(num_scalar_...  47.3 us
    ppermute x33, starting transfers between devices, exchange(): return lax.ppermute(block, 'seq', [(i, i ^ mask) for i in range(n)])  44.9 us
    ppermute x33, waiting for transfers between devices, exchange(): return lax.ppermute(block, 'seq', [(i, i ^ mask) for i in range(n)])  22.4 us
    dot_general x1, matrix products, dot(): lax.dot_general(left, right, (dims, ((), ())), preferred_element_type=F32)  2.87 us
  transfers between devices with their start and end apart: 34, of which 15 were waited for; matrix products, arithmetic and copies ran while one was open for 4% of the time, Pallas kernels for 23%

profile of v7, /device:TPU:0, one launch (start us, length us, event | category | flops | bytes accessed | tf_op | source)
XLA Modules:
  0.0 121.7 jit_solution(11793472627580766554)
XLA Ops:
  0.8 1.7 %means.1 = bf16[16,1024]{1,0:T(8,128)(2,1)S(1)} custom-call(bf16[1024,512]{1,0:T(8,128)(2,1)} %q_ref.5, bf16[1024,512]{1,0:T(8,128)(2,1)} %k_ref.4), custom_call_target="tpu_custom_call" | custom-call | bytes 4194304 | tf_op jit(solution)/shard_map/means/pallas_call | solution.py:489
  2.5 5.1 %collective-permute-start.2 = (bf16[1,16,1024]{2,1,0:T(8,128)(2,1)S(1)}, bf16[1,16,1024]{2,1,0:T(8,128)(2,1)S(1)}, u32[]{:S(2)}, u32[]{:S(2)}) collective-permute-start(bf16[1,16,1024]{2,1,0:T(8,128)(2,1)S(1)} %bitcast.63), channel_id=1, source_target_pairs={{0,24},{2,26},{4,28},{6,30},{8,16},{10,18},{12,20},{14,22},{16,8},... | collective-permute-start | bytes 98312 | tf_op jit(solution)/shard_map/ppermute | solution.py:61
  9.5 2.9 %collective-permute-done.1 = bf16[1,16,1024]{2,1,0:T(8,128)(2,1)S(1)} collective-permute-done((bf16[1,16,1024]{2,1,0:T(8,128)(2,1)S(1)}, bf16[1,16,1024]{2,1,0:T(8,128)(2,1)S(1)}, u32[]{:S(2)}, u32[]{:S(2)}) %collective-permute-start.1) | collective-permute-done | bytes 32800 | tf_op jit(solution)/shard_map/ppermute | solution.py:61
  12.5 1.6 %collective-permute-start.3 = (bf16[4,16,1024]{2,1,0:T(8,128)(2,1)S(1)}, bf16[4,16,1024]{2,1,0:T(8,128)(2,1)S(1)}, u32[]{:S(2)}, u32[]{:S(2)}) collective-permute-start(bf16[4,16,1024]{2,1,0:T(8,128)(2,1)S(1)} %maximum_bitcast_fusion.2.refs_0_), channel_id=1, source_target_pairs={{0,2},{2,0},{4,6},{6,4},{8,10},{10,8},{12,14},{14,12},{16,18},{18,... | collective-permute-start | bytes 393224 | tf_op jit(solution)/shard_map/ppermute | solution.py:61
  14.0 1.5 %collective-permute-start.4 = (bf16[4,16,1024]{2,1,0:T(8,128)(2,1)S(1)}, bf16[4,16,1024]{2,1,0:T(8,128)(2,1)S(1)}, u32[]{:S(2)}, u32[]{:S(2)}) collective-permute-start(bf16[4,16,1024]{2,1,0:T(8,128)(2,1)S(1)} %maximum_bitcast_fusion.2.refs_0_), channel_id=1, source_target_pairs={{0,4},{2,6},{4,0},{6,2},{8,12},{10,14},{12,8},{14,10},{16,20},{18,... | collective-permute-start | bytes 393224 | tf_op jit(solution)/shard_map/ppermute | solution.py:61
  16.0 2.9 %convolution_convert_fusion.g_ref = bf16[1024,512]{1,0:T(8,128)(2,1)S(1)} fusion(bf16[1024,1024]{1,0:T(8,128)(2,1)} %cot_ref.1, bf16[512,1024]{1,0:T(8,128)(2,1)S(1)} %copy-done), kind=kOutput, calls=%fused_computation.4 | convolution fusion | flops 1074266112 | bytes 4194304 | tf_op jit(solution)/shard_map/dot_general | solution.py:23
  20.0 1.5 %collective-permute-done.5.refs_3_ = bf16[4,16,1024]{2,1,0:T(8,128)(2,1)S(1)} collective-permute-done((bf16[4,16,1024]{2,1,0:T(8,128)(2,1)S(1)}, bf16[4,16,1024]{2,1,0:T(8,128)(2,1)S(1)}, u32[]{:S(2)}, u32[]{:S(2)}) %collective-permute-start.5) | collective-permute-done | bytes 131104 | tf_op jit(solution)/shard_map/ppermute | solution.py:61
  21.4 10.0 %forward.1 = (bf16[1024,2048]{1,0:T(8,128)(2,1)S(1)}, bf16[1024,2048]{1,0:T(8,128)(2,1)S(1)}, f32[4,8,256]{2,1,0:T(8,128)S(1)}, bf16[256,1024]{1,0:T(8,128)(2,1)...) custom-call(s32[2]{0:T(128)S(1)} %pad_add_fusion.me_ref, ...), custom_call_target="tpu_custom_call" | custom-call | flops 8589934592 | bytes 4194304 | tf_op jit(solution)/shard_map/forward/pallas_call | solution.py:489
  32.6 2.4 %collective-permute-start.8 = (bf16[4,72,256]{2,1,0:T(8,128)(2,1)S(1)}, bf16[4,72,256]{2,1,0:T(8,128)(2,1)S(1)}, u32[]{:S(2)}, u32[]{:S(2)}) collective-permute-start(bf16[4,72,256]{2,1,0:T(8,128)(2,1)S(1)} %get-tuple-element.102), channel_id=1, source_target_pairs={{0,6},{2,4},{4,2},{6,0},{8,14},{10,12},{12,10},{14,8},{16,22},{18,... | collective-permute-start | bytes 442376 | tf_op jit(solution)/shard_map/ppermute | solution.py:61
  35.0 3.6 %newton.1 = (f32[9,256,256]{2,1,0:T(8,128)S(1)}, f32[1,256,256]{2,1,0:T(8,128)S(1)}) custom-call(s32[3]{0:T(128)S(1)} %pad_add_fusion.1.own_ref, bf16[256,1024]{1,0:T(8,128)(2,1)S(1)} %get-tuple-element.103.lq_ref.lk_ref, bf16[256,1024]{1,0:T(8,128)(2,1)S(1)} %get-tuple-element.103.lq_ref.lk_ref), custom_call_target="tpu_custom_call" | custom-call | flops 4294967296 | bytes 4194304 | tf_op jit(solution)/shard_map/newton/pallas_call | solution.py:489
  39.1 2.2 %collective-permute-start.10 = (bf16[1,72,256]{2,1,0:T(8,128)(2,1)S(1)}, bf16[1,72,256]{2,1,0:T(8,128)(2,1)S(1)}, u32[]{:S(2)}, u32[]{:S(2)}) collective-permute-start(bf16[1,72,256]{2,1,0:T(8,128)(2,1)S(1)} %get-tuple-element.111), channel_id=1, source_target_pairs={{0,16},{2,18},{4,20},{6,22},{8,24},{10,26},{12,28},{14,30},{16,0},... | collective-permute-start | bytes 110600 | tf_op jit(solution)/shard_map/ppermute | solution.py:61
  41.3 2.1 %collective-permute-start.11 = (bf16[1,72,256]{2,1,0:T(8,128)(2,1)S(1)}, bf16[1,72,256]{2,1,0:T(8,128)(2,1)S(1)}, u32[]{:S(2)}, u32[]{:S(2)}) collective-permute-start(bf16[1,72,256]{2,1,0:T(8,128)(2,1)S(1)} %get-tuple-element.112), channel_id=1, source_target_pairs={{0,24},{2,26},{4,28},{6,30},{8,16},{10,18},{12,20},{14,22},{16,8},... | collective-permute-start | bytes 110600 | tf_op jit(solution)/shard_map/ppermute | solution.py:61
  44.0 3.1 %collective-permute-done.11.refs_3_ = bf16[1,72,256]{2,1,0:T(8,128)(2,1)S(1)} collective-permute-done((bf16[1,72,256]{2,1,0:T(8,128)(2,1)S(1)}, bf16[1,72,256]{2,1,0:T(8,128)(2,1)S(1)}, u32[]{:S(2)}, u32[]{:S(2)}) %collective-permute-start.11) | collective-permute-done | bytes 36896 | tf_op jit(solution)/shard_map/ppermute | solution.py:61
  47.4 2.2 %collective-permute-start.14 = (bf16[1,72,256]{2,1,0:T(8,128)(2,1)S(1)}, bf16[1,72,256]{2,1,0:T(8,128)(2,1)S(1)}, u32[]{:S(2)}, u32[]{:S(2)}) collective-permute-start(bf16[1,72,256]{2,1,0:T(8,128)(2,1)S(1)} %get-tuple-element.114), channel_id=1, source_target_pairs={{0,24},{2,26},{4,28},{6,30},{8,16},{10,18},{12,20},{14,22},{16,8},... | collective-permute-start | bytes 110600 | tf_op jit(solution)/shard_map/ppermute | solution.py:61
  49.6 2.3 %collective-permute-start.12 = (bf16[1,72,256]{2,1,0:T(8,128)(2,1)S(1)}, bf16[1,72,256]{2,1,0:T(8,128)(2,1)S(1)}, u32[]{:S(2)}, u32[]{:S(2)}) collective-permute-start(bf16[1,72,256]{2,1,0:T(8,128)(2,1)S(1)} %get-tuple-element.114), channel_id=1, source_target_pairs={{0,8},{2,10},{4,12},{6,14},{8,0},{10,2},{12,4},{14,6},{16,24},{18,... | collective-permute-start | bytes 110600 | tf_op jit(solution)/shard_map/ppermute | solution.py:61
  51.8 1.4 %collective-permute-done.14 = bf16[1,72,256]{2,1,0:T(8,128)(2,1)S(1)} collective-permute-done((bf16[1,72,256]{2,1,0:T(8,128)(2,1)S(1)}, bf16[1,72,256]{2,1,0:T(8,128)(2,1)S(1)}, u32[]{:S(2)}, u32[]{:S(2)}) %collective-permute-start.14) | collective-permute-done | bytes 36896 | tf_op jit(solution)/shard_map/ppermute | solution.py:61
  54.5 2.1 %collective-permute-start.15 = (bf16[4,72,256]{2,1,0:T(8,128)(2,1)S(1)}, bf16[4,72,256]{2,1,0:T(8,128)(2,1)S(1)}, u32[]{:S(2)}, u32[]{:S(2)}) collective-permute-start(bf16[4,72,256]{2,1,0:T(8,128)(2,1)S(1)} %maximum_bitcast_fusion.1.refs_0_), channel_id=1, source_target_pairs={{0,2},{2,0},{4,6},{6,4},{8,10},{10,8},{12,14},{14,12},{16,18},{18,... | collective-permute-start | bytes 442376 | tf_op jit(solution)/shard_map/ppermute | solution.py:61
  58.1 4.3 %newton_grad.1 = (f32[256,128]{1,0:T(8,128)S(1)}, f32[256,128]{1,0:T(8,128)S(1)}) custom-call(s32[3]{0:T(128)S(1)} %pad_add_fusion.1.own_ref, f32[9,256,256]{2,1,0:T(8,128)S(1)} %get-tuple-element.115.saved_ref, f32[32,256]{1,0:T(8,128)S(1)} %get-tuple-element.116.values_ref, f32[32,256]{1,0:T(8,128)S(1)} %get-tuple-element.117.grads_ref, ...), custom_call_target="tpu_custom_call" | custom-call | flops 8589934592 | bytes 4194304 | tf_op jit(solution)/shard_map/newton_grad/pallas_call | solution.py:489
  63.5 4.7 %attend.1 = (bf16[1024,512]{1,0:T(8,128)(2,1)S(1)}, bf16[512,256]{1,0:T(8,128)(2,1)S(1)}, bf16[512,256]{1,0:T(8,128)(2,1)S(1)}, f32[8,256]{1,0:T(8,128)S(1)}, bf...) custom-call(s32[2]{0:T(128)S(1)} %pad_add_fusion.me_ref, ...), custom_call_target="tpu_custom_call" | custom-call | flops 4294967296 | bytes 4194304 | tf_op jit(solution)/shard_map/attend/pallas_call | solution.py:489
  71.8 5.4 %query_land.1 = (bf16[256,512]{1,0:T(8,128)(2,1)S(1)}, bf16[1024,2048]{1,0:T(8,128)(2,1)S(1)}) custom-call(s32[3]{0:T(128)S(1)} %pad_add_fusion.1.own_ref, bf16[1024,512]{1,0:T(8,128)(2,1)S(1)} %copy-done.1, bf16[1024,512]{1,0:T(8,128)(2,1)S(1)} %convolution_convert_fusion.g_ref, bf16[1024,2048]{1,0:T(8,128)(2,1)S(1)} %get-tuple-element.97.fb_ref, ...), custom_call_target="tpu_custom_call" | custom-call | flops 4294967296 | bytes 4194304 | tf_op jit(solution)/shard_map/query_land/pallas_call | solution.py:489
  78.6 2.0 %collective-permute-start.23 = (bf16[1,32,1024]{2,1,0:T(8,128)(2,1)S(1)}, bf16[1,32,1024]{2,1,0:T(8,128)(2,1)S(1)}, u32[]{:S(2)}, u32[]{:S(2)}) collective-permute-start(bf16[1,32,1024]{2,1,0:T(8,128)(2,1)S(1)} %get-tuple-element.182), channel_id=1, source_target_pairs={{0,24},{2,26},{4,28},{6,30},{8,16},{10,18},{12,20},{14,22},{16,8},... | collective-permute-start | bytes 196616 | tf_op jit(solution)/shard_map/ppermute | solution.py:61
  81.7 1.3 %collective-permute-start.21 = (bf16[1,32,1024]{2,1,0:T(8,128)(2,1)S(1)}, bf16[1,32,1024]{2,1,0:T(8,128)(2,1)S(1)}, u32[]{:S(2)}, u32[]{:S(2)}) collective-permute-start(bf16[1,32,1024]{2,1,0:T(8,128)(2,1)S(1)} %get-tuple-element.181), channel_id=1, source_target_pairs={{0,8},{2,10},{4,12},{6,14},{8,0},{10,2},{12,4},{14,6},{16,24},{18,... | collective-permute-start | bytes 196616 | tf_op jit(solution)/shard_map/ppermute | solution.py:61
  83.0 4.6 %key_land.1 = (bf16[1024,2048]{1,0:T(8,128)(2,1)S(1)}, bf16[4,16,1024]{2,1,0:T(8,128)(2,1)S(1)}, bf16[4,16,1024]{2,1,0:T(8,128)(2,1)S(1)}, bf16[4,16,1024]{2,1,0:T(8,128)(2,1)S(1)}, bf16[4,16,1024]{2,1,0:T(8,128)(2,1)S(1)}) custom-call(s32[3]{0:T(128)S(1)} %pad_add_fusion.1.own_ref, bf16[1024,512]{1,0:T(8,128)(2,1)S(1)} %copy-done.2, ...), custom_call_target="tpu_custom_call" | custom-call | flops 4294967296 | bytes 4194304 | tf_op jit(solution)/shard_map/key_land/pallas_call | solution.py:489
  91.3 2.3 %query_grad.1 = bf16[1024,512]{1,0:T(8,128)(2,1)S(1)} custom-call(bf16[1024,2048]{1,0:T(8,128)(2,1)S(1)} %get-tuple-element.157.ds_ref, bf16[256,1024]{1,0:T(8,128)(2,1)S(1)} %get-tuple-element.103.lq_ref.lk_ref), custom_call_target="tpu_custom_call" | custom-call | flops 2147483648 | bytes 4194304 | tf_op jit(solution)/shard_map/query_grad/pallas_call | solution.py:489
  93.6 1.3 %part.1 = bf16[1024,512]{1,0:T(8,128)(2,1)S(1)} custom-call(s32[1]{0:T(128)} %bitcast.1._, bf16[1024,512]{1,0:T(8,128)(2,1)S(1)} %get-tuple-element.159.attn_ref, bf16[512,1024]{1,0:T(8,128)(2,1)S(1)} %copy-done), custom_call_target="tpu_custom_call" | custom-call | flops 1073741824 | bytes 4194304 | tf_op jit(solution)/shard_map/part/pallas_call | solution.py:489
  96.0 1.8 %collective-permute-start.28 = (bf16[48,1024]{1,0:T(8,128)(2,1)S(1)}, bf16[48,1024]{1,0:T(8,128)(2,1)S(1)}, u32[]{:S(2)}, u32[]{:S(2)}) collective-permute-start(bf16[48,1024]{1,0:T(8,128)(2,1)S(1)} %get-tuple-element.190), channel_id=1, source_target_pairs={{0,16},{2,18},{4,20},{6,22},{8,24},{10,26},{12,28},{14,30},{16,0},... | collective-permute-start | bytes 294920 | tf_op jit(solution)/shard_map/ppermute | solution.py:61
  97.8 1.9 %collective-permute-start.29 = (bf16[48,1024]{1,0:T(8,128)(2,1)S(1)}, bf16[48,1024]{1,0:T(8,128)(2,1)S(1)}, u32[]{:S(2)}, u32[]{:S(2)}) collective-permute-start(bf16[48,1024]{1,0:T(8,128)(2,1)S(1)} %get-tuple-element.189), channel_id=1, source_target_pairs={{0,24},{2,26},{4,28},{6,30},{8,16},{10,18},{12,20},{14,22},{16,8},... | collective-permute-start | bytes 294920 | tf_op jit(solution)/shard_map/ppermute | solution.py:61
  99.6 4.5 %key_grad.1 = (bf16[1024,512]{1,0:T(8,128)(2,1)S(1)}, bf16[1024,512]{1,0:T(8,128)(2,1)}) custom-call(bf16[1024,2048]{1,0:T(8,128)(2,1)S(1)} %get-tuple-element.165.ds_ref, bf16[1024,2048]{1,0:T(8,128)(2,1)S(1)} %get-tuple-element.136.pb_ref, bf16[256,1024]{1,0:T(8,128)(2,1)S(1)} %get-tuple-element.103.lq_ref.lk_ref, ...), custom_call_target="tpu_custom_call" | custom-call | flops 4294967296 | bytes 4194304 | tf_op jit(solution)/shard_map/key_grad/pallas_call | solution.py:489
  106.6 1.4 %collective-permute-start.33 = (bf16[4,32,1024]{2,1,0:T(8,128)(2,1)S(1)}, bf16[4,32,1024]{2,1,0:T(8,128)(2,1)S(1)}, u32[]{:S(2)}, u32[]{:S(2)}) collective-permute-start(bf16[4,32,1024]{2,1,0:T(8,128)(2,1)S(1)} %maximum_bitcast_fusion.refs_0_), channel_id=1, source_target_pairs={{0,6},{2,4},{4,2},{6,0},{8,14},{10,12},{12,10},{14,8},{16,22},{18,... | collective-permute-start | bytes 786440 | tf_op jit(solution)/shard_map/ppermute | solution.py:61
  110.3 2.4 %mixed.1 = bf16[1024,512]{1,0:T(8,128)(2,1)} custom-call(s32[1]{0:T(128)} %bitcast.1._, bf16[1024,512]{1,0:T(8,128)(2,1)S(1)} %get-tuple-element.159.attn_ref, bf16[512,1024]{1,0:T(8,128)(2,1)S(1)} %copy-done, bf16[1024,512]{1,0:T(8,128)(2,1)S(1)} %collective-permute-done.30.other_ref), custom_call_target="tpu_custom_call" | custom-call | flops 1073741824 | bytes 4194304 | tf_op jit(solution)/shard_map/mixed/pallas_call | solution.py:489
  113.6 6.0 %collective-permute-done.32.refs_2_ = bf16[4,32,1024]{2,1,0:T(8,128)(2,1)S(1)} collective-permute-done((bf16[4,32,1024]{2,1,0:T(8,128)(2,1)S(1)}, bf16[4,32,1024]{2,1,0:T(8,128)(2,1)S(1)}, u32[]{:S(2)}, u32[]{:S(2)}) %collective-permute-start.32) | collective-permute-done | bytes 262176 | tf_op jit(solution)/shard_map/ppermute | solution.py:61
  119.5 2.0 %unpack.1 = f32[512,1024]{1,0:T(8,128)} custom-call(s32[2]{0:T(128)S(1)} %pad_add_fusion.me_ref, bf16[4,32,1024]{2,1,0:T(8,128)(2,1)S(1)} %maximum_bitcast_fusion.refs_0_, bf16[4,32,1024]{2,1,0:T(8,128)(2,1)S(1)} %collective-permute-done.31.refs_1_, bf16[4,32,1024]{2,1,0:T(8,128)(2,1)S(1)} %collective-permute-done.32.refs_2_, ...), custom_call_target="tpu_custom_call" | custom-call | bytes 4194304 | tf_op jit(solution)/shard_map/unpack/pallas_call | solution.py:489
  (79 shorter events, 26.2 us)
Async XLA Ops:
  2.5 7.0 %collective-permute-start.2 = (bf16[1,16,1024]{2,1,0:T(8,128)(2,1)S(1)}, bf16[1,16,1024]{2,1,0:T(8,128)(2,1)S(1)}, u32[]{:S(2)}, u32[]{:S(2)}) collective-permute-start(bf16[1,16,1024]{2,1,0:T(8,128)(2,1)S(1)} %bitcast.63), channel_id=1, source_target_pairs={{0,24},{2,26},{4,28},{6,30},{8,16},{10,18},{12,20},{14,22},{16,8},... | collective-permute-start | bytes 98312 | tf_op jit(solution)/shard_map/ppermute | solution.py:61
  7.6 4.8 %collective-permute-start.1 = (bf16[1,16,1024]{2,1,0:T(8,128)(2,1)S(1)}, bf16[1,16,1024]{2,1,0:T(8,128)(2,1)S(1)}, u32[]{:S(2)}, u32[]{:S(2)}) collective-permute-start(bf16[1,16,1024]{2,1,0:T(8,128)(2,1)S(1)} %bitcast.64), channel_id=1, source_target_pairs={{0,16},{2,18},{4,20},{6,22},{8,24},{10,26},{12,28},{14,30},{16,0},... | collective-permute-start | bytes 98312 | tf_op jit(solution)/shard_map/ppermute | solution.py:61
  7.6 4.8 %collective-permute-start = (bf16[1,16,1024]{2,1,0:T(8,128)(2,1)S(1)}, bf16[1,16,1024]{2,1,0:T(8,128)(2,1)S(1)}, u32[]{:S(2)}, u32[]{:S(2)}) collective-permute-start(bf16[1,16,1024]{2,1,0:T(8,128)(2,1)S(1)} %bitcast.65), channel_id=1, source_target_pairs={{0,8},{2,10},{4,12},{6,14},{8,0},{10,2},{12,4},{14,6},{16,24},{18,... | collective-permute-start | bytes 98312 | tf_op jit(solution)/shard_map/ppermute | solution.py:61
  12.5 6.4 %collective-permute-start.3 = (bf16[4,16,1024]{2,1,0:T(8,128)(2,1)S(1)}, bf16[4,16,1024]{2,1,0:T(8,128)(2,1)S(1)}, u32[]{:S(2)}, u32[]{:S(2)}) collective-permute-start(bf16[4,16,1024]{2,1,0:T(8,128)(2,1)S(1)} %maximum_bitcast_fusion.2.refs_0_), channel_id=1, source_target_pairs={{0,2},{2,0},{4,6},{6,4},{8,10},{10,8},{12,14},{14,12},{16,18},{18,... | collective-permute-start | bytes 393224 | tf_op jit(solution)/shard_map/ppermute | solution.py:61
  14.0 5.9 %collective-permute-start.4 = (bf16[4,16,1024]{2,1,0:T(8,128)(2,1)S(1)}, bf16[4,16,1024]{2,1,0:T(8,128)(2,1)S(1)}, u32[]{:S(2)}, u32[]{:S(2)}) collective-permute-start(bf16[4,16,1024]{2,1,0:T(8,128)(2,1)S(1)} %maximum_bitcast_fusion.2.refs_0_), channel_id=1, source_target_pairs={{0,4},{2,6},{4,0},{6,2},{8,12},{10,14},{12,8},{14,10},{16,20},{18,... | collective-permute-start | bytes 393224 | tf_op jit(solution)/shard_map/ppermute | solution.py:61
  15.6 5.9 %collective-permute-start.5 = (bf16[4,16,1024]{2,1,0:T(8,128)(2,1)S(1)}, bf16[4,16,1024]{2,1,0:T(8,128)(2,1)S(1)}, u32[]{:S(2)}, u32[]{:S(2)}) collective-permute-start(bf16[4,16,1024]{2,1,0:T(8,128)(2,1)S(1)} %maximum_bitcast_fusion.2.refs_0_), channel_id=1, source_target_pairs={{0,6},{2,4},{4,2},{6,0},{8,14},{10,12},{12,10},{14,8},{16,22},{18,... | collective-permute-start | bytes 393224 | tf_op jit(solution)/shard_map/ppermute | solution.py:61
  31.5 7.2 %collective-permute-start.6 = (bf16[4,72,256]{2,1,0:T(8,128)(2,1)S(1)}, bf16[4,72,256]{2,1,0:T(8,128)(2,1)S(1)}, u32[]{:S(2)}, u32[]{:S(2)}) collective-permute-start(bf16[4,72,256]{2,1,0:T(8,128)(2,1)S(1)} %get-tuple-element.100), channel_id=1, source_target_pairs={{0,2},{2,0},{4,6},{6,4},{8,10},{10,8},{12,14},{14,12},{16,18},{18,... | collective-permute-start | bytes 442376 | tf_op jit(solution)/shard_map/ppermute | solution.py:61
  32.1 6.7 %collective-permute-start.7 = (bf16[4,72,256]{2,1,0:T(8,128)(2,1)S(1)}, bf16[4,72,256]{2,1,0:T(8,128)(2,1)S(1)}, u32[]{:S(2)}, u32[]{:S(2)}) collective-permute-start(bf16[4,72,256]{2,1,0:T(8,128)(2,1)S(1)} %get-tuple-element.101), channel_id=1, source_target_pairs={{0,4},{2,6},{4,0},{6,2},{8,12},{10,14},{12,8},{14,10},{16,20},{18,... | collective-permute-start | bytes 442376 | tf_op jit(solution)/shard_map/ppermute | solution.py:61
  32.6 6.2 %collective-permute-start.8 = (bf16[4,72,256]{2,1,0:T(8,128)(2,1)S(1)}, bf16[4,72,256]{2,1,0:T(8,128)(2,1)S(1)}, u32[]{:S(2)}, u32[]{:S(2)}) collective-permute-start(bf16[4,72,256]{2,1,0:T(8,128)(2,1)S(1)} %get-tuple-element.102), channel_id=1, source_target_pairs={{0,6},{2,4},{4,2},{6,0},{8,14},{10,12},{12,10},{14,8},{16,22},{18,... | collective-permute-start | bytes 442376 | tf_op jit(solution)/shard_map/ppermute | solution.py:61
  39.1 4.9 %collective-permute-start.10 = (bf16[1,72,256]{2,1,0:T(8,128)(2,1)S(1)}, bf16[1,72,256]{2,1,0:T(8,128)(2,1)S(1)}, u32[]{:S(2)}, u32[]{:S(2)}) collective-permute-start(bf16[1,72,256]{2,1,0:T(8,128)(2,1)S(1)} %get-tuple-element.111), channel_id=1, source_target_pairs={{0,16},{2,18},{4,20},{6,22},{8,24},{10,26},{12,28},{14,30},{16,0},... | collective-permute-start | bytes 110600 | tf_op jit(solution)/shard_map/ppermute | solution.py:61
  41.3 5.8 %collective-permute-start.11 = (bf16[1,72,256]{2,1,0:T(8,128)(2,1)S(1)}, bf16[1,72,256]{2,1,0:T(8,128)(2,1)S(1)}, u32[]{:S(2)}, u32[]{:S(2)}) collective-permute-start(bf16[1,72,256]{2,1,0:T(8,128)(2,1)S(1)} %get-tuple-element.112), channel_id=1, source_target_pairs={{0,24},{2,26},{4,28},{6,30},{8,16},{10,18},{12,20},{14,22},{16,8},... | collective-permute-start | bytes 110600 | tf_op jit(solution)/shard_map/ppermute | solution.py:61
  47.4 5.8 %collective-permute-start.14 = (bf16[1,72,256]{2,1,0:T(8,128)(2,1)S(1)}, bf16[1,72,256]{2,1,0:T(8,128)(2,1)S(1)}, u32[]{:S(2)}, u32[]{:S(2)}) collective-permute-start(bf16[1,72,256]{2,1,0:T(8,128)(2,1)S(1)} %get-tuple-element.114), channel_id=1, source_target_pairs={{0,24},{2,26},{4,28},{6,30},{8,16},{10,18},{12,20},{14,22},{16,8},... | collective-permute-start | bytes 110600 | tf_op jit(solution)/shard_map/ppermute | solution.py:61
  49.6 4.9 %collective-permute-start.13 = (bf16[1,72,256]{2,1,0:T(8,128)(2,1)S(1)}, bf16[1,72,256]{2,1,0:T(8,128)(2,1)S(1)}, u32[]{:S(2)}, u32[]{:S(2)}) collective-permute-start(bf16[1,72,256]{2,1,0:T(8,128)(2,1)S(1)} %get-tuple-element.114), channel_id=1, source_target_pairs={{0,16},{2,18},{4,20},{6,22},{8,24},{10,26},{12,28},{14,30},{16,0},... | collective-permute-start | bytes 110600 | tf_op jit(solution)/shard_map/ppermute | solution.py:61
  49.6 4.9 %collective-permute-start.12 = (bf16[1,72,256]{2,1,0:T(8,128)(2,1)S(1)}, bf16[1,72,256]{2,1,0:T(8,128)(2,1)S(1)}, u32[]{:S(2)}, u32[]{:S(2)}) collective-permute-start(bf16[1,72,256]{2,1,0:T(8,128)(2,1)S(1)} %get-tuple-element.114), channel_id=1, source_target_pairs={{0,8},{2,10},{4,12},{6,14},{8,0},{10,2},{12,4},{14,6},{16,24},{18,... | collective-permute-start | bytes 110600 | tf_op jit(solution)/shard_map/ppermute | solution.py:61
  54.5 7.9 %collective-permute-start.15 = (bf16[4,72,256]{2,1,0:T(8,128)(2,1)S(1)}, bf16[4,72,256]{2,1,0:T(8,128)(2,1)S(1)}, u32[]{:S(2)}, u32[]{:S(2)}) collective-permute-start(bf16[4,72,256]{2,1,0:T(8,128)(2,1)S(1)} %maximum_bitcast_fusion.1.refs_0_), channel_id=1, source_target_pairs={{0,2},{2,0},{4,6},{6,4},{8,10},{10,8},{12,14},{14,12},{16,18},{18,... | collective-permute-start | bytes 442376 | tf_op jit(solution)/shard_map/ppermute | solution.py:61
  56.5 5.8 %collective-permute-start.16 = (bf16[4,72,256]{2,1,0:T(8,128)(2,1)S(1)}, bf16[4,72,256]{2,1,0:T(8,128)(2,1)S(1)}, u32[]{:S(2)}, u32[]{:S(2)}) collective-permute-start(bf16[4,72,256]{2,1,0:T(8,128)(2,1)S(1)} %maximum_bitcast_fusion.1.refs_0_), channel_id=1, source_target_pairs={{0,4},{2,6},{4,0},{6,2},{8,12},{10,14},{12,8},{14,10},{16,20},{18,... | collective-permute-start | bytes 442376 | tf_op jit(solution)/shard_map/ppermute | solution.py:61
  57.5 6.0 %collective-permute-start.17 = (bf16[4,72,256]{2,1,0:T(8,128)(2,1)S(1)}, bf16[4,72,256]{2,1,0:T(8,128)(2,1)S(1)}, u32[]{:S(2)}, u32[]{:S(2)}) collective-permute-start(bf16[4,72,256]{2,1,0:T(8,128)(2,1)S(1)} %maximum_bitcast_fusion.1.refs_0_), channel_id=1, source_target_pairs={{0,6},{2,4},{4,2},{6,0},{8,14},{10,12},{12,10},{14,8},{16,22},{18,... | collective-permute-start | bytes 442376 | tf_op jit(solution)/shard_map/ppermute | solution.py:61
  68.2 9.0 %collective-permute-start.20 = (bf16[4,32,1024]{2,1,0:T(8,128)(2,1)S(1)}, bf16[4,32,1024]{2,1,0:T(8,128)(2,1)S(1)}, u32[]{:S(2)}, u32[]{:S(2)}) collective-permute-start(bf16[4,32,1024]{2,1,0:T(8,128)(2,1)S(1)} %get-tuple-element.127), channel_id=1, source_target_pairs={{0,6},{2,4},{4,2},{6,0},{8,14},{10,12},{12,10},{14,8},{16,22},{18,... | collective-permute-start | bytes 786440 | tf_op jit(solution)/shard_map/ppermute | solution.py:61
  69.5 8.9 %collective-permute-start.19 = (bf16[4,32,1024]{2,1,0:T(8,128)(2,1)S(1)}, bf16[4,32,1024]{2,1,0:T(8,128)(2,1)S(1)}, u32[]{:S(2)}, u32[]{:S(2)}) collective-permute-start(bf16[4,32,1024]{2,1,0:T(8,128)(2,1)S(1)} %get-tuple-element.126), channel_id=1, source_target_pairs={{0,4},{2,6},{4,0},{6,2},{8,12},{10,14},{12,8},{14,10},{16,20},{18,... | collective-permute-start | bytes 786440 | tf_op jit(solution)/shard_map/ppermute | solution.py:61
  70.5 7.8 %collective-permute-start.18 = (bf16[4,32,1024]{2,1,0:T(8,128)(2,1)S(1)}, bf16[4,32,1024]{2,1,0:T(8,128)(2,1)S(1)}, u32[]{:S(2)}, u32[]{:S(2)}) collective-permute-start(bf16[4,32,1024]{2,1,0:T(8,128)(2,1)S(1)} %get-tuple-element.125), channel_id=1, source_target_pairs={{0,2},{2,0},{4,6},{6,4},{8,10},{10,8},{12,14},{14,12},{16,18},{18,... | collective-permute-start | bytes 786440 | tf_op jit(solution)/shard_map/ppermute | solution.py:61
  78.6 9.1 %collective-permute-start.23 = (bf16[1,32,1024]{2,1,0:T(8,128)(2,1)S(1)}, bf16[1,32,1024]{2,1,0:T(8,128)(2,1)S(1)}, u32[]{:S(2)}, u32[]{:S(2)}) collective-permute-start(bf16[1,32,1024]{2,1,0:T(8,128)(2,1)S(1)} %get-tuple-element.182), channel_id=1, source_target_pairs={{0,24},{2,26},{4,28},{6,30},{8,16},{10,18},{12,20},{14,22},{16,8},... | collective-permute-start | bytes 196616 | tf_op jit(solution)/shard_map/ppermute | solution.py:61
  80.6 7.1 %collective-permute-start.22 = (bf16[1,32,1024]{2,1,0:T(8,128)(2,1)S(1)}, bf16[1,32,1024]{2,1,0:T(8,128)(2,1)S(1)}, u32[]{:S(2)}, u32[]{:S(2)}) collective-permute-start(bf16[1,32,1024]{2,1,0:T(8,128)(2,1)S(1)} %get-tuple-element.183), channel_id=1, source_target_pairs={{0,16},{2,18},{4,20},{6,22},{8,24},{10,26},{12,28},{14,30},{16,0},... | collective-permute-start | bytes 196616 | tf_op jit(solution)/shard_map/ppermute | solution.py:61
  81.7 5.9 %collective-permute-start.21 = (bf16[1,32,1024]{2,1,0:T(8,128)(2,1)S(1)}, bf16[1,32,1024]{2,1,0:T(8,128)(2,1)S(1)}, u32[]{:S(2)}, u32[]{:S(2)}) collective-permute-start(bf16[1,32,1024]{2,1,0:T(8,128)(2,1)S(1)} %get-tuple-element.181), channel_id=1, source_target_pairs={{0,8},{2,10},{4,12},{6,14},{8,0},{10,2},{12,4},{14,6},{16,24},{18,... | collective-permute-start | bytes 196616 | tf_op jit(solution)/shard_map/ppermute | solution.py:61
  87.7 7.2 %collective-permute-start.26 = (bf16[4,16,1024]{2,1,0:T(8,128)(2,1)S(1)}, bf16[4,16,1024]{2,1,0:T(8,128)(2,1)S(1)}, u32[]{:S(2)}, u32[]{:S(2)}) collective-permute-start(bf16[4,16,1024]{2,1,0:T(8,128)(2,1)S(1)} %get-tuple-element.155), channel_id=1, source_target_pairs={{0,6},{2,4},{4,2},{6,0},{8,14},{10,12},{12,10},{14,8},{16,22},{18,... | collective-permute-start | bytes 393224 | tf_op jit(solution)/shard_map/ppermute | solution.py:61
  89.0 6.1 %collective-permute-start.25 = (bf16[4,16,1024]{2,1,0:T(8,128)(2,1)S(1)}, bf16[4,16,1024]{2,1,0:T(8,128)(2,1)S(1)}, u32[]{:S(2)}, u32[]{:S(2)}) collective-permute-start(bf16[4,16,1024]{2,1,0:T(8,128)(2,1)S(1)} %get-tuple-element.154), channel_id=1, source_target_pairs={{0,4},{2,6},{4,0},{6,2},{8,12},{10,14},{12,8},{14,10},{16,20},{18,... | collective-permute-start | bytes 393224 | tf_op jit(solution)/shard_map/ppermute | solution.py:61
  90.0 5.0 %collective-permute-start.24 = (bf16[4,16,1024]{2,1,0:T(8,128)(2,1)S(1)}, bf16[4,16,1024]{2,1,0:T(8,128)(2,1)S(1)}, u32[]{:S(2)}, u32[]{:S(2)}) collective-permute-start(bf16[4,16,1024]{2,1,0:T(8,128)(2,1)S(1)} %get-tuple-element.153), channel_id=1, source_target_pairs={{0,2},{2,0},{4,6},{6,4},{8,10},{10,8},{12,14},{14,12},{16,18},{18,... | collective-permute-start | bytes 393224 | tf_op jit(solution)/shard_map/ppermute | solution.py:61
  95.2 8.9 %collective-permute-start.27 = (bf16[48,1024]{1,0:T(8,128)(2,1)S(1)}, bf16[48,1024]{1,0:T(8,128)(2,1)S(1)}, u32[]{:S(2)}, u32[]{:S(2)}) collective-permute-start(bf16[48,1024]{1,0:T(8,128)(2,1)S(1)} %get-tuple-element.191), channel_id=1, source_target_pairs={{0,8},{2,10},{4,12},{6,14},{8,0},{10,2},{12,4},{14,6},{16,24},{18,... | collective-permute-start | bytes 294920 | tf_op jit(solution)/shard_map/ppermute | solution.py:61
  96.0 8.2 %collective-permute-start.28 = (bf16[48,1024]{1,0:T(8,128)(2,1)S(1)}, bf16[48,1024]{1,0:T(8,128)(2,1)S(1)}, u32[]{:S(2)}, u32[]{:S(2)}) collective-permute-start(bf16[48,1024]{1,0:T(8,128)(2,1)S(1)} %get-tuple-element.190), channel_id=1, source_target_pairs={{0,16},{2,18},{4,20},{6,22},{8,24},{10,26},{12,28},{14,30},{16,0},... | collective-permute-start | bytes 294920 | tf_op jit(solution)/shard_map/ppermute | solution.py:61
  97.8 6.5 %collective-permute-start.29 = (bf16[48,1024]{1,0:T(8,128)(2,1)S(1)}, bf16[48,1024]{1,0:T(8,128)(2,1)S(1)}, u32[]{:S(2)}, u32[]{:S(2)}) collective-permute-start(bf16[48,1024]{1,0:T(8,128)(2,1)S(1)} %get-tuple-element.189), channel_id=1, source_target_pairs={{0,24},{2,26},{4,28},{6,30},{8,16},{10,18},{12,20},{14,22},{16,8},... | collective-permute-start | bytes 294920 | tf_op jit(solution)/shard_map/ppermute | solution.py:61
  104.4 9.2 %collective-permute-start.31 = (bf16[4,32,1024]{2,1,0:T(8,128)(2,1)S(1)}, bf16[4,32,1024]{2,1,0:T(8,128)(2,1)S(1)}, u32[]{:S(2)}, u32[]{:S(2)}) collective-permute-start(bf16[4,32,1024]{2,1,0:T(8,128)(2,1)S(1)} %maximum_bitcast_fusion.refs_0_), channel_id=1, source_target_pairs={{0,2},{2,0},{4,6},{6,4},{8,10},{10,8},{12,14},{14,12},{16,18},{18,... | collective-permute-start | bytes 786440 | tf_op jit(solution)/shard_map/ppermute | solution.py:61
  105.6 13.9 %collective-permute-start.32 = (bf16[4,32,1024]{2,1,0:T(8,128)(2,1)S(1)}, bf16[4,32,1024]{2,1,0:T(8,128)(2,1)S(1)}, u32[]{:S(2)}, u32[]{:S(2)}) collective-permute-start(bf16[4,32,1024]{2,1,0:T(8,128)(2,1)S(1)} %maximum_bitcast_fusion.refs_0_), channel_id=1, source_target_pairs={{0,4},{2,6},{4,0},{6,2},{8,12},{10,14},{12,8},{14,10},{16,20},{18,... | collective-permute-start | bytes 786440 | tf_op jit(solution)/shard_map/ppermute | solution.py:61
  106.6 13.0 %collective-permute-start.33 = (bf16[4,32,1024]{2,1,0:T(8,128)(2,1)S(1)}, bf16[4,32,1024]{2,1,0:T(8,128)(2,1)S(1)}, u32[]{:S(2)}, u32[]{:S(2)}) collective-permute-start(bf16[4,32,1024]{2,1,0:T(8,128)(2,1)S(1)} %maximum_bitcast_fusion.refs_0_), channel_id=1, source_target_pairs={{0,6},{2,4},{4,2},{6,0},{8,14},{10,12},{12,10},{14,8},{16,22},{18,... | collective-permute-start | bytes 786440 | tf_op jit(solution)/shard_map/ppermute | solution.py:61
  (7 other events, 56.9 us)

commit v8 on v7

--- a/solution.py
+++ b/solution.py
@@ -748,10 +748,9 @@
     weight_own = scatter_pieces([weight_sum[:, m] for m in range(following)], n, later)[0].astype(BF16)
     land_pieces, weight_own = lax.optimization_barrier((land_pieces, weight_own))
     land_sum = scatter_step(land_pieces, shift, count, n).astype(BF16)
-    land_sum, weight_own, query_f, there = lax.optimization_barrier(
-        (land_sum, weight_own, query_f, there)
-    )
-    land_sum, weight_own, grad_sb = lax.optimization_barrier((land_sum, weight_own, grad_sb))
+    weights = gather_first(weight_own, n)
+    land_sum, weights, query_f, there = lax.optimization_barrier((land_sum, weights, query_f, there))
+    land_sum, weights, grad_sb = lax.optimization_barrier((land_sum, weights, grad_sb))
     key_b, value_grad = call(
         key_kernel,
         (pairs,),
@@ -765,20 +764,13 @@
     )
 
     arrived = lax.ppermute(there, "head", [(0, 1), (1, 0)])
-    if len(later) == 1 and weight_own.shape[1] == land_sum.shape[2]:
-        (shift, count), tall = later[0], weight_own.shape[0]
-        got = [
-            exchange(jnp.concatenate([weight_own, land_sum[m]], axis=0), m << shift, n)
-            for m in range(1, count)
-        ]
-        weights = [weight_own[None]] + [part[None, :tall] for part in got]
-        land_own = sum(part.astype(F32) for part in [land_sum[0]] + [part[tall:] for part in got])
-    else:
-        weights = gather_first(weight_own, n)
-        land_sum = land_sum.reshape((-1, following) + land_sum.shape[1:])
-        land_own = scatter_pieces([land_sum[:, m] for m in range(following)], n, later)[0]
+    mask = size
+    while land_sum.shape[0] > 1:
+        given = exchange(land_sum[1::2], mask, n)
+        land_sum = (land_sum[::2].astype(F32) + given.astype(F32)).astype(BF16)
+        mask *= 2
+    land_own = land_sum[0].astype(F32)
     land_own = land_own * (1.0 / seg_len)
-    weights, key_b, arrived = lax.optimization_barrier((weights, key_b, arrived))
     mixed = call(
         mixed_kernel,
         (4,),

time: 122 us -> 121 us (level)
  waiting for transfers between devices: 22.4 us -> 20.1 us
  starting transfers between devices: 44.9 us -> 46.7 us
    ppermute x33 -> x35, waiting for transfers between devices: 22.4 us -> 20.1 us  [exchange(): return lax.ppermute(block, 'seq', [(i, i ^ mask) for i in range(n)])]
    ppermute x33 -> x35, starting transfers between devices: 44.9 us -> 46.7 us  [exchange(): return lax.ppermute(block, 'seq', [(i, i ^ mask) for i in range(n)])]
  transfers between devices with their start and end apart: 34 -> 36, of which waited for: 15 -> 14; matrix products, arithmetic and copies ran while one was open for 4% -> 4% of each run, Pallas kernels for 23% -> 23%
where the time goes in v8:
time: 121 us
  Pallas kernels  47.3 us (39%)
  starting transfers between devices  46.7 us (39%)
  waiting for transfers between devices  20.1 us (17%)
  other arithmetic  2.92 us (2%)
  matrix products  2.87 us (2%)
    pallas_call x14, Pallas kernels, call(): pl.pallas_call(kernel, grid_spec=pltpu.PrefetchScalarGridSpec(num_scalar_...  47.3 us
    ppermute x35, starting transfers between devices, exchange(): return lax.ppermute(block, 'seq', [(i, i ^ mask) for i in range(n)])  46.7 us
    ppermute x35, waiting for transfers between devices, exchange(): return lax.ppermute(block, 'seq', [(i, i ^ mask) for i in range(n)])  20.1 us
    dot_general x1, matrix products, dot(): lax.dot_general(left, right, (dims, ((), ())), preferred_element_type=F32)  2.87 us
  transfers between devices with their start and end apart: 36, of which 14 were waited for; matrix products, arithmetic and copies ran while one was open for 4% of the time, Pallas kernels for 23%

profile of v8, /device:TPU:0, one launch (start us, length us, event | category | flops | bytes accessed | tf_op | source)
XLA Modules:
  0.0 121.1 jit_solution(512980263665239283)
XLA Ops:
  0.8 1.7 %means.1 = bf16[16,1024]{1,0:T(8,128)(2,1)S(1)} custom-call(bf16[1024,512]{1,0:T(8,128)(2,1)} %q_ref.5, bf16[1024,512]{1,0:T(8,128)(2,1)} %k_ref.4), custom_call_target="tpu_custom_call" | custom-call | bytes 4194304 | tf_op jit(solution)/shard_map/means/pallas_call | solution.py:489
  2.5 5.1 %collective-permute-start.2 = (bf16[1,16,1024]{2,1,0:T(8,128)(2,1)S(1)}, bf16[1,16,1024]{2,1,0:T(8,128)(2,1)S(1)}, u32[]{:S(2)}, u32[]{:S(2)}) collective-permute-start(bf16[1,16,1024]{2,1,0:T(8,128)(2,1)S(1)} %bitcast.50), channel_id=1, source_target_pairs={{0,24},{2,26},{4,28},{6,30},{8,16},{10,18},{12,20},{14,22},{16,8},... | collective-permute-start | bytes 98312 | tf_op jit(solution)/shard_map/ppermute | solution.py:61
  9.5 2.9 %collective-permute-done.1 = bf16[1,16,1024]{2,1,0:T(8,128)(2,1)S(1)} collective-permute-done((bf16[1,16,1024]{2,1,0:T(8,128)(2,1)S(1)}, bf16[1,16,1024]{2,1,0:T(8,128)(2,1)S(1)}, u32[]{:S(2)}, u32[]{:S(2)}) %collective-permute-start.1) | collective-permute-done | bytes 32800 | tf_op jit(solution)/shard_map/ppermute | solution.py:61
  12.5 1.6 %collective-permute-start.3 = (bf16[4,16,1024]{2,1,0:T(8,128)(2,1)S(1)}, bf16[4,16,1024]{2,1,0:T(8,128)(2,1)S(1)}, u32[]{:S(2)}, u32[]{:S(2)}) collective-permute-start(bf16[4,16,1024]{2,1,0:T(8,128)(2,1)S(1)} %maximum_bitcast_fusion.2.refs_0_), channel_id=1, source_target_pairs={{0,2},{2,0},{4,6},{6,4},{8,10},{10,8},{12,14},{14,12},{16,18},{18,... | collective-permute-start | bytes 393224 | tf_op jit(solution)/shard_map/ppermute | solution.py:61
  14.0 1.5 %collective-permute-start.4 = (bf16[4,16,1024]{2,1,0:T(8,128)(2,1)S(1)}, bf16[4,16,1024]{2,1,0:T(8,128)(2,1)S(1)}, u32[]{:S(2)}, u32[]{:S(2)}) collective-permute-start(bf16[4,16,1024]{2,1,0:T(8,128)(2,1)S(1)} %maximum_bitcast_fusion.2.refs_0_), channel_id=1, source_target_pairs={{0,4},{2,6},{4,0},{6,2},{8,12},{10,14},{12,8},{14,10},{16,20},{18,... | collective-permute-start | bytes 393224 | tf_op jit(solution)/shard_map/ppermute | solution.py:61
  16.0 2.9 %convolution_convert_fusion.g_ref = bf16[1024,512]{1,0:T(8,128)(2,1)S(1)} fusion(bf16[1024,1024]{1,0:T(8,128)(2,1)} %cot_ref.1, bf16[512,1024]{1,0:T(8,128)(2,1)S(1)} %copy-done), kind=kOutput, calls=%fused_computation.4 | convolution fusion | flops 1074266112 | bytes 4194304 | tf_op jit(solution)/shard_map/dot_general | solution.py:23
  20.0 1.5 %collective-permute-done.5.refs_3_ = bf16[4,16,1024]{2,1,0:T(8,128)(2,1)S(1)} collective-permute-done((bf16[4,16,1024]{2,1,0:T(8,128)(2,1)S(1)}, bf16[4,16,1024]{2,1,0:T(8,128)(2,1)S(1)}, u32[]{:S(2)}, u32[]{:S(2)}) %collective-permute-start.5) | collective-permute-done | bytes 131104 | tf_op jit(solution)/shard_map/ppermute | solution.py:61
  21.4 10.0 %forward.1 = (bf16[1024,2048]{1,0:T(8,128)(2,1)S(1)}, bf16[1024,2048]{1,0:T(8,128)(2,1)S(1)}, f32[4,8,256]{2,1,0:T(8,128)S(1)}, bf16[256,1024]{1,0:T(8,128)(2,1)...) custom-call(s32[2]{0:T(128)S(1)} %pad_add_fusion.me_ref, ...), custom_call_target="tpu_custom_call" | custom-call | flops 8589934592 | bytes 4194304 | tf_op jit(solution)/shard_map/forward/pallas_call | solution.py:489
  32.6 2.4 %collective-permute-start.8 = (bf16[4,72,256]{2,1,0:T(8,128)(2,1)S(1)}, bf16[4,72,256]{2,1,0:T(8,128)(2,1)S(1)}, u32[]{:S(2)}, u32[]{:S(2)}) collective-permute-start(bf16[4,72,256]{2,1,0:T(8,128)(2,1)S(1)} %get-tuple-element.102), channel_id=1, source_target_pairs={{0,6},{2,4},{4,2},{6,0},{8,14},{10,12},{12,10},{14,8},{16,22},{18,... | collective-permute-start | bytes 442376 | tf_op jit(solution)/shard_map/ppermute | solution.py:61
  35.0 3.6 %newton.1 = (f32[9,256,256]{2,1,0:T(8,128)S(1)}, f32[1,256,256]{2,1,0:T(8,128)S(1)}) custom-call(s32[3]{0:T(128)S(1)} %pad_add_fusion.1.own_ref, bf16[256,1024]{1,0:T(8,128)(2,1)S(1)} %get-tuple-element.103.lq_ref.lk_ref, bf16[256,1024]{1,0:T(8,128)(2,1)S(1)} %get-tuple-element.103.lq_ref.lk_ref), custom_call_target="tpu_custom_call" | custom-call | flops 4294967296 | bytes 4194304 | tf_op jit(solution)/shard_map/newton/pallas_call | solution.py:489
  39.1 2.2 %collective-permute-start.10 = (bf16[1,72,256]{2,1,0:T(8,128)(2,1)S(1)}, bf16[1,72,256]{2,1,0:T(8,128)(2,1)S(1)}, u32[]{:S(2)}, u32[]{:S(2)}) collective-permute-start(bf16[1,72,256]{2,1,0:T(8,128)(2,1)S(1)} %get-tuple-element.111), channel_id=1, source_target_pairs={{0,16},{2,18},{4,20},{6,22},{8,24},{10,26},{12,28},{14,30},{16,0},... | collective-permute-start | bytes 110600 | tf_op jit(solution)/shard_map/ppermute | solution.py:61
  41.3 2.1 %collective-permute-start.11 = (bf16[1,72,256]{2,1,0:T(8,128)(2,1)S(1)}, bf16[1,72,256]{2,1,0:T(8,128)(2,1)S(1)}, u32[]{:S(2)}, u32[]{:S(2)}) collective-permute-start(bf16[1,72,256]{2,1,0:T(8,128)(2,1)S(1)} %get-tuple-element.112), channel_id=1, source_target_pairs={{0,24},{2,26},{4,28},{6,30},{8,16},{10,18},{12,20},{14,22},{16,8},... | collective-permute-start | bytes 110600 | tf_op jit(solution)/shard_map/ppermute | solution.py:61
  44.0 3.1 %collective-permute-done.11.refs_3_ = bf16[1,72,256]{2,1,0:T(8,128)(2,1)S(1)} collective-permute-done((bf16[1,72,256]{2,1,0:T(8,128)(2,1)S(1)}, bf16[1,72,256]{2,1,0:T(8,128)(2,1)S(1)}, u32[]{:S(2)}, u32[]{:S(2)}) %collective-permute-start.11) | collective-permute-done | bytes 36896 | tf_op jit(solution)/shard_map/ppermute | solution.py:61
  47.4 2.2 %collective-permute-start.14 = (bf16[1,72,256]{2,1,0:T(8,128)(2,1)S(1)}, bf16[1,72,256]{2,1,0:T(8,128)(2,1)S(1)}, u32[]{:S(2)}, u32[]{:S(2)}) collective-permute-start(bf16[1,72,256]{2,1,0:T(8,128)(2,1)S(1)} %get-tuple-element.114), channel_id=1, source_target_pairs={{0,24},{2,26},{4,28},{6,30},{8,16},{10,18},{12,20},{14,22},{16,8},... | collective-permute-start | bytes 110600 | tf_op jit(solution)/shard_map/ppermute | solution.py:61
  49.6 2.3 %collective-permute-start.12 = (bf16[1,72,256]{2,1,0:T(8,128)(2,1)S(1)}, bf16[1,72,256]{2,1,0:T(8,128)(2,1)S(1)}, u32[]{:S(2)}, u32[]{:S(2)}) collective-permute-start(bf16[1,72,256]{2,1,0:T(8,128)(2,1)S(1)} %get-tuple-element.114), channel_id=1, source_target_pairs={{0,8},{2,10},{4,12},{6,14},{8,0},{10,2},{12,4},{14,6},{16,24},{18,... | collective-permute-start | bytes 110600 | tf_op jit(solution)/shard_map/ppermute | solution.py:61
  51.8 1.4 %collective-permute-done.14 = bf16[1,72,256]{2,1,0:T(8,128)(2,1)S(1)} collective-permute-done((bf16[1,72,256]{2,1,0:T(8,128)(2,1)S(1)}, bf16[1,72,256]{2,1,0:T(8,128)(2,1)S(1)}, u32[]{:S(2)}, u32[]{:S(2)}) %collective-permute-start.14) | collective-permute-done | bytes 36896 | tf_op jit(solution)/shard_map/ppermute | solution.py:61
  54.5 2.1 %collective-permute-start.15 = (bf16[4,72,256]{2,1,0:T(8,128)(2,1)S(1)}, bf16[4,72,256]{2,1,0:T(8,128)(2,1)S(1)}, u32[]{:S(2)}, u32[]{:S(2)}) collective-permute-start(bf16[4,72,256]{2,1,0:T(8,128)(2,1)S(1)} %maximum_bitcast_fusion.1.refs_0_), channel_id=1, source_target_pairs={{0,2},{2,0},{4,6},{6,4},{8,10},{10,8},{12,14},{14,12},{16,18},{18,... | collective-permute-start | bytes 442376 | tf_op jit(solution)/shard_map/ppermute | solution.py:61
  58.1 4.3 %newton_grad.1 = (f32[256,128]{1,0:T(8,128)S(1)}, f32[256,128]{1,0:T(8,128)S(1)}) custom-call(s32[3]{0:T(128)S(1)} %pad_add_fusion.1.own_ref, f32[9,256,256]{2,1,0:T(8,128)S(1)} %get-tuple-element.115.saved_ref, f32[32,256]{1,0:T(8,128)S(1)} %get-tuple-element.116.values_ref, f32[32,256]{1,0:T(8,128)S(1)} %get-tuple-element.117.grads_ref, ...), custom_call_target="tpu_custom_call" | custom-call | flops 8589934592 | bytes 4194304 | tf_op jit(solution)/shard_map/newton_grad/pallas_call | solution.py:489
  63.5 4.7 %attend.1 = (bf16[1024,512]{1,0:T(8,128)(2,1)S(1)}, bf16[512,256]{1,0:T(8,128)(2,1)S(1)}, bf16[512,256]{1,0:T(8,128)(2,1)S(1)}, f32[8,256]{1,0:T(8,128)S(1)}, bf...) custom-call(s32[2]{0:T(128)S(1)} %pad_add_fusion.me_ref, ...), custom_call_target="tpu_custom_call" | custom-call | flops 4294967296 | bytes 4194304 | tf_op jit(solution)/shard_map/attend/pallas_call | solution.py:489
  71.8 5.4 %query_land.1 = (bf16[256,512]{1,0:T(8,128)(2,1)S(1)}, bf16[1024,2048]{1,0:T(8,128)(2,1)S(1)}) custom-call(s32[3]{0:T(128)S(1)} %pad_add_fusion.1.own_ref, bf16[1024,512]{1,0:T(8,128)(2,1)S(1)} %copy-done.1, bf16[1024,512]{1,0:T(8,128)(2,1)S(1)} %convolution_convert_fusion.g_ref, bf16[1024,2048]{1,0:T(8,128)(2,1)S(1)} %get-tuple-element.97.fb_ref, ...), custom_call_target="tpu_custom_call" | custom-call | flops 4294967296 | bytes 4194304 | tf_op jit(solution)/shard_map/query_land/pallas_call | solution.py:489
  78.6 2.0 %collective-permute-start.23 = (bf16[1,32,1024]{2,1,0:T(8,128)(2,1)S(1)}, bf16[1,32,1024]{2,1,0:T(8,128)(2,1)S(1)}, u32[]{:S(2)}, u32[]{:S(2)}) collective-permute-start(bf16[1,32,1024]{2,1,0:T(8,128)(2,1)S(1)} %get-tuple-element.182), channel_id=1, source_target_pairs={{0,24},{2,26},{4,28},{6,30},{8,16},{10,18},{12,20},{14,22},{16,8},... | collective-permute-start | bytes 196616 | tf_op jit(solution)/shard_map/ppermute | solution.py:61
  83.0 4.6 %key_land.1 = (bf16[1024,2048]{1,0:T(8,128)(2,1)S(1)}, bf16[4,16,1024]{2,1,0:T(8,128)(2,1)S(1)}, bf16[4,16,1024]{2,1,0:T(8,128)(2,1)S(1)}, bf16[4,16,1024]{2,1,0:T(8,128)(2,1)S(1)}, bf16[4,16,1024]{2,1,0:T(8,128)(2,1)S(1)}) custom-call(s32[3]{0:T(128)S(1)} %pad_add_fusion.1.own_ref, bf16[1024,512]{1,0:T(8,128)(2,1)S(1)} %copy-done.2, ...), custom_call_target="tpu_custom_call" | custom-call | flops 4294967296 | bytes 4194304 | tf_op jit(solution)/shard_map/key_land/pallas_call | solution.py:489
  91.3 2.3 %query_grad.1 = bf16[1024,512]{1,0:T(8,128)(2,1)S(1)} custom-call(bf16[1024,2048]{1,0:T(8,128)(2,1)S(1)} %get-tuple-element.157.ds_ref, bf16[256,1024]{1,0:T(8,128)(2,1)S(1)} %get-tuple-element.103.lq_ref.lk_ref), custom_call_target="tpu_custom_call" | custom-call | flops 2147483648 | bytes 4194304 | tf_op jit(solution)/shard_map/query_grad/pallas_call | solution.py:489
  95.7 1.8 %collective-permute-start.28 = (bf16[1,32,1024]{2,1,0:T(8,128)(2,1)S(1)}, bf16[1,32,1024]{2,1,0:T(8,128)(2,1)S(1)}, u32[]{:S(2)}, u32[]{:S(2)}) collective-permute-start(bf16[1,32,1024]{2,1,0:T(8,128)(2,1)S(1)} %bitcast.58), channel_id=1, source_target_pairs={{0,16},{2,18},{4,20},{6,22},{8,24},{10,26},{12,28},{14,30},{16,0},... | collective-permute-start | bytes 196616 | tf_op jit(solution)/shard_map/ppermute | solution.py:61
  97.5 1.9 %collective-permute-start.29 = (bf16[1,32,1024]{2,1,0:T(8,128)(2,1)S(1)}, bf16[1,32,1024]{2,1,0:T(8,128)(2,1)S(1)}, u32[]{:S(2)}, u32[]{:S(2)}) collective-permute-start(bf16[1,32,1024]{2,1,0:T(8,128)(2,1)S(1)} %bitcast.59), channel_id=1, source_target_pairs={{0,24},{2,26},{4,28},{6,30},{8,16},{10,18},{12,20},{14,22},{16,8},... | collective-permute-start | bytes 196616 | tf_op jit(solution)/shard_map/ppermute | solution.py:61
  99.5 1.4 %collective-permute-done.28 = bf16[1,32,1024]{2,1,0:T(8,128)(2,1)S(1)} collective-permute-done((bf16[1,32,1024]{2,1,0:T(8,128)(2,1)S(1)}, bf16[1,32,1024]{2,1,0:T(8,128)(2,1)S(1)}, u32[]{:S(2)}, u32[]{:S(2)}) %collective-permute-start.28) | collective-permute-done | bytes 65568 | tf_op jit(solution)/shard_map/ppermute | solution.py:61
  100.9 2.7 %collective-permute-done.29 = bf16[1,32,1024]{2,1,0:T(8,128)(2,1)S(1)} collective-permute-done((bf16[1,32,1024]{2,1,0:T(8,128)(2,1)S(1)}, bf16[1,32,1024]{2,1,0:T(8,128)(2,1)S(1)}, u32[]{:S(2)}, u32[]{:S(2)}) %collective-permute-start.29) | collective-permute-done | bytes 65568 | tf_op jit(solution)/shard_map/ppermute | solution.py:61
  105.4 1.8 %collective-permute-start.32 = (bf16[4,32,1024]{2,1,0:T(8,128)(2,1)S(1)}, bf16[4,32,1024]{2,1,0:T(8,128)(2,1)S(1)}, u32[]{:S(2)}, u32[]{:S(2)}) collective-permute-start(bf16[4,32,1024]{2,1,0:T(8,128)(2,1)S(1)} %maximum_bitcast_fusion.refs_0_), channel_id=1, source_target_pairs={{0,6},{2,4},{4,2},{6,0},{8,14},{10,12},{12,10},{14,8},{16,22},{18,... | collective-permute-start | bytes 786440 | tf_op jit(solution)/shard_map/ppermute | solution.py:61
  107.9 1.8 %collective-permute-start.35 = (bf16[1,16,1024]{2,1,0:T(8,128)(2,1)S(1)}, bf16[1,16,1024]{2,1,0:T(8,128)(2,1)S(1)}, u32[]{:S(2)}, u32[]{:S(2)}) collective-permute-start(bf16[1,16,1024]{2,1,0:T(8,128)(2,1)S(1)} %slice.47), channel_id=1, source_target_pairs={{0,16},{2,18},{4,20},{6,22},{8,24},{10,26},{12,28},{14,30},{16,0},... | collective-permute-start | bytes 98312 | tf_op jit(solution)/shard_map/ppermute | solution.py:61
  109.7 4.5 %key_grad.1 = (bf16[1024,512]{1,0:T(8,128)(2,1)S(1)}, bf16[1024,512]{1,0:T(8,128)(2,1)}) custom-call(bf16[1024,2048]{1,0:T(8,128)(2,1)S(1)} %get-tuple-element.174.ds_ref, bf16[1024,2048]{1,0:T(8,128)(2,1)S(1)} %get-tuple-element.136.pb_ref, bf16[256,1024]{1,0:T(8,128)(2,1)S(1)} %get-tuple-element.103.lq_ref.lk_ref, ...), custom_call_target="tpu_custom_call" | custom-call | flops 4294967296 | bytes 4194304 | tf_op jit(solution)/shard_map/key_grad/pallas_call | solution.py:489
  116.6 2.4 %mixed.1 = bf16[1024,512]{1,0:T(8,128)(2,1)} custom-call(s32[1]{0:T(128)} %bitcast.1._, bf16[1024,512]{1,0:T(8,128)(2,1)S(1)} %get-tuple-element.159.attn_ref, bf16[512,1024]{1,0:T(8,128)(2,1)S(1)} %copy-done, bf16[1024,512]{1,0:T(8,128)(2,1)S(1)} %collective-permute-done.33.other_ref), custom_call_target="tpu_custom_call" | custom-call | flops 1073741824 | bytes 4194304 | tf_op jit(solution)/shard_map/mixed/pallas_call | solution.py:489
  119.0 2.0 %unpack.1 = f32[512,1024]{1,0:T(8,128)} custom-call(s32[2]{0:T(128)S(1)} %pad_add_fusion.me_ref, bf16[4,32,1024]{2,1,0:T(8,128)(2,1)S(1)} %maximum_bitcast_fusion.refs_0_, bf16[4,32,1024]{2,1,0:T(8,128)(2,1)S(1)} %collective-permute-done.30.refs_1_, bf16[4,32,1024]{2,1,0:T(8,128)(2,1)S(1)} %collective-permute-done.31.refs_2_, ...), custom_call_target="tpu_custom_call" | custom-call | bytes 4194304 | tf_op jit(solution)/shard_map/unpack/pallas_call | solution.py:489
  (81 shorter events, 27.9 us)
Async XLA Ops:
  2.5 7.0 %collective-permute-start.2 = (bf16[1,16,1024]{2,1,0:T(8,128)(2,1)S(1)}, bf16[1,16,1024]{2,1,0:T(8,128)(2,1)S(1)}, u32[]{:S(2)}, u32[]{:S(2)}) collective-permute-start(bf16[1,16,1024]{2,1,0:T(8,128)(2,1)S(1)} %bitcast.50), channel_id=1, source_target_pairs={{0,24},{2,26},{4,28},{6,30},{8,16},{10,18},{12,20},{14,22},{16,8},... | collective-permute-start | bytes 98312 | tf_op jit(solution)/shard_map/ppermute | solution.py:61
  7.6 4.8 %collective-permute-start.1 = (bf16[1,16,1024]{2,1,0:T(8,128)(2,1)S(1)}, bf16[1,16,1024]{2,1,0:T(8,128)(2,1)S(1)}, u32[]{:S(2)}, u32[]{:S(2)}) collective-permute-start(bf16[1,16,1024]{2,1,0:T(8,128)(2,1)S(1)} %bitcast.51), channel_id=1, source_target_pairs={{0,16},{2,18},{4,20},{6,22},{8,24},{10,26},{12,28},{14,30},{16,0},... | collective-permute-start | bytes 98312 | tf_op jit(solution)/shard_map/ppermute | solution.py:61
  12.5 6.4 %collective-permute-start.3 = (bf16[4,16,1024]{2,1,0:T(8,128)(2,1)S(1)}, bf16[4,16,1024]{2,1,0:T(8,128)(2,1)S(1)}, u32[]{:S(2)}, u32[]{:S(2)}) collective-permute-start(bf16[4,16,1024]{2,1,0:T(8,128)(2,1)S(1)} %maximum_bitcast_fusion.2.refs_0_), channel_id=1, source_target_pairs={{0,2},{2,0},{4,6},{6,4},{8,10},{10,8},{12,14},{14,12},{16,18},{18,... | collective-permute-start | bytes 393224 | tf_op jit(solution)/shard_map/ppermute | solution.py:61
  14.0 5.9 %collective-permute-start.4 = (bf16[4,16,1024]{2,1,0:T(8,128)(2,1)S(1)}, bf16[4,16,1024]{2,1,0:T(8,128)(2,1)S(1)}, u32[]{:S(2)}, u32[]{:S(2)}) collective-permute-start(bf16[4,16,1024]{2,1,0:T(8,128)(2,1)S(1)} %maximum_bitcast_fusion.2.refs_0_), channel_id=1, source_target_pairs={{0,4},{2,6},{4,0},{6,2},{8,12},{10,14},{12,8},{14,10},{16,20},{18,... | collective-permute-start | bytes 393224 | tf_op jit(solution)/shard_map/ppermute | solution.py:61
  15.6 5.9 %collective-permute-start.5 = (bf16[4,16,1024]{2,1,0:T(8,128)(2,1)S(1)}, bf16[4,16,1024]{2,1,0:T(8,128)(2,1)S(1)}, u32[]{:S(2)}, u32[]{:S(2)}) collective-permute-start(bf16[4,16,1024]{2,1,0:T(8,128)(2,1)S(1)} %maximum_bitcast_fusion.2.refs_0_), channel_id=1, source_target_pairs={{0,6},{2,4},{4,2},{6,0},{8,14},{10,12},{12,10},{14,8},{16,22},{18,... | collective-permute-start | bytes 393224 | tf_op jit(solution)/shard_map/ppermute | solution.py:61
  31.5 7.2 %collective-permute-start.6 = (bf16[4,72,256]{2,1,0:T(8,128)(2,1)S(1)}, bf16[4,72,256]{2,1,0:T(8,128)(2,1)S(1)}, u32[]{:S(2)}, u32[]{:S(2)}) collective-permute-start(bf16[4,72,256]{2,1,0:T(8,128)(2,1)S(1)} %get-tuple-element.100), channel_id=1, source_target_pairs={{0,2},{2,0},{4,6},{6,4},{8,10},{10,8},{12,14},{14,12},{16,18},{18,... | collective-permute-start | bytes 442376 | tf_op jit(solution)/shard_map/ppermute | solution.py:61
  32.1 6.7 %collective-permute-start.7 = (bf16[4,72,256]{2,1,0:T(8,128)(2,1)S(1)}, bf16[4,72,256]{2,1,0:T(8,128)(2,1)S(1)}, u32[]{:S(2)}, u32[]{:S(2)}) collective-permute-start(bf16[4,72,256]{2,1,0:T(8,128)(2,1)S(1)} %get-tuple-element.101), channel_id=1, source_target_pairs={{0,4},{2,6},{4,0},{6,2},{8,12},{10,14},{12,8},{14,10},{16,20},{18,... | collective-permute-start | bytes 442376 | tf_op jit(solution)/shard_map/ppermute | solution.py:61
  32.6 6.2 %collective-permute-start.8 = (bf16[4,72,256]{2,1,0:T(8,128)(2,1)S(1)}, bf16[4,72,256]{2,1,0:T(8,128)(2,1)S(1)}, u32[]{:S(2)}, u32[]{:S(2)}) collective-permute-start(bf16[4,72,256]{2,1,0:T(8,128)(2,1)S(1)} %get-tuple-element.102), channel_id=1, source_target_pairs={{0,6},{2,4},{4,2},{6,0},{8,14},{10,12},{12,10},{14,8},{16,22},{18,... | collective-permute-start | bytes 442376 | tf_op jit(solution)/shard_map/ppermute | solution.py:61
  39.1 4.9 %collective-permute-start.10 = (bf16[1,72,256]{2,1,0:T(8,128)(2,1)S(1)}, bf16[1,72,256]{2,1,0:T(8,128)(2,1)S(1)}, u32[]{:S(2)}, u32[]{:S(2)}) collective-permute-start(bf16[1,72,256]{2,1,0:T(8,128)(2,1)S(1)} %get-tuple-element.111), channel_id=1, source_target_pairs={{0,16},{2,18},{4,20},{6,22},{8,24},{10,26},{12,28},{14,30},{16,0},... | collective-permute-start | bytes 110600 | tf_op jit(solution)/shard_map/ppermute | solution.py:61
  41.3 5.8 %collective-permute-start.11 = (bf16[1,72,256]{2,1,0:T(8,128)(2,1)S(1)}, bf16[1,72,256]{2,1,0:T(8,128)(2,1)S(1)}, u32[]{:S(2)}, u32[]{:S(2)}) collective-permute-start(bf16[1,72,256]{2,1,0:T(8,128)(2,1)S(1)} %get-tuple-element.112), channel_id=1, source_target_pairs={{0,24},{2,26},{4,28},{6,30},{8,16},{10,18},{12,20},{14,22},{16,8},... | collective-permute-start | bytes 110600 | tf_op jit(solution)/shard_map/ppermute | solution.py:61
  47.4 5.8 %collective-permute-start.14 = (bf16[1,72,256]{2,1,0:T(8,128)(2,1)S(1)}, bf16[1,72,256]{2,1,0:T(8,128)(2,1)S(1)}, u32[]{:S(2)}, u32[]{:S(2)}) collective-permute-start(bf16[1,72,256]{2,1,0:T(8,128)(2,1)S(1)} %get-tuple-element.114), channel_id=1, source_target_pairs={{0,24},{2,26},{4,28},{6,30},{8,16},{10,18},{12,20},{14,22},{16,8},... | collective-permute-start | bytes 110600 | tf_op jit(solution)/shard_map/ppermute | solution.py:61
  49.6 4.9 %collective-permute-start.13 = (bf16[1,72,256]{2,1,0:T(8,128)(2,1)S(1)}, bf16[1,72,256]{2,1,0:T(8,128)(2,1)S(1)}, u32[]{:S(2)}, u32[]{:S(2)}) collective-permute-start(bf16[1,72,256]{2,1,0:T(8,128)(2,1)S(1)} %get-tuple-element.114), channel_id=1, source_target_pairs={{0,16},{2,18},{4,20},{6,22},{8,24},{10,26},{12,28},{14,30},{16,0},... | collective-permute-start | bytes 110600 | tf_op jit(solution)/shard_map/ppermute | solution.py:61
  49.6 4.9 %collective-permute-start.12 = (bf16[1,72,256]{2,1,0:T(8,128)(2,1)S(1)}, bf16[1,72,256]{2,1,0:T(8,128)(2,1)S(1)}, u32[]{:S(2)}, u32[]{:S(2)}) collective-permute-start(bf16[1,72,256]{2,1,0:T(8,128)(2,1)S(1)} %get-tuple-element.114), channel_id=1, source_target_pairs={{0,8},{2,10},{4,12},{6,14},{8,0},{10,2},{12,4},{14,6},{16,24},{18,... | collective-permute-start | bytes 110600 | tf_op jit(solution)/shard_map/ppermute | solution.py:61
  54.5 7.9 %collective-permute-start.15 = (bf16[4,72,256]{2,1,0:T(8,128)(2,1)S(1)}, bf16[4,72,256]{2,1,0:T(8,128)(2,1)S(1)}, u32[]{:S(2)}, u32[]{:S(2)}) collective-permute-start(bf16[4,72,256]{2,1,0:T(8,128)(2,1)S(1)} %maximum_bitcast_fusion.1.refs_0_), channel_id=1, source_target_pairs={{0,2},{2,0},{4,6},{6,4},{8,10},{10,8},{12,14},{14,12},{16,18},{18,... | collective-permute-start | bytes 442376 | tf_op jit(solution)/shard_map/ppermute | solution.py:61
  56.5 5.8 %collective-permute-start.16 = (bf16[4,72,256]{2,1,0:T(8,128)(2,1)S(1)}, bf16[4,72,256]{2,1,0:T(8,128)(2,1)S(1)}, u32[]{:S(2)}, u32[]{:S(2)}) collective-permute-start(bf16[4,72,256]{2,1,0:T(8,128)(2,1)S(1)} %maximum_bitcast_fusion.1.refs_0_), channel_id=1, source_target_pairs={{0,4},{2,6},{4,0},{6,2},{8,12},{10,14},{12,8},{14,10},{16,20},{18,... | collective-permute-start | bytes 442376 | tf_op jit(solution)/shard_map/ppermute | solution.py:61
  57.5 6.0 %collective-permute-start.17 = (bf16[4,72,256]{2,1,0:T(8,128)(2,1)S(1)}, bf16[4,72,256]{2,1,0:T(8,128)(2,1)S(1)}, u32[]{:S(2)}, u32[]{:S(2)}) collective-permute-start(bf16[4,72,256]{2,1,0:T(8,128)(2,1)S(1)} %maximum_bitcast_fusion.1.refs_0_), channel_id=1, source_target_pairs={{0,6},{2,4},{4,2},{6,0},{8,14},{10,12},{12,10},{14,8},{16,22},{18,... | collective-permute-start | bytes 442376 | tf_op jit(solution)/shard_map/ppermute | solution.py:61
  68.2 9.0 %collective-permute-start.20 = (bf16[4,32,1024]{2,1,0:T(8,128)(2,1)S(1)}, bf16[4,32,1024]{2,1,0:T(8,128)(2,1)S(1)}, u32[]{:S(2)}, u32[]{:S(2)}) collective-permute-start(bf16[4,32,1024]{2,1,0:T(8,128)(2,1)S(1)} %get-tuple-element.127), channel_id=1, source_target_pairs={{0,6},{2,4},{4,2},{6,0},{8,14},{10,12},{12,10},{14,8},{16,22},{18,... | collective-permute-start | bytes 786440 | tf_op jit(solution)/shard_map/ppermute | solution.py:61
  69.5 8.9 %collective-permute-start.19 = (bf16[4,32,1024]{2,1,0:T(8,128)(2,1)S(1)}, bf16[4,32,1024]{2,1,0:T(8,128)(2,1)S(1)}, u32[]{:S(2)}, u32[]{:S(2)}) collective-permute-start(bf16[4,32,1024]{2,1,0:T(8,128)(2,1)S(1)} %get-tuple-element.126), channel_id=1, source_target_pairs={{0,4},{2,6},{4,0},{6,2},{8,12},{10,14},{12,8},{14,10},{16,20},{18,... | collective-permute-start | bytes 786440 | tf_op jit(solution)/shard_map/ppermute | solution.py:61
  70.5 7.8 %collective-permute-start.18 = (bf16[4,32,1024]{2,1,0:T(8,128)(2,1)S(1)}, bf16[4,32,1024]{2,1,0:T(8,128)(2,1)S(1)}, u32[]{:S(2)}, u32[]{:S(2)}) collective-permute-start(bf16[4,32,1024]{2,1,0:T(8,128)(2,1)S(1)} %get-tuple-element.125), channel_id=1, source_target_pairs={{0,2},{2,0},{4,6},{6,4},{8,10},{10,8},{12,14},{14,12},{16,18},{18,... | collective-permute-start | bytes 786440 | tf_op jit(solution)/shard_map/ppermute | solution.py:61
  78.6 9.1 %collective-permute-start.23 = (bf16[1,32,1024]{2,1,0:T(8,128)(2,1)S(1)}, bf16[1,32,1024]{2,1,0:T(8,128)(2,1)S(1)}, u32[]{:S(2)}, u32[]{:S(2)}) collective-permute-start(bf16[1,32,1024]{2,1,0:T(8,128)(2,1)S(1)} %get-tuple-element.182), channel_id=1, source_target_pairs={{0,24},{2,26},{4,28},{6,30},{8,16},{10,18},{12,20},{14,22},{16,8},... | collective-permute-start | bytes 196616 | tf_op jit(solution)/shard_map/ppermute | solution.py:61
  80.6 7.1 %collective-permute-start.22 = (bf16[1,32,1024]{2,1,0:T(8,128)(2,1)S(1)}, bf16[1,32,1024]{2,1,0:T(8,128)(2,1)S(1)}, u32[]{:S(2)}, u32[]{:S(2)}) collective-permute-start(bf16[1,32,1024]{2,1,0:T(8,128)(2,1)S(1)} %get-tuple-element.183), channel_id=1, source_target_pairs={{0,16},{2,18},{4,20},{6,22},{8,24},{10,26},{12,28},{14,30},{16,0},... | collective-permute-start | bytes 196616 | tf_op jit(solution)/shard_map/ppermute | solution.py:61
  81.7 5.9 %collective-permute-start.21 = (bf16[1,32,1024]{2,1,0:T(8,128)(2,1)S(1)}, bf16[1,32,1024]{2,1,0:T(8,128)(2,1)S(1)}, u32[]{:S(2)}, u32[]{:S(2)}) collective-permute-start(bf16[1,32,1024]{2,1,0:T(8,128)(2,1)S(1)} %get-tuple-element.181), channel_id=1, source_target_pairs={{0,8},{2,10},{4,12},{6,14},{8,0},{10,2},{12,4},{14,6},{16,24},{18,... | collective-permute-start | bytes 196616 | tf_op jit(solution)/shard_map/ppermute | solution.py:61
  87.7 9.8 %collective-permute-start.26 = (bf16[4,16,1024]{2,1,0:T(8,128)(2,1)S(1)}, bf16[4,16,1024]{2,1,0:T(8,128)(2,1)S(1)}, u32[]{:S(2)}, u32[]{:S(2)}) collective-permute-start(bf16[4,16,1024]{2,1,0:T(8,128)(2,1)S(1)} %get-tuple-element.155), channel_id=1, source_target_pairs={{0,6},{2,4},{4,2},{6,0},{8,14},{10,12},{12,10},{14,8},{16,22},{18,... | collective-permute-start | bytes 393224 | tf_op jit(solution)/shard_map/ppermute | solution.py:61
  89.0 10.4 %collective-permute-start.25 = (bf16[4,16,1024]{2,1,0:T(8,128)(2,1)S(1)}, bf16[4,16,1024]{2,1,0:T(8,128)(2,1)S(1)}, u32[]{:S(2)}, u32[]{:S(2)}) collective-permute-start(bf16[4,16,1024]{2,1,0:T(8,128)(2,1)S(1)} %get-tuple-element.154), channel_id=1, source_target_pairs={{0,4},{2,6},{4,0},{6,2},{8,12},{10,14},{12,8},{14,10},{16,20},{18,... | collective-permute-start | bytes 393224 | tf_op jit(solution)/shard_map/ppermute | solution.py:61
  90.0 9.4 %collective-permute-start.24 = (bf16[4,16,1024]{2,1,0:T(8,128)(2,1)S(1)}, bf16[4,16,1024]{2,1,0:T(8,128)(2,1)S(1)}, u32[]{:S(2)}, u32[]{:S(2)}) collective-permute-start(bf16[4,16,1024]{2,1,0:T(8,128)(2,1)S(1)} %get-tuple-element.153), channel_id=1, source_target_pairs={{0,2},{2,0},{4,6},{6,4},{8,10},{10,8},{12,14},{14,12},{16,18},{18,... | collective-permute-start | bytes 393224 | tf_op jit(solution)/shard_map/ppermute | solution.py:61
  95.7 5.2 %collective-permute-start.28 = (bf16[1,32,1024]{2,1,0:T(8,128)(2,1)S(1)}, bf16[1,32,1024]{2,1,0:T(8,128)(2,1)S(1)}, u32[]{:S(2)}, u32[]{:S(2)}) collective-permute-start(bf16[1,32,1024]{2,1,0:T(8,128)(2,1)S(1)} %bitcast.58), channel_id=1, source_target_pairs={{0,16},{2,18},{4,20},{6,22},{8,24},{10,26},{12,28},{14,30},{16,0},... | collective-permute-start | bytes 196616 | tf_op jit(solution)/shard_map/ppermute | solution.py:61
  97.5 6.1 %collective-permute-start.29 = (bf16[1,32,1024]{2,1,0:T(8,128)(2,1)S(1)}, bf16[1,32,1024]{2,1,0:T(8,128)(2,1)S(1)}, u32[]{:S(2)}, u32[]{:S(2)}) collective-permute-start(bf16[1,32,1024]{2,1,0:T(8,128)(2,1)S(1)} %bitcast.59), channel_id=1, source_target_pairs={{0,24},{2,26},{4,28},{6,30},{8,16},{10,18},{12,20},{14,22},{16,8},... | collective-permute-start | bytes 196616 | tf_op jit(solution)/shard_map/ppermute | solution.py:61
  103.6 15.3 %collective-permute-start.30 = (bf16[4,32,1024]{2,1,0:T(8,128)(2,1)S(1)}, bf16[4,32,1024]{2,1,0:T(8,128)(2,1)S(1)}, u32[]{:S(2)}, u32[]{:S(2)}) collective-permute-start(bf16[4,32,1024]{2,1,0:T(8,128)(2,1)S(1)} %maximum_bitcast_fusion.refs_0_), channel_id=1, source_target_pairs={{0,2},{2,0},{4,6},{6,4},{8,10},{10,8},{12,14},{14,12},{16,18},{18,... | collective-permute-start | bytes 786440 | tf_op jit(solution)/shard_map/ppermute | solution.py:61
  104.4 14.6 %collective-permute-start.31 = (bf16[4,32,1024]{2,1,0:T(8,128)(2,1)S(1)}, bf16[4,32,1024]{2,1,0:T(8,128)(2,1)S(1)}, u32[]{:S(2)}, u32[]{:S(2)}) collective-permute-start(bf16[4,32,1024]{2,1,0:T(8,128)(2,1)S(1)} %maximum_bitcast_fusion.refs_0_), channel_id=1, source_target_pairs={{0,4},{2,6},{4,0},{6,2},{8,12},{10,14},{12,8},{14,10},{16,20},{18,... | collective-permute-start | bytes 786440 | tf_op jit(solution)/shard_map/ppermute | solution.py:61
  105.4 13.5 %collective-permute-start.32 = (bf16[4,32,1024]{2,1,0:T(8,128)(2,1)S(1)}, bf16[4,32,1024]{2,1,0:T(8,128)(2,1)S(1)}, u32[]{:S(2)}, u32[]{:S(2)}) collective-permute-start(bf16[4,32,1024]{2,1,0:T(8,128)(2,1)S(1)} %maximum_bitcast_fusion.refs_0_), channel_id=1, source_target_pairs={{0,6},{2,4},{4,2},{6,0},{8,14},{10,12},{12,10},{14,8},{16,22},{18,... | collective-permute-start | bytes 786440 | tf_op jit(solution)/shard_map/ppermute | solution.py:61
  107.2 9.4 %collective-permute-start.33 = (bf16[1024,512]{1,0:T(8,128)(2,1)S(1)}, bf16[1024,512]{1,0:T(8,128)(2,1)S(1)}, u32[]{:S(2)}, u32[]{:S(2)}) collective-permute-start(bf16[1024,512]{1,0:T(8,128)(2,1)S(1)} %part.1), channel_id=1, source_target_pairs={{0,1},{1,0},{2,3},{3,2},{4,5},{5,4},{6,7},{7,6},{8,9},{9,8},{10,11... | collective-permute-start | bytes 3145736 | tf_op jit(solution)/shard_map/ppermute | solution.py:766
  107.9 6.3 %collective-permute-start.35 = (bf16[1,16,1024]{2,1,0:T(8,128)(2,1)S(1)}, bf16[1,16,1024]{2,1,0:T(8,128)(2,1)S(1)}, u32[]{:S(2)}, u32[]{:S(2)}) collective-permute-start(bf16[1,16,1024]{2,1,0:T(8,128)(2,1)S(1)} %slice.47), channel_id=1, source_target_pairs={{0,16},{2,18},{4,20},{6,22},{8,24},{10,26},{12,28},{14,30},{16,0},... | collective-permute-start | bytes 98312 | tf_op jit(solution)/shard_map/ppermute | solution.py:61
  (9 other events, 65.9 us)

commit v9 on v8

--- a/solution.py
+++ b/solution.py
@@ -715,18 +715,7 @@
         flops=4 << 30,
         name="key_land",
     )
-    land_pieces, grad_sf, attn = lax.optimization_barrier((land_pieces, grad_sf, attn))
-    query_f = call(
-        query_kernel,
-        (pairs,),
-        [],
-        [grad_sf, land],
-        [factor_pair, lk_pair],
-        tokens,
-        token_pair,
-        flops=2 << 30,
-        name="query_grad",
-    )
+    land_pieces, attn = lax.optimization_barrier((land_pieces, attn))
     half = width // 2
     row_block = pl.BlockSpec((rows // 4, columns), lambda j, _: (j, 0))
     half_block = pl.BlockSpec((rows // 4, half), lambda j, _: (j, 0))
@@ -749,6 +738,18 @@
     land_pieces, weight_own = lax.optimization_barrier((land_pieces, weight_own))
     land_sum = scatter_step(land_pieces, shift, count, n).astype(BF16)
     weights = gather_first(weight_own, n)
+    land_sum, grad_sf = lax.optimization_barrier((land_sum, grad_sf))
+    query_f = call(
+        query_kernel,
+        (pairs,),
+        [],
+        [grad_sf, land],
+        [factor_pair, lk_pair],
+        tokens,
+        token_pair,
+        flops=2 << 30,
+        name="query_grad",
+    )
     land_sum, weights, query_f, there = lax.optimization_barrier((land_sum, weights, query_f, there))
     land_sum, weights, grad_sb = lax.optimization_barrier((land_sum, weights, grad_sb))
     key_b, value_grad = call(

time: 121 us -> 119 us (0.983)
  waiting for transfers between devices: 20.1 us -> 17.9 us
    ppermute x35, waiting for transfers between devices: 20.1 us -> 17.9 us  [exchange(): return lax.ppermute(block, 'seq', [(i, i ^ mask) for i in range(n)])]
  transfers between devices with their start and end apart: 36 -> 36, of which waited for: 14 -> 15; matrix products, arithmetic and copies ran while one was open for 4% -> 5% of each run, Pallas kernels for 23% -> 24%
where the time goes in v9:
time: 119 us
  Pallas kernels  47.3 us (40%)
  starting transfers between devices  46.8 us (39%)
  waiting for transfers between devices  17.9 us (15%)
  other arithmetic  2.92 us (2%)
  matrix products  2.87 us (2%)
    pallas_call x14, Pallas kernels, call(): pl.pallas_call(kernel, grid_spec=pltpu.PrefetchScalarGridSpec(num_scalar_...  47.3 us
    ppermute x35, starting transfers between devices, exchange(): return lax.ppermute(block, 'seq', [(i, i ^ mask) for i in range(n)])  46.8 us
    ppermute x35, waiting for transfers between devices, exchange(): return lax.ppermute(block, 'seq', [(i, i ^ mask) for i in range(n)])  17.9 us
    dot_general x1, matrix products, dot(): lax.dot_general(left, right, (dims, ((), ())), preferred_element_type=F32)  2.87 us
    convert_element_type x2, other arithmetic, finish(): return (token_part.reshape(land_dev, seg_len, columns) + land_part[:, Non...  2.38 us
  transfers between devices with their start and end apart: 36, of which 15 were waited for; matrix products, arithmetic and copies ran while one was open for 5% of the time, Pallas kernels for 24%

profile of v9, /device:TPU:0, one launch (start us, length us, event | category | flops | bytes accessed | tf_op | source)
XLA Modules:
  0.0 119.0 jit_solution(9347263019211065942)
XLA Ops:
  0.8 1.7 %means.1 = bf16[16,1024]{1,0:T(8,128)(2,1)S(1)} custom-call(bf16[1024,512]{1,0:T(8,128)(2,1)} %q_ref.5, bf16[1024,512]{1,0:T(8,128)(2,1)} %k_ref.4), custom_call_target="tpu_custom_call" | custom-call | bytes 4194304 | tf_op jit(solution)/shard_map/means/pallas_call | solution.py:489
  2.5 5.1 %collective-permute-start.2 = (bf16[1,16,1024]{2,1,0:T(8,128)(2,1)S(1)}, bf16[1,16,1024]{2,1,0:T(8,128)(2,1)S(1)}, u32[]{:S(2)}, u32[]{:S(2)}) collective-permute-start(bf16[1,16,1024]{2,1,0:T(8,128)(2,1)S(1)} %bitcast.50), channel_id=1, source_target_pairs={{0,24},{2,26},{4,28},{6,30},{8,16},{10,18},{12,20},{14,22},{16,8},... | collective-permute-start | bytes 98312 | tf_op jit(solution)/shard_map/ppermute | solution.py:61
  9.5 2.9 %collective-permute-done.1 = bf16[1,16,1024]{2,1,0:T(8,128)(2,1)S(1)} collective-permute-done((bf16[1,16,1024]{2,1,0:T(8,128)(2,1)S(1)}, bf16[1,16,1024]{2,1,0:T(8,128)(2,1)S(1)}, u32[]{:S(2)}, u32[]{:S(2)}) %collective-permute-start.1) | collective-permute-done | bytes 32800 | tf_op jit(solution)/shard_map/ppermute | solution.py:61
  12.5 1.6 %collective-permute-start.3 = (bf16[4,16,1024]{2,1,0:T(8,128)(2,1)S(1)}, bf16[4,16,1024]{2,1,0:T(8,128)(2,1)S(1)}, u32[]{:S(2)}, u32[]{:S(2)}) collective-permute-start(bf16[4,16,1024]{2,1,0:T(8,128)(2,1)S(1)} %maximum_bitcast_fusion.2.refs_0_), channel_id=1, source_target_pairs={{0,2},{2,0},{4,6},{6,4},{8,10},{10,8},{12,14},{14,12},{16,18},{18,... | collective-permute-start | bytes 393224 | tf_op jit(solution)/shard_map/ppermute | solution.py:61
  14.0 1.5 %collective-permute-start.4 = (bf16[4,16,1024]{2,1,0:T(8,128)(2,1)S(1)}, bf16[4,16,1024]{2,1,0:T(8,128)(2,1)S(1)}, u32[]{:S(2)}, u32[]{:S(2)}) collective-permute-start(bf16[4,16,1024]{2,1,0:T(8,128)(2,1)S(1)} %maximum_bitcast_fusion.2.refs_0_), channel_id=1, source_target_pairs={{0,4},{2,6},{4,0},{6,2},{8,12},{10,14},{12,8},{14,10},{16,20},{18,... | collective-permute-start | bytes 393224 | tf_op jit(solution)/shard_map/ppermute | solution.py:61
  16.0 2.9 %convolution_convert_fusion.g_ref = bf16[1024,512]{1,0:T(8,128)(2,1)S(1)} fusion(bf16[1024,1024]{1,0:T(8,128)(2,1)} %cot_ref.1, bf16[512,1024]{1,0:T(8,128)(2,1)S(1)} %copy-done), kind=kOutput, calls=%fused_computation.4 | convolution fusion | flops 1074266112 | bytes 4194304 | tf_op jit(solution)/shard_map/dot_general | solution.py:23
  20.0 1.5 %collective-permute-done.5.refs_3_ = bf16[4,16,1024]{2,1,0:T(8,128)(2,1)S(1)} collective-permute-done((bf16[4,16,1024]{2,1,0:T(8,128)(2,1)S(1)}, bf16[4,16,1024]{2,1,0:T(8,128)(2,1)S(1)}, u32[]{:S(2)}, u32[]{:S(2)}) %collective-permute-start.5) | collective-permute-done | bytes 131104 | tf_op jit(solution)/shard_map/ppermute | solution.py:61
  21.4 10.0 %forward.1 = (bf16[1024,2048]{1,0:T(8,128)(2,1)S(1)}, bf16[1024,2048]{1,0:T(8,128)(2,1)S(1)}, f32[4,8,256]{2,1,0:T(8,128)S(1)}, bf16[256,1024]{1,0:T(8,128)(2,1)...) custom-call(s32[2]{0:T(128)S(1)} %pad_add_fusion.me_ref, ...), custom_call_target="tpu_custom_call" | custom-call | flops 8589934592 | bytes 4194304 | tf_op jit(solution)/shard_map/forward/pallas_call | solution.py:489
  32.6 2.4 %collective-permute-start.8 = (bf16[4,72,256]{2,1,0:T(8,128)(2,1)S(1)}, bf16[4,72,256]{2,1,0:T(8,128)(2,1)S(1)}, u32[]{:S(2)}, u32[]{:S(2)}) collective-permute-start(bf16[4,72,256]{2,1,0:T(8,128)(2,1)S(1)} %get-tuple-element.103), channel_id=1, source_target_pairs={{0,6},{2,4},{4,2},{6,0},{8,14},{10,12},{12,10},{14,8},{16,22},{18,... | collective-permute-start | bytes 442376 | tf_op jit(solution)/shard_map/ppermute | solution.py:61
  35.0 3.6 %newton.1 = (f32[9,256,256]{2,1,0:T(8,128)S(1)}, f32[1,256,256]{2,1,0:T(8,128)S(1)}) custom-call(s32[3]{0:T(128)S(1)} %pad_add_fusion.1.own_ref, bf16[256,1024]{1,0:T(8,128)(2,1)S(1)} %get-tuple-element.104.lq_ref.lk_ref, bf16[256,1024]{1,0:T(8,128)(2,1)S(1)} %get-tuple-element.104.lq_ref.lk_ref), custom_call_target="tpu_custom_call" | custom-call | flops 4294967296 | bytes 4194304 | tf_op jit(solution)/shard_map/newton/pallas_call | solution.py:489
  39.1 2.2 %collective-permute-start.10 = (bf16[1,72,256]{2,1,0:T(8,128)(2,1)S(1)}, bf16[1,72,256]{2,1,0:T(8,128)(2,1)S(1)}, u32[]{:S(2)}, u32[]{:S(2)}) collective-permute-start(bf16[1,72,256]{2,1,0:T(8,128)(2,1)S(1)} %get-tuple-element.112), channel_id=1, source_target_pairs={{0,16},{2,18},{4,20},{6,22},{8,24},{10,26},{12,28},{14,30},{16,0},... | collective-permute-start | bytes 110600 | tf_op jit(solution)/shard_map/ppermute | solution.py:61
  41.3 2.1 %collective-permute-start.11 = (bf16[1,72,256]{2,1,0:T(8,128)(2,1)S(1)}, bf16[1,72,256]{2,1,0:T(8,128)(2,1)S(1)}, u32[]{:S(2)}, u32[]{:S(2)}) collective-permute-start(bf16[1,72,256]{2,1,0:T(8,128)(2,1)S(1)} %get-tuple-element.113), channel_id=1, source_target_pairs={{0,24},{2,26},{4,28},{6,30},{8,16},{10,18},{12,20},{14,22},{16,8},... | collective-permute-start | bytes 110600 | tf_op jit(solution)/shard_map/ppermute | solution.py:61
  44.0 3.1 %collective-permute-done.11.refs_3_ = bf16[1,72,256]{2,1,0:T(8,128)(2,1)S(1)} collective-permute-done((bf16[1,72,256]{2,1,0:T(8,128)(2,1)S(1)}, bf16[1,72,256]{2,1,0:T(8,128)(2,1)S(1)}, u32[]{:S(2)}, u32[]{:S(2)}) %collective-permute-start.11) | collective-permute-done | bytes 36896 | tf_op jit(solution)/shard_map/ppermute | solution.py:61
  47.4 2.2 %collective-permute-start.14 = (bf16[1,72,256]{2,1,0:T(8,128)(2,1)S(1)}, bf16[1,72,256]{2,1,0:T(8,128)(2,1)S(1)}, u32[]{:S(2)}, u32[]{:S(2)}) collective-permute-start(bf16[1,72,256]{2,1,0:T(8,128)(2,1)S(1)} %get-tuple-element.115), channel_id=1, source_target_pairs={{0,24},{2,26},{4,28},{6,30},{8,16},{10,18},{12,20},{14,22},{16,8},... | collective-permute-start | bytes 110600 | tf_op jit(solution)/shard_map/ppermute | solution.py:61
  49.6 2.3 %collective-permute-start.12 = (bf16[1,72,256]{2,1,0:T(8,128)(2,1)S(1)}, bf16[1,72,256]{2,1,0:T(8,128)(2,1)S(1)}, u32[]{:S(2)}, u32[]{:S(2)}) collective-permute-start(bf16[1,72,256]{2,1,0:T(8,128)(2,1)S(1)} %get-tuple-element.115), channel_id=1, source_target_pairs={{0,8},{2,10},{4,12},{6,14},{8,0},{10,2},{12,4},{14,6},{16,24},{18,... | collective-permute-start | bytes 110600 | tf_op jit(solution)/shard_map/ppermute | solution.py:61
  51.8 1.4 %collective-permute-done.14 = bf16[1,72,256]{2,1,0:T(8,128)(2,1)S(1)} collective-permute-done((bf16[1,72,256]{2,1,0:T(8,128)(2,1)S(1)}, bf16[1,72,256]{2,1,0:T(8,128)(2,1)S(1)}, u32[]{:S(2)}, u32[]{:S(2)}) %collective-permute-start.14) | collective-permute-done | bytes 36896 | tf_op jit(solution)/shard_map/ppermute | solution.py:61
  54.5 2.1 %collective-permute-start.15 = (bf16[4,72,256]{2,1,0:T(8,128)(2,1)S(1)}, bf16[4,72,256]{2,1,0:T(8,128)(2,1)S(1)}, u32[]{:S(2)}, u32[]{:S(2)}) collective-permute-start(bf16[4,72,256]{2,1,0:T(8,128)(2,1)S(1)} %maximum_bitcast_fusion.1.refs_0_), channel_id=1, source_target_pairs={{0,2},{2,0},{4,6},{6,4},{8,10},{10,8},{12,14},{14,12},{16,18},{18,... | collective-permute-start | bytes 442376 | tf_op jit(solution)/shard_map/ppermute | solution.py:61
  58.1 4.3 %newton_grad.1 = (f32[256,128]{1,0:T(8,128)S(1)}, f32[256,128]{1,0:T(8,128)S(1)}) custom-call(s32[3]{0:T(128)S(1)} %pad_add_fusion.1.own_ref, f32[9,256,256]{2,1,0:T(8,128)S(1)} %get-tuple-element.116.saved_ref, f32[32,256]{1,0:T(8,128)S(1)} %get-tuple-element.117.values_ref, f32[32,256]{1,0:T(8,128)S(1)} %get-tuple-element.118.grads_ref, ...), custom_call_target="tpu_custom_call" | custom-call | flops 8589934592 | bytes 4194304 | tf_op jit(solution)/shard_map/newton_grad/pallas_call | solution.py:489
  63.5 4.7 %attend.1 = (bf16[1024,512]{1,0:T(8,128)(2,1)S(1)}, bf16[512,256]{1,0:T(8,128)(2,1)S(1)}, bf16[512,256]{1,0:T(8,128)(2,1)S(1)}, f32[8,256]{1,0:T(8,128)S(1)}, bf...) custom-call(s32[2]{0:T(128)S(1)} %pad_add_fusion.me_ref, ...), custom_call_target="tpu_custom_call" | custom-call | flops 4294967296 | bytes 4194304 | tf_op jit(solution)/shard_map/attend/pallas_call | solution.py:489
  71.8 5.4 %query_land.1 = (bf16[256,512]{1,0:T(8,128)(2,1)S(1)}, bf16[1024,2048]{1,0:T(8,128)(2,1)S(1)}) custom-call(s32[3]{0:T(128)S(1)} %pad_add_fusion.1.own_ref, bf16[1024,512]{1,0:T(8,128)(2,1)S(1)} %copy-done.1, bf16[1024,512]{1,0:T(8,128)(2,1)S(1)} %convolution_convert_fusion.g_ref, bf16[1024,2048]{1,0:T(8,128)(2,1)S(1)} %get-tuple-element.98.fb_ref, ...), custom_call_target="tpu_custom_call" | custom-call | flops 4294967296 | bytes 4194304 | tf_op jit(solution)/shard_map/query_land/pallas_call | solution.py:489
  78.6 2.0 %collective-permute-start.23 = (bf16[1,32,1024]{2,1,0:T(8,128)(2,1)S(1)}, bf16[1,32,1024]{2,1,0:T(8,128)(2,1)S(1)}, u32[]{:S(2)}, u32[]{:S(2)}) collective-permute-start(bf16[1,32,1024]{2,1,0:T(8,128)(2,1)S(1)} %get-tuple-element.184), channel_id=1, source_target_pairs={{0,24},{2,26},{4,28},{6,30},{8,16},{10,18},{12,20},{14,22},{16,8},... | collective-permute-start | bytes 196616 | tf_op jit(solution)/shard_map/ppermute | solution.py:61
  83.0 4.6 %key_land.1 = (bf16[1024,2048]{1,0:T(8,128)(2,1)S(1)}, bf16[4,16,1024]{2,1,0:T(8,128)(2,1)S(1)}, bf16[4,16,1024]{2,1,0:T(8,128)(2,1)S(1)}, bf16[4,16,1024]{2,1,0:T(8,128)(2,1)S(1)}, bf16[4,16,1024]{2,1,0:T(8,128)(2,1)S(1)}) custom-call(s32[3]{0:T(128)S(1)} %pad_add_fusion.1.own_ref, bf16[1024,512]{1,0:T(8,128)(2,1)S(1)} %copy-done.2, ...), custom_call_target="tpu_custom_call" | custom-call | flops 4294967296 | bytes 4194304 | tf_op jit(solution)/shard_map/key_land/pallas_call | solution.py:489
  90.0 1.4 %collective-permute-start.24 = (bf16[4,16,1024]{2,1,0:T(8,128)(2,1)S(1)}, bf16[4,16,1024]{2,1,0:T(8,128)(2,1)S(1)}, u32[]{:S(2)}, u32[]{:S(2)}) collective-permute-start(bf16[4,16,1024]{2,1,0:T(8,128)(2,1)S(1)} %get-tuple-element.153), channel_id=1, source_target_pairs={{0,2},{2,0},{4,6},{6,4},{8,10},{10,8},{12,14},{14,12},{16,18},{18,... | collective-permute-start | bytes 393224 | tf_op jit(solution)/shard_map/ppermute | solution.py:61
  93.3 1.9 %collective-permute-start.28 = (bf16[1,32,1024]{2,1,0:T(8,128)(2,1)S(1)}, bf16[1,32,1024]{2,1,0:T(8,128)(2,1)S(1)}, u32[]{:S(2)}, u32[]{:S(2)}) collective-permute-start(bf16[1,32,1024]{2,1,0:T(8,128)(2,1)S(1)} %bitcast.58), channel_id=1, source_target_pairs={{0,16},{2,18},{4,20},{6,22},{8,24},{10,26},{12,28},{14,30},{16,0},... | collective-permute-start | bytes 196616 | tf_op jit(solution)/shard_map/ppermute | solution.py:61
  95.2 2.0 %collective-permute-start.29 = (bf16[1,32,1024]{2,1,0:T(8,128)(2,1)S(1)}, bf16[1,32,1024]{2,1,0:T(8,128)(2,1)S(1)}, u32[]{:S(2)}, u32[]{:S(2)}) collective-permute-start(bf16[1,32,1024]{2,1,0:T(8,128)(2,1)S(1)} %bitcast.59), channel_id=1, source_target_pairs={{0,24},{2,26},{4,28},{6,30},{8,16},{10,18},{12,20},{14,22},{16,8},... | collective-permute-start | bytes 196616 | tf_op jit(solution)/shard_map/ppermute | solution.py:61
  97.3 2.4 %query_grad.1 = bf16[1024,512]{1,0:T(8,128)(2,1)S(1)} custom-call(bf16[1024,2048]{1,0:T(8,128)(2,1)S(1)} %get-tuple-element.159.ds_ref, bf16[256,1024]{1,0:T(8,128)(2,1)S(1)} %get-tuple-element.104.lq_ref.lk_ref), custom_call_target="tpu_custom_call" | custom-call | flops 2147483648 | bytes 4194304 | tf_op jit(solution)/shard_map/query_grad/pallas_call | solution.py:489
  99.7 1.6 %collective-permute-done.29 = bf16[1,32,1024]{2,1,0:T(8,128)(2,1)S(1)} collective-permute-done((bf16[1,32,1024]{2,1,0:T(8,128)(2,1)S(1)}, bf16[1,32,1024]{2,1,0:T(8,128)(2,1)S(1)}, u32[]{:S(2)}, u32[]{:S(2)}) %collective-permute-start.29) | collective-permute-done | bytes 65568 | tf_op jit(solution)/shard_map/ppermute | solution.py:61
  103.1 1.9 %collective-permute-start.32 = (bf16[4,32,1024]{2,1,0:T(8,128)(2,1)S(1)}, bf16[4,32,1024]{2,1,0:T(8,128)(2,1)S(1)}, u32[]{:S(2)}, u32[]{:S(2)}) collective-permute-start(bf16[4,32,1024]{2,1,0:T(8,128)(2,1)S(1)} %maximum_bitcast_fusion.refs_0_), channel_id=1, source_target_pairs={{0,6},{2,4},{4,2},{6,0},{8,14},{10,12},{12,10},{14,8},{16,22},{18,... | collective-permute-start | bytes 786440 | tf_op jit(solution)/shard_map/ppermute | solution.py:61
  105.6 1.9 %collective-permute-start.35 = (bf16[1,16,1024]{2,1,0:T(8,128)(2,1)S(1)}, bf16[1,16,1024]{2,1,0:T(8,128)(2,1)S(1)}, u32[]{:S(2)}, u32[]{:S(2)}) collective-permute-start(bf16[1,16,1024]{2,1,0:T(8,128)(2,1)S(1)} %slice.47), channel_id=1, source_target_pairs={{0,16},{2,18},{4,20},{6,22},{8,24},{10,26},{12,28},{14,30},{16,0},... | collective-permute-start | bytes 98312 | tf_op jit(solution)/shard_map/ppermute | solution.py:61
  107.5 4.5 %key_grad.1 = (bf16[1024,512]{1,0:T(8,128)(2,1)S(1)}, bf16[1024,512]{1,0:T(8,128)(2,1)}) custom-call(bf16[1024,2048]{1,0:T(8,128)(2,1)S(1)} %get-tuple-element.176.ds_ref, bf16[1024,2048]{1,0:T(8,128)(2,1)S(1)} %get-tuple-element.137.pb_ref, bf16[256,1024]{1,0:T(8,128)(2,1)S(1)} %get-tuple-element.104.lq_ref.lk_ref, ...), custom_call_target="tpu_custom_call" | custom-call | flops 4294967296 | bytes 4194304 | tf_op jit(solution)/shard_map/key_grad/pallas_call | solution.py:489
  114.4 2.4 %mixed.1 = bf16[1024,512]{1,0:T(8,128)(2,1)} custom-call(s32[1]{0:T(128)} %bitcast.1._, bf16[1024,512]{1,0:T(8,128)(2,1)S(1)} %get-tuple-element.161.attn_ref, bf16[512,1024]{1,0:T(8,128)(2,1)S(1)} %copy-done, bf16[1024,512]{1,0:T(8,128)(2,1)S(1)} %collective-permute-done.33.other_ref), custom_call_target="tpu_custom_call" | custom-call | flops 1073741824 | bytes 4194304 | tf_op jit(solution)/shard_map/mixed/pallas_call | solution.py:489
  116.8 2.0 %unpack.1 = f32[512,1024]{1,0:T(8,128)} custom-call(s32[2]{0:T(128)S(1)} %pad_add_fusion.me_ref, bf16[4,32,1024]{2,1,0:T(8,128)(2,1)S(1)} %maximum_bitcast_fusion.refs_0_, bf16[4,32,1024]{2,1,0:T(8,128)(2,1)S(1)} %collective-permute-done.30.refs_1_, bf16[4,32,1024]{2,1,0:T(8,128)(2,1)S(1)} %collective-permute-done.31.refs_2_, ...), custom_call_target="tpu_custom_call" | custom-call | bytes 4194304 | tf_op jit(solution)/shard_map/unpack/pallas_call | solution.py:489
  (81 shorter events, 26.5 us)
Async XLA Ops:
  2.5 7.0 %collective-permute-start.2 = (bf16[1,16,1024]{2,1,0:T(8,128)(2,1)S(1)}, bf16[1,16,1024]{2,1,0:T(8,128)(2,1)S(1)}, u32[]{:S(2)}, u32[]{:S(2)}) collective-permute-start(bf16[1,16,1024]{2,1,0:T(8,128)(2,1)S(1)} %bitcast.50), channel_id=1, source_target_pairs={{0,24},{2,26},{4,28},{6,30},{8,16},{10,18},{12,20},{14,22},{16,8},... | collective-permute-start | bytes 98312 | tf_op jit(solution)/shard_map/ppermute | solution.py:61
  12.5 6.4 %collective-permute-start.3 = (bf16[4,16,1024]{2,1,0:T(8,128)(2,1)S(1)}, bf16[4,16,1024]{2,1,0:T(8,128)(2,1)S(1)}, u32[]{:S(2)}, u32[]{:S(2)}) collective-permute-start(bf16[4,16,1024]{2,1,0:T(8,128)(2,1)S(1)} %maximum_bitcast_fusion.2.refs_0_), channel_id=1, source_target_pairs={{0,2},{2,0},{4,6},{6,4},{8,10},{10,8},{12,14},{14,12},{16,18},{18,... | collective-permute-start | bytes 393224 | tf_op jit(solution)/shard_map/ppermute | solution.py:61
  14.0 5.9 %collective-permute-start.4 = (bf16[4,16,1024]{2,1,0:T(8,128)(2,1)S(1)}, bf16[4,16,1024]{2,1,0:T(8,128)(2,1)S(1)}, u32[]{:S(2)}, u32[]{:S(2)}) collective-permute-start(bf16[4,16,1024]{2,1,0:T(8,128)(2,1)S(1)} %maximum_bitcast_fusion.2.refs_0_), channel_id=1, source_target_pairs={{0,4},{2,6},{4,0},{6,2},{8,12},{10,14},{12,8},{14,10},{16,20},{18,... | collective-permute-start | bytes 393224 | tf_op jit(solution)/shard_map/ppermute | solution.py:61
  15.6 5.9 %collective-permute-start.5 = (bf16[4,16,1024]{2,1,0:T(8,128)(2,1)S(1)}, bf16[4,16,1024]{2,1,0:T(8,128)(2,1)S(1)}, u32[]{:S(2)}, u32[]{:S(2)}) collective-permute-start(bf16[4,16,1024]{2,1,0:T(8,128)(2,1)S(1)} %maximum_bitcast_fusion.2.refs_0_), channel_id=1, source_target_pairs={{0,6},{2,4},{4,2},{6,0},{8,14},{10,12},{12,10},{14,8},{16,22},{18,... | collective-permute-start | bytes 393224 | tf_op jit(solution)/shard_map/ppermute | solution.py:61
  31.5 7.2 %collective-permute-start.6 = (bf16[4,72,256]{2,1,0:T(8,128)(2,1)S(1)}, bf16[4,72,256]{2,1,0:T(8,128)(2,1)S(1)}, u32[]{:S(2)}, u32[]{:S(2)}) collective-permute-start(bf16[4,72,256]{2,1,0:T(8,128)(2,1)S(1)} %get-tuple-element.101), channel_id=1, source_target_pairs={{0,2},{2,0},{4,6},{6,4},{8,10},{10,8},{12,14},{14,12},{16,18},{18,... | collective-permute-start | bytes 442376 | tf_op jit(solution)/shard_map/ppermute | solution.py:61
  32.1 6.7 %collective-permute-start.7 = (bf16[4,72,256]{2,1,0:T(8,128)(2,1)S(1)}, bf16[4,72,256]{2,1,0:T(8,128)(2,1)S(1)}, u32[]{:S(2)}, u32[]{:S(2)}) collective-permute-start(bf16[4,72,256]{2,1,0:T(8,128)(2,1)S(1)} %get-tuple-element.102), channel_id=1, source_target_pairs={{0,4},{2,6},{4,0},{6,2},{8,12},{10,14},{12,8},{14,10},{16,20},{18,... | collective-permute-start | bytes 442376 | tf_op jit(solution)/shard_map/ppermute | solution.py:61
  32.6 6.2 %collective-permute-start.8 = (bf16[4,72,256]{2,1,0:T(8,128)(2,1)S(1)}, bf16[4,72,256]{2,1,0:T(8,128)(2,1)S(1)}, u32[]{:S(2)}, u32[]{:S(2)}) collective-permute-start(bf16[4,72,256]{2,1,0:T(8,128)(2,1)S(1)} %get-tuple-element.103), channel_id=1, source_target_pairs={{0,6},{2,4},{4,2},{6,0},{8,14},{10,12},{12,10},{14,8},{16,22},{18,... | collective-permute-start | bytes 442376 | tf_op jit(solution)/shard_map/ppermute | solution.py:61
  39.1 4.9 %collective-permute-start.10 = (bf16[1,72,256]{2,1,0:T(8,128)(2,1)S(1)}, bf16[1,72,256]{2,1,0:T(8,128)(2,1)S(1)}, u32[]{:S(2)}, u32[]{:S(2)}) collective-permute-start(bf16[1,72,256]{2,1,0:T(8,128)(2,1)S(1)} %get-tuple-element.112), channel_id=1, source_target_pairs={{0,16},{2,18},{4,20},{6,22},{8,24},{10,26},{12,28},{14,30},{16,0},... | collective-permute-start | bytes 110600 | tf_op jit(solution)/shard_map/ppermute | solution.py:61
  41.3 5.8 %collective-permute-start.11 = (bf16[1,72,256]{2,1,0:T(8,128)(2,1)S(1)}, bf16[1,72,256]{2,1,0:T(8,128)(2,1)S(1)}, u32[]{:S(2)}, u32[]{:S(2)}) collective-permute-start(bf16[1,72,256]{2,1,0:T(8,128)(2,1)S(1)} %get-tuple-element.113), channel_id=1, source_target_pairs={{0,24},{2,26},{4,28},{6,30},{8,16},{10,18},{12,20},{14,22},{16,8},... | collective-permute-start | bytes 110600 | tf_op jit(solution)/shard_map/ppermute | solution.py:61
  47.4 5.8 %collective-permute-start.14 = (bf16[1,72,256]{2,1,0:T(8,128)(2,1)S(1)}, bf16[1,72,256]{2,1,0:T(8,128)(2,1)S(1)}, u32[]{:S(2)}, u32[]{:S(2)}) collective-permute-start(bf16[1,72,256]{2,1,0:T(8,128)(2,1)S(1)} %get-tuple-element.115), channel_id=1, source_target_pairs={{0,24},{2,26},{4,28},{6,30},{8,16},{10,18},{12,20},{14,22},{16,8},... | collective-permute-start | bytes 110600 | tf_op jit(solution)/shard_map/ppermute | solution.py:61
  49.6 4.9 %collective-permute-start.13 = (bf16[1,72,256]{2,1,0:T(8,128)(2,1)S(1)}, bf16[1,72,256]{2,1,0:T(8,128)(2,1)S(1)}, u32[]{:S(2)}, u32[]{:S(2)}) collective-permute-start(bf16[1,72,256]{2,1,0:T(8,128)(2,1)S(1)} %get-tuple-element.115), channel_id=1, source_target_pairs={{0,16},{2,18},{4,20},{6,22},{8,24},{10,26},{12,28},{14,30},{16,0},... | collective-permute-start | bytes 110600 | tf_op jit(solution)/shard_map/ppermute | solution.py:61
  49.6 4.9 %collective-permute-start.12 = (bf16[1,72,256]{2,1,0:T(8,128)(2,1)S(1)}, bf16[1,72,256]{2,1,0:T(8,128)(2,1)S(1)}, u32[]{:S(2)}, u32[]{:S(2)}) collective-permute-start(bf16[1,72,256]{2,1,0:T(8,128)(2,1)S(1)} %get-tuple-element.115), channel_id=1, source_target_pairs={{0,8},{2,10},{4,12},{6,14},{8,0},{10,2},{12,4},{14,6},{16,24},{18,... | collective-permute-start | bytes 110600 | tf_op jit(solution)/shard_map/ppermute | solution.py:61
  54.5 7.9 %collective-permute-start.15 = (bf16[4,72,256]{2,1,0:T(8,128)(2,1)S(1)}, bf16[4,72,256]{2,1,0:T(8,128)(2,1)S(1)}, u32[]{:S(2)}, u32[]{:S(2)}) collective-permute-start(bf16[4,72,256]{2,1,0:T(8,128)(2,1)S(1)} %maximum_bitcast_fusion.1.refs_0_), channel_id=1, source_target_pairs={{0,2},{2,0},{4,6},{6,4},{8,10},{10,8},{12,14},{14,12},{16,18},{18,... | collective-permute-start | bytes 442376 | tf_op jit(solution)/shard_map/ppermute | solution.py:61
  56.5 5.8 %collective-permute-start.16 = (bf16[4,72,256]{2,1,0:T(8,128)(2,1)S(1)}, bf16[4,72,256]{2,1,0:T(8,128)(2,1)S(1)}, u32[]{:S(2)}, u32[]{:S(2)}) collective-permute-start(bf16[4,72,256]{2,1,0:T(8,128)(2,1)S(1)} %maximum_bitcast_fusion.1.refs_0_), channel_id=1, source_target_pairs={{0,4},{2,6},{4,0},{6,2},{8,12},{10,14},{12,8},{14,10},{16,20},{18,... | collective-permute-start | bytes 442376 | tf_op jit(solution)/shard_map/ppermute | solution.py:61
  57.5 6.0 %collective-permute-start.17 = (bf16[4,72,256]{2,1,0:T(8,128)(2,1)S(1)}, bf16[4,72,256]{2,1,0:T(8,128)(2,1)S(1)}, u32[]{:S(2)}, u32[]{:S(2)}) collective-permute-start(bf16[4,72,256]{2,1,0:T(8,128)(2,1)S(1)} %maximum_bitcast_fusion.1.refs_0_), channel_id=1, source_target_pairs={{0,6},{2,4},{4,2},{6,0},{8,14},{10,12},{12,10},{14,8},{16,22},{18,... | collective-permute-start | bytes 442376 | tf_op jit(solution)/shard_map/ppermute | solution.py:61
  68.2 9.0 %collective-permute-start.20 = (bf16[4,32,1024]{2,1,0:T(8,128)(2,1)S(1)}, bf16[4,32,1024]{2,1,0:T(8,128)(2,1)S(1)}, u32[]{:S(2)}, u32[]{:S(2)}) collective-permute-start(bf16[4,32,1024]{2,1,0:T(8,128)(2,1)S(1)} %get-tuple-element.128), channel_id=1, source_target_pairs={{0,6},{2,4},{4,2},{6,0},{8,14},{10,12},{12,10},{14,8},{16,22},{18,... | collective-permute-start | bytes 786440 | tf_op jit(solution)/shard_map/ppermute | solution.py:61
  69.5 8.9 %collective-permute-start.19 = (bf16[4,32,1024]{2,1,0:T(8,128)(2,1)S(1)}, bf16[4,32,1024]{2,1,0:T(8,128)(2,1)S(1)}, u32[]{:S(2)}, u32[]{:S(2)}) collective-permute-start(bf16[4,32,1024]{2,1,0:T(8,128)(2,1)S(1)} %get-tuple-element.127), channel_id=1, source_target_pairs={{0,4},{2,6},{4,0},{6,2},{8,12},{10,14},{12,8},{14,10},{16,20},{18,... | collective-permute-start | bytes 786440 | tf_op jit(solution)/shard_map/ppermute | solution.py:61
  70.5 7.8 %collective-permute-start.18 = (bf16[4,32,1024]{2,1,0:T(8,128)(2,1)S(1)}, bf16[4,32,1024]{2,1,0:T(8,128)(2,1)S(1)}, u32[]{:S(2)}, u32[]{:S(2)}) collective-permute-start(bf16[4,32,1024]{2,1,0:T(8,128)(2,1)S(1)} %get-tuple-element.126), channel_id=1, source_target_pairs={{0,2},{2,0},{4,6},{6,4},{8,10},{10,8},{12,14},{14,12},{16,18},{18,... | collective-permute-start | bytes 786440 | tf_op jit(solution)/shard_map/ppermute | solution.py:61
  78.6 9.1 %collective-permute-start.23 = (bf16[1,32,1024]{2,1,0:T(8,128)(2,1)S(1)}, bf16[1,32,1024]{2,1,0:T(8,128)(2,1)S(1)}, u32[]{:S(2)}, u32[]{:S(2)}) collective-permute-start(bf16[1,32,1024]{2,1,0:T(8,128)(2,1)S(1)} %get-tuple-element.184), channel_id=1, source_target_pairs={{0,24},{2,26},{4,28},{6,30},{8,16},{10,18},{12,20},{14,22},{16,8},... | collective-permute-start | bytes 196616 | tf_op jit(solution)/shard_map/ppermute | solution.py:61
  80.6 7.1 %collective-permute-start.22 = (bf16[1,32,1024]{2,1,0:T(8,128)(2,1)S(1)}, bf16[1,32,1024]{2,1,0:T(8,128)(2,1)S(1)}, u32[]{:S(2)}, u32[]{:S(2)}) collective-permute-start(bf16[1,32,1024]{2,1,0:T(8,128)(2,1)S(1)} %get-tuple-element.185), channel_id=1, source_target_pairs={{0,16},{2,18},{4,20},{6,22},{8,24},{10,26},{12,28},{14,30},{16,0},... | collective-permute-start | bytes 196616 | tf_op jit(solution)/shard_map/ppermute | solution.py:61
  81.7 6.2 %collective-permute-start.21 = (bf16[1,32,1024]{2,1,0:T(8,128)(2,1)S(1)}, bf16[1,32,1024]{2,1,0:T(8,128)(2,1)S(1)}, u32[]{:S(2)}, u32[]{:S(2)}) collective-permute-start(bf16[1,32,1024]{2,1,0:T(8,128)(2,1)S(1)} %get-tuple-element.183), channel_id=1, source_target_pairs={{0,8},{2,10},{4,12},{6,14},{8,0},{10,2},{12,4},{14,6},{16,24},{18,... | collective-permute-start | bytes 196616 | tf_op jit(solution)/shard_map/ppermute | solution.py:61
  87.9 7.3 %collective-permute-start.26 = (bf16[4,16,1024]{2,1,0:T(8,128)(2,1)S(1)}, bf16[4,16,1024]{2,1,0:T(8,128)(2,1)S(1)}, u32[]{:S(2)}, u32[]{:S(2)}) collective-permute-start(bf16[4,16,1024]{2,1,0:T(8,128)(2,1)S(1)} %get-tuple-element.155), channel_id=1, source_target_pairs={{0,6},{2,4},{4,2},{6,0},{8,14},{10,12},{12,10},{14,8},{16,22},{18,... | collective-permute-start | bytes 393224 | tf_op jit(solution)/shard_map/ppermute | solution.py:61
  89.0 8.2 %collective-permute-start.25 = (bf16[4,16,1024]{2,1,0:T(8,128)(2,1)S(1)}, bf16[4,16,1024]{2,1,0:T(8,128)(2,1)S(1)}, u32[]{:S(2)}, u32[]{:S(2)}) collective-permute-start(bf16[4,16,1024]{2,1,0:T(8,128)(2,1)S(1)} %get-tuple-element.154), channel_id=1, source_target_pairs={{0,4},{2,6},{4,0},{6,2},{8,12},{10,14},{12,8},{14,10},{16,20},{18,... | collective-permute-start | bytes 393224 | tf_op jit(solution)/shard_map/ppermute | solution.py:61
  90.0 7.2 %collective-permute-start.24 = (bf16[4,16,1024]{2,1,0:T(8,128)(2,1)S(1)}, bf16[4,16,1024]{2,1,0:T(8,128)(2,1)S(1)}, u32[]{:S(2)}, u32[]{:S(2)}) collective-permute-start(bf16[4,16,1024]{2,1,0:T(8,128)(2,1)S(1)} %get-tuple-element.153), channel_id=1, source_target_pairs={{0,2},{2,0},{4,6},{6,4},{8,10},{10,8},{12,14},{14,12},{16,18},{18,... | collective-permute-start | bytes 393224 | tf_op jit(solution)/shard_map/ppermute | solution.py:61
  92.7 7.0 %collective-permute-start.27 = (bf16[1,32,1024]{2,1,0:T(8,128)(2,1)S(1)}, bf16[1,32,1024]{2,1,0:T(8,128)(2,1)S(1)}, u32[]{:S(2)}, u32[]{:S(2)}) collective-permute-start(bf16[1,32,1024]{2,1,0:T(8,128)(2,1)S(1)} %bitcast.57), channel_id=1, source_target_pairs={{0,8},{2,10},{4,12},{6,14},{8,0},{10,2},{12,4},{14,6},{16,24},{18,... | collective-permute-start | bytes 196616 | tf_op jit(solution)/shard_map/ppermute | solution.py:61
  93.3 6.4 %collective-permute-start.28 = (bf16[1,32,1024]{2,1,0:T(8,128)(2,1)S(1)}, bf16[1,32,1024]{2,1,0:T(8,128)(2,1)S(1)}, u32[]{:S(2)}, u32[]{:S(2)}) collective-permute-start(bf16[1,32,1024]{2,1,0:T(8,128)(2,1)S(1)} %bitcast.58), channel_id=1, source_target_pairs={{0,16},{2,18},{4,20},{6,22},{8,24},{10,26},{12,28},{14,30},{16,0},... | collective-permute-start | bytes 196616 | tf_op jit(solution)/shard_map/ppermute | solution.py:61
  95.2 6.1 %collective-permute-start.29 = (bf16[1,32,1024]{2,1,0:T(8,128)(2,1)S(1)}, bf16[1,32,1024]{2,1,0:T(8,128)(2,1)S(1)}, u32[]{:S(2)}, u32[]{:S(2)}) collective-permute-start(bf16[1,32,1024]{2,1,0:T(8,128)(2,1)S(1)} %bitcast.59), channel_id=1, source_target_pairs={{0,24},{2,26},{4,28},{6,30},{8,16},{10,18},{12,20},{14,22},{16,8},... | collective-permute-start | bytes 196616 | tf_op jit(solution)/shard_map/ppermute | solution.py:61
  101.4 15.4 %collective-permute-start.30 = (bf16[4,32,1024]{2,1,0:T(8,128)(2,1)S(1)}, bf16[4,32,1024]{2,1,0:T(8,128)(2,1)S(1)}, u32[]{:S(2)}, u32[]{:S(2)}) collective-permute-start(bf16[4,32,1024]{2,1,0:T(8,128)(2,1)S(1)} %maximum_bitcast_fusion.refs_0_), channel_id=1, source_target_pairs={{0,2},{2,0},{4,6},{6,4},{8,10},{10,8},{12,14},{14,12},{16,18},{18,... | collective-permute-start | bytes 786440 | tf_op jit(solution)/shard_map/ppermute | solution.py:61
  102.2 14.6 %collective-permute-start.31 = (bf16[4,32,1024]{2,1,0:T(8,128)(2,1)S(1)}, bf16[4,32,1024]{2,1,0:T(8,128)(2,1)S(1)}, u32[]{:S(2)}, u32[]{:S(2)}) collective-permute-start(bf16[4,32,1024]{2,1,0:T(8,128)(2,1)S(1)} %maximum_bitcast_fusion.refs_0_), channel_id=1, source_target_pairs={{0,4},{2,6},{4,0},{6,2},{8,12},{10,14},{12,8},{14,10},{16,20},{18,... | collective-permute-start | bytes 786440 | tf_op jit(solution)/shard_map/ppermute | solution.py:61
  103.1 13.7 %collective-permute-start.32 = (bf16[4,32,1024]{2,1,0:T(8,128)(2,1)S(1)}, bf16[4,32,1024]{2,1,0:T(8,128)(2,1)S(1)}, u32[]{:S(2)}, u32[]{:S(2)}) collective-permute-start(bf16[4,32,1024]{2,1,0:T(8,128)(2,1)S(1)} %maximum_bitcast_fusion.refs_0_), channel_id=1, source_target_pairs={{0,6},{2,4},{4,2},{6,0},{8,14},{10,12},{12,10},{14,8},{16,22},{18,... | collective-permute-start | bytes 786440 | tf_op jit(solution)/shard_map/ppermute | solution.py:61
  104.9 9.5 %collective-permute-start.33 = (bf16[1024,512]{1,0:T(8,128)(2,1)S(1)}, bf16[1024,512]{1,0:T(8,128)(2,1)S(1)}, u32[]{:S(2)}, u32[]{:S(2)}) collective-permute-start(bf16[1024,512]{1,0:T(8,128)(2,1)S(1)} %part.1), channel_id=1, source_target_pairs={{0,1},{1,0},{2,3},{3,2},{4,5},{5,4},{6,7},{7,6},{8,9},{9,8},{10,11... | collective-permute-start | bytes 3145736 | tf_op jit(solution)/shard_map/ppermute | solution.py:767
  105.6 6.4 %collective-permute-start.35 = (bf16[1,16,1024]{2,1,0:T(8,128)(2,1)S(1)}, bf16[1,16,1024]{2,1,0:T(8,128)(2,1)S(1)}, u32[]{:S(2)}, u32[]{:S(2)}) collective-permute-start(bf16[1,16,1024]{2,1,0:T(8,128)(2,1)S(1)} %slice.47), channel_id=1, source_target_pairs={{0,16},{2,18},{4,20},{6,22},{8,24},{10,26},{12,28},{14,30},{16,0},... | collective-permute-start | bytes 98312 | tf_op jit(solution)/shard_map/ppermute | solution.py:61
  (9 other events, 66.1 us)

commit v10 on v8

--- a/solution.py
+++ b/solution.py
@@ -444,6 +444,17 @@
     ).astype(BF16)
 
 
+def finish_kernel(query_ref, key_ref, query_own_ref, key_own_ref, query_out_ref, key_out_ref):
+    for in_ref, own_ref, out_ref in (
+        (query_ref, query_own_ref, query_out_ref),
+        (key_ref, key_own_ref, key_out_ref),
+    ):
+        own = own_ref[...]
+        segments = (own.shape[0], in_ref.shape[0] // own.shape[0], PAIR)
+        total = in_ref[...].astype(F32).reshape(segments) + own[:, None, :]
+        out_ref[...] = total.reshape(in_ref.shape).astype(BF16)
+
+
 def part_kernel(_, attn_ref, weight_ref, out_ref):
     out_ref[...] = dot(attn_ref[...], weight_ref[...]).astype(BF16)
 
@@ -715,7 +726,18 @@
         flops=4 << 30,
         name="key_land",
     )
-    land_pieces, grad_sf, attn = lax.optimization_barrier((land_pieces, grad_sf, attn))
+    half = width // 2
+    row_block = pl.BlockSpec((rows // 4, columns), lambda j, _: (j, 0))
+    half_block = pl.BlockSpec((rows // 4, half), lambda j, _: (j, 0))
+
+    if not sorted_here:
+        land_pieces = split_by_partner(land_pieces[0].reshape(n, land_dev, 2 * columns), n, me)
+    weight_sum = weight_sum.reshape((-1, following) + weight_sum.shape[1:])
+    weight_own = scatter_pieces([weight_sum[:, m] for m in range(following)], n, later)[0].astype(BF16)
+    land_pieces, weight_own = lax.optimization_barrier((land_pieces, weight_own))
+    land_sum = scatter_step(land_pieces, shift, count, n).astype(BF16)
+    weights = gather_first(weight_own, n)
+    land_sum, grad_sf, attn = lax.optimization_barrier((land_sum, grad_sf, attn))
     query_f = call(
         query_kernel,
         (pairs,),
@@ -727,9 +749,6 @@
         flops=2 << 30,
         name="query_grad",
     )
-    half = width // 2
-    row_block = pl.BlockSpec((rows // 4, columns), lambda j, _: (j, 0))
-    half_block = pl.BlockSpec((rows // 4, half), lambda j, _: (j, 0))
     there = call(
         part_kernel,
         (4,),
@@ -741,14 +760,6 @@
         flops=1 << 30,
         name="part",
     )
-
-    if not sorted_here:
-        land_pieces = split_by_partner(land_pieces[0].reshape(n, land_dev, 2 * columns), n, me)
-    weight_sum = weight_sum.reshape((-1, following) + weight_sum.shape[1:])
-    weight_own = scatter_pieces([weight_sum[:, m] for m in range(following)], n, later)[0].astype(BF16)
-    land_pieces, weight_own = lax.optimization_barrier((land_pieces, weight_own))
-    land_sum = scatter_step(land_pieces, shift, count, n).astype(BF16)
-    weights = gather_first(weight_own, n)
     land_sum, weights, query_f, there = lax.optimization_barrier((land_sum, weights, query_f, there))
     land_sum, weights, grad_sb = lax.optimization_barrier((land_sum, weights, grad_sb))
     key_b, value_grad = call(
@@ -796,15 +807,19 @@
         name="unpack",
     )
 
-    def finish(token_part, land_part):
-        return (
-            (token_part.reshape(land_dev, seg_len, columns) + land_part[:, None, :])
-            .astype(BF16)
-            .reshape(rows, columns)
-        )
-
-    query_grad = finish(query_f, land_own[:, :columns])
-    key_grad = finish(key_b, land_own[:, columns:])
+    def own_pair(first):
+        return pl.BlockSpec((land_dev, PAIR), lambda j, *_: (0, j + first))
+
+    query_grad, key_grad = call(
+        finish_kernel,
+        (pairs,),
+        [],
+        [query_f, key_b, land_own, land_own],
+        [token_pair, token_pair, own_pair(0), own_pair(pairs)],
+        [tokens, tokens],
+        [token_pair, token_pair],
+        name="finish",
+    )
     return (mixed, query_grad, key_grad, value_grad, weight_grad)
 
 

time: 121 us -> 119 us (0.983)
  waiting for transfers between devices: 20.1 us -> 17.6 us
  other arithmetic: 2.92 us -> 0.54 us
  Pallas kernels: 47.3 us -> 49.5 us
    ppermute x35, waiting for transfers between devices: 20.1 us -> 17.6 us  [exchange(): return lax.ppermute(block, 'seq', [(i, i ^ mask) for i in range(n)])]
    convert_element_type x2 -> x0, other arithmetic: 2.38 us -> none  [finish(): return (token_part.reshape(land_dev, seg_len, columns) + land_part[:, Non...]
    pallas_call x14 -> x15, Pallas kernels: 47.3 us -> 49.5 us  [call(): pl.pallas_call(kernel, grid_spec=pltpu.PrefetchScalarGridSpec(num_scalar_...]
  transfers between devices with their start and end apart: 36 -> 36, of which waited for: 14 -> 14; matrix products, arithmetic and copies ran while one was open for 4% -> 3% of each run, Pallas kernels for 23% -> 26%
where the time goes in v10:
time: 119 us; the launch traced here: 118 us
  Pallas kernels  49.5 us (42%)
  starting transfers between devices  46.6 us (39%)
  waiting for transfers between devices  17.6 us (15%)
  matrix products  2.87 us (2%)
    pallas_call x15, Pallas kernels, call(): pl.pallas_call(kernel, grid_spec=pltpu.PrefetchScalarGridSpec(num_scalar_...  49.5 us
    ppermute x35, starting transfers between devices, exchange(): return lax.ppermute(block, 'seq', [(i, i ^ mask) for i in range(n)])  46.6 us
    ppermute x35, waiting for transfers between devices, exchange(): return lax.ppermute(block, 'seq', [(i, i ^ mask) for i in range(n)])  17.6 us
    dot_general x1, matrix products, dot(): lax.dot_general(left, right, (dims, ((), ())), preferred_element_type=F32)  2.87 us
  transfers between devices with their start and end apart: 36, of which 14 were waited for; matrix products, arithmetic and copies ran while one was open for 3% of the time, Pallas kernels for 26%

profile of v10, /device:TPU:0, one launch (start us, length us, event | category | flops | bytes accessed | tf_op | source)
XLA Modules:
  0.0 118.4 jit_solution(15822507598921285081)
XLA Ops:
  0.8 1.7 %means.1 = bf16[16,1024]{1,0:T(8,128)(2,1)S(1)} custom-call(bf16[1024,512]{1,0:T(8,128)(2,1)} %q_ref.5, bf16[1024,512]{1,0:T(8,128)(2,1)} %k_ref.4), custom_call_target="tpu_custom_call" | custom-call | bytes 4194304 | tf_op jit(solution)/shard_map/means/pallas_call | solution.py:500
  2.5 5.1 %collective-permute-start.2 = (bf16[1,16,1024]{2,1,0:T(8,128)(2,1)S(1)}, bf16[1,16,1024]{2,1,0:T(8,128)(2,1)S(1)}, u32[]{:S(2)}, u32[]{:S(2)}) collective-permute-start(bf16[1,16,1024]{2,1,0:T(8,128)(2,1)S(1)} %bitcast.42), channel_id=1, source_target_pairs={{0,24},{2,26},{4,28},{6,30},{8,16},{10,18},{12,20},{14,22},{16,8},... | collective-permute-start | bytes 98312 | tf_op jit(solution)/shard_map/ppermute | solution.py:61
  9.5 2.9 %collective-permute-done.1 = bf16[1,16,1024]{2,1,0:T(8,128)(2,1)S(1)} collective-permute-done((bf16[1,16,1024]{2,1,0:T(8,128)(2,1)S(1)}, bf16[1,16,1024]{2,1,0:T(8,128)(2,1)S(1)}, u32[]{:S(2)}, u32[]{:S(2)}) %collective-permute-start.1) | collective-permute-done | bytes 32800 | tf_op jit(solution)/shard_map/ppermute | solution.py:61
  12.5 1.6 %collective-permute-start.3 = (bf16[4,16,1024]{2,1,0:T(8,128)(2,1)S(1)}, bf16[4,16,1024]{2,1,0:T(8,128)(2,1)S(1)}, u32[]{:S(2)}, u32[]{:S(2)}) collective-permute-start(bf16[4,16,1024]{2,1,0:T(8,128)(2,1)S(1)} %maximum_bitcast_fusion.2.refs_0_), channel_id=1, source_target_pairs={{0,2},{2,0},{4,6},{6,4},{8,10},{10,8},{12,14},{14,12},{16,18},{18,... | collective-permute-start | bytes 393224 | tf_op jit(solution)/shard_map/ppermute | solution.py:61
  14.0 1.5 %collective-permute-start.4 = (bf16[4,16,1024]{2,1,0:T(8,128)(2,1)S(1)}, bf16[4,16,1024]{2,1,0:T(8,128)(2,1)S(1)}, u32[]{:S(2)}, u32[]{:S(2)}) collective-permute-start(bf16[4,16,1024]{2,1,0:T(8,128)(2,1)S(1)} %maximum_bitcast_fusion.2.refs_0_), channel_id=1, source_target_pairs={{0,4},{2,6},{4,0},{6,2},{8,12},{10,14},{12,8},{14,10},{16,20},{18,... | collective-permute-start | bytes 393224 | tf_op jit(solution)/shard_map/ppermute | solution.py:61
  16.0 2.9 %convolution_convert_fusion.g_ref = bf16[1024,512]{1,0:T(8,128)(2,1)S(1)} fusion(bf16[1024,1024]{1,0:T(8,128)(2,1)} %cot_ref.1, bf16[512,1024]{1,0:T(8,128)(2,1)S(1)} %copy-done), kind=kOutput, calls=%fused_computation | convolution fusion | flops 1074266112 | bytes 4194304 | tf_op jit(solution)/shard_map/dot_general | solution.py:23
  20.0 1.5 %collective-permute-done.5.refs_3_ = bf16[4,16,1024]{2,1,0:T(8,128)(2,1)S(1)} collective-permute-done((bf16[4,16,1024]{2,1,0:T(8,128)(2,1)S(1)}, bf16[4,16,1024]{2,1,0:T(8,128)(2,1)S(1)}, u32[]{:S(2)}, u32[]{:S(2)}) %collective-permute-start.5) | collective-permute-done | bytes 131104 | tf_op jit(solution)/shard_map/ppermute | solution.py:61
  21.4 10.0 %forward.1 = (bf16[1024,2048]{1,0:T(8,128)(2,1)S(1)}, bf16[1024,2048]{1,0:T(8,128)(2,1)S(1)}, f32[4,8,256]{2,1,0:T(8,128)S(1)}, bf16[256,1024]{1,0:T(8,128)(2,1)...) custom-call(s32[2]{0:T(128)S(1)} %pad_add_fusion.me_ref, ...), custom_call_target="tpu_custom_call" | custom-call | flops 8589934592 | bytes 4194304 | tf_op jit(solution)/shard_map/forward/pallas_call | solution.py:500
  32.6 2.4 %collective-permute-start.8 = (bf16[4,72,256]{2,1,0:T(8,128)(2,1)S(1)}, bf16[4,72,256]{2,1,0:T(8,128)(2,1)S(1)}, u32[]{:S(2)}, u32[]{:S(2)}) collective-permute-start(bf16[4,72,256]{2,1,0:T(8,128)(2,1)S(1)} %get-tuple-element.101), channel_id=1, source_target_pairs={{0,6},{2,4},{4,2},{6,0},{8,14},{10,12},{12,10},{14,8},{16,22},{18,... | collective-permute-start | bytes 442376 | tf_op jit(solution)/shard_map/ppermute | solution.py:61
  35.0 3.6 %newton.1 = (f32[9,256,256]{2,1,0:T(8,128)S(1)}, f32[1,256,256]{2,1,0:T(8,128)S(1)}) custom-call(s32[3]{0:T(128)S(1)} %pad_add_fusion.1.own_ref, bf16[256,1024]{1,0:T(8,128)(2,1)S(1)} %get-tuple-element.102.lq_ref.lk_ref, bf16[256,1024]{1,0:T(8,128)(2,1)S(1)} %get-tuple-element.102.lq_ref.lk_ref), custom_call_target="tpu_custom_call" | custom-call | flops 4294967296 | bytes 4194304 | tf_op jit(solution)/shard_map/newton/pallas_call | solution.py:500
  39.1 2.2 %collective-permute-start.10 = (bf16[1,72,256]{2,1,0:T(8,128)(2,1)S(1)}, bf16[1,72,256]{2,1,0:T(8,128)(2,1)S(1)}, u32[]{:S(2)}, u32[]{:S(2)}) collective-permute-start(bf16[1,72,256]{2,1,0:T(8,128)(2,1)S(1)} %get-tuple-element.110), channel_id=1, source_target_pairs={{0,16},{2,18},{4,20},{6,22},{8,24},{10,26},{12,28},{14,30},{16,0},... | collective-permute-start | bytes 110600 | tf_op jit(solution)/shard_map/ppermute | solution.py:61
  41.3 2.1 %collective-permute-start.11 = (bf16[1,72,256]{2,1,0:T(8,128)(2,1)S(1)}, bf16[1,72,256]{2,1,0:T(8,128)(2,1)S(1)}, u32[]{:S(2)}, u32[]{:S(2)}) collective-permute-start(bf16[1,72,256]{2,1,0:T(8,128)(2,1)S(1)} %get-tuple-element.111), channel_id=1, source_target_pairs={{0,24},{2,26},{4,28},{6,30},{8,16},{10,18},{12,20},{14,22},{16,8},... | collective-permute-start | bytes 110600 | tf_op jit(solution)/shard_map/ppermute | solution.py:61
  44.0 3.1 %collective-permute-done.11.refs_3_ = bf16[1,72,256]{2,1,0:T(8,128)(2,1)S(1)} collective-permute-done((bf16[1,72,256]{2,1,0:T(8,128)(2,1)S(1)}, bf16[1,72,256]{2,1,0:T(8,128)(2,1)S(1)}, u32[]{:S(2)}, u32[]{:S(2)}) %collective-permute-start.11) | collective-permute-done | bytes 36896 | tf_op jit(solution)/shard_map/ppermute | solution.py:61
  47.4 2.2 %collective-permute-start.14 = (bf16[1,72,256]{2,1,0:T(8,128)(2,1)S(1)}, bf16[1,72,256]{2,1,0:T(8,128)(2,1)S(1)}, u32[]{:S(2)}, u32[]{:S(2)}) collective-permute-start(bf16[1,72,256]{2,1,0:T(8,128)(2,1)S(1)} %get-tuple-element.113), channel_id=1, source_target_pairs={{0,24},{2,26},{4,28},{6,30},{8,16},{10,18},{12,20},{14,22},{16,8},... | collective-permute-start | bytes 110600 | tf_op jit(solution)/shard_map/ppermute | solution.py:61
  49.6 2.3 %collective-permute-start.12 = (bf16[1,72,256]{2,1,0:T(8,128)(2,1)S(1)}, bf16[1,72,256]{2,1,0:T(8,128)(2,1)S(1)}, u32[]{:S(2)}, u32[]{:S(2)}) collective-permute-start(bf16[1,72,256]{2,1,0:T(8,128)(2,1)S(1)} %get-tuple-element.113), channel_id=1, source_target_pairs={{0,8},{2,10},{4,12},{6,14},{8,0},{10,2},{12,4},{14,6},{16,24},{18,... | collective-permute-start | bytes 110600 | tf_op jit(solution)/shard_map/ppermute | solution.py:61
  51.8 1.4 %collective-permute-done.14 = bf16[1,72,256]{2,1,0:T(8,128)(2,1)S(1)} collective-permute-done((bf16[1,72,256]{2,1,0:T(8,128)(2,1)S(1)}, bf16[1,72,256]{2,1,0:T(8,128)(2,1)S(1)}, u32[]{:S(2)}, u32[]{:S(2)}) %collective-permute-start.14) | collective-permute-done | bytes 36896 | tf_op jit(solution)/shard_map/ppermute | solution.py:61
  54.5 2.1 %collective-permute-start.15 = (bf16[4,72,256]{2,1,0:T(8,128)(2,1)S(1)}, bf16[4,72,256]{2,1,0:T(8,128)(2,1)S(1)}, u32[]{:S(2)}, u32[]{:S(2)}) collective-permute-start(bf16[4,72,256]{2,1,0:T(8,128)(2,1)S(1)} %maximum_bitcast_fusion.1.refs_0_), channel_id=1, source_target_pairs={{0,2},{2,0},{4,6},{6,4},{8,10},{10,8},{12,14},{14,12},{16,18},{18,... | collective-permute-start | bytes 442376 | tf_op jit(solution)/shard_map/ppermute | solution.py:61
  58.1 4.3 %newton_grad.1 = (f32[256,128]{1,0:T(8,128)S(1)}, f32[256,128]{1,0:T(8,128)S(1)}) custom-call(s32[3]{0:T(128)S(1)} %pad_add_fusion.1.own_ref, f32[9,256,256]{2,1,0:T(8,128)S(1)} %get-tuple-element.114.saved_ref, f32[32,256]{1,0:T(8,128)S(1)} %get-tuple-element.115.values_ref, f32[32,256]{1,0:T(8,128)S(1)} %get-tuple-element.116.grads_ref, ...), custom_call_target="tpu_custom_call" | custom-call | flops 8589934592 | bytes 4194304 | tf_op jit(solution)/shard_map/newton_grad/pallas_call | solution.py:500
  63.5 4.7 %attend.1 = (bf16[1024,512]{1,0:T(8,128)(2,1)S(1)}, bf16[512,256]{1,0:T(8,128)(2,1)S(1)}, bf16[512,256]{1,0:T(8,128)(2,1)S(1)}, f32[8,256]{1,0:T(8,128)S(1)}, bf...) custom-call(s32[2]{0:T(128)S(1)} %pad_add_fusion.me_ref, ...), custom_call_target="tpu_custom_call" | custom-call | flops 4294967296 | bytes 4194304 | tf_op jit(solution)/shard_map/attend/pallas_call | solution.py:500
  71.8 5.4 %query_land.1 = (bf16[256,512]{1,0:T(8,128)(2,1)S(1)}, bf16[1024,2048]{1,0:T(8,128)(2,1)S(1)}) custom-call(s32[3]{0:T(128)S(1)} %pad_add_fusion.1.own_ref, bf16[1024,512]{1,0:T(8,128)(2,1)S(1)} %copy-done.1, bf16[1024,512]{1,0:T(8,128)(2,1)S(1)} %convolution_convert_fusion.g_ref, bf16[1024,2048]{1,0:T(8,128)(2,1)S(1)} %get-tuple-element.96.fb_ref, ...), custom_call_target="tpu_custom_call" | custom-call | flops 4294967296 | bytes 4194304 | tf_op jit(solution)/shard_map/query_land/pallas_call | solution.py:500
  78.6 2.0 %collective-permute-start.23 = (bf16[1,32,1024]{2,1,0:T(8,128)(2,1)S(1)}, bf16[1,32,1024]{2,1,0:T(8,128)(2,1)S(1)}, u32[]{:S(2)}, u32[]{:S(2)}) collective-permute-start(bf16[1,32,1024]{2,1,0:T(8,128)(2,1)S(1)} %get-tuple-element.180), channel_id=1, source_target_pairs={{0,24},{2,26},{4,28},{6,30},{8,16},{10,18},{12,20},{14,22},{16,8},... | collective-permute-start | bytes 196616 | tf_op jit(solution)/shard_map/ppermute | solution.py:61
  83.0 4.6 %key_land.1 = (bf16[1024,2048]{1,0:T(8,128)(2,1)S(1)}, bf16[4,16,1024]{2,1,0:T(8,128)(2,1)S(1)}, bf16[4,16,1024]{2,1,0:T(8,128)(2,1)S(1)}, bf16[4,16,1024]{2,1,0:T(8,128)(2,1)S(1)}, bf16[4,16,1024]{2,1,0:T(8,128)(2,1)S(1)}) custom-call(s32[3]{0:T(128)S(1)} %pad_add_fusion.1.own_ref, bf16[1024,512]{1,0:T(8,128)(2,1)S(1)} %copy-done.2, ...), custom_call_target="tpu_custom_call" | custom-call | flops 4294967296 | bytes 4194304 | tf_op jit(solution)/shard_map/key_land/pallas_call | solution.py:500
  90.1 2.2 %collective-permute-start.24 = (bf16[4,16,1024]{2,1,0:T(8,128)(2,1)S(1)}, bf16[4,16,1024]{2,1,0:T(8,128)(2,1)S(1)}, u32[]{:S(2)}, u32[]{:S(2)}) collective-permute-start(bf16[4,16,1024]{2,1,0:T(8,128)(2,1)S(1)} %get-tuple-element.146), channel_id=1, source_target_pairs={{0,2},{2,0},{4,6},{6,4},{8,10},{10,8},{12,14},{14,12},{16,18},{18,... | collective-permute-start | bytes 393224 | tf_op jit(solution)/shard_map/ppermute | solution.py:61
  92.3 2.5 %collective-permute-start.28 = (bf16[1,32,1024]{2,1,0:T(8,128)(2,1)S(1)}, bf16[1,32,1024]{2,1,0:T(8,128)(2,1)S(1)}, u32[]{:S(2)}, u32[]{:S(2)}) collective-permute-start(bf16[1,32,1024]{2,1,0:T(8,128)(2,1)S(1)} %bitcast.50), channel_id=1, source_target_pairs={{0,16},{2,18},{4,20},{6,22},{8,24},{10,26},{12,28},{14,30},{16,0},... | collective-permute-start | bytes 196616 | tf_op jit(solution)/shard_map/ppermute | solution.py:61
  94.8 1.9 %collective-permute-start.29 = (bf16[1,32,1024]{2,1,0:T(8,128)(2,1)S(1)}, bf16[1,32,1024]{2,1,0:T(8,128)(2,1)S(1)}, u32[]{:S(2)}, u32[]{:S(2)}) collective-permute-start(bf16[1,32,1024]{2,1,0:T(8,128)(2,1)S(1)} %bitcast.51), channel_id=1, source_target_pairs={{0,24},{2,26},{4,28},{6,30},{8,16},{10,18},{12,20},{14,22},{16,8},... | collective-permute-start | bytes 196616 | tf_op jit(solution)/shard_map/ppermute | solution.py:61
  96.8 2.4 %query_grad.1.query_ref = bf16[1024,512]{1,0:T(8,128)(2,1)S(1)} custom-call(bf16[1024,2048]{1,0:T(8,128)(2,1)S(1)} %get-tuple-element.153.ds_ref, bf16[256,1024]{1,0:T(8,128)(2,1)S(1)} %get-tuple-element.102.lq_ref.lk_ref), custom_call_target="tpu_custom_call" | custom-call | flops 2147483648 | bytes 4194304 | tf_op jit(solution)/shard_map/query_grad/pallas_call | solution.py:500
  102.4 2.2 %collective-permute-start.32 = (bf16[4,32,1024]{2,1,0:T(8,128)(2,1)S(1)}, bf16[4,32,1024]{2,1,0:T(8,128)(2,1)S(1)}, u32[]{:S(2)}, u32[]{:S(2)}) collective-permute-start(bf16[4,32,1024]{2,1,0:T(8,128)(2,1)S(1)} %maximum_bitcast_fusion.refs_0_), channel_id=1, source_target_pairs={{0,6},{2,4},{4,2},{6,0},{8,14},{10,12},{12,10},{14,8},{16,22},{18,... | collective-permute-start | bytes 786440 | tf_op jit(solution)/shard_map/ppermute | solution.py:61
  105.4 1.7 %collective-permute-start.35 = (bf16[1,16,1024]{2,1,0:T(8,128)(2,1)S(1)}, bf16[1,16,1024]{2,1,0:T(8,128)(2,1)S(1)}, u32[]{:S(2)}, u32[]{:S(2)}) collective-permute-start(bf16[1,16,1024]{2,1,0:T(8,128)(2,1)S(1)} %slice.39), channel_id=1, source_target_pairs={{0,16},{2,18},{4,20},{6,22},{8,24},{10,26},{12,28},{14,30},{16,0},... | collective-permute-start | bytes 98312 | tf_op jit(solution)/shard_map/ppermute | solution.py:61
  107.1 4.5 %key_grad.1 = (bf16[1024,512]{1,0:T(8,128)(2,1)S(1)}, bf16[1024,512]{1,0:T(8,128)(2,1)}) custom-call(bf16[1024,2048]{1,0:T(8,128)(2,1)S(1)} %get-tuple-element.169.ds_ref, bf16[1024,2048]{1,0:T(8,128)(2,1)S(1)} %get-tuple-element.135.pb_ref, bf16[256,1024]{1,0:T(8,128)(2,1)S(1)} %get-tuple-element.102.lq_ref.lk_ref, ...), custom_call_target="tpu_custom_call" | custom-call | flops 4294967296 | bytes 4194304 | tf_op jit(solution)/shard_map/key_grad/pallas_call | solution.py:500
  111.6 2.2 %finish.1 = (bf16[1024,512]{1,0:T(8,128)(2,1)}, bf16[1024,512]{1,0:T(8,128)(2,1)}) custom-call(bf16[1024,512]{1,0:T(8,128)(2,1)S(1)} %query_grad.1.query_ref, bf16[1024,512]{1,0:T(8,128)(2,1)S(1)} %get-tuple-element.170.key_ref, f32[16,1024]{1,0:T(8,128)S(1)} %multiply_bitcast_fusion.query_own_ref.key_own_ref, ...), custom_call_target="tpu_custom_call" | custom-call | bytes 4194304 | tf_op jit(solution)/shard_map/finish/pallas_call | solution.py:500
  113.8 2.4 %mixed.1 = bf16[1024,512]{1,0:T(8,128)(2,1)} custom-call(s32[1]{0:T(128)} %bitcast.1._, bf16[1024,512]{1,0:T(8,128)(2,1)S(1)} %get-tuple-element.155.attn_ref, bf16[512,1024]{1,0:T(8,128)(2,1)S(1)} %copy-done, bf16[1024,512]{1,0:T(8,128)(2,1)S(1)} %collective-permute-done.33.other_ref), custom_call_target="tpu_custom_call" | custom-call | flops 1073741824 | bytes 4194304 | tf_op jit(solution)/shard_map/mixed/pallas_call | solution.py:500
  116.2 2.0 %unpack.1 = f32[512,1024]{1,0:T(8,128)} custom-call(s32[2]{0:T(128)S(1)} %pad_add_fusion.me_ref, bf16[4,32,1024]{2,1,0:T(8,128)(2,1)S(1)} %maximum_bitcast_fusion.refs_0_, bf16[4,32,1024]{2,1,0:T(8,128)(2,1)S(1)} %collective-permute-done.30.refs_1_, bf16[4,32,1024]{2,1,0:T(8,128)(2,1)S(1)} %collective-permute-done.31.refs_2_, ...), custom_call_target="tpu_custom_call" | custom-call | bytes 4194304 | tf_op jit(solution)/shard_map/unpack/pallas_call | solution.py:500
  (79 shorter events, 23.8 us)
Async XLA Ops:
  2.5 7.0 %collective-permute-start.2 = (bf16[1,16,1024]{2,1,0:T(8,128)(2,1)S(1)}, bf16[1,16,1024]{2,1,0:T(8,128)(2,1)S(1)}, u32[]{:S(2)}, u32[]{:S(2)}) collective-permute-start(bf16[1,16,1024]{2,1,0:T(8,128)(2,1)S(1)} %bitcast.42), channel_id=1, source_target_pairs={{0,24},{2,26},{4,28},{6,30},{8,16},{10,18},{12,20},{14,22},{16,8},... | collective-permute-start | bytes 98312 | tf_op jit(solution)/shard_map/ppermute | solution.py:61
  12.5 6.4 %collective-permute-start.3 = (bf16[4,16,1024]{2,1,0:T(8,128)(2,1)S(1)}, bf16[4,16,1024]{2,1,0:T(8,128)(2,1)S(1)}, u32[]{:S(2)}, u32[]{:S(2)}) collective-permute-start(bf16[4,16,1024]{2,1,0:T(8,128)(2,1)S(1)} %maximum_bitcast_fusion.2.refs_0_), channel_id=1, source_target_pairs={{0,2},{2,0},{4,6},{6,4},{8,10},{10,8},{12,14},{14,12},{16,18},{18,... | collective-permute-start | bytes 393224 | tf_op jit(solution)/shard_map/ppermute | solution.py:61
  14.0 5.9 %collective-permute-start.4 = (bf16[4,16,1024]{2,1,0:T(8,128)(2,1)S(1)}, bf16[4,16,1024]{2,1,0:T(8,128)(2,1)S(1)}, u32[]{:S(2)}, u32[]{:S(2)}) collective-permute-start(bf16[4,16,1024]{2,1,0:T(8,128)(2,1)S(1)} %maximum_bitcast_fusion.2.refs_0_), channel_id=1, source_target_pairs={{0,4},{2,6},{4,0},{6,2},{8,12},{10,14},{12,8},{14,10},{16,20},{18,... | collective-permute-start | bytes 393224 | tf_op jit(solution)/shard_map/ppermute | solution.py:61
  15.6 5.9 %collective-permute-start.5 = (bf16[4,16,1024]{2,1,0:T(8,128)(2,1)S(1)}, bf16[4,16,1024]{2,1,0:T(8,128)(2,1)S(1)}, u32[]{:S(2)}, u32[]{:S(2)}) collective-permute-start(bf16[4,16,1024]{2,1,0:T(8,128)(2,1)S(1)} %maximum_bitcast_fusion.2.refs_0_), channel_id=1, source_target_pairs={{0,6},{2,4},{4,2},{6,0},{8,14},{10,12},{12,10},{14,8},{16,22},{18,... | collective-permute-start | bytes 393224 | tf_op jit(solution)/shard_map/ppermute | solution.py:61
  31.5 7.2 %collective-permute-start.6 = (bf16[4,72,256]{2,1,0:T(8,128)(2,1)S(1)}, bf16[4,72,256]{2,1,0:T(8,128)(2,1)S(1)}, u32[]{:S(2)}, u32[]{:S(2)}) collective-permute-start(bf16[4,72,256]{2,1,0:T(8,128)(2,1)S(1)} %get-tuple-element.99), channel_id=1, source_target_pairs={{0,2},{2,0},{4,6},{6,4},{8,10},{10,8},{12,14},{14,12},{16,18},{18,... | collective-permute-start | bytes 442376 | tf_op jit(solution)/shard_map/ppermute | solution.py:61
  32.1 6.7 %collective-permute-start.7 = (bf16[4,72,256]{2,1,0:T(8,128)(2,1)S(1)}, bf16[4,72,256]{2,1,0:T(8,128)(2,1)S(1)}, u32[]{:S(2)}, u32[]{:S(2)}) collective-permute-start(bf16[4,72,256]{2,1,0:T(8,128)(2,1)S(1)} %get-tuple-element.100), channel_id=1, source_target_pairs={{0,4},{2,6},{4,0},{6,2},{8,12},{10,14},{12,8},{14,10},{16,20},{18,... | collective-permute-start | bytes 442376 | tf_op jit(solution)/shard_map/ppermute | solution.py:61
  32.6 6.2 %collective-permute-start.8 = (bf16[4,72,256]{2,1,0:T(8,128)(2,1)S(1)}, bf16[4,72,256]{2,1,0:T(8,128)(2,1)S(1)}, u32[]{:S(2)}, u32[]{:S(2)}) collective-permute-start(bf16[4,72,256]{2,1,0:T(8,128)(2,1)S(1)} %get-tuple-element.101), channel_id=1, source_target_pairs={{0,6},{2,4},{4,2},{6,0},{8,14},{10,12},{12,10},{14,8},{16,22},{18,... | collective-permute-start | bytes 442376 | tf_op jit(solution)/shard_map/ppermute | solution.py:61
  39.1 4.9 %collective-permute-start.10 = (bf16[1,72,256]{2,1,0:T(8,128)(2,1)S(1)}, bf16[1,72,256]{2,1,0:T(8,128)(2,1)S(1)}, u32[]{:S(2)}, u32[]{:S(2)}) collective-permute-start(bf16[1,72,256]{2,1,0:T(8,128)(2,1)S(1)} %get-tuple-element.110), channel_id=1, source_target_pairs={{0,16},{2,18},{4,20},{6,22},{8,24},{10,26},{12,28},{14,30},{16,0},... | collective-permute-start | bytes 110600 | tf_op jit(solution)/shard_map/ppermute | solution.py:61
  41.3 5.8 %collective-permute-start.11 = (bf16[1,72,256]{2,1,0:T(8,128)(2,1)S(1)}, bf16[1,72,256]{2,1,0:T(8,128)(2,1)S(1)}, u32[]{:S(2)}, u32[]{:S(2)}) collective-permute-start(bf16[1,72,256]{2,1,0:T(8,128)(2,1)S(1)} %get-tuple-element.111), channel_id=1, source_target_pairs={{0,24},{2,26},{4,28},{6,30},{8,16},{10,18},{12,20},{14,22},{16,8},... | collective-permute-start | bytes 110600 | tf_op jit(solution)/shard_map/ppermute | solution.py:61
  47.4 5.8 %collective-permute-start.14 = (bf16[1,72,256]{2,1,0:T(8,128)(2,1)S(1)}, bf16[1,72,256]{2,1,0:T(8,128)(2,1)S(1)}, u32[]{:S(2)}, u32[]{:S(2)}) collective-permute-start(bf16[1,72,256]{2,1,0:T(8,128)(2,1)S(1)} %get-tuple-element.113), channel_id=1, source_target_pairs={{0,24},{2,26},{4,28},{6,30},{8,16},{10,18},{12,20},{14,22},{16,8},... | collective-permute-start | bytes 110600 | tf_op jit(solution)/shard_map/ppermute | solution.py:61
  49.6 4.9 %collective-permute-start.13 = (bf16[1,72,256]{2,1,0:T(8,128)(2,1)S(1)}, bf16[1,72,256]{2,1,0:T(8,128)(2,1)S(1)}, u32[]{:S(2)}, u32[]{:S(2)}) collective-permute-start(bf16[1,72,256]{2,1,0:T(8,128)(2,1)S(1)} %get-tuple-element.113), channel_id=1, source_target_pairs={{0,16},{2,18},{4,20},{6,22},{8,24},{10,26},{12,28},{14,30},{16,0},... | collective-permute-start | bytes 110600 | tf_op jit(solution)/shard_map/ppermute | solution.py:61
  49.6 4.9 %collective-permute-start.12 = (bf16[1,72,256]{2,1,0:T(8,128)(2,1)S(1)}, bf16[1,72,256]{2,1,0:T(8,128)(2,1)S(1)}, u32[]{:S(2)}, u32[]{:S(2)}) collective-permute-start(bf16[1,72,256]{2,1,0:T(8,128)(2,1)S(1)} %get-tuple-element.113), channel_id=1, source_target_pairs={{0,8},{2,10},{4,12},{6,14},{8,0},{10,2},{12,4},{14,6},{16,24},{18,... | collective-permute-start | bytes 110600 | tf_op jit(solution)/shard_map/ppermute | solution.py:61
  54.5 7.9 %collective-permute-start.15 = (bf16[4,72,256]{2,1,0:T(8,128)(2,1)S(1)}, bf16[4,72,256]{2,1,0:T(8,128)(2,1)S(1)}, u32[]{:S(2)}, u32[]{:S(2)}) collective-permute-start(bf16[4,72,256]{2,1,0:T(8,128)(2,1)S(1)} %maximum_bitcast_fusion.1.refs_0_), channel_id=1, source_target_pairs={{0,2},{2,0},{4,6},{6,4},{8,10},{10,8},{12,14},{14,12},{16,18},{18,... | collective-permute-start | bytes 442376 | tf_op jit(solution)/shard_map/ppermute | solution.py:61
  56.5 5.8 %collective-permute-start.16 = (bf16[4,72,256]{2,1,0:T(8,128)(2,1)S(1)}, bf16[4,72,256]{2,1,0:T(8,128)(2,1)S(1)}, u32[]{:S(2)}, u32[]{:S(2)}) collective-permute-start(bf16[4,72,256]{2,1,0:T(8,128)(2,1)S(1)} %maximum_bitcast_fusion.1.refs_0_), channel_id=1, source_target_pairs={{0,4},{2,6},{4,0},{6,2},{8,12},{10,14},{12,8},{14,10},{16,20},{18,... | collective-permute-start | bytes 442376 | tf_op jit(solution)/shard_map/ppermute | solution.py:61
  57.5 6.0 %collective-permute-start.17 = (bf16[4,72,256]{2,1,0:T(8,128)(2,1)S(1)}, bf16[4,72,256]{2,1,0:T(8,128)(2,1)S(1)}, u32[]{:S(2)}, u32[]{:S(2)}) collective-permute-start(bf16[4,72,256]{2,1,0:T(8,128)(2,1)S(1)} %maximum_bitcast_fusion.1.refs_0_), channel_id=1, source_target_pairs={{0,6},{2,4},{4,2},{6,0},{8,14},{10,12},{12,10},{14,8},{16,22},{18,... | collective-permute-start | bytes 442376 | tf_op jit(solution)/shard_map/ppermute | solution.py:61
  68.2 9.0 %collective-permute-start.20 = (bf16[4,32,1024]{2,1,0:T(8,128)(2,1)S(1)}, bf16[4,32,1024]{2,1,0:T(8,128)(2,1)S(1)}, u32[]{:S(2)}, u32[]{:S(2)}) collective-permute-start(bf16[4,32,1024]{2,1,0:T(8,128)(2,1)S(1)} %get-tuple-element.126), channel_id=1, source_target_pairs={{0,6},{2,4},{4,2},{6,0},{8,14},{10,12},{12,10},{14,8},{16,22},{18,... | collective-permute-start | bytes 786440 | tf_op jit(solution)/shard_map/ppermute | solution.py:61
  69.5 8.9 %collective-permute-start.19 = (bf16[4,32,1024]{2,1,0:T(8,128)(2,1)S(1)}, bf16[4,32,1024]{2,1,0:T(8,128)(2,1)S(1)}, u32[]{:S(2)}, u32[]{:S(2)}) collective-permute-start(bf16[4,32,1024]{2,1,0:T(8,128)(2,1)S(1)} %get-tuple-element.125), channel_id=1, source_target_pairs={{0,4},{2,6},{4,0},{6,2},{8,12},{10,14},{12,8},{14,10},{16,20},{18,... | collective-permute-start | bytes 786440 | tf_op jit(solution)/shard_map/ppermute | solution.py:61
  70.5 7.8 %collective-permute-start.18 = (bf16[4,32,1024]{2,1,0:T(8,128)(2,1)S(1)}, bf16[4,32,1024]{2,1,0:T(8,128)(2,1)S(1)}, u32[]{:S(2)}, u32[]{:S(2)}) collective-permute-start(bf16[4,32,1024]{2,1,0:T(8,128)(2,1)S(1)} %get-tuple-element.124), channel_id=1, source_target_pairs={{0,2},{2,0},{4,6},{6,4},{8,10},{10,8},{12,14},{14,12},{16,18},{18,... | collective-permute-start | bytes 786440 | tf_op jit(solution)/shard_map/ppermute | solution.py:61
  78.6 9.1 %collective-permute-start.23 = (bf16[1,32,1024]{2,1,0:T(8,128)(2,1)S(1)}, bf16[1,32,1024]{2,1,0:T(8,128)(2,1)S(1)}, u32[]{:S(2)}, u32[]{:S(2)}) collective-permute-start(bf16[1,32,1024]{2,1,0:T(8,128)(2,1)S(1)} %get-tuple-element.180), channel_id=1, source_target_pairs={{0,24},{2,26},{4,28},{6,30},{8,16},{10,18},{12,20},{14,22},{16,8},... | collective-permute-start | bytes 196616 | tf_op jit(solution)/shard_map/ppermute | solution.py:61
  80.6 8.1 %collective-permute-start.22 = (bf16[1,32,1024]{2,1,0:T(8,128)(2,1)S(1)}, bf16[1,32,1024]{2,1,0:T(8,128)(2,1)S(1)}, u32[]{:S(2)}, u32[]{:S(2)}) collective-permute-start(bf16[1,32,1024]{2,1,0:T(8,128)(2,1)S(1)} %get-tuple-element.181), channel_id=1, source_target_pairs={{0,16},{2,18},{4,20},{6,22},{8,24},{10,26},{12,28},{14,30},{16,0},... | collective-permute-start | bytes 196616 | tf_op jit(solution)/shard_map/ppermute | solution.py:61
  81.7 7.0 %collective-permute-start.21 = (bf16[1,32,1024]{2,1,0:T(8,128)(2,1)S(1)}, bf16[1,32,1024]{2,1,0:T(8,128)(2,1)S(1)}, u32[]{:S(2)}, u32[]{:S(2)}) collective-permute-start(bf16[1,32,1024]{2,1,0:T(8,128)(2,1)S(1)} %get-tuple-element.179), channel_id=1, source_target_pairs={{0,8},{2,10},{4,12},{6,14},{8,0},{10,2},{12,4},{14,6},{16,24},{18,... | collective-permute-start | bytes 196616 | tf_op jit(solution)/shard_map/ppermute | solution.py:61
  88.8 6.0 %collective-permute-start.26 = (bf16[4,16,1024]{2,1,0:T(8,128)(2,1)S(1)}, bf16[4,16,1024]{2,1,0:T(8,128)(2,1)S(1)}, u32[]{:S(2)}, u32[]{:S(2)}) collective-permute-start(bf16[4,16,1024]{2,1,0:T(8,128)(2,1)S(1)} %get-tuple-element.148), channel_id=1, source_target_pairs={{0,6},{2,4},{4,2},{6,0},{8,14},{10,12},{12,10},{14,8},{16,22},{18,... | collective-permute-start | bytes 393224 | tf_op jit(solution)/shard_map/ppermute | solution.py:61
  89.0 7.8 %collective-permute-start.25 = (bf16[4,16,1024]{2,1,0:T(8,128)(2,1)S(1)}, bf16[4,16,1024]{2,1,0:T(8,128)(2,1)S(1)}, u32[]{:S(2)}, u32[]{:S(2)}) collective-permute-start(bf16[4,16,1024]{2,1,0:T(8,128)(2,1)S(1)} %get-tuple-element.147), channel_id=1, source_target_pairs={{0,4},{2,6},{4,0},{6,2},{8,12},{10,14},{12,8},{14,10},{16,20},{18,... | collective-permute-start | bytes 393224 | tf_op jit(solution)/shard_map/ppermute | solution.py:61
  90.1 6.6 %collective-permute-start.24 = (bf16[4,16,1024]{2,1,0:T(8,128)(2,1)S(1)}, bf16[4,16,1024]{2,1,0:T(8,128)(2,1)S(1)}, u32[]{:S(2)}, u32[]{:S(2)}) collective-permute-start(bf16[4,16,1024]{2,1,0:T(8,128)(2,1)S(1)} %get-tuple-element.146), channel_id=1, source_target_pairs={{0,2},{2,0},{4,6},{6,4},{8,10},{10,8},{12,14},{14,12},{16,18},{18,... | collective-permute-start | bytes 393224 | tf_op jit(solution)/shard_map/ppermute | solution.py:61
  92.3 8.2 %collective-permute-start.27 = (bf16[1,32,1024]{2,1,0:T(8,128)(2,1)S(1)}, bf16[1,32,1024]{2,1,0:T(8,128)(2,1)S(1)}, u32[]{:S(2)}, u32[]{:S(2)}) collective-permute-start(bf16[1,32,1024]{2,1,0:T(8,128)(2,1)S(1)} %bitcast.49), channel_id=1, source_target_pairs={{0,8},{2,10},{4,12},{6,14},{8,0},{10,2},{12,4},{14,6},{16,24},{18,... | collective-permute-start | bytes 196616 | tf_op jit(solution)/shard_map/ppermute | solution.py:61
  92.3 8.2 %collective-permute-start.28 = (bf16[1,32,1024]{2,1,0:T(8,128)(2,1)S(1)}, bf16[1,32,1024]{2,1,0:T(8,128)(2,1)S(1)}, u32[]{:S(2)}, u32[]{:S(2)}) collective-permute-start(bf16[1,32,1024]{2,1,0:T(8,128)(2,1)S(1)} %bitcast.50), channel_id=1, source_target_pairs={{0,16},{2,18},{4,20},{6,22},{8,24},{10,26},{12,28},{14,30},{16,0},... | collective-permute-start | bytes 196616 | tf_op jit(solution)/shard_map/ppermute | solution.py:61
  94.8 6.1 %collective-permute-start.29 = (bf16[1,32,1024]{2,1,0:T(8,128)(2,1)S(1)}, bf16[1,32,1024]{2,1,0:T(8,128)(2,1)S(1)}, u32[]{:S(2)}, u32[]{:S(2)}) collective-permute-start(bf16[1,32,1024]{2,1,0:T(8,128)(2,1)S(1)} %bitcast.51), channel_id=1, source_target_pairs={{0,24},{2,26},{4,28},{6,30},{8,16},{10,18},{12,20},{14,22},{16,8},... | collective-permute-start | bytes 196616 | tf_op jit(solution)/shard_map/ppermute | solution.py:61
  100.9 12.9 %collective-permute-start.33 = (bf16[1024,512]{1,0:T(8,128)(2,1)S(1)}, bf16[1024,512]{1,0:T(8,128)(2,1)S(1)}, u32[]{:S(2)}, u32[]{:S(2)}) collective-permute-start(bf16[1024,512]{1,0:T(8,128)(2,1)S(1)} %part.1), channel_id=1, source_target_pairs={{0,1},{1,0},{2,3},{3,2},{4,5},{5,4},{6,7},{7,6},{8,9},{9,8},{10,11... | collective-permute-start | bytes 3145736 | tf_op jit(solution)/shard_map/ppermute | solution.py:777
  101.0 15.2 %collective-permute-start.30 = (bf16[4,32,1024]{2,1,0:T(8,128)(2,1)S(1)}, bf16[4,32,1024]{2,1,0:T(8,128)(2,1)S(1)}, u32[]{:S(2)}, u32[]{:S(2)}) collective-permute-start(bf16[4,32,1024]{2,1,0:T(8,128)(2,1)S(1)} %maximum_bitcast_fusion.refs_0_), channel_id=1, source_target_pairs={{0,2},{2,0},{4,6},{6,4},{8,10},{10,8},{12,14},{14,12},{16,18},{18,... | collective-permute-start | bytes 786440 | tf_op jit(solution)/shard_map/ppermute | solution.py:61
  101.4 14.8 %collective-permute-start.31 = (bf16[4,32,1024]{2,1,0:T(8,128)(2,1)S(1)}, bf16[4,32,1024]{2,1,0:T(8,128)(2,1)S(1)}, u32[]{:S(2)}, u32[]{:S(2)}) collective-permute-start(bf16[4,32,1024]{2,1,0:T(8,128)(2,1)S(1)} %maximum_bitcast_fusion.refs_0_), channel_id=1, source_target_pairs={{0,4},{2,6},{4,0},{6,2},{8,12},{10,14},{12,8},{14,10},{16,20},{18,... | collective-permute-start | bytes 786440 | tf_op jit(solution)/shard_map/ppermute | solution.py:61
  102.4 13.8 %collective-permute-start.32 = (bf16[4,32,1024]{2,1,0:T(8,128)(2,1)S(1)}, bf16[4,32,1024]{2,1,0:T(8,128)(2,1)S(1)}, u32[]{:S(2)}, u32[]{:S(2)}) collective-permute-start(bf16[4,32,1024]{2,1,0:T(8,128)(2,1)S(1)} %maximum_bitcast_fusion.refs_0_), channel_id=1, source_target_pairs={{0,6},{2,4},{4,2},{6,0},{8,14},{10,12},{12,10},{14,8},{16,22},{18,... | collective-permute-start | bytes 786440 | tf_op jit(solution)/shard_map/ppermute | solution.py:61
  105.4 6.2 %collective-permute-start.35 = (bf16[1,16,1024]{2,1,0:T(8,128)(2,1)S(1)}, bf16[1,16,1024]{2,1,0:T(8,128)(2,1)S(1)}, u32[]{:S(2)}, u32[]{:S(2)}) collective-permute-start(bf16[1,16,1024]{2,1,0:T(8,128)(2,1)S(1)} %slice.39), channel_id=1, source_target_pairs={{0,16},{2,18},{4,20},{6,22},{8,24},{10,26},{12,28},{14,30},{16,0},... | collective-permute-start | bytes 98312 | tf_op jit(solution)/shard_map/ppermute | solution.py:61
  (9 other events, 66.4 us)

commit v11 on v10

--- a/solution.py
+++ b/solution.py
@@ -13,7 +13,7 @@
 ITERS = 2
 SCALE = 0.125
 CHUNK = 256
-EXTRA = 8
+EXTRA = 16
 F32 = jnp.float32
 BF16 = jnp.bfloat16
 PARAMS = pltpu.CompilerParams(vmem_limit_bytes=24 * 1024 * 1024)

time: 119 us -> 119 us (level)
  no operation moved by 1% of the time
where the time goes in v11:
time: 119 us
  Pallas kernels  49.5 us (42%)
  starting transfers between devices  46.6 us (39%)
  waiting for transfers between devices  18.4 us (15%)
  matrix products  2.87 us (2%)
    pallas_call x15, Pallas kernels, call(): pl.pallas_call(kernel, grid_spec=pltpu.PrefetchScalarGridSpec(num_scalar_...  49.5 us
    ppermute x35, starting transfers between devices, exchange(): return lax.ppermute(block, 'seq', [(i, i ^ mask) for i in range(n)])  46.6 us
    ppermute x35, waiting for transfers between devices, exchange(): return lax.ppermute(block, 'seq', [(i, i ^ mask) for i in range(n)])  18.4 us
    dot_general x1, matrix products, dot(): lax.dot_general(left, right, (dims, ((), ())), preferred_element_type=F32)  2.87 us
  transfers between devices with their start and end apart: 36, of which 14 were waited for; matrix products, arithmetic and copies ran while one was open for 3% of the time, Pallas kernels for 26%

profile of v11, /device:TPU:0, one launch (start us, length us, event | category | flops | bytes accessed | tf_op | source)
XLA Modules:
  0.0 119.2 jit_solution(2733607599237681779)
XLA Ops:
  0.8 1.7 %means.1 = bf16[16,1024]{1,0:T(8,128)(2,1)S(1)} custom-call(bf16[1024,512]{1,0:T(8,128)(2,1)} %q_ref.5, bf16[1024,512]{1,0:T(8,128)(2,1)} %k_ref.4), custom_call_target="tpu_custom_call" | custom-call | bytes 4194304 | tf_op jit(solution)/shard_map/means/pallas_call | solution.py:500
  2.5 5.1 %collective-permute-start.2 = (bf16[1,16,1024]{2,1,0:T(8,128)(2,1)S(1)}, bf16[1,16,1024]{2,1,0:T(8,128)(2,1)S(1)}, u32[]{:S(2)}, u32[]{:S(2)}) collective-permute-start(bf16[1,16,1024]{2,1,0:T(8,128)(2,1)S(1)} %bitcast.42), channel_id=1, source_target_pairs={{0,24},{2,26},{4,28},{6,30},{8,16},{10,18},{12,20},{14,22},{16,8},... | collective-permute-start | bytes 98312 | tf_op jit(solution)/shard_map/ppermute | solution.py:61
  9.5 2.9 %collective-permute-done.1 = bf16[1,16,1024]{2,1,0:T(8,128)(2,1)S(1)} collective-permute-done((bf16[1,16,1024]{2,1,0:T(8,128)(2,1)S(1)}, bf16[1,16,1024]{2,1,0:T(8,128)(2,1)S(1)}, u32[]{:S(2)}, u32[]{:S(2)}) %collective-permute-start.1) | collective-permute-done | bytes 32800 | tf_op jit(solution)/shard_map/ppermute | solution.py:61
  12.5 1.6 %collective-permute-start.3 = (bf16[4,16,1024]{2,1,0:T(8,128)(2,1)S(1)}, bf16[4,16,1024]{2,1,0:T(8,128)(2,1)S(1)}, u32[]{:S(2)}, u32[]{:S(2)}) collective-permute-start(bf16[4,16,1024]{2,1,0:T(8,128)(2,1)S(1)} %maximum_bitcast_fusion.2.refs_0_), channel_id=1, source_target_pairs={{0,2},{2,0},{4,6},{6,4},{8,10},{10,8},{12,14},{14,12},{16,18},{18,... | collective-permute-start | bytes 393224 | tf_op jit(solution)/shard_map/ppermute | solution.py:61
  14.0 1.5 %collective-permute-start.4 = (bf16[4,16,1024]{2,1,0:T(8,128)(2,1)S(1)}, bf16[4,16,1024]{2,1,0:T(8,128)(2,1)S(1)}, u32[]{:S(2)}, u32[]{:S(2)}) collective-permute-start(bf16[4,16,1024]{2,1,0:T(8,128)(2,1)S(1)} %maximum_bitcast_fusion.2.refs_0_), channel_id=1, source_target_pairs={{0,4},{2,6},{4,0},{6,2},{8,12},{10,14},{12,8},{14,10},{16,20},{18,... | collective-permute-start | bytes 393224 | tf_op jit(solution)/shard_map/ppermute | solution.py:61
  16.0 2.9 %convolution_convert_fusion.g_ref = bf16[1024,512]{1,0:T(8,128)(2,1)S(1)} fusion(bf16[1024,1024]{1,0:T(8,128)(2,1)} %cot_ref.1, bf16[512,1024]{1,0:T(8,128)(2,1)S(1)} %copy-done), kind=kOutput, calls=%fused_computation | convolution fusion | flops 1074266112 | bytes 4194304 | tf_op jit(solution)/shard_map/dot_general | solution.py:23
  20.0 1.5 %collective-permute-done.5.refs_3_ = bf16[4,16,1024]{2,1,0:T(8,128)(2,1)S(1)} collective-permute-done((bf16[4,16,1024]{2,1,0:T(8,128)(2,1)S(1)}, bf16[4,16,1024]{2,1,0:T(8,128)(2,1)S(1)}, u32[]{:S(2)}, u32[]{:S(2)}) %collective-permute-start.5) | collective-permute-done | bytes 131104 | tf_op jit(solution)/shard_map/ppermute | solution.py:61
  21.4 10.1 %forward.1 = (bf16[1024,2048]{1,0:T(8,128)(2,1)S(1)}, bf16[1024,2048]{1,0:T(8,128)(2,1)S(1)}, f32[4,8,256]{2,1,0:T(8,128)S(1)}, bf16[256,1024]{1,0:T(8,128)(2,1)...) custom-call(s32[2]{0:T(128)S(1)} %pad_add_fusion.me_ref, ...), custom_call_target="tpu_custom_call" | custom-call | flops 8589934592 | bytes 4194304 | tf_op jit(solution)/shard_map/forward/pallas_call | solution.py:500
  32.6 2.4 %collective-permute-start.8 = (bf16[4,80,256]{2,1,0:T(8,128)(2,1)S(1)}, bf16[4,80,256]{2,1,0:T(8,128)(2,1)S(1)}, u32[]{:S(2)}, u32[]{:S(2)}) collective-permute-start(bf16[4,80,256]{2,1,0:T(8,128)(2,1)S(1)} %get-tuple-element.101), channel_id=1, source_target_pairs={{0,6},{2,4},{4,2},{6,0},{8,14},{10,12},{12,10},{14,8},{16,22},{18,... | collective-permute-start | bytes 491528 | tf_op jit(solution)/shard_map/ppermute | solution.py:61
  35.1 3.7 %newton.1 = (f32[9,256,256]{2,1,0:T(8,128)S(1)}, f32[1,256,256]{2,1,0:T(8,128)S(1)}) custom-call(s32[3]{0:T(128)S(1)} %pad_add_fusion.1.own_ref, bf16[256,1024]{1,0:T(8,128)(2,1)S(1)} %get-tuple-element.102.lq_ref.lk_ref, bf16[256,1024]{1,0:T(8,128)(2,1)S(1)} %get-tuple-element.102.lq_ref.lk_ref), custom_call_target="tpu_custom_call" | custom-call | flops 4294967296 | bytes 4194304 | tf_op jit(solution)/shard_map/newton/pallas_call | solution.py:500
  39.7 2.1 %collective-permute-start.10 = (bf16[1,80,256]{2,1,0:T(8,128)(2,1)S(1)}, bf16[1,80,256]{2,1,0:T(8,128)(2,1)S(1)}, u32[]{:S(2)}, u32[]{:S(2)}) collective-permute-start(bf16[1,80,256]{2,1,0:T(8,128)(2,1)S(1)} %get-tuple-element.110), channel_id=1, source_target_pairs={{0,16},{2,18},{4,20},{6,22},{8,24},{10,26},{12,28},{14,30},{16,0},... | collective-permute-start | bytes 122888 | tf_op jit(solution)/shard_map/ppermute | solution.py:61
  41.9 1.9 %collective-permute-start.11 = (bf16[1,80,256]{2,1,0:T(8,128)(2,1)S(1)}, bf16[1,80,256]{2,1,0:T(8,128)(2,1)S(1)}, u32[]{:S(2)}, u32[]{:S(2)}) collective-permute-start(bf16[1,80,256]{2,1,0:T(8,128)(2,1)S(1)} %get-tuple-element.111), channel_id=1, source_target_pairs={{0,24},{2,26},{4,28},{6,30},{8,16},{10,18},{12,20},{14,22},{16,8},... | collective-permute-start | bytes 122888 | tf_op jit(solution)/shard_map/ppermute | solution.py:61
  44.6 3.3 %collective-permute-done.11.refs_3_ = bf16[1,80,256]{2,1,0:T(8,128)(2,1)S(1)} collective-permute-done((bf16[1,80,256]{2,1,0:T(8,128)(2,1)S(1)}, bf16[1,80,256]{2,1,0:T(8,128)(2,1)S(1)}, u32[]{:S(2)}, u32[]{:S(2)}) %collective-permute-start.11) | collective-permute-done | bytes 40992 | tf_op jit(solution)/shard_map/ppermute | solution.py:61
  48.2 2.0 %collective-permute-start.14 = (bf16[1,80,256]{2,1,0:T(8,128)(2,1)S(1)}, bf16[1,80,256]{2,1,0:T(8,128)(2,1)S(1)}, u32[]{:S(2)}, u32[]{:S(2)}) collective-permute-start(bf16[1,80,256]{2,1,0:T(8,128)(2,1)S(1)} %get-tuple-element.113), channel_id=1, source_target_pairs={{0,24},{2,26},{4,28},{6,30},{8,16},{10,18},{12,20},{14,22},{16,8},... | collective-permute-start | bytes 122888 | tf_op jit(solution)/shard_map/ppermute | solution.py:61
  50.3 2.4 %collective-permute-start.12 = (bf16[1,80,256]{2,1,0:T(8,128)(2,1)S(1)}, bf16[1,80,256]{2,1,0:T(8,128)(2,1)S(1)}, u32[]{:S(2)}, u32[]{:S(2)}) collective-permute-start(bf16[1,80,256]{2,1,0:T(8,128)(2,1)S(1)} %get-tuple-element.113), channel_id=1, source_target_pairs={{0,8},{2,10},{4,12},{6,14},{8,0},{10,2},{12,4},{14,6},{16,24},{18,... | collective-permute-start | bytes 122888 | tf_op jit(solution)/shard_map/ppermute | solution.py:61
  55.2 1.9 %collective-permute-start.15 = (bf16[4,80,256]{2,1,0:T(8,128)(2,1)S(1)}, bf16[4,80,256]{2,1,0:T(8,128)(2,1)S(1)}, u32[]{:S(2)}, u32[]{:S(2)}) collective-permute-start(bf16[4,80,256]{2,1,0:T(8,128)(2,1)S(1)} %maximum_bitcast_fusion.1.refs_0_), channel_id=1, source_target_pairs={{0,2},{2,0},{4,6},{6,4},{8,10},{10,8},{12,14},{14,12},{16,18},{18,... | collective-permute-start | bytes 491528 | tf_op jit(solution)/shard_map/ppermute | solution.py:61
  58.8 4.3 %newton_grad.1 = (f32[256,128]{1,0:T(8,128)S(1)}, f32[256,128]{1,0:T(8,128)S(1)}) custom-call(s32[3]{0:T(128)S(1)} %pad_add_fusion.1.own_ref, f32[9,256,256]{2,1,0:T(8,128)S(1)} %get-tuple-element.114.saved_ref, f32[32,256]{1,0:T(8,128)S(1)} %get-tuple-element.115.values_ref, f32[32,256]{1,0:T(8,128)S(1)} %get-tuple-element.116.grads_ref, ...), custom_call_target="tpu_custom_call" | custom-call | flops 8589934592 | bytes 4194304 | tf_op jit(solution)/shard_map/newton_grad/pallas_call | solution.py:500
  64.4 4.7 %attend.1 = (bf16[1024,512]{1,0:T(8,128)(2,1)S(1)}, bf16[512,256]{1,0:T(8,128)(2,1)S(1)}, bf16[512,256]{1,0:T(8,128)(2,1)S(1)}, f32[8,256]{1,0:T(8,128)S(1)}, bf...) custom-call(s32[2]{0:T(128)S(1)} %pad_add_fusion.me_ref, ...), custom_call_target="tpu_custom_call" | custom-call | flops 4294967296 | bytes 4194304 | tf_op jit(solution)/shard_map/attend/pallas_call | solution.py:500
  71.1 1.5 %collective-permute-start.18 = (bf16[4,32,1024]{2,1,0:T(8,128)(2,1)S(1)}, bf16[4,32,1024]{2,1,0:T(8,128)(2,1)S(1)}, u32[]{:S(2)}, u32[]{:S(2)}) collective-permute-start(bf16[4,32,1024]{2,1,0:T(8,128)(2,1)S(1)} %get-tuple-element.124), channel_id=1, source_target_pairs={{0,2},{2,0},{4,6},{6,4},{8,10},{10,8},{12,14},{14,12},{16,18},{18,... | collective-permute-start | bytes 786440 | tf_op jit(solution)/shard_map/ppermute | solution.py:61
  72.6 5.4 %query_land.1 = (bf16[256,512]{1,0:T(8,128)(2,1)S(1)}, bf16[1024,2048]{1,0:T(8,128)(2,1)S(1)}) custom-call(s32[3]{0:T(128)S(1)} %pad_add_fusion.1.own_ref, bf16[1024,512]{1,0:T(8,128)(2,1)S(1)} %copy-done.1, bf16[1024,512]{1,0:T(8,128)(2,1)S(1)} %convolution_convert_fusion.g_ref, bf16[1024,2048]{1,0:T(8,128)(2,1)S(1)} %get-tuple-element.96.fb_ref, ...), custom_call_target="tpu_custom_call" | custom-call | flops 4294967296 | bytes 4194304 | tf_op jit(solution)/shard_map/query_land/pallas_call | solution.py:500
  79.4 2.0 %collective-permute-start.23 = (bf16[1,32,1024]{2,1,0:T(8,128)(2,1)S(1)}, bf16[1,32,1024]{2,1,0:T(8,128)(2,1)S(1)}, u32[]{:S(2)}, u32[]{:S(2)}) collective-permute-start(bf16[1,32,1024]{2,1,0:T(8,128)(2,1)S(1)} %get-tuple-element.180), channel_id=1, source_target_pairs={{0,24},{2,26},{4,28},{6,30},{8,16},{10,18},{12,20},{14,22},{16,8},... | collective-permute-start | bytes 196616 | tf_op jit(solution)/shard_map/ppermute | solution.py:61
  83.8 4.6 %key_land.1 = (bf16[1024,2048]{1,0:T(8,128)(2,1)S(1)}, bf16[4,16,1024]{2,1,0:T(8,128)(2,1)S(1)}, bf16[4,16,1024]{2,1,0:T(8,128)(2,1)S(1)}, bf16[4,16,1024]{2,1,0:T(8,128)(2,1)S(1)}, bf16[4,16,1024]{2,1,0:T(8,128)(2,1)S(1)}) custom-call(s32[3]{0:T(128)S(1)} %pad_add_fusion.1.own_ref, bf16[1024,512]{1,0:T(8,128)(2,1)S(1)} %copy-done.2, ...), custom_call_target="tpu_custom_call" | custom-call | flops 4294967296 | bytes 4194304 | tf_op jit(solution)/shard_map/key_land/pallas_call | solution.py:500
  90.9 2.2 %collective-permute-start.24 = (bf16[4,16,1024]{2,1,0:T(8,128)(2,1)S(1)}, bf16[4,16,1024]{2,1,0:T(8,128)(2,1)S(1)}, u32[]{:S(2)}, u32[]{:S(2)}) collective-permute-start(bf16[4,16,1024]{2,1,0:T(8,128)(2,1)S(1)} %get-tuple-element.146), channel_id=1, source_target_pairs={{0,2},{2,0},{4,6},{6,4},{8,10},{10,8},{12,14},{14,12},{16,18},{18,... | collective-permute-start | bytes 393224 | tf_op jit(solution)/shard_map/ppermute | solution.py:61
  93.1 2.5 %collective-permute-start.28 = (bf16[1,32,1024]{2,1,0:T(8,128)(2,1)S(1)}, bf16[1,32,1024]{2,1,0:T(8,128)(2,1)S(1)}, u32[]{:S(2)}, u32[]{:S(2)}) collective-permute-start(bf16[1,32,1024]{2,1,0:T(8,128)(2,1)S(1)} %bitcast.50), channel_id=1, source_target_pairs={{0,16},{2,18},{4,20},{6,22},{8,24},{10,26},{12,28},{14,30},{16,0},... | collective-permute-start | bytes 196616 | tf_op jit(solution)/shard_map/ppermute | solution.py:61
  95.6 1.9 %collective-permute-start.29 = (bf16[1,32,1024]{2,1,0:T(8,128)(2,1)S(1)}, bf16[1,32,1024]{2,1,0:T(8,128)(2,1)S(1)}, u32[]{:S(2)}, u32[]{:S(2)}) collective-permute-start(bf16[1,32,1024]{2,1,0:T(8,128)(2,1)S(1)} %bitcast.51), channel_id=1, source_target_pairs={{0,24},{2,26},{4,28},{6,30},{8,16},{10,18},{12,20},{14,22},{16,8},... | collective-permute-start | bytes 196616 | tf_op jit(solution)/shard_map/ppermute | solution.py:61
  97.6 2.3 %query_grad.1.query_ref = bf16[1024,512]{1,0:T(8,128)(2,1)S(1)} custom-call(bf16[1024,2048]{1,0:T(8,128)(2,1)S(1)} %get-tuple-element.153.ds_ref, bf16[256,1024]{1,0:T(8,128)(2,1)S(1)} %get-tuple-element.102.lq_ref.lk_ref), custom_call_target="tpu_custom_call" | custom-call | flops 2147483648 | bytes 4194304 | tf_op jit(solution)/shard_map/query_grad/pallas_call | solution.py:500
  103.1 2.2 %collective-permute-start.32 = (bf16[4,32,1024]{2,1,0:T(8,128)(2,1)S(1)}, bf16[4,32,1024]{2,1,0:T(8,128)(2,1)S(1)}, u32[]{:S(2)}, u32[]{:S(2)}) collective-permute-start(bf16[4,32,1024]{2,1,0:T(8,128)(2,1)S(1)} %maximum_bitcast_fusion.refs_0_), channel_id=1, source_target_pairs={{0,6},{2,4},{4,2},{6,0},{8,14},{10,12},{12,10},{14,8},{16,22},{18,... | collective-permute-start | bytes 786440 | tf_op jit(solution)/shard_map/ppermute | solution.py:61
  106.2 1.7 %collective-permute-start.35 = (bf16[1,16,1024]{2,1,0:T(8,128)(2,1)S(1)}, bf16[1,16,1024]{2,1,0:T(8,128)(2,1)S(1)}, u32[]{:S(2)}, u32[]{:S(2)}) collective-permute-start(bf16[1,16,1024]{2,1,0:T(8,128)(2,1)S(1)} %slice.39), channel_id=1, source_target_pairs={{0,16},{2,18},{4,20},{6,22},{8,24},{10,26},{12,28},{14,30},{16,0},... | collective-permute-start | bytes 98312 | tf_op jit(solution)/shard_map/ppermute | solution.py:61
  107.9 4.5 %key_grad.1 = (bf16[1024,512]{1,0:T(8,128)(2,1)S(1)}, bf16[1024,512]{1,0:T(8,128)(2,1)}) custom-call(bf16[1024,2048]{1,0:T(8,128)(2,1)S(1)} %get-tuple-element.169.ds_ref, bf16[1024,2048]{1,0:T(8,128)(2,1)S(1)} %get-tuple-element.135.pb_ref, bf16[256,1024]{1,0:T(8,128)(2,1)S(1)} %get-tuple-element.102.lq_ref.lk_ref, ...), custom_call_target="tpu_custom_call" | custom-call | flops 4294967296 | bytes 4194304 | tf_op jit(solution)/shard_map/key_grad/pallas_call | solution.py:500
  112.4 2.2 %finish.1 = (bf16[1024,512]{1,0:T(8,128)(2,1)}, bf16[1024,512]{1,0:T(8,128)(2,1)}) custom-call(bf16[1024,512]{1,0:T(8,128)(2,1)S(1)} %query_grad.1.query_ref, bf16[1024,512]{1,0:T(8,128)(2,1)S(1)} %get-tuple-element.170.key_ref, f32[16,1024]{1,0:T(8,128)S(1)} %multiply_bitcast_fusion.query_own_ref.key_own_ref, ...), custom_call_target="tpu_custom_call" | custom-call | bytes 4194304 | tf_op jit(solution)/shard_map/finish/pallas_call | solution.py:500
  114.6 2.4 %mixed.1 = bf16[1024,512]{1,0:T(8,128)(2,1)} custom-call(s32[1]{0:T(128)} %bitcast.1._, bf16[1024,512]{1,0:T(8,128)(2,1)S(1)} %get-tuple-element.155.attn_ref, bf16[512,1024]{1,0:T(8,128)(2,1)S(1)} %copy-done, bf16[1024,512]{1,0:T(8,128)(2,1)S(1)} %collective-permute-done.33.other_ref), custom_call_target="tpu_custom_call" | custom-call | flops 1073741824 | bytes 4194304 | tf_op jit(solution)/shard_map/mixed/pallas_call | solution.py:500
  117.0 2.0 %unpack.1 = f32[512,1024]{1,0:T(8,128)} custom-call(s32[2]{0:T(128)S(1)} %pad_add_fusion.me_ref, bf16[4,32,1024]{2,1,0:T(8,128)(2,1)S(1)} %maximum_bitcast_fusion.refs_0_, bf16[4,32,1024]{2,1,0:T(8,128)(2,1)S(1)} %collective-permute-done.30.refs_1_, bf16[4,32,1024]{2,1,0:T(8,128)(2,1)S(1)} %collective-permute-done.31.refs_2_, ...), custom_call_target="tpu_custom_call" | custom-call | bytes 4194304 | tf_op jit(solution)/shard_map/unpack/pallas_call | solution.py:500
  (79 shorter events, 24.7 us)
Async XLA Ops:
  2.5 7.0 %collective-permute-start.2 = (bf16[1,16,1024]{2,1,0:T(8,128)(2,1)S(1)}, bf16[1,16,1024]{2,1,0:T(8,128)(2,1)S(1)}, u32[]{:S(2)}, u32[]{:S(2)}) collective-permute-start(bf16[1,16,1024]{2,1,0:T(8,128)(2,1)S(1)} %bitcast.42), channel_id=1, source_target_pairs={{0,24},{2,26},{4,28},{6,30},{8,16},{10,18},{12,20},{14,22},{16,8},... | collective-permute-start | bytes 98312 | tf_op jit(solution)/shard_map/ppermute | solution.py:61
  12.5 6.4 %collective-permute-start.3 = (bf16[4,16,1024]{2,1,0:T(8,128)(2,1)S(1)}, bf16[4,16,1024]{2,1,0:T(8,128)(2,1)S(1)}, u32[]{:S(2)}, u32[]{:S(2)}) collective-permute-start(bf16[4,16,1024]{2,1,0:T(8,128)(2,1)S(1)} %maximum_bitcast_fusion.2.refs_0_), channel_id=1, source_target_pairs={{0,2},{2,0},{4,6},{6,4},{8,10},{10,8},{12,14},{14,12},{16,18},{18,... | collective-permute-start | bytes 393224 | tf_op jit(solution)/shard_map/ppermute | solution.py:61
  14.0 5.9 %collective-permute-start.4 = (bf16[4,16,1024]{2,1,0:T(8,128)(2,1)S(1)}, bf16[4,16,1024]{2,1,0:T(8,128)(2,1)S(1)}, u32[]{:S(2)}, u32[]{:S(2)}) collective-permute-start(bf16[4,16,1024]{2,1,0:T(8,128)(2,1)S(1)} %maximum_bitcast_fusion.2.refs_0_), channel_id=1, source_target_pairs={{0,4},{2,6},{4,0},{6,2},{8,12},{10,14},{12,8},{14,10},{16,20},{18,... | collective-permute-start | bytes 393224 | tf_op jit(solution)/shard_map/ppermute | solution.py:61
  15.6 5.9 %collective-permute-start.5 = (bf16[4,16,1024]{2,1,0:T(8,128)(2,1)S(1)}, bf16[4,16,1024]{2,1,0:T(8,128)(2,1)S(1)}, u32[]{:S(2)}, u32[]{:S(2)}) collective-permute-start(bf16[4,16,1024]{2,1,0:T(8,128)(2,1)S(1)} %maximum_bitcast_fusion.2.refs_0_), channel_id=1, source_target_pairs={{0,6},{2,4},{4,2},{6,0},{8,14},{10,12},{12,10},{14,8},{16,22},{18,... | collective-permute-start | bytes 393224 | tf_op jit(solution)/shard_map/ppermute | solution.py:61
  31.5 7.2 %collective-permute-start.6 = (bf16[4,80,256]{2,1,0:T(8,128)(2,1)S(1)}, bf16[4,80,256]{2,1,0:T(8,128)(2,1)S(1)}, u32[]{:S(2)}, u32[]{:S(2)}) collective-permute-start(bf16[4,80,256]{2,1,0:T(8,128)(2,1)S(1)} %get-tuple-element.99), channel_id=1, source_target_pairs={{0,2},{2,0},{4,6},{6,4},{8,10},{10,8},{12,14},{14,12},{16,18},{18,... | collective-permute-start | bytes 491528 | tf_op jit(solution)/shard_map/ppermute | solution.py:61
  32.1 6.6 %collective-permute-start.7 = (bf16[4,80,256]{2,1,0:T(8,128)(2,1)S(1)}, bf16[4,80,256]{2,1,0:T(8,128)(2,1)S(1)}, u32[]{:S(2)}, u32[]{:S(2)}) collective-permute-start(bf16[4,80,256]{2,1,0:T(8,128)(2,1)S(1)} %get-tuple-element.100), channel_id=1, source_target_pairs={{0,4},{2,6},{4,0},{6,2},{8,12},{10,14},{12,8},{14,10},{16,20},{18,... | collective-permute-start | bytes 491528 | tf_op jit(solution)/shard_map/ppermute | solution.py:61
  32.6 6.6 %collective-permute-start.8 = (bf16[4,80,256]{2,1,0:T(8,128)(2,1)S(1)}, bf16[4,80,256]{2,1,0:T(8,128)(2,1)S(1)}, u32[]{:S(2)}, u32[]{:S(2)}) collective-permute-start(bf16[4,80,256]{2,1,0:T(8,128)(2,1)S(1)} %get-tuple-element.101), channel_id=1, source_target_pairs={{0,6},{2,4},{4,2},{6,0},{8,14},{10,12},{12,10},{14,8},{16,22},{18,... | collective-permute-start | bytes 491528 | tf_op jit(solution)/shard_map/ppermute | solution.py:61
  39.7 4.9 %collective-permute-start.10 = (bf16[1,80,256]{2,1,0:T(8,128)(2,1)S(1)}, bf16[1,80,256]{2,1,0:T(8,128)(2,1)S(1)}, u32[]{:S(2)}, u32[]{:S(2)}) collective-permute-start(bf16[1,80,256]{2,1,0:T(8,128)(2,1)S(1)} %get-tuple-element.110), channel_id=1, source_target_pairs={{0,16},{2,18},{4,20},{6,22},{8,24},{10,26},{12,28},{14,30},{16,0},... | collective-permute-start | bytes 122888 | tf_op jit(solution)/shard_map/ppermute | solution.py:61
  41.9 6.0 %collective-permute-start.11 = (bf16[1,80,256]{2,1,0:T(8,128)(2,1)S(1)}, bf16[1,80,256]{2,1,0:T(8,128)(2,1)S(1)}, u32[]{:S(2)}, u32[]{:S(2)}) collective-permute-start(bf16[1,80,256]{2,1,0:T(8,128)(2,1)S(1)} %get-tuple-element.111), channel_id=1, source_target_pairs={{0,24},{2,26},{4,28},{6,30},{8,16},{10,18},{12,20},{14,22},{16,8},... | collective-permute-start | bytes 122888 | tf_op jit(solution)/shard_map/ppermute | solution.py:61
  48.2 5.9 %collective-permute-start.14 = (bf16[1,80,256]{2,1,0:T(8,128)(2,1)S(1)}, bf16[1,80,256]{2,1,0:T(8,128)(2,1)S(1)}, u32[]{:S(2)}, u32[]{:S(2)}) collective-permute-start(bf16[1,80,256]{2,1,0:T(8,128)(2,1)S(1)} %get-tuple-element.113), channel_id=1, source_target_pairs={{0,24},{2,26},{4,28},{6,30},{8,16},{10,18},{12,20},{14,22},{16,8},... | collective-permute-start | bytes 122888 | tf_op jit(solution)/shard_map/ppermute | solution.py:61
  50.3 4.9 %collective-permute-start.13 = (bf16[1,80,256]{2,1,0:T(8,128)(2,1)S(1)}, bf16[1,80,256]{2,1,0:T(8,128)(2,1)S(1)}, u32[]{:S(2)}, u32[]{:S(2)}) collective-permute-start(bf16[1,80,256]{2,1,0:T(8,128)(2,1)S(1)} %get-tuple-element.113), channel_id=1, source_target_pairs={{0,16},{2,18},{4,20},{6,22},{8,24},{10,26},{12,28},{14,30},{16,0},... | collective-permute-start | bytes 122888 | tf_op jit(solution)/shard_map/ppermute | solution.py:61
  50.3 4.9 %collective-permute-start.12 = (bf16[1,80,256]{2,1,0:T(8,128)(2,1)S(1)}, bf16[1,80,256]{2,1,0:T(8,128)(2,1)S(1)}, u32[]{:S(2)}, u32[]{:S(2)}) collective-permute-start(bf16[1,80,256]{2,1,0:T(8,128)(2,1)S(1)} %get-tuple-element.113), channel_id=1, source_target_pairs={{0,8},{2,10},{4,12},{6,14},{8,0},{10,2},{12,4},{14,6},{16,24},{18,... | collective-permute-start | bytes 122888 | tf_op jit(solution)/shard_map/ppermute | solution.py:61
  55.2 7.8 %collective-permute-start.15 = (bf16[4,80,256]{2,1,0:T(8,128)(2,1)S(1)}, bf16[4,80,256]{2,1,0:T(8,128)(2,1)S(1)}, u32[]{:S(2)}, u32[]{:S(2)}) collective-permute-start(bf16[4,80,256]{2,1,0:T(8,128)(2,1)S(1)} %maximum_bitcast_fusion.1.refs_0_), channel_id=1, source_target_pairs={{0,2},{2,0},{4,6},{6,4},{8,10},{10,8},{12,14},{14,12},{16,18},{18,... | collective-permute-start | bytes 491528 | tf_op jit(solution)/shard_map/ppermute | solution.py:61
  57.1 5.9 %collective-permute-start.16 = (bf16[4,80,256]{2,1,0:T(8,128)(2,1)S(1)}, bf16[4,80,256]{2,1,0:T(8,128)(2,1)S(1)}, u32[]{:S(2)}, u32[]{:S(2)}) collective-permute-start(bf16[4,80,256]{2,1,0:T(8,128)(2,1)S(1)} %maximum_bitcast_fusion.1.refs_0_), channel_id=1, source_target_pairs={{0,4},{2,6},{4,0},{6,2},{8,12},{10,14},{12,8},{14,10},{16,20},{18,... | collective-permute-start | bytes 491528 | tf_op jit(solution)/shard_map/ppermute | solution.py:61
  58.2 6.2 %collective-permute-start.17 = (bf16[4,80,256]{2,1,0:T(8,128)(2,1)S(1)}, bf16[4,80,256]{2,1,0:T(8,128)(2,1)S(1)}, u32[]{:S(2)}, u32[]{:S(2)}) collective-permute-start(bf16[4,80,256]{2,1,0:T(8,128)(2,1)S(1)} %maximum_bitcast_fusion.1.refs_0_), channel_id=1, source_target_pairs={{0,6},{2,4},{4,2},{6,0},{8,14},{10,12},{12,10},{14,8},{16,22},{18,... | collective-permute-start | bytes 491528 | tf_op jit(solution)/shard_map/ppermute | solution.py:61
  69.0 9.0 %collective-permute-start.20 = (bf16[4,32,1024]{2,1,0:T(8,128)(2,1)S(1)}, bf16[4,32,1024]{2,1,0:T(8,128)(2,1)S(1)}, u32[]{:S(2)}, u32[]{:S(2)}) collective-permute-start(bf16[4,32,1024]{2,1,0:T(8,128)(2,1)S(1)} %get-tuple-element.126), channel_id=1, source_target_pairs={{0,6},{2,4},{4,2},{6,0},{8,14},{10,12},{12,10},{14,8},{16,22},{18,... | collective-permute-start | bytes 786440 | tf_op jit(solution)/shard_map/ppermute | solution.py:61
  70.1 9.1 %collective-permute-start.19 = (bf16[4,32,1024]{2,1,0:T(8,128)(2,1)S(1)}, bf16[4,32,1024]{2,1,0:T(8,128)(2,1)S(1)}, u32[]{:S(2)}, u32[]{:S(2)}) collective-permute-start(bf16[4,32,1024]{2,1,0:T(8,128)(2,1)S(1)} %get-tuple-element.125), channel_id=1, source_target_pairs={{0,4},{2,6},{4,0},{6,2},{8,12},{10,14},{12,8},{14,10},{16,20},{18,... | collective-permute-start | bytes 786440 | tf_op jit(solution)/shard_map/ppermute | solution.py:61
  71.1 8.1 %collective-permute-start.18 = (bf16[4,32,1024]{2,1,0:T(8,128)(2,1)S(1)}, bf16[4,32,1024]{2,1,0:T(8,128)(2,1)S(1)}, u32[]{:S(2)}, u32[]{:S(2)}) collective-permute-start(bf16[4,32,1024]{2,1,0:T(8,128)(2,1)S(1)} %get-tuple-element.124), channel_id=1, source_target_pairs={{0,2},{2,0},{4,6},{6,4},{8,10},{10,8},{12,14},{14,12},{16,18},{18,... | collective-permute-start | bytes 786440 | tf_op jit(solution)/shard_map/ppermute | solution.py:61
  79.4 9.1 %collective-permute-start.23 = (bf16[1,32,1024]{2,1,0:T(8,128)(2,1)S(1)}, bf16[1,32,1024]{2,1,0:T(8,128)(2,1)S(1)}, u32[]{:S(2)}, u32[]{:S(2)}) collective-permute-start(bf16[1,32,1024]{2,1,0:T(8,128)(2,1)S(1)} %get-tuple-element.180), channel_id=1, source_target_pairs={{0,24},{2,26},{4,28},{6,30},{8,16},{10,18},{12,20},{14,22},{16,8},... | collective-permute-start | bytes 196616 | tf_op jit(solution)/shard_map/ppermute | solution.py:61
  81.4 8.1 %collective-permute-start.22 = (bf16[1,32,1024]{2,1,0:T(8,128)(2,1)S(1)}, bf16[1,32,1024]{2,1,0:T(8,128)(2,1)S(1)}, u32[]{:S(2)}, u32[]{:S(2)}) collective-permute-start(bf16[1,32,1024]{2,1,0:T(8,128)(2,1)S(1)} %get-tuple-element.181), channel_id=1, source_target_pairs={{0,16},{2,18},{4,20},{6,22},{8,24},{10,26},{12,28},{14,30},{16,0},... | collective-permute-start | bytes 196616 | tf_op jit(solution)/shard_map/ppermute | solution.py:61
  82.5 7.0 %collective-permute-start.21 = (bf16[1,32,1024]{2,1,0:T(8,128)(2,1)S(1)}, bf16[1,32,1024]{2,1,0:T(8,128)(2,1)S(1)}, u32[]{:S(2)}, u32[]{:S(2)}) collective-permute-start(bf16[1,32,1024]{2,1,0:T(8,128)(2,1)S(1)} %get-tuple-element.179), channel_id=1, source_target_pairs={{0,8},{2,10},{4,12},{6,14},{8,0},{10,2},{12,4},{14,6},{16,24},{18,... | collective-permute-start | bytes 196616 | tf_op jit(solution)/shard_map/ppermute | solution.py:61
  89.5 6.1 %collective-permute-start.26 = (bf16[4,16,1024]{2,1,0:T(8,128)(2,1)S(1)}, bf16[4,16,1024]{2,1,0:T(8,128)(2,1)S(1)}, u32[]{:S(2)}, u32[]{:S(2)}) collective-permute-start(bf16[4,16,1024]{2,1,0:T(8,128)(2,1)S(1)} %get-tuple-element.148), channel_id=1, source_target_pairs={{0,6},{2,4},{4,2},{6,0},{8,14},{10,12},{12,10},{14,8},{16,22},{18,... | collective-permute-start | bytes 393224 | tf_op jit(solution)/shard_map/ppermute | solution.py:61
  89.6 7.9 %collective-permute-start.25 = (bf16[4,16,1024]{2,1,0:T(8,128)(2,1)S(1)}, bf16[4,16,1024]{2,1,0:T(8,128)(2,1)S(1)}, u32[]{:S(2)}, u32[]{:S(2)}) collective-permute-start(bf16[4,16,1024]{2,1,0:T(8,128)(2,1)S(1)} %get-tuple-element.147), channel_id=1, source_target_pairs={{0,4},{2,6},{4,0},{6,2},{8,12},{10,14},{12,8},{14,10},{16,20},{18,... | collective-permute-start | bytes 393224 | tf_op jit(solution)/shard_map/ppermute | solution.py:61
  90.9 6.7 %collective-permute-start.24 = (bf16[4,16,1024]{2,1,0:T(8,128)(2,1)S(1)}, bf16[4,16,1024]{2,1,0:T(8,128)(2,1)S(1)}, u32[]{:S(2)}, u32[]{:S(2)}) collective-permute-start(bf16[4,16,1024]{2,1,0:T(8,128)(2,1)S(1)} %get-tuple-element.146), channel_id=1, source_target_pairs={{0,2},{2,0},{4,6},{6,4},{8,10},{10,8},{12,14},{14,12},{16,18},{18,... | collective-permute-start | bytes 393224 | tf_op jit(solution)/shard_map/ppermute | solution.py:61
  93.1 8.2 %collective-permute-start.27 = (bf16[1,32,1024]{2,1,0:T(8,128)(2,1)S(1)}, bf16[1,32,1024]{2,1,0:T(8,128)(2,1)S(1)}, u32[]{:S(2)}, u32[]{:S(2)}) collective-permute-start(bf16[1,32,1024]{2,1,0:T(8,128)(2,1)S(1)} %bitcast.49), channel_id=1, source_target_pairs={{0,8},{2,10},{4,12},{6,14},{8,0},{10,2},{12,4},{14,6},{16,24},{18,... | collective-permute-start | bytes 196616 | tf_op jit(solution)/shard_map/ppermute | solution.py:61
  93.1 8.2 %collective-permute-start.28 = (bf16[1,32,1024]{2,1,0:T(8,128)(2,1)S(1)}, bf16[1,32,1024]{2,1,0:T(8,128)(2,1)S(1)}, u32[]{:S(2)}, u32[]{:S(2)}) collective-permute-start(bf16[1,32,1024]{2,1,0:T(8,128)(2,1)S(1)} %bitcast.50), channel_id=1, source_target_pairs={{0,16},{2,18},{4,20},{6,22},{8,24},{10,26},{12,28},{14,30},{16,0},... | collective-permute-start | bytes 196616 | tf_op jit(solution)/shard_map/ppermute | solution.py:61
  95.6 6.1 %collective-permute-start.29 = (bf16[1,32,1024]{2,1,0:T(8,128)(2,1)S(1)}, bf16[1,32,1024]{2,1,0:T(8,128)(2,1)S(1)}, u32[]{:S(2)}, u32[]{:S(2)}) collective-permute-start(bf16[1,32,1024]{2,1,0:T(8,128)(2,1)S(1)} %bitcast.51), channel_id=1, source_target_pairs={{0,24},{2,26},{4,28},{6,30},{8,16},{10,18},{12,20},{14,22},{16,8},... | collective-permute-start | bytes 196616 | tf_op jit(solution)/shard_map/ppermute | solution.py:61
  101.7 12.9 %collective-permute-start.33 = (bf16[1024,512]{1,0:T(8,128)(2,1)S(1)}, bf16[1024,512]{1,0:T(8,128)(2,1)S(1)}, u32[]{:S(2)}, u32[]{:S(2)}) collective-permute-start(bf16[1024,512]{1,0:T(8,128)(2,1)S(1)} %part.1), channel_id=1, source_target_pairs={{0,1},{1,0},{2,3},{3,2},{4,5},{5,4},{6,7},{7,6},{8,9},{9,8},{10,11... | collective-permute-start | bytes 3145736 | tf_op jit(solution)/shard_map/ppermute | solution.py:777
  101.8 15.2 %collective-permute-start.30 = (bf16[4,32,1024]{2,1,0:T(8,128)(2,1)S(1)}, bf16[4,32,1024]{2,1,0:T(8,128)(2,1)S(1)}, u32[]{:S(2)}, u32[]{:S(2)}) collective-permute-start(bf16[4,32,1024]{2,1,0:T(8,128)(2,1)S(1)} %maximum_bitcast_fusion.refs_0_), channel_id=1, source_target_pairs={{0,2},{2,0},{4,6},{6,4},{8,10},{10,8},{12,14},{14,12},{16,18},{18,... | collective-permute-start | bytes 786440 | tf_op jit(solution)/shard_map/ppermute | solution.py:61
  102.1 14.9 %collective-permute-start.31 = (bf16[4,32,1024]{2,1,0:T(8,128)(2,1)S(1)}, bf16[4,32,1024]{2,1,0:T(8,128)(2,1)S(1)}, u32[]{:S(2)}, u32[]{:S(2)}) collective-permute-start(bf16[4,32,1024]{2,1,0:T(8,128)(2,1)S(1)} %maximum_bitcast_fusion.refs_0_), channel_id=1, source_target_pairs={{0,4},{2,6},{4,0},{6,2},{8,12},{10,14},{12,8},{14,10},{16,20},{18,... | collective-permute-start | bytes 786440 | tf_op jit(solution)/shard_map/ppermute | solution.py:61
  103.1 13.8 %collective-permute-start.32 = (bf16[4,32,1024]{2,1,0:T(8,128)(2,1)S(1)}, bf16[4,32,1024]{2,1,0:T(8,128)(2,1)S(1)}, u32[]{:S(2)}, u32[]{:S(2)}) collective-permute-start(bf16[4,32,1024]{2,1,0:T(8,128)(2,1)S(1)} %maximum_bitcast_fusion.refs_0_), channel_id=1, source_target_pairs={{0,6},{2,4},{4,2},{6,0},{8,14},{10,12},{12,10},{14,8},{16,22},{18,... | collective-permute-start | bytes 786440 | tf_op jit(solution)/shard_map/ppermute | solution.py:61
  106.2 6.2 %collective-permute-start.35 = (bf16[1,16,1024]{2,1,0:T(8,128)(2,1)S(1)}, bf16[1,16,1024]{2,1,0:T(8,128)(2,1)S(1)}, u32[]{:S(2)}, u32[]{:S(2)}) collective-permute-start(bf16[1,16,1024]{2,1,0:T(8,128)(2,1)S(1)} %slice.39), channel_id=1, source_target_pairs={{0,16},{2,18},{4,20},{6,22},{8,24},{10,26},{12,28},{14,30},{16,0},... | collective-permute-start | bytes 98312 | tf_op jit(solution)/shard_map/ppermute | solution.py:61
  (9 other events, 66.5 us)

commit v12 on v11

--- a/solution.py
+++ b/solution.py
@@ -727,8 +727,8 @@
         name="key_land",
     )
     half = width // 2
-    row_block = pl.BlockSpec((rows // 4, columns), lambda j, _: (j, 0))
-    half_block = pl.BlockSpec((rows // 4, half), lambda j, _: (j, 0))
+    row_block = pl.BlockSpec((rows // 2, columns), lambda j, _: (j, 0))
+    half_block = pl.BlockSpec((rows // 2, half), lambda j, _: (j, 0))
 
     if not sorted_here:
         land_pieces = split_by_partner(land_pieces[0].reshape(n, land_dev, 2 * columns), n, me)
@@ -751,7 +751,7 @@
     )
     there = call(
         part_kernel,
-        (4,),
+        (2,),
         [mine_arr],
         [attn, out_weight],
         [row_block, pl.BlockSpec((columns, half), lambda j, mine: (0, 1 - mine[0]))],
@@ -784,7 +784,7 @@
     land_own = land_own * (1.0 / seg_len)
     mixed = call(
         mixed_kernel,
-        (4,),
+        (2,),
         [mine_arr],
         [attn, out_weight, arrived],
         [row_block, pl.BlockSpec((columns, half), lambda j, mine: (0, mine[0])), half_block],

time: 119 us -> 119 us (level)
  transfers between devices with their start and end apart: 36 -> 36, of which waited for: 14 -> 15; matrix products, arithmetic and copies ran while one was open for 3% -> 3% of each run, Pallas kernels for 26% -> 25%
where the time goes in v12:
time: 119 us
  Pallas kernels  48.5 us (41%)
  starting transfers between devices  46.6 us (39%)
  waiting for transfers between devices  19 us (16%)
  matrix products  2.87 us (2%)
    pallas_call x15, Pallas kernels, call(): pl.pallas_call(kernel, grid_spec=pltpu.PrefetchScalarGridSpec(num_scalar_...  48.5 us
    ppermute x35, starting transfers between devices, exchange(): return lax.ppermute(block, 'seq', [(i, i ^ mask) for i in range(n)])  46.6 us
    ppermute x35, waiting for transfers between devices, exchange(): return lax.ppermute(block, 'seq', [(i, i ^ mask) for i in range(n)])  19 us
    dot_general x1, matrix products, dot(): lax.dot_general(left, right, (dims, ((), ())), preferred_element_type=F32)  2.87 us
  transfers between devices with their start and end apart: 36, of which 15 were waited for; matrix products, arithmetic and copies ran while one was open for 3% of the time, Pallas kernels for 25%

profile of v12, /device:TPU:0, one launch (start us, length us, event | category | flops | bytes accessed | tf_op | source)
XLA Modules:
  0.0 118.7 jit_solution(2134367173358366117)
XLA Ops:
  0.8 1.7 %means.1 = bf16[16,1024]{1,0:T(8,128)(2,1)S(1)} custom-call(bf16[1024,512]{1,0:T(8,128)(2,1)} %q_ref.5, bf16[1024,512]{1,0:T(8,128)(2,1)} %k_ref.4), custom_call_target="tpu_custom_call" | custom-call | bytes 4194304 | tf_op jit(solution)/shard_map/means/pallas_call | solution.py:500
  2.5 5.1 %collective-permute-start.2 = (bf16[1,16,1024]{2,1,0:T(8,128)(2,1)S(1)}, bf16[1,16,1024]{2,1,0:T(8,128)(2,1)S(1)}, u32[]{:S(2)}, u32[]{:S(2)}) collective-permute-start(bf16[1,16,1024]{2,1,0:T(8,128)(2,1)S(1)} %bitcast.42), channel_id=1, source_target_pairs={{0,24},{2,26},{4,28},{6,30},{8,16},{10,18},{12,20},{14,22},{16,8},... | collective-permute-start | bytes 98312 | tf_op jit(solution)/shard_map/ppermute | solution.py:61
  9.5 2.9 %collective-permute-done.1 = bf16[1,16,1024]{2,1,0:T(8,128)(2,1)S(1)} collective-permute-done((bf16[1,16,1024]{2,1,0:T(8,128)(2,1)S(1)}, bf16[1,16,1024]{2,1,0:T(8,128)(2,1)S(1)}, u32[]{:S(2)}, u32[]{:S(2)}) %collective-permute-start.1) | collective-permute-done | bytes 32800 | tf_op jit(solution)/shard_map/ppermute | solution.py:61
  12.5 1.6 %collective-permute-start.3 = (bf16[4,16,1024]{2,1,0:T(8,128)(2,1)S(1)}, bf16[4,16,1024]{2,1,0:T(8,128)(2,1)S(1)}, u32[]{:S(2)}, u32[]{:S(2)}) collective-permute-start(bf16[4,16,1024]{2,1,0:T(8,128)(2,1)S(1)} %maximum_bitcast_fusion.2.refs_0_), channel_id=1, source_target_pairs={{0,2},{2,0},{4,6},{6,4},{8,10},{10,8},{12,14},{14,12},{16,18},{18,... | collective-permute-start | bytes 393224 | tf_op jit(solution)/shard_map/ppermute | solution.py:61
  14.0 1.5 %collective-permute-start.4 = (bf16[4,16,1024]{2,1,0:T(8,128)(2,1)S(1)}, bf16[4,16,1024]{2,1,0:T(8,128)(2,1)S(1)}, u32[]{:S(2)}, u32[]{:S(2)}) collective-permute-start(bf16[4,16,1024]{2,1,0:T(8,128)(2,1)S(1)} %maximum_bitcast_fusion.2.refs_0_), channel_id=1, source_target_pairs={{0,4},{2,6},{4,0},{6,2},{8,12},{10,14},{12,8},{14,10},{16,20},{18,... | collective-permute-start | bytes 393224 | tf_op jit(solution)/shard_map/ppermute | solution.py:61
  16.0 2.9 %convolution_convert_fusion.g_ref = bf16[1024,512]{1,0:T(8,128)(2,1)S(1)} fusion(bf16[1024,1024]{1,0:T(8,128)(2,1)} %cot_ref.1, bf16[512,1024]{1,0:T(8,128)(2,1)S(1)} %copy-done), kind=kOutput, calls=%fused_computation | convolution fusion | flops 1074266112 | bytes 4194304 | tf_op jit(solution)/shard_map/dot_general | solution.py:23
  20.0 1.5 %collective-permute-done.5.refs_3_ = bf16[4,16,1024]{2,1,0:T(8,128)(2,1)S(1)} collective-permute-done((bf16[4,16,1024]{2,1,0:T(8,128)(2,1)S(1)}, bf16[4,16,1024]{2,1,0:T(8,128)(2,1)S(1)}, u32[]{:S(2)}, u32[]{:S(2)}) %collective-permute-start.5) | collective-permute-done | bytes 131104 | tf_op jit(solution)/shard_map/ppermute | solution.py:61
  21.4 10.1 %forward.1 = (bf16[1024,2048]{1,0:T(8,128)(2,1)S(1)}, bf16[1024,2048]{1,0:T(8,128)(2,1)S(1)}, f32[4,8,256]{2,1,0:T(8,128)S(1)}, bf16[256,1024]{1,0:T(8,128)(2,1)...) custom-call(s32[2]{0:T(128)S(1)} %pad_add_fusion.me_ref, ...), custom_call_target="tpu_custom_call" | custom-call | flops 8589934592 | bytes 4194304 | tf_op jit(solution)/shard_map/forward/pallas_call | solution.py:500
  32.6 2.4 %collective-permute-start.8 = (bf16[4,80,256]{2,1,0:T(8,128)(2,1)S(1)}, bf16[4,80,256]{2,1,0:T(8,128)(2,1)S(1)}, u32[]{:S(2)}, u32[]{:S(2)}) collective-permute-start(bf16[4,80,256]{2,1,0:T(8,128)(2,1)S(1)} %get-tuple-element.101), channel_id=1, source_target_pairs={{0,6},{2,4},{4,2},{6,0},{8,14},{10,12},{12,10},{14,8},{16,22},{18,... | collective-permute-start | bytes 491528 | tf_op jit(solution)/shard_map/ppermute | solution.py:61
  35.1 3.7 %newton.1 = (f32[9,256,256]{2,1,0:T(8,128)S(1)}, f32[1,256,256]{2,1,0:T(8,128)S(1)}) custom-call(s32[3]{0:T(128)S(1)} %pad_add_fusion.1.own_ref, bf16[256,1024]{1,0:T(8,128)(2,1)S(1)} %get-tuple-element.102.lq_ref.lk_ref, bf16[256,1024]{1,0:T(8,128)(2,1)S(1)} %get-tuple-element.102.lq_ref.lk_ref), custom_call_target="tpu_custom_call" | custom-call | flops 4294967296 | bytes 4194304 | tf_op jit(solution)/shard_map/newton/pallas_call | solution.py:500
  39.7 2.1 %collective-permute-start.10 = (bf16[1,80,256]{2,1,0:T(8,128)(2,1)S(1)}, bf16[1,80,256]{2,1,0:T(8,128)(2,1)S(1)}, u32[]{:S(2)}, u32[]{:S(2)}) collective-permute-start(bf16[1,80,256]{2,1,0:T(8,128)(2,1)S(1)} %get-tuple-element.110), channel_id=1, source_target_pairs={{0,16},{2,18},{4,20},{6,22},{8,24},{10,26},{12,28},{14,30},{16,0},... | collective-permute-start | bytes 122888 | tf_op jit(solution)/shard_map/ppermute | solution.py:61
  41.9 1.9 %collective-permute-start.11 = (bf16[1,80,256]{2,1,0:T(8,128)(2,1)S(1)}, bf16[1,80,256]{2,1,0:T(8,128)(2,1)S(1)}, u32[]{:S(2)}, u32[]{:S(2)}) collective-permute-start(bf16[1,80,256]{2,1,0:T(8,128)(2,1)S(1)} %get-tuple-element.111), channel_id=1, source_target_pairs={{0,24},{2,26},{4,28},{6,30},{8,16},{10,18},{12,20},{14,22},{16,8},... | collective-permute-start | bytes 122888 | tf_op jit(solution)/shard_map/ppermute | solution.py:61
  44.6 3.3 %collective-permute-done.11.refs_3_ = bf16[1,80,256]{2,1,0:T(8,128)(2,1)S(1)} collective-permute-done((bf16[1,80,256]{2,1,0:T(8,128)(2,1)S(1)}, bf16[1,80,256]{2,1,0:T(8,128)(2,1)S(1)}, u32[]{:S(2)}, u32[]{:S(2)}) %collective-permute-start.11) | collective-permute-done | bytes 40992 | tf_op jit(solution)/shard_map/ppermute | solution.py:61
  48.2 2.0 %collective-permute-start.14 = (bf16[1,80,256]{2,1,0:T(8,128)(2,1)S(1)}, bf16[1,80,256]{2,1,0:T(8,128)(2,1)S(1)}, u32[]{:S(2)}, u32[]{:S(2)}) collective-permute-start(bf16[1,80,256]{2,1,0:T(8,128)(2,1)S(1)} %get-tuple-element.113), channel_id=1, source_target_pairs={{0,24},{2,26},{4,28},{6,30},{8,16},{10,18},{12,20},{14,22},{16,8},... | collective-permute-start | bytes 122888 | tf_op jit(solution)/shard_map/ppermute | solution.py:61
  50.3 2.4 %collective-permute-start.12 = (bf16[1,80,256]{2,1,0:T(8,128)(2,1)S(1)}, bf16[1,80,256]{2,1,0:T(8,128)(2,1)S(1)}, u32[]{:S(2)}, u32[]{:S(2)}) collective-permute-start(bf16[1,80,256]{2,1,0:T(8,128)(2,1)S(1)} %get-tuple-element.113), channel_id=1, source_target_pairs={{0,8},{2,10},{4,12},{6,14},{8,0},{10,2},{12,4},{14,6},{16,24},{18,... | collective-permute-start | bytes 122888 | tf_op jit(solution)/shard_map/ppermute | solution.py:61
  55.2 1.9 %collective-permute-start.15 = (bf16[4,80,256]{2,1,0:T(8,128)(2,1)S(1)}, bf16[4,80,256]{2,1,0:T(8,128)(2,1)S(1)}, u32[]{:S(2)}, u32[]{:S(2)}) collective-permute-start(bf16[4,80,256]{2,1,0:T(8,128)(2,1)S(1)} %maximum_bitcast_fusion.1.refs_0_), channel_id=1, source_target_pairs={{0,2},{2,0},{4,6},{6,4},{8,10},{10,8},{12,14},{14,12},{16,18},{18,... | collective-permute-start | bytes 491528 | tf_op jit(solution)/shard_map/ppermute | solution.py:61
  58.8 4.3 %newton_grad.1 = (f32[256,128]{1,0:T(8,128)S(1)}, f32[256,128]{1,0:T(8,128)S(1)}) custom-call(s32[3]{0:T(128)S(1)} %pad_add_fusion.1.own_ref, f32[9,256,256]{2,1,0:T(8,128)S(1)} %get-tuple-element.114.saved_ref, f32[32,256]{1,0:T(8,128)S(1)} %get-tuple-element.115.values_ref, f32[32,256]{1,0:T(8,128)S(1)} %get-tuple-element.116.grads_ref, ...), custom_call_target="tpu_custom_call" | custom-call | flops 8589934592 | bytes 4194304 | tf_op jit(solution)/shard_map/newton_grad/pallas_call | solution.py:500
  64.4 4.7 %attend.1 = (bf16[1024,512]{1,0:T(8,128)(2,1)S(1)}, bf16[512,256]{1,0:T(8,128)(2,1)S(1)}, bf16[512,256]{1,0:T(8,128)(2,1)S(1)}, f32[8,256]{1,0:T(8,128)S(1)}, bf...) custom-call(s32[2]{0:T(128)S(1)} %pad_add_fusion.me_ref, ...), custom_call_target="tpu_custom_call" | custom-call | flops 4294967296 | bytes 4194304 | tf_op jit(solution)/shard_map/attend/pallas_call | solution.py:500
  71.1 1.5 %collective-permute-start.18 = (bf16[4,32,1024]{2,1,0:T(8,128)(2,1)S(1)}, bf16[4,32,1024]{2,1,0:T(8,128)(2,1)S(1)}, u32[]{:S(2)}, u32[]{:S(2)}) collective-permute-start(bf16[4,32,1024]{2,1,0:T(8,128)(2,1)S(1)} %get-tuple-element.124), channel_id=1, source_target_pairs={{0,2},{2,0},{4,6},{6,4},{8,10},{10,8},{12,14},{14,12},{16,18},{18,... | collective-permute-start | bytes 786440 | tf_op jit(solution)/shard_map/ppermute | solution.py:61
  72.6 5.4 %query_land.1 = (bf16[256,512]{1,0:T(8,128)(2,1)S(1)}, bf16[1024,2048]{1,0:T(8,128)(2,1)S(1)}) custom-call(s32[3]{0:T(128)S(1)} %pad_add_fusion.1.own_ref, bf16[1024,512]{1,0:T(8,128)(2,1)S(1)} %copy-done.1, bf16[1024,512]{1,0:T(8,128)(2,1)S(1)} %convolution_convert_fusion.g_ref, bf16[1024,2048]{1,0:T(8,128)(2,1)S(1)} %get-tuple-element.96.fb_ref, ...), custom_call_target="tpu_custom_call" | custom-call | flops 4294967296 | bytes 4194304 | tf_op jit(solution)/shard_map/query_land/pallas_call | solution.py:500
  79.4 2.0 %collective-permute-start.23 = (bf16[1,32,1024]{2,1,0:T(8,128)(2,1)S(1)}, bf16[1,32,1024]{2,1,0:T(8,128)(2,1)S(1)}, u32[]{:S(2)}, u32[]{:S(2)}) collective-permute-start(bf16[1,32,1024]{2,1,0:T(8,128)(2,1)S(1)} %get-tuple-element.180), channel_id=1, source_target_pairs={{0,24},{2,26},{4,28},{6,30},{8,16},{10,18},{12,20},{14,22},{16,8},... | collective-permute-start | bytes 196616 | tf_op jit(solution)/shard_map/ppermute | solution.py:61
  83.8 4.6 %key_land.1 = (bf16[1024,2048]{1,0:T(8,128)(2,1)S(1)}, bf16[4,16,1024]{2,1,0:T(8,128)(2,1)S(1)}, bf16[4,16,1024]{2,1,0:T(8,128)(2,1)S(1)}, bf16[4,16,1024]{2,1,0:T(8,128)(2,1)S(1)}, bf16[4,16,1024]{2,1,0:T(8,128)(2,1)S(1)}) custom-call(s32[3]{0:T(128)S(1)} %pad_add_fusion.1.own_ref, bf16[1024,512]{1,0:T(8,128)(2,1)S(1)} %copy-done.2, ...), custom_call_target="tpu_custom_call" | custom-call | flops 4294967296 | bytes 4194304 | tf_op jit(solution)/shard_map/key_land/pallas_call | solution.py:500
  90.9 2.2 %collective-permute-start.24 = (bf16[4,16,1024]{2,1,0:T(8,128)(2,1)S(1)}, bf16[4,16,1024]{2,1,0:T(8,128)(2,1)S(1)}, u32[]{:S(2)}, u32[]{:S(2)}) collective-permute-start(bf16[4,16,1024]{2,1,0:T(8,128)(2,1)S(1)} %get-tuple-element.146), channel_id=1, source_target_pairs={{0,2},{2,0},{4,6},{6,4},{8,10},{10,8},{12,14},{14,12},{16,18},{18,... | collective-permute-start | bytes 393224 | tf_op jit(solution)/shard_map/ppermute | solution.py:61
  93.1 2.5 %collective-permute-start.28 = (bf16[1,32,1024]{2,1,0:T(8,128)(2,1)S(1)}, bf16[1,32,1024]{2,1,0:T(8,128)(2,1)S(1)}, u32[]{:S(2)}, u32[]{:S(2)}) collective-permute-start(bf16[1,32,1024]{2,1,0:T(8,128)(2,1)S(1)} %bitcast.50), channel_id=1, source_target_pairs={{0,16},{2,18},{4,20},{6,22},{8,24},{10,26},{12,28},{14,30},{16,0},... | collective-permute-start | bytes 196616 | tf_op jit(solution)/shard_map/ppermute | solution.py:61
  95.6 1.9 %collective-permute-start.29 = (bf16[1,32,1024]{2,1,0:T(8,128)(2,1)S(1)}, bf16[1,32,1024]{2,1,0:T(8,128)(2,1)S(1)}, u32[]{:S(2)}, u32[]{:S(2)}) collective-permute-start(bf16[1,32,1024]{2,1,0:T(8,128)(2,1)S(1)} %bitcast.51), channel_id=1, source_target_pairs={{0,24},{2,26},{4,28},{6,30},{8,16},{10,18},{12,20},{14,22},{16,8},... | collective-permute-start | bytes 196616 | tf_op jit(solution)/shard_map/ppermute | solution.py:61
  97.6 2.3 %query_grad.1.query_ref = bf16[1024,512]{1,0:T(8,128)(2,1)S(1)} custom-call(bf16[1024,2048]{1,0:T(8,128)(2,1)S(1)} %get-tuple-element.153.ds_ref, bf16[256,1024]{1,0:T(8,128)(2,1)S(1)} %get-tuple-element.102.lq_ref.lk_ref), custom_call_target="tpu_custom_call" | custom-call | flops 2147483648 | bytes 4194304 | tf_op jit(solution)/shard_map/query_grad/pallas_call | solution.py:500
  102.9 2.4 %collective-permute-start.32 = (bf16[4,32,1024]{2,1,0:T(8,128)(2,1)S(1)}, bf16[4,32,1024]{2,1,0:T(8,128)(2,1)S(1)}, u32[]{:S(2)}, u32[]{:S(2)}) collective-permute-start(bf16[4,32,1024]{2,1,0:T(8,128)(2,1)S(1)} %maximum_bitcast_fusion.refs_0_), channel_id=1, source_target_pairs={{0,6},{2,4},{4,2},{6,0},{8,14},{10,12},{12,10},{14,8},{16,22},{18,... | collective-permute-start | bytes 786440 | tf_op jit(solution)/shard_map/ppermute | solution.py:61
  106.2 1.7 %collective-permute-start.35 = (bf16[1,16,1024]{2,1,0:T(8,128)(2,1)S(1)}, bf16[1,16,1024]{2,1,0:T(8,128)(2,1)S(1)}, u32[]{:S(2)}, u32[]{:S(2)}) collective-permute-start(bf16[1,16,1024]{2,1,0:T(8,128)(2,1)S(1)} %slice.39), channel_id=1, source_target_pairs={{0,16},{2,18},{4,20},{6,22},{8,24},{10,26},{12,28},{14,30},{16,0},... | collective-permute-start | bytes 98312 | tf_op jit(solution)/shard_map/ppermute | solution.py:61
  107.9 4.5 %key_grad.1 = (bf16[1024,512]{1,0:T(8,128)(2,1)S(1)}, bf16[1024,512]{1,0:T(8,128)(2,1)}) custom-call(bf16[1024,2048]{1,0:T(8,128)(2,1)S(1)} %get-tuple-element.169.ds_ref, bf16[1024,2048]{1,0:T(8,128)(2,1)S(1)} %get-tuple-element.135.pb_ref, bf16[256,1024]{1,0:T(8,128)(2,1)S(1)} %get-tuple-element.102.lq_ref.lk_ref, ...), custom_call_target="tpu_custom_call" | custom-call | flops 4294967296 | bytes 4194304 | tf_op jit(solution)/shard_map/key_grad/pallas_call | solution.py:500
  112.4 2.2 %finish.1 = (bf16[1024,512]{1,0:T(8,128)(2,1)}, bf16[1024,512]{1,0:T(8,128)(2,1)}) custom-call(bf16[1024,512]{1,0:T(8,128)(2,1)S(1)} %query_grad.1.query_ref, bf16[1024,512]{1,0:T(8,128)(2,1)S(1)} %get-tuple-element.170.key_ref, f32[16,1024]{1,0:T(8,128)S(1)} %multiply_bitcast_fusion.query_own_ref.key_own_ref, ...), custom_call_target="tpu_custom_call" | custom-call | bytes 4194304 | tf_op jit(solution)/shard_map/finish/pallas_call | solution.py:500
  114.6 1.7 %mixed.1 = bf16[1024,512]{1,0:T(8,128)(2,1)} custom-call(s32[1]{0:T(128)} %bitcast.1._, bf16[1024,512]{1,0:T(8,128)(2,1)S(1)} %get-tuple-element.155.attn_ref, bf16[512,1024]{1,0:T(8,128)(2,1)S(1)} %copy-done, bf16[1024,512]{1,0:T(8,128)(2,1)S(1)} %collective-permute-done.33.other_ref), custom_call_target="tpu_custom_call" | custom-call | flops 1073741824 | bytes 4194304 | tf_op jit(solution)/shard_map/mixed/pallas_call | solution.py:500
  116.6 2.0 %unpack.1 = f32[512,1024]{1,0:T(8,128)} custom-call(s32[2]{0:T(128)S(1)} %pad_add_fusion.me_ref, bf16[4,32,1024]{2,1,0:T(8,128)(2,1)S(1)} %maximum_bitcast_fusion.refs_0_, bf16[4,32,1024]{2,1,0:T(8,128)(2,1)S(1)} %collective-permute-done.30.refs_1_, bf16[4,32,1024]{2,1,0:T(8,128)(2,1)S(1)} %collective-permute-done.31.refs_2_, ...), custom_call_target="tpu_custom_call" | custom-call | bytes 4194304 | tf_op jit(solution)/shard_map/unpack/pallas_call | solution.py:500
  (79 shorter events, 24.8 us)
Async XLA Ops:
  2.5 7.0 %collective-permute-start.2 = (bf16[1,16,1024]{2,1,0:T(8,128)(2,1)S(1)}, bf16[1,16,1024]{2,1,0:T(8,128)(2,1)S(1)}, u32[]{:S(2)}, u32[]{:S(2)}) collective-permute-start(bf16[1,16,1024]{2,1,0:T(8,128)(2,1)S(1)} %bitcast.42), channel_id=1, source_target_pairs={{0,24},{2,26},{4,28},{6,30},{8,16},{10,18},{12,20},{14,22},{16,8},... | collective-permute-start | bytes 98312 | tf_op jit(solution)/shard_map/ppermute | solution.py:61
  12.5 6.4 %collective-permute-start.3 = (bf16[4,16,1024]{2,1,0:T(8,128)(2,1)S(1)}, bf16[4,16,1024]{2,1,0:T(8,128)(2,1)S(1)}, u32[]{:S(2)}, u32[]{:S(2)}) collective-permute-start(bf16[4,16,1024]{2,1,0:T(8,128)(2,1)S(1)} %maximum_bitcast_fusion.2.refs_0_), channel_id=1, source_target_pairs={{0,2},{2,0},{4,6},{6,4},{8,10},{10,8},{12,14},{14,12},{16,18},{18,... | collective-permute-start | bytes 393224 | tf_op jit(solution)/shard_map/ppermute | solution.py:61
  14.0 5.9 %collective-permute-start.4 = (bf16[4,16,1024]{2,1,0:T(8,128)(2,1)S(1)}, bf16[4,16,1024]{2,1,0:T(8,128)(2,1)S(1)}, u32[]{:S(2)}, u32[]{:S(2)}) collective-permute-start(bf16[4,16,1024]{2,1,0:T(8,128)(2,1)S(1)} %maximum_bitcast_fusion.2.refs_0_), channel_id=1, source_target_pairs={{0,4},{2,6},{4,0},{6,2},{8,12},{10,14},{12,8},{14,10},{16,20},{18,... | collective-permute-start | bytes 393224 | tf_op jit(solution)/shard_map/ppermute | solution.py:61
  15.6 5.9 %collective-permute-start.5 = (bf16[4,16,1024]{2,1,0:T(8,128)(2,1)S(1)}, bf16[4,16,1024]{2,1,0:T(8,128)(2,1)S(1)}, u32[]{:S(2)}, u32[]{:S(2)}) collective-permute-start(bf16[4,16,1024]{2,1,0:T(8,128)(2,1)S(1)} %maximum_bitcast_fusion.2.refs_0_), channel_id=1, source_target_pairs={{0,6},{2,4},{4,2},{6,0},{8,14},{10,12},{12,10},{14,8},{16,22},{18,... | collective-permute-start | bytes 393224 | tf_op jit(solution)/shard_map/ppermute | solution.py:61
  31.5 7.2 %collective-permute-start.6 = (bf16[4,80,256]{2,1,0:T(8,128)(2,1)S(1)}, bf16[4,80,256]{2,1,0:T(8,128)(2,1)S(1)}, u32[]{:S(2)}, u32[]{:S(2)}) collective-permute-start(bf16[4,80,256]{2,1,0:T(8,128)(2,1)S(1)} %get-tuple-element.99), channel_id=1, source_target_pairs={{0,2},{2,0},{4,6},{6,4},{8,10},{10,8},{12,14},{14,12},{16,18},{18,... | collective-permute-start | bytes 491528 | tf_op jit(solution)/shard_map/ppermute | solution.py:61
  32.1 6.6 %collective-permute-start.7 = (bf16[4,80,256]{2,1,0:T(8,128)(2,1)S(1)}, bf16[4,80,256]{2,1,0:T(8,128)(2,1)S(1)}, u32[]{:S(2)}, u32[]{:S(2)}) collective-permute-start(bf16[4,80,256]{2,1,0:T(8,128)(2,1)S(1)} %get-tuple-element.100), channel_id=1, source_target_pairs={{0,4},{2,6},{4,0},{6,2},{8,12},{10,14},{12,8},{14,10},{16,20},{18,... | collective-permute-start | bytes 491528 | tf_op jit(solution)/shard_map/ppermute | solution.py:61
  32.6 6.6 %collective-permute-start.8 = (bf16[4,80,256]{2,1,0:T(8,128)(2,1)S(1)}, bf16[4,80,256]{2,1,0:T(8,128)(2,1)S(1)}, u32[]{:S(2)}, u32[]{:S(2)}) collective-permute-start(bf16[4,80,256]{2,1,0:T(8,128)(2,1)S(1)} %get-tuple-element.101), channel_id=1, source_target_pairs={{0,6},{2,4},{4,2},{6,0},{8,14},{10,12},{12,10},{14,8},{16,22},{18,... | collective-permute-start | bytes 491528 | tf_op jit(solution)/shard_map/ppermute | solution.py:61
  39.7 4.9 %collective-permute-start.10 = (bf16[1,80,256]{2,1,0:T(8,128)(2,1)S(1)}, bf16[1,80,256]{2,1,0:T(8,128)(2,1)S(1)}, u32[]{:S(2)}, u32[]{:S(2)}) collective-permute-start(bf16[1,80,256]{2,1,0:T(8,128)(2,1)S(1)} %get-tuple-element.110), channel_id=1, source_target_pairs={{0,16},{2,18},{4,20},{6,22},{8,24},{10,26},{12,28},{14,30},{16,0},... | collective-permute-start | bytes 122888 | tf_op jit(solution)/shard_map/ppermute | solution.py:61
  41.9 6.0 %collective-permute-start.11 = (bf16[1,80,256]{2,1,0:T(8,128)(2,1)S(1)}, bf16[1,80,256]{2,1,0:T(8,128)(2,1)S(1)}, u32[]{:S(2)}, u32[]{:S(2)}) collective-permute-start(bf16[1,80,256]{2,1,0:T(8,128)(2,1)S(1)} %get-tuple-element.111), channel_id=1, source_target_pairs={{0,24},{2,26},{4,28},{6,30},{8,16},{10,18},{12,20},{14,22},{16,8},... | collective-permute-start | bytes 122888 | tf_op jit(solution)/shard_map/ppermute | solution.py:61
  48.2 5.9 %collective-permute-start.14 = (bf16[1,80,256]{2,1,0:T(8,128)(2,1)S(1)}, bf16[1,80,256]{2,1,0:T(8,128)(2,1)S(1)}, u32[]{:S(2)}, u32[]{:S(2)}) collective-permute-start(bf16[1,80,256]{2,1,0:T(8,128)(2,1)S(1)} %get-tuple-element.113), channel_id=1, source_target_pairs={{0,24},{2,26},{4,28},{6,30},{8,16},{10,18},{12,20},{14,22},{16,8},... | collective-permute-start | bytes 122888 | tf_op jit(solution)/shard_map/ppermute | solution.py:61
  50.3 4.9 %collective-permute-start.13 = (bf16[1,80,256]{2,1,0:T(8,128)(2,1)S(1)}, bf16[1,80,256]{2,1,0:T(8,128)(2,1)S(1)}, u32[]{:S(2)}, u32[]{:S(2)}) collective-permute-start(bf16[1,80,256]{2,1,0:T(8,128)(2,1)S(1)} %get-tuple-element.113), channel_id=1, source_target_pairs={{0,16},{2,18},{4,20},{6,22},{8,24},{10,26},{12,28},{14,30},{16,0},... | collective-permute-start | bytes 122888 | tf_op jit(solution)/shard_map/ppermute | solution.py:61
  50.3 4.9 %collective-permute-start.12 = (bf16[1,80,256]{2,1,0:T(8,128)(2,1)S(1)}, bf16[1,80,256]{2,1,0:T(8,128)(2,1)S(1)}, u32[]{:S(2)}, u32[]{:S(2)}) collective-permute-start(bf16[1,80,256]{2,1,0:T(8,128)(2,1)S(1)} %get-tuple-element.113), channel_id=1, source_target_pairs={{0,8},{2,10},{4,12},{6,14},{8,0},{10,2},{12,4},{14,6},{16,24},{18,... | collective-permute-start | bytes 122888 | tf_op jit(solution)/shard_map/ppermute | solution.py:61
  55.2 7.8 %collective-permute-start.15 = (bf16[4,80,256]{2,1,0:T(8,128)(2,1)S(1)}, bf16[4,80,256]{2,1,0:T(8,128)(2,1)S(1)}, u32[]{:S(2)}, u32[]{:S(2)}) collective-permute-start(bf16[4,80,256]{2,1,0:T(8,128)(2,1)S(1)} %maximum_bitcast_fusion.1.refs_0_), channel_id=1, source_target_pairs={{0,2},{2,0},{4,6},{6,4},{8,10},{10,8},{12,14},{14,12},{16,18},{18,... | collective-permute-start | bytes 491528 | tf_op jit(solution)/shard_map/ppermute | solution.py:61
  57.1 5.9 %collective-permute-start.16 = (bf16[4,80,256]{2,1,0:T(8,128)(2,1)S(1)}, bf16[4,80,256]{2,1,0:T(8,128)(2,1)S(1)}, u32[]{:S(2)}, u32[]{:S(2)}) collective-permute-start(bf16[4,80,256]{2,1,0:T(8,128)(2,1)S(1)} %maximum_bitcast_fusion.1.refs_0_), channel_id=1, source_target_pairs={{0,4},{2,6},{4,0},{6,2},{8,12},{10,14},{12,8},{14,10},{16,20},{18,... | collective-permute-start | bytes 491528 | tf_op jit(solution)/shard_map/ppermute | solution.py:61
  58.2 6.2 %collective-permute-start.17 = (bf16[4,80,256]{2,1,0:T(8,128)(2,1)S(1)}, bf16[4,80,256]{2,1,0:T(8,128)(2,1)S(1)}, u32[]{:S(2)}, u32[]{:S(2)}) collective-permute-start(bf16[4,80,256]{2,1,0:T(8,128)(2,1)S(1)} %maximum_bitcast_fusion.1.refs_0_), channel_id=1, source_target_pairs={{0,6},{2,4},{4,2},{6,0},{8,14},{10,12},{12,10},{14,8},{16,22},{18,... | collective-permute-start | bytes 491528 | tf_op jit(solution)/shard_map/ppermute | solution.py:61
  69.0 9.0 %collective-permute-start.20 = (bf16[4,32,1024]{2,1,0:T(8,128)(2,1)S(1)}, bf16[4,32,1024]{2,1,0:T(8,128)(2,1)S(1)}, u32[]{:S(2)}, u32[]{:S(2)}) collective-permute-start(bf16[4,32,1024]{2,1,0:T(8,128)(2,1)S(1)} %get-tuple-element.126), channel_id=1, source_target_pairs={{0,6},{2,4},{4,2},{6,0},{8,14},{10,12},{12,10},{14,8},{16,22},{18,... | collective-permute-start | bytes 786440 | tf_op jit(solution)/shard_map/ppermute | solution.py:61
  70.1 9.1 %collective-permute-start.19 = (bf16[4,32,1024]{2,1,0:T(8,128)(2,1)S(1)}, bf16[4,32,1024]{2,1,0:T(8,128)(2,1)S(1)}, u32[]{:S(2)}, u32[]{:S(2)}) collective-permute-start(bf16[4,32,1024]{2,1,0:T(8,128)(2,1)S(1)} %get-tuple-element.125), channel_id=1, source_target_pairs={{0,4},{2,6},{4,0},{6,2},{8,12},{10,14},{12,8},{14,10},{16,20},{18,... | collective-permute-start | bytes 786440 | tf_op jit(solution)/shard_map/ppermute | solution.py:61
  71.1 8.1 %collective-permute-start.18 = (bf16[4,32,1024]{2,1,0:T(8,128)(2,1)S(1)}, bf16[4,32,1024]{2,1,0:T(8,128)(2,1)S(1)}, u32[]{:S(2)}, u32[]{:S(2)}) collective-permute-start(bf16[4,32,1024]{2,1,0:T(8,128)(2,1)S(1)} %get-tuple-element.124), channel_id=1, source_target_pairs={{0,2},{2,0},{4,6},{6,4},{8,10},{10,8},{12,14},{14,12},{16,18},{18,... | collective-permute-start | bytes 786440 | tf_op jit(solution)/shard_map/ppermute | solution.py:61
  79.4 9.1 %collective-permute-start.23 = (bf16[1,32,1024]{2,1,0:T(8,128)(2,1)S(1)}, bf16[1,32,1024]{2,1,0:T(8,128)(2,1)S(1)}, u32[]{:S(2)}, u32[]{:S(2)}) collective-permute-start(bf16[1,32,1024]{2,1,0:T(8,128)(2,1)S(1)} %get-tuple-element.180), channel_id=1, source_target_pairs={{0,24},{2,26},{4,28},{6,30},{8,16},{10,18},{12,20},{14,22},{16,8},... | collective-permute-start | bytes 196616 | tf_op jit(solution)/shard_map/ppermute | solution.py:61
  81.4 8.1 %collective-permute-start.22 = (bf16[1,32,1024]{2,1,0:T(8,128)(2,1)S(1)}, bf16[1,32,1024]{2,1,0:T(8,128)(2,1)S(1)}, u32[]{:S(2)}, u32[]{:S(2)}) collective-permute-start(bf16[1,32,1024]{2,1,0:T(8,128)(2,1)S(1)} %get-tuple-element.181), channel_id=1, source_target_pairs={{0,16},{2,18},{4,20},{6,22},{8,24},{10,26},{12,28},{14,30},{16,0},... | collective-permute-start | bytes 196616 | tf_op jit(solution)/shard_map/ppermute | solution.py:61
  82.5 7.0 %collective-permute-start.21 = (bf16[1,32,1024]{2,1,0:T(8,128)(2,1)S(1)}, bf16[1,32,1024]{2,1,0:T(8,128)(2,1)S(1)}, u32[]{:S(2)}, u32[]{:S(2)}) collective-permute-start(bf16[1,32,1024]{2,1,0:T(8,128)(2,1)S(1)} %get-tuple-element.179), channel_id=1, source_target_pairs={{0,8},{2,10},{4,12},{6,14},{8,0},{10,2},{12,4},{14,6},{16,24},{18,... | collective-permute-start | bytes 196616 | tf_op jit(solution)/shard_map/ppermute | solution.py:61
  89.5 6.1 %collective-permute-start.26 = (bf16[4,16,1024]{2,1,0:T(8,128)(2,1)S(1)}, bf16[4,16,1024]{2,1,0:T(8,128)(2,1)S(1)}, u32[]{:S(2)}, u32[]{:S(2)}) collective-permute-start(bf16[4,16,1024]{2,1,0:T(8,128)(2,1)S(1)} %get-tuple-element.148), channel_id=1, source_target_pairs={{0,6},{2,4},{4,2},{6,0},{8,14},{10,12},{12,10},{14,8},{16,22},{18,... | collective-permute-start | bytes 393224 | tf_op jit(solution)/shard_map/ppermute | solution.py:61
  89.6 7.9 %collective-permute-start.25 = (bf16[4,16,1024]{2,1,0:T(8,128)(2,1)S(1)}, bf16[4,16,1024]{2,1,0:T(8,128)(2,1)S(1)}, u32[]{:S(2)}, u32[]{:S(2)}) collective-permute-start(bf16[4,16,1024]{2,1,0:T(8,128)(2,1)S(1)} %get-tuple-element.147), channel_id=1, source_target_pairs={{0,4},{2,6},{4,0},{6,2},{8,12},{10,14},{12,8},{14,10},{16,20},{18,... | collective-permute-start | bytes 393224 | tf_op jit(solution)/shard_map/ppermute | solution.py:61
  90.9 6.7 %collective-permute-start.24 = (bf16[4,16,1024]{2,1,0:T(8,128)(2,1)S(1)}, bf16[4,16,1024]{2,1,0:T(8,128)(2,1)S(1)}, u32[]{:S(2)}, u32[]{:S(2)}) collective-permute-start(bf16[4,16,1024]{2,1,0:T(8,128)(2,1)S(1)} %get-tuple-element.146), channel_id=1, source_target_pairs={{0,2},{2,0},{4,6},{6,4},{8,10},{10,8},{12,14},{14,12},{16,18},{18,... | collective-permute-start | bytes 393224 | tf_op jit(solution)/shard_map/ppermute | solution.py:61
  93.1 7.9 %collective-permute-start.27 = (bf16[1,32,1024]{2,1,0:T(8,128)(2,1)S(1)}, bf16[1,32,1024]{2,1,0:T(8,128)(2,1)S(1)}, u32[]{:S(2)}, u32[]{:S(2)}) collective-permute-start(bf16[1,32,1024]{2,1,0:T(8,128)(2,1)S(1)} %bitcast.49), channel_id=1, source_target_pairs={{0,8},{2,10},{4,12},{6,14},{8,0},{10,2},{12,4},{14,6},{16,24},{18,... | collective-permute-start | bytes 196616 | tf_op jit(solution)/shard_map/ppermute | solution.py:61
  93.1 7.9 %collective-permute-start.28 = (bf16[1,32,1024]{2,1,0:T(8,128)(2,1)S(1)}, bf16[1,32,1024]{2,1,0:T(8,128)(2,1)S(1)}, u32[]{:S(2)}, u32[]{:S(2)}) collective-permute-start(bf16[1,32,1024]{2,1,0:T(8,128)(2,1)S(1)} %bitcast.50), channel_id=1, source_target_pairs={{0,16},{2,18},{4,20},{6,22},{8,24},{10,26},{12,28},{14,30},{16,0},... | collective-permute-start | bytes 196616 | tf_op jit(solution)/shard_map/ppermute | solution.py:61
  95.6 6.1 %collective-permute-start.29 = (bf16[1,32,1024]{2,1,0:T(8,128)(2,1)S(1)}, bf16[1,32,1024]{2,1,0:T(8,128)(2,1)S(1)}, u32[]{:S(2)}, u32[]{:S(2)}) collective-permute-start(bf16[1,32,1024]{2,1,0:T(8,128)(2,1)S(1)} %bitcast.51), channel_id=1, source_target_pairs={{0,24},{2,26},{4,28},{6,30},{8,16},{10,18},{12,20},{14,22},{16,8},... | collective-permute-start | bytes 196616 | tf_op jit(solution)/shard_map/ppermute | solution.py:61
  101.7 12.9 %collective-permute-start.33 = (bf16[1024,512]{1,0:T(8,128)(2,1)S(1)}, bf16[1024,512]{1,0:T(8,128)(2,1)S(1)}, u32[]{:S(2)}, u32[]{:S(2)}) collective-permute-start(bf16[1024,512]{1,0:T(8,128)(2,1)S(1)} %part.1), channel_id=1, source_target_pairs={{0,1},{1,0},{2,3},{3,2},{4,5},{5,4},{6,7},{7,6},{8,9},{9,8},{10,11... | collective-permute-start | bytes 3145736 | tf_op jit(solution)/shard_map/ppermute | solution.py:777
  101.8 14.5 %collective-permute-start.30 = (bf16[4,32,1024]{2,1,0:T(8,128)(2,1)S(1)}, bf16[4,32,1024]{2,1,0:T(8,128)(2,1)S(1)}, u32[]{:S(2)}, u32[]{:S(2)}) collective-permute-start(bf16[4,32,1024]{2,1,0:T(8,128)(2,1)S(1)} %maximum_bitcast_fusion.refs_0_), channel_id=1, source_target_pairs={{0,2},{2,0},{4,6},{6,4},{8,10},{10,8},{12,14},{14,12},{16,18},{18,... | collective-permute-start | bytes 786440 | tf_op jit(solution)/shard_map/ppermute | solution.py:61
  101.9 14.4 %collective-permute-start.31 = (bf16[4,32,1024]{2,1,0:T(8,128)(2,1)S(1)}, bf16[4,32,1024]{2,1,0:T(8,128)(2,1)S(1)}, u32[]{:S(2)}, u32[]{:S(2)}) collective-permute-start(bf16[4,32,1024]{2,1,0:T(8,128)(2,1)S(1)} %maximum_bitcast_fusion.refs_0_), channel_id=1, source_target_pairs={{0,4},{2,6},{4,0},{6,2},{8,12},{10,14},{12,8},{14,10},{16,20},{18,... | collective-permute-start | bytes 786440 | tf_op jit(solution)/shard_map/ppermute | solution.py:61
  102.9 13.6 %collective-permute-start.32 = (bf16[4,32,1024]{2,1,0:T(8,128)(2,1)S(1)}, bf16[4,32,1024]{2,1,0:T(8,128)(2,1)S(1)}, u32[]{:S(2)}, u32[]{:S(2)}) collective-permute-start(bf16[4,32,1024]{2,1,0:T(8,128)(2,1)S(1)} %maximum_bitcast_fusion.refs_0_), channel_id=1, source_target_pairs={{0,6},{2,4},{4,2},{6,0},{8,14},{10,12},{12,10},{14,8},{16,22},{18,... | collective-permute-start | bytes 786440 | tf_op jit(solution)/shard_map/ppermute | solution.py:61
  106.2 6.2 %collective-permute-start.35 = (bf16[1,16,1024]{2,1,0:T(8,128)(2,1)S(1)}, bf16[1,16,1024]{2,1,0:T(8,128)(2,1)S(1)}, u32[]{:S(2)}, u32[]{:S(2)}) collective-permute-start(bf16[1,16,1024]{2,1,0:T(8,128)(2,1)S(1)} %slice.39), channel_id=1, source_target_pairs={{0,16},{2,18},{4,20},{6,22},{8,24},{10,26},{12,28},{14,30},{16,0},... | collective-permute-start | bytes 98312 | tf_op jit(solution)/shard_map/ppermute | solution.py:61
  (9 other events, 66.5 us)
